TPU v7x, 32 devices: a whole 2x2x4 slice. The times are simulated.
32 devices in a mesh: cls: 4 (over x, core), ori: 8 (over z, y).
Axes of the slice: x: 2, y: 2, z: 4, core: 2. Of those that a mesh axis runs over, the one named last changes fastest.
Arguments:
- images: bfloat16 [512, 20480], P('ori'), may hold values from -6 to 6
- projections: bfloat16 [4, 1152, 20480], P('cls', 'ori'), may hold values from -0.0390625 to 0.0390625
- log_prior: float32 [4, 1152], P('cls', 'ori'), may hold values from -4 to 300
- significant: int32 [512, 4], P('ori'), may hold values from 0 to 7, all different within a row; in each aligned block of 64 rows (0 to 63, 64 to 127, ...) at most 48 rows name the same one
- shell_index: int32 [20480], replicated, may hold values from 0 to 99
- noise_inv: float32 [100], replicated, may hold values from 0.5 to 4
Outputs:
- class_sums: bfloat16 [4, 1152, 20480], P('cls', None, 'ori')
- log_evidence: float32 [512], P('ori')
Inputs may be any that keep to these rules, and one draw needn't show every extreme that they name: `significant`: each row names 4 different blocks. Among the rows of one index of ori no block is named more than 48 times, and some block is named exactly 48 times.
All inputs are finite; a program needn't handle non-finite values.
Results may differ from a plain program's by a relative error of at most 0.0076.
Values may be sent and summed in bfloat16 or wider, within the bound.
No kernel may reach another device: no remote copies, remote signals or barrier semaphores. Data moves between devices by JAX's collectives and lax.ppermute only.
A program may use at most 128 MiB of HBM per device.

v0:
```python
import jax
import jax.numpy as jnp
from jax import lax
from jax.sharding import PartitionSpec as P

SENTINEL = -1e30


def shell_weights(noise_inv, shell_index):
    levels = jnp.arange(noise_inv.shape[0], dtype=jnp.int32)
    table = (shell_index[:, None] == levels[None, :]).astype(jnp.float32)
    return jnp.sum(table * noise_inv[None, :], axis=1)


def body(images, projections, log_prior, significant, shell_index, noise_inv):
    owners = lax.axis_size("ori")
    own_index = lax.axis_index("ori")
    img_rows, width = images.shape
    listed = significant.shape[1]
    capacity = max(2, 3 * img_rows * listed // (2 * owners))
    slot_count = owners * capacity
    weight = shell_weights(noise_inv, shell_index)
    weighted = (images.astype(jnp.float32) * weight[None, :]).astype(jnp.bfloat16)
    blocks = jnp.arange(owners, dtype=jnp.int32)
    listed_mask = jnp.any(significant[:, :, None] == blocks[None, None, :], axis=1)
    listed_int = listed_mask.astype(jnp.int32)
    ranks = jnp.cumsum(listed_int, axis=0) - listed_int
    places = jnp.arange(capacity, dtype=jnp.int32)
    chosen = listed_mask.T[:, None, :] & (ranks.T[:, None, :] == places[None, :, None])
    packed = jnp.einsum(
        "dsi,if->dsf", chosen.astype(jnp.bfloat16), weighted, preferred_element_type=jnp.float32
    ).astype(jnp.bfloat16)
    image_ids = own_index * img_rows + jnp.arange(img_rows, dtype=jnp.int32)
    slot_ids = jnp.where(
        jnp.any(chosen, axis=2), jnp.sum(jnp.where(chosen, image_ids[None, None, :], 0), axis=2), -1
    )
    received, recv_ids = (
        lax.all_to_all(packed, "ori", split_axis=0, concat_axis=0, tiled=True),
        lax.all_to_all(slot_ids, "ori", split_axis=0, concat_axis=0, tiled=True),
    )
    received = received.reshape(slot_count, width)
    recv_ids = recv_ids.reshape(slot_count)
    filled = recv_ids >= 0
    projection = projections[0]
    prior_row = log_prior[0]
    half_norm = 0.5 * jnp.sum(jnp.square(projection.astype(jnp.float32)) * weight[None, :], axis=1)
    scores = (
        jnp.dot(received, projection.T, preferred_element_type=jnp.float32)
        - half_norm[None, :]
        + prior_row[None, :]
    )
    part_max = jnp.where(filled, jnp.max(scores, axis=1), SENTINEL)
    part_sum = jnp.where(filled, jnp.sum(jnp.exp(scores - part_max[:, None]), axis=1), 0.0)
    back_max, back_sum = (
        lax.all_to_all(
            part_max.reshape(owners, capacity), "ori", split_axis=0, concat_axis=0, tiled=True
        ),
        lax.all_to_all(
            part_sum.reshape(owners, capacity), "ori", split_axis=0, concat_axis=0, tiled=True
        ),
    )
    image_best = jnp.max(jnp.where(chosen, back_max[:, :, None], SENTINEL), axis=(0, 1))
    image_sum = jnp.sum(
        jnp.where(
            chosen,
            back_sum[:, :, None] * jnp.exp(back_max[:, :, None] - image_best[None, None, :]),
            0.0,
        ),
        axis=(0, 1),
    )
    class_best = lax.pmax(image_best, "cls")
    class_total = lax.psum(image_sum * jnp.exp(image_best - class_best), "cls")
    slot_best = jnp.sum(jnp.where(chosen, class_best[None, None, :], 0.0), axis=2)
    slot_total = jnp.sum(jnp.where(chosen, class_total[None, None, :], 0.0), axis=2)
    got_best, got_total = (
        lax.all_to_all(slot_best, "ori", split_axis=0, concat_axis=0, tiled=True),
        lax.all_to_all(slot_total, "ori", split_axis=0, concat_axis=0, tiled=True),
    )
    got_best = got_best.reshape(slot_count)
    got_total = got_total.reshape(slot_count)
    log_evidence = class_best + jnp.log(class_total)
    safe_total = jnp.where(filled, got_total, 1.0)
    posterior = jnp.where(
        filled[:, None], jnp.exp(scores - got_best[:, None]) / safe_total[:, None], 0.0
    ).astype(jnp.bfloat16)
    local_sums = jnp.einsum(
        "sr,sf->rf", posterior, received, preferred_element_type=jnp.float32
    ).astype(jnp.bfloat16)
    relaid = lax.all_to_all(local_sums, "ori", split_axis=1, concat_axis=0, tiled=True)
    return (relaid[None], log_evidence)


def solution(mesh):
    in_specs = (P("ori", None), P("cls", "ori", None), P("cls", "ori"), P("ori", None), P(), P())
    out_specs = (P("cls", None, "ori"), P("ori"))
    return jax.shard_map(body, mesh=mesh, in_specs=in_specs, out_specs=out_specs, check_vma=False)
```

profile of v0, /device:TPU:0, one launch (start us, length us, event | category | flops | bytes accessed | tf_op | source)
XLA Modules:
  0.0 578.6 jit_solution(3882640956788941073)
XLA Ops:
  0.6 0.7 fusion.20
  1.3 0.1 copy.25
  1.4 0.1 reduce_window_sum.13
  1.5 0.1 copy.26
  1.6 0.2 fusion.13
  1.8 0.2 select_reduce_fusion.5
  2.0 0.6 broadcast_select_fusion.2
  2.7 7.3 %all-to-all-start = ((s32[8,1,48]{2,1,0:T(1,128)}), s32[8,1,48]{2,1,0:T(1,128)S(1)}, u32[]{:S(2)}, u32[]{:S(2)}) async-start(s32[8,1,48]{2,1,0:T(1,128)} %bitcast.2), calls=%async_computation | async-start | bytes 8192 | tf_op jit(solution)/shard_map/all_to_all | solution.py:39
  9.9 2.4 select_reduce_fusion
  12.3 9.4 %convolution_convert_fusion = bf16[8,48,20480]{2,1,0:T(8,128)(2,1)} fusion(bf16[64,20480]{1,0:T(8,128)(2,1)} %param.6, f32[20480]{0:T(1024)S(1)} %select_reduce_fusion, s32[8,64]{1,0:T(8,128)S(1)} %bitcast_subtract_fusion, pred[8,64]{1,0:T(8,128)(4,1)S(1)} %bitcast.37), kind=kOutput, calls=%fused_computation | convolution fusion | flops 1018478592 | bytes 18434560 | tf_op jit(solution)/shard_map/dsi,if->dsf/dot_general | solution.py:30
  21.7 0.0 copy-start
  21.7 0.0 all-to-all-done
  21.7 6.1 %all-to-all-start.1 = ((bf16[8,48,20480]{2,1,0:T(8,128)(2,1)}), bf16[8,48,20480]{2,1,0:T(8,128)(2,1)}, u32[]{:S(2)}, u32[]{:S(2)}) async-start(bf16[8,48,20480]{2,1,0:T(8,128)(2,1)} %convolution_convert_fusion), calls=%async_computation.1 | async-start | bytes 31457280 | tf_op jit(solution)/shard_map/all_to_all | solution.py:38
  27.9 4.3 multiply_reduce_fusion
  32.2 0.1 ge.25
  32.3 335.6 %all-to-all-done.1 = bf16[8,48,20480]{2,1,0:T(8,128)(2,1)} async-done(((bf16[8,48,20480]{2,1,0:T(8,128)(2,1)}), bf16[8,48,20480]{2,1,0:T(8,128)(2,1)}, u32[]{:S(2)}, u32[]{:S(2)}) %all-to-all-start.1) | async-done | bytes 15728672 | tf_op jit(solution)/shard_map/all_to_all | solution.py:38
  367.9 0.0 copy-done
  367.9 12.0 %fusion.23 = (f32[384]{0:T(512)S(1)}, f32[384,144]{0,1:T(8,128)S(1)}) fusion(f32[144]{0:T(256)S(1)} %bitcast.45, f32[144]{0:T(256)S(1)} %broadcast_multiply_fusion, bf16[384,20480]{1,0:T(8,128)(2,1)} %bitcast.4, bf16[1,144,20480]{2,1,0:T(8,128)(2,1)} %param.7), kind=kOutput, calls=%fused_computation.44 | convolution fusion | flops 2265089536 | bytes 21850752 | tf_op jit(solution)/shard_map/dot_general | solution.py:48
  379.9 0.1 reduce_max.21
  380.0 0.1 exponential_reduce_fusion
  380.1 0.1 reduce_sum.70
  380.2 0.6 broadcast_select_fusion
  380.8 9.8 %all_to_all.57 = f32[8,1,48]{2,1,0:T(1,128)S(1)} all-to-all(f32[8,1,48]{2,1,0:T(1,128)S(1)} %get-tuple-element.5), channel_id=1, replica_groups=mesh['cls'=4,'ori'=8] {'ori'}, dimensions={0} | all-to-all | bytes 3072 | tf_op jit(solution)/shard_map/all_to_all | solution.py:55
  390.6 3.3 all-to-all-start.4
  393.9 0.1 select_reduce_fusion.4
  394.1 5.7 pmax.7
  399.7 0.5 all-to-all-done.4
  400.3 0.2 select_reduce_fusion.2
  400.5 6.1 %psum.7 = f32[64]{0:T(128)S(1)} all-reduce(f32[64]{0:T(128)S(1)} %exponential_multiply_fusion), channel_id=1, replica_groups=mesh['cls'=4,'ori'=8] {'cls'}, use_global_device_ids=true, to_apply=%region_12.13 | all-reduce | flops 64 | bytes 512 | tf_op jit(solution)/shard_map/psum | solution.py:72
  406.5 0.7 select_reduce_fusion.3
  407.3 12.2 %all_to_all.58 = f32[8,1,48]{2,1,0:T(1,128)S(1)} all-to-all(f32[8,1,48]{2,1,0:T(1,128)S(1)} %bitcast.41), channel_id=1, replica_groups=mesh['cls'=4,'ori'=8] {'ori'}, dimensions={0} | all-to-all | bytes 3072 | tf_op jit(solution)/shard_map/all_to_all | solution.py:77
  419.5 3.5 all-to-all-start.3
  423.0 0.5 broadcast.66
  423.5 0.7 reduce.8
  424.1 0.1 reshape.92
  424.2 4.9 all-to-all-done.3
  429.1 0.7 reduce.9
  429.8 0.1 sub.47
  429.8 8.7 %convolution_convert_fusion.1 = bf16[144,20480]{1,0:T(8,128)(2,1)S(1)} fusion(bf16[384,20480]{1,0:T(8,128)(2,1)} %bitcast.4, f32[384,144]{0,1:T(8,128)S(1)} %get-tuple-element.7, f32[384]{0:T(512)S(1)} %broadcast_select_fusion.3, f32[384]{0:T(512)S(1)} %sub.47, pred[384]{0:T(512)(128)(4,1)S(1)} %ge.25), kind=kOutput, calls=%fused_computation.1 | convolution fusion | flops 2268094464 | bytes 21851520 | tf_op jit(solution)/shard_map/sr,sf->rf/dot_general | solution.py:86
  438.6 3.2 copy.30
  441.7 4.7 all-to-all-start.6
  446.4 0.5 log_add_fusion
  447.0 126.0 %all-to-all-done.6 = bf16[144,8,2560]{2,0,1:T(8,128)(2,1)} async-done(((bf16[144,8,2560]{2,0,1:T(8,128)(2,1)}), bf16[144,8,2560]{2,0,1:T(8,128)(2,1)}, u32[]{:S(2)}, u32[]{:S(2)}) %all-to-all-start.6) | async-done | bytes 5898272 | tf_op jit(solution)/shard_map/all_to_all | solution.py:89
  573.0 5.6 copy.32
  (8 shorter events, 0.1 us)
Async XLA Ops:
  2.7 19.1 %all-to-all-start = ((s32[8,1,48]{2,1,0:T(1,128)}), s32[8,1,48]{2,1,0:T(1,128)S(1)}, u32[]{:S(2)}, u32[]{:S(2)}) async-start(s32[8,1,48]{2,1,0:T(1,128)} %bitcast.2), calls=%async_computation | async-start | bytes 8192 | tf_op jit(solution)/shard_map/all_to_all | solution.py:39
  21.7 346.2 %copy-start = (f32[1,144]{1,0:T(1,128)S(1)}, f32[1,144]{1,0:T(1,128)}, u32[]{:S(2)}) copy-start(f32[1,144]{1,0:T(1,128)} %param.8) | copy-start | bytes 1732
  21.7 346.2 %all-to-all-start.1 = ((bf16[8,48,20480]{2,1,0:T(8,128)(2,1)}), bf16[8,48,20480]{2,1,0:T(8,128)(2,1)}, u32[]{:S(2)}, u32[]{:S(2)}) async-start(bf16[8,48,20480]{2,1,0:T(8,128)(2,1)} %convolution_convert_fusion), calls=%async_computation.1 | async-start | bytes 31457280 | tf_op jit(solution)/shard_map/all_to_all | solution.py:38
  390.6 9.6 %all-to-all-start.4 = ((f32[8,1,48]{2,1,0:T(1,128)}), f32[8,1,48]{2,1,0:T(1,128)S(1)}, u32[]{:S(2)}, u32[]{:S(2)}) async-start(f32[8,1,48]{2,1,0:T(1,128)} %get-tuple-element.4), calls=%async_computation.4 | async-start | bytes 8192 | tf_op jit(solution)/shard_map/all_to_all | solution.py:58
  419.5 9.6 %all-to-all-start.3 = ((f32[8,1,48]{2,1,0:T(1,128)}), f32[8,1,48]{2,1,0:T(1,128)S(1)}, u32[]{:S(2)}, u32[]{:S(2)}) async-start(f32[8,1,48]{2,1,0:T(1,128)} %bitcast.8), calls=%async_computation.3 | async-start | bytes 8192 | tf_op jit(solution)/shard_map/all_to_all | solution.py:76
  441.7 131.3 %all-to-all-start.6 = ((bf16[144,8,2560]{2,0,1:T(8,128)(2,1)}), bf16[144,8,2560]{2,0,1:T(8,128)(2,1)}, u32[]{:S(2)}, u32[]{:S(2)}) async-start(bf16[144,8,2560]{2,0,1:T(8,128)(2,1)} %bitcast.33), calls=%async_computation.6 | async-start | bytes 11796480 | tf_op jit(solution)/shard_map/all_to_all | solution.py:89
where the time goes:
time: 579 us
  waiting for transfers between devices  467 us (81%)
  blocking collectives  33.7 us (6%)
  matrix products  30.1 us (5%)
  starting transfers between devices  24.9 us (4%)
  other arithmetic  12.2 us (2%)
  local copies, waits for them, and re-layouts  9.87 us (2%)
    all_to_all x1, waiting for transfers between devices, body(): lax.all_to_all(packed, 'ori', split_axis=0, concat_axis=0, tiled=True)  336 us
    all_to_all x1, waiting for transfers between devices, body(): lax.all_to_all(local_sums, 'ori', split_axis=1, concat_axis=0, tiled=True)  126 us
    all_to_all x1, blocking collectives, body(): lax.all_to_all(slot_total, 'ori', split_axis=0, concat_axis=0, tiled=True)  12.2 us
    dot_general x1, matrix products, body(): jnp.dot(received, projection.T, preferred_element_type=jnp.float32)  12 us
  transfers between devices with their start and end apart: 5, of which 4 were waited for; matrix products, arithmetic and copies ran while one was open for 3% of the time, Pallas kernels for 0%

commit v1 on v0

v1 whole, which is shorter than its diff:
```python
import functools
import math

import jax
import jax.numpy as jnp
from jax import lax
from jax.experimental import pallas as pl
from jax.experimental.pallas import tpu as pltpu
from jax.sharding import PartitionSpec as P

BF16 = jnp.bfloat16
F32 = jnp.float32
MASKED = -1e30
LANES = 128
MIB = 1 << 20


def cycle_of(count):
    deep = math.isqrt(count // 2)
    tall = count // deep
    walk = [(z, 0) for z in range(tall)]
    for z in range(tall - 1, -1, -1):
        cols = list(range(1, deep))
        walk += [(z, y) for y in (cols if (tall - 1 - z) % 2 == 0 else cols[::-1])]
    return [z * deep + y for z, y in walk]


def weight_table(index, noise):
    levels = noise.shape[1]
    row = jnp.concatenate([noise, jnp.zeros((1, LANES - levels), F32)], axis=1)
    table = jnp.broadcast_to(row, index.shape)
    return jnp.take_along_axis(table, index, axis=1, mode="promise_in_bounds")


def at(start, size):
    return pl.ds(pl.multiple_of(start, LANES), size)


def image_kernel(n, wo, ws, img_ref, index_ref, noise_ref, sig_ref, own_ref, oth_ref, sh_ref, w_ref):
    cls = lax.axis_index("cls")
    core, side = cls % 2, (cls // 2) % 2
    half = 2 * wo + ws
    w_ref[...] = weight_table(index_ref[...], noise_ref[...])
    for i in range(n):
        base = (2 * i + core) * half
        for ref, start, count, spot in (
            (own_ref, base + side * wo, wo, i * wo),
            (oth_ref, base + (1 - side) * wo, wo, i * wo),
            (sh_ref, base + 2 * wo, ws, i * ws),
        ):
            for j in range(0, count, LANES):
                weight = w_ref[pl.ds(start // LANES + j // LANES, 1), :]
                wide = img_ref[:, at(start + j, LANES)].astype(F32) * weight
                ref[:, spot + j : spot + j + LANES] = wide.astype(BF16)
    rows = img_ref.shape[0]
    block = lax.broadcasted_iota(jnp.int32, (LANES, rows), 0)
    listed = block < 0
    for j in range(sig_ref.shape[0]):
        listed = listed | (sig_ref[j : j + 1, :] == block)
    unlisted = jnp.where(listed, 0.0, 1.0).astype(BF16)
    same = lax.broadcasted_iota(jnp.int32, (rows, rows), 0) == lax.broadcasted_iota(jnp.int32, (rows, rows), 1)
    eye = jnp.where(same, 1.0, 0.0).astype(BF16)
    turned = lax.dot_general(eye, unlisted, (((1,), (1,)), ((), ())), preferred_element_type=F32)
    own_ref[:, n * wo :] = turned.astype(BF16)


def prep_images(images, weight_of, significant, core, side, wo, ws, n):
    rows = images.shape[0]
    half = 2 * wo + ws
    if wo % LANES == 0:
        index, noise = weight_of
        out = [
            jax.ShapeDtypeStruct((rows, n * wo + LANES), BF16),
            jax.ShapeDtypeStruct((rows, n * wo), BF16),
            jax.ShapeDtypeStruct((rows, n * ws), BF16),
        ]
        vmem = pl.BlockSpec(memory_space=pltpu.VMEM)
        return pl.pallas_call(
            functools.partial(image_kernel, n, wo, ws),
            in_specs=[vmem] * 4,
            out_specs=[vmem] * 3,
            out_shape=out,
            scratch_shapes=[pltpu.VMEM(index.shape, F32)],
            compiler_params=pltpu.CompilerParams(vmem_limit_bytes=32 * MIB),
            name="prep_images",
        )(images, index, noise, significant.T)
    weight = full_weights(weight_of)
    weighted = (images.astype(F32) * weight).astype(BF16).reshape(rows, n, 2, half)
    mine = lax.dynamic_index_in_dim(weighted, core, 2, keepdims=False)
    own, oth, shared = cut(mine, side, wo)
    lane = jnp.arange(LANES, dtype=jnp.int32)
    listed = jnp.any(significant[:, :, None] == lane[None, None, :], axis=1)
    return jnp.concatenate([own, jnp.where(listed, 0.0, 1.0).astype(BF16)], axis=1), oth, shared


def full_weights(weight_of):
    index, noise = weight_of
    levels = jnp.arange(noise.shape[1], dtype=jnp.int32)
    return jnp.sum(jnp.where(index.reshape(-1, 1) == levels[None, :], noise, 0.0), axis=1)[None, :]


def cut(mine, side, wo):
    rows, n, _ = mine.shape
    own = lax.dynamic_slice_in_dim(mine, side * wo, wo, 2).reshape(rows, n * wo)
    oth = lax.dynamic_slice_in_dim(mine, (1 - side) * wo, wo, 2).reshape(rows, n * wo)
    return own, oth, mine[:, :, 2 * wo :].reshape(rows, -1)


def projection_kernel(wo, ws, n, proj_ref, index_ref, noise_ref, prior_ref, keep_ref, send_ref, bias_ref, acc, w_ref):
    step = pl.program_id(0)
    half = 2 * wo + ws
    cls, owner = lax.axis_index("cls"), lax.axis_index("ori")
    core, side = cls % 2, (cls // 2) % 2

    @pl.when(step == 0)
    def _():
        acc[...] = jnp.zeros_like(acc)
        w_ref[...] = weight_table(index_ref[...], noise_ref[...])
        lane = lax.broadcasted_iota(jnp.int32, (proj_ref.shape[0], LANES), 1)
        gate = jnp.where(lane == owner, MASKED, 0.0).astype(BF16)
        keep_ref[:, n * wo : n * wo + LANES] = gate
        send_ref[:, n * wo : n * wo + LANES] = gate

    total = acc[...]
    for j in range(2 * half // LANES):
        weight = w_ref[pl.ds(step * (2 * half // LANES) + j, 1), :]
        wide = proj_ref[:, j * LANES : (j + 1) * LANES].astype(F32)
        total = total + wide * wide * weight
    acc[...] = total
    for ref, which in ((keep_ref, core), (send_ref, 1 - core)):
        base = which * half
        ref[:, at(step * wo, wo)] = proj_ref[:, at(base + side * wo, wo)]
        ref[:, at(n * wo + LANES + step * wo, wo)] = proj_ref[:, at(base + (1 - side) * wo, wo)]
        ref[:, at(2 * n * wo + LANES + step * ws, ws)] = proj_ref[:, at(base + 2 * wo, ws)]

    @pl.when(step == pl.num_programs(0) - 1)
    def _():
        half_norm = 0.5 * jnp.sum(acc[...], axis=1, keepdims=True)
        bias_ref[...] = jnp.broadcast_to(prior_ref[...] - half_norm, bias_ref.shape)


def prep_projections(projection, weight_of, prior, core, side, owner, wo, ws, n):
    rows = projection.shape[0]
    half = 2 * wo + ws
    width = n * half + LANES
    if wo % LANES == 0:
        index, noise = weight_of
        out = [
            jax.ShapeDtypeStruct((rows, width), BF16),
            jax.ShapeDtypeStruct((rows, width), BF16),
            jax.ShapeDtypeStruct((rows, LANES), F32),
        ]
        fixed = lambda i: (0, 0)
        return pl.pallas_call(
            functools.partial(projection_kernel, wo, ws, n),
            grid=(n,),
            in_specs=[
                pl.BlockSpec((rows, 2 * half), lambda i: (0, i)),
                pl.BlockSpec(index.shape, fixed),
                pl.BlockSpec(noise.shape, fixed),
                pl.BlockSpec(prior.shape, fixed),
            ],
            out_specs=[pl.BlockSpec(o.shape, fixed) for o in out],
            out_shape=out,
            scratch_shapes=[pltpu.VMEM((rows, LANES), F32), pltpu.VMEM(index.shape, F32)],
            compiler_params=pltpu.CompilerParams(vmem_limit_bytes=32 * MIB),
            name="prep_projections",
        )(projection, index, noise, prior)
    weight = full_weights(weight_of)
    half_norm = 0.5 * jnp.sum(jnp.square(projection.astype(F32)) * weight, axis=1, keepdims=True)
    bias = jnp.broadcast_to(prior - half_norm, (rows, LANES))
    lane = jnp.arange(LANES, dtype=jnp.int32)
    gate = jnp.broadcast_to(jnp.where(lane == owner, MASKED, 0.0).astype(BF16)[None, :], (rows, LANES))
    split = projection.reshape(rows, n, 2, half)
    both = []
    for which in (core, 1 - core):
        own, oth, shared = cut(lax.dynamic_index_in_dim(split, which, 2, keepdims=False), side, wo)
        both.append(jnp.concatenate([own, gate, oth, shared], axis=1))
    return both[0], both[1], bias


def pack_kernel(cols, *refs):
    row = 0
    for ref in refs[:-1]:
        refs[-1][row : row + ref.shape[0], :] = ref[:, :cols]
        row += ref.shape[0]


def pack(pieces, cols):
    vmem = pl.BlockSpec(memory_space=pltpu.VMEM)
    return pl.pallas_call(
        functools.partial(pack_kernel, cols),
        in_specs=[vmem] * len(pieces),
        out_specs=vmem,
        out_shape=jax.ShapeDtypeStruct((sum(p.shape[0] for p in pieces), cols), BF16),
        compiler_params=pltpu.CompilerParams(vmem_limit_bytes=16 * MIB),
        name="pack",
    )(*pieces)


def score_kernel(wo, ws, counts, aligned, where_ref, own_ref, mate_ref, bias_ref, *refs):
    kinds, at_ref = [], 0
    for count in counts:
        kinds.append(refs[at_ref : at_ref + count])
        at_ref += count
    part_ref = refs[at_ref]
    rows = own_ref.shape[0]
    acc = None
    base = 0
    for pieces in kinds:
        width = pieces[0].shape[1]
        for start in range(0, width, 1024):
            size = min(1024, width - start)
            x = jnp.concatenate([p[:, start : start + size] for p in pieces], axis=0)
            cols = slice(base + start, base + start + size)
            p = jnp.concatenate([own_ref[:, cols], mate_ref[:, cols]], axis=0)
            term = lax.dot_general(p, x, (((1,), (1,)), ((), ())), preferred_element_type=F32)
            acc = term if acc is None else acc + term
        base += width
    part_ref[:rows, :] = acc[:rows] + bias_ref[...]
    part_ref[rows:, :] = acc[rows:]
    if aligned:
        side, owner = where_ref[1], where_ref[2]
        slice_ref = refs[at_ref + 1]
        spots = ((side * wo, wo), ((1 - side) * wo, wo), (2 * wo, ws))
        for pieces, (spot, size) in zip(kinds, spots, strict=True):
            row = 0
            for p in pieces:
                slice_ref[row : row + p.shape[0], at(spot, size)] = p[:, at(owner * size, size)]
                row += p.shape[0]


def group_scores(where, own, mate, bias, kinds, wo, ws):
    aligned = wo % LANES == 0
    rows = own.shape[0]
    count = sum(p.shape[0] for p in kinds[0])
    half = 2 * wo + ws
    out = [jax.ShapeDtypeStruct((2 * rows, count), F32)]
    if aligned:
        out.append(jax.ShapeDtypeStruct((count, half), BF16))
    flat = [p for pieces in kinds for p in pieces]
    vmem = pl.BlockSpec(memory_space=pltpu.VMEM)
    got = pl.pallas_call(
        functools.partial(score_kernel, wo, ws, [len(k) for k in kinds], aligned),
        in_specs=[pl.BlockSpec(memory_space=pltpu.SMEM)] + [vmem] * (3 + len(flat)),
        out_specs=[vmem] * len(out),
        out_shape=out,
        compiler_params=pltpu.CompilerParams(vmem_limit_bytes=40 * MIB),
        cost_estimate=pl.CostEstimate(
            flops=4 * rows * count * own.shape[1], bytes_accessed=4 * own.size + 2 * count * own.shape[1], transcendentals=0
        ),
        name="group_scores",
    )(where, own, mate, bias, *flat)
    if aligned:
        return got
    side, owner = where[1], where[2]
    own_o, oth_o, shared = (jnp.concatenate(k, axis=0) for k in kinds)
    a = lax.dynamic_slice_in_dim(own_o, owner * wo, wo, 1)
    b = lax.dynamic_slice_in_dim(oth_o, owner * wo, wo, 1)
    c = lax.dynamic_slice_in_dim(shared, owner * ws, ws, 1)
    first, second = jnp.where(side == 0, a, b), jnp.where(side == 0, b, a)
    return got[0], jnp.concatenate([first, second, c], axis=1)


def stats_kernel(groups, *refs):
    parts, recvs = refs[:groups], refs[groups : 2 * groups]
    score_ref, stat_ref = refs[2 * groups :]
    rows = score_ref.shape[0]
    for g in range(groups):
        count = parts[g].shape[1]
        cols = slice(g * count, (g + 1) * count)
        mine = parts[g][:rows, :] + recvs[g][rows:, :]
        other = parts[g][rows:, :] + recvs[g][:rows, :]
        best = jnp.maximum(jnp.max(mine, axis=0, keepdims=True), jnp.max(other, axis=0, keepdims=True))
        total = jnp.sum(jnp.exp(mine - best), axis=0, keepdims=True) + jnp.sum(jnp.exp(other - best), axis=0, keepdims=True)
        score_ref[:, cols] = mine
        stat_ref[0:1, cols] = best
        stat_ref[1:2, cols] = total
        stat_ref[2:8, cols] = jnp.zeros((6, count), F32)


def ring_order(n):
    return [(0, n // 2)] + [(d, n - d) for d in range(1, n // 2)]


def payload_kernel(n, turns, where_ref, score_ref, *refs):
    stats, out_ref = refs[:turns], refs[turns]
    rows, width = score_ref.shape
    per = width // n
    plane = where_ref[3]
    best = functools.reduce(jnp.maximum, [s[0:1, :] for s in stats])
    terms = [s[1:2, :] * jnp.exp(s[0:1, :] - best) for s in stats]
    total = None
    for a in range(turns):
        back = lax.rem(plane - a + turns, turns)
        term = sum(jnp.where(back == j, terms[j], 0.0) for j in range(turns))
        total = term if total is None else total + term
    out_ref[:rows, :] = jnp.exp(score_ref[...] - best).astype(BF16)
    tops, sums = [None] * n, [None] * n
    for g, pair in enumerate(ring_order(n)):
        for h, r in enumerate(pair):
            cols = slice((2 * g + h) * per, (2 * g + h + 1) * per)
            tops[r], sums[r] = best[:, cols], total[:, cols]
    both = jnp.concatenate([jnp.concatenate(tops, axis=0), jnp.concatenate(sums, axis=0)], axis=1)
    tail = out_ref.shape[0] - rows
    if tail > n:
        both = jnp.concatenate([both, jnp.zeros((tail - n, 2 * per), F32)], axis=0)
    left = both
    for j in range(3):
        piece = left.astype(BF16)
        out_ref[rows:, j * 2 * per : (j + 1) * 2 * per] = piece
        left = left - piece.astype(F32)
    out_ref[rows:, 6 * per :] = jnp.zeros((tail, width - 6 * per), BF16)


def sums_kernel(n, rows, halves, blocks_ref, *refs):
    payloads = refs[:n]
    w_own_ref, w_oth_ref = refs[n], refs[n + 1]
    out_ref, evidence_ref = refs[n + 2], refs[n + 3]
    posterior = refs[n + 4]
    step = pl.program_id(0)
    width = payloads[0].shape[1]
    per = width // n
    order = ring_order(n)

    @pl.when(step == 0)
    def _():
        tops, sums = [], []
        for d in range(n):
            raw = [payloads[d][rows:, j * 2 * per : (j + 1) * 2 * per].astype(F32)[:n] for j in range(3)]
            both = raw[0] + raw[1] + raw[2]
            both = jnp.concatenate([both[n - d :], both[: n - d]], axis=0) if d else both
            tops.append(both[:, :per])
            sums.append(both[:, per:])
        best = functools.reduce(jnp.maximum, tops)
        grow = [jnp.exp(t - best) for t in tops]
        total = functools.reduce(lambda a, b: a + b, [s * g for s, g in zip(sums, grow, strict=True)])
        evidence_ref[...] = best + jnp.log(total)
        for d in range(n):
            scale = grow[d] / total
            wide = jnp.concatenate([scale, scale], axis=1)
            held = payloads[d][:rows, :]
            chunks = [None] * n
            for g, pair in enumerate(order):
                for h, r in enumerate(pair):
                    c = (2 * g + h) * per
                    s = (d + r) % n
                    tile = held[:, c : c + per].astype(F32)
                    chunks[s] = (tile * wide[s : s + 1, :per]).astype(BF16)
            row = pl.multiple_of(blocks_ref[d] * rows, 16)
            for g, (a, b) in enumerate(order):
                posterior[pl.ds(row, rows), 2 * g * per : 2 * (g + 1) * per] = jnp.concatenate([chunks[a], chunks[b]], axis=1)

    if halves:
        w = jnp.where(step < pl.num_programs(0) // 2, w_own_ref[...], w_oth_ref[...])
        left = posterior[...]
    else:
        w = w_own_ref[...]
        left = posterior[pl.ds(pl.multiple_of(step * out_ref.shape[0], 16), out_ref.shape[0]), :]
    out_ref[...] = jnp.dot(left, w, preferred_element_type=F32).astype(BF16)


def body(images, projections, log_prior, significant, shell_index, noise_inv):
    n = lax.axis_size("ori")
    n_cls = lax.axis_size("cls")
    turns = n_cls // 2
    owner = lax.axis_index("ori")
    cls = lax.axis_index("cls")
    core, plane = cls % 2, cls // 2
    side = plane % 2
    rows, freqs = images.shape
    ori_rows = projections.shape[1]
    half = freqs // n // 2
    wo = 3 * half // 10
    ws = half - 2 * wo
    cycle = cycle_of(n)
    spot_of = [cycle.index(o) for o in range(n)]

    def ring(x, d):
        return lax.ppermute(x, "ori", [(cycle[i], cycle[(i + d) % n]) for i in range(n)])

    def swap(x):
        return lax.ppermute(x, "cls", [(i, i ^ 1) for i in range(n_cls)])

    def cross(x):
        return lax.ppermute(x, "cls", [(i, i ^ 2) for i in range(n_cls)])

    weight_of = (shell_index.reshape(freqs // LANES, LANES), noise_inv.reshape(1, -1))
    where = jnp.stack([core, side, owner, plane])
    own, oth, shared = prep_images(images, weight_of, significant, core, side, wo, ws, n)
    projections, own, oth, shared = lax.optimization_barrier((projections, own, oth, shared))
    keep, send, bias = prep_projections(
        projections[0], weight_of, log_prior[0].reshape(ori_rows, 1), core, side, owner, wo, ws, n
    )
    mate = swap(send)

    groups = []
    fo, bo, fs, bs = own, own, shared, shared
    cutoff = rows // 2
    crossed = {}
    for d in range(1, n // 2 + 1):
        if d == n // 2:
            fo, bo, fs, bs = fo[:cutoff], bo[cutoff:], fs[:cutoff], bs[cutoff:]
        if d > 2:
            fo, bo, crossed[d - 2] = lax.optimization_barrier((fo, bo, crossed[d - 2]))
        fo, bo = ring(fo, 1), ring(bo, -1)
        fs, bs = ring(fs, 1), ring(bs, -1)
        fp, bp = fo, bo
        if d == 1:
            fp, bp, mate = lax.optimization_barrier((fp, bp, mate))
        crossed[d] = cross(pack([fp, bp], n * wo))
        if d < n // 2:
            groups.append([[fo, bo], [crossed[d]], [fs, bs]])
        else:
            groups.insert(0, [[own, fo, bo], [oth, crossed[d]], [shared, fs, bs]])

    parts, slices = [None] * len(groups), [None] * len(groups)
    for g in list(range(1, len(groups))) + [0]:
        parts[g], slices[g] = group_scores(where, keep, mate, bias, groups[g], wo, ws)
    recvs = [swap(p) for p in parts]
    other_slices = [swap(s) for s in slices]

    vmem = pl.BlockSpec(memory_space=pltpu.VMEM)
    smem = pl.BlockSpec(memory_space=pltpu.SMEM)
    width = n * rows
    scores, stats = pl.pallas_call(
        functools.partial(stats_kernel, len(groups)),
        in_specs=[vmem] * (2 * len(groups)),
        out_specs=[vmem, vmem],
        out_shape=[jax.ShapeDtypeStruct((ori_rows, width), F32), jax.ShapeDtypeStruct((8, width), F32)],
        compiler_params=pltpu.CompilerParams(vmem_limit_bytes=32 * MIB),
        name="local_stats",
    )(*parts, *recvs)
    all_stats = [stats] + [
        lax.ppermute(stats, "cls", [(i, (i + 2 * j) % n_cls) for i in range(n_cls)]) for j in range(1, turns)
    ]
    tail = max(16, n)
    payload = pl.pallas_call(
        functools.partial(payload_kernel, n, turns),
        in_specs=[smem] + [vmem] * (1 + turns),
        out_specs=vmem,
        out_shape=jax.ShapeDtypeStruct((ori_rows + tail, width), BF16),
        compiler_params=pltpu.CompilerParams(vmem_limit_bytes=32 * MIB),
        name="payload",
    )(where, scores, *all_stats)

    payloads = [payload] + [None] * (n - 1)
    fp = bp = payload
    for d in range(1, n // 2 + 1):
        fp = payloads[d] = ring(fp, 1)
        if d < n // 2:
            bp = payloads[n - d] = ring(bp, -1)

    spots = jnp.array(spot_of, dtype=jnp.int32)
    order = jnp.array(cycle, dtype=jnp.int32)
    blocks = order[(spots[owner] - jnp.arange(n, dtype=jnp.int32)) % n]
    w_own, w_oth = jnp.concatenate(slices, axis=0), jnp.concatenate(other_slices, axis=0)
    fixed = lambda i, b: (0, 0)
    halves = half % 256 == 0
    if halves:
        per_half = half // 256
        steps = 2 * per_half
        scalars = jnp.concatenate([blocks, core[None].astype(jnp.int32)])
        first = lambda i, b: (0, jnp.minimum(i, per_half - 1))
        second = lambda i, b: (0, jnp.maximum(i - per_half, 0))
        target = lambda i, b: (0, jnp.where(i < per_half, b[n] * per_half + i, (1 - b[n]) * per_half + i - per_half))
        w_specs = [pl.BlockSpec((width, 256), first), pl.BlockSpec((width, 256), second)]
        out_spec = pl.BlockSpec((n * ori_rows, 256), target)
    else:
        steps = max(1, n // 8)
        scalars = blocks
        low, high = jnp.where(core == 0, w_own, w_oth), jnp.where(core == 0, w_oth, w_own)
        w_own = jnp.concatenate([low, high], axis=1)
        w_specs = [pl.BlockSpec((width, 2 * half), fixed), pl.BlockSpec((16, 128), fixed)]
        out_spec = pl.BlockSpec((n * ori_rows // steps, 2 * half), lambda i, b: (i, 0))
    sums, evidence = pl.pallas_call(
        functools.partial(sums_kernel, n, ori_rows, halves),
        grid_spec=pltpu.PrefetchScalarGridSpec(
            num_scalar_prefetch=1,
            grid=(steps,),
            in_specs=[pl.BlockSpec(payload.shape, fixed, pipeline_mode=pl.Buffered(1))] * n + w_specs,
            out_specs=[out_spec, pl.BlockSpec((n, rows), fixed)],
            scratch_shapes=[pltpu.VMEM((n * ori_rows, width), BF16)],
        ),
        out_shape=[jax.ShapeDtypeStruct((n * ori_rows, 2 * half), BF16), jax.ShapeDtypeStruct((n, rows), F32)],
        compiler_params=pltpu.CompilerParams(vmem_limit_bytes=58 * MIB),
        name="class_sums",
    )(scalars, *payloads, w_own, w_oth)
    return sums[None], evidence[0]


def solution(mesh):
    in_specs = (P("ori", None), P("cls", "ori", None), P("cls", "ori"), P("ori", None), P(), P())
    out_specs = (P("cls", None, "ori"), P("ori"))
    return jax.shard_map(body, mesh=mesh, in_specs=in_specs, out_specs=out_specs, check_vma=False)
```

time: 579 us -> 162 us (0.28)
  waiting for transfers between devices: 467 us -> 63.7 us
  blocking collectives: 33.7 us -> 0 us
  matrix products: 30.1 us -> 0 us
  Pallas kernels: 0 us -> 29.1 us
  local copies, waits for them, and re-layouts: 9.87 us -> 29.4 us
  starting transfers between devices: 24.9 us -> 32.9 us
  other arithmetic: 12.2 us -> 4.86 us
    all_to_all x5 -> x0, waiting for transfers between devices: 467 us -> none  [the longest x1 336 us: body(): lax.all_to_all(packed, 'ori', split_axis=0, concat_axis=0, tiled=True)]
    ppermute x0 -> x37, waiting for transfers between devices: none -> 63.7 us  [the longest x23 59.6 us: ring(): lax.ppermute(x, 'ori', [(cycle[i], cycle[(i + d) % n]) for i in range(n)])]
    ppermute x0 -> x37, starting transfers between devices: none -> 32.9 us  [the longest x23 24.5 us: ring(): lax.ppermute(x, 'ori', [(cycle[i], cycle[(i + d) % n]) for i in range(n)])]
    dot_general x3 -> x0, matrix products: 30.1 us -> none  [the longest x1 12 us: body(): jnp.dot(received, projection.T, preferred_element_type=jnp.float32)]
    pallas_call x0 -> x13, Pallas kernels: none -> 29.1 us  [the longest x1 11.9 us: body(): pl.pallas_call(functools.partial(sums_kernel, n, ori_rows, halves), grid_...]
    all_to_all x5 -> x0, starting transfers between devices: 24.9 us -> none  [the longest x1 7.28 us: body(): lax.all_to_all(slot_ids, 'ori', split_axis=0, concat_axis=0, tiled=True)]
    all_to_all x2 -> x0, blocking collectives: 22 us -> none  [the longest x1 12.2 us: body(): lax.all_to_all(slot_total, 'ori', split_axis=0, concat_axis=0, tiled=True)]
    unnamed x3 -> x122, local copies, waits for them, and re-layouts: 5.63 us -> 24.7 us
  transfers between devices with their start and end apart: 5 -> 37, of which waited for: 4 -> 17; matrix products, arithmetic and copies ran while one was open for 3% -> 5% of each run, Pallas kernels for 0% -> 9%
where the time goes in v1:
time: 162 us; the launch traced here: 161 us
  waiting for transfers between devices  63.7 us (39%)
  starting transfers between devices  32.9 us (20%)
  local copies, waits for them, and re-layouts  29.4 us (18%)
  Pallas kernels  29.1 us (18%)
  other arithmetic  4.86 us (3%)
    ppermute x23, waiting for transfers between devices, ring(): lax.ppermute(x, 'ori', [(cycle[i], cycle[(i + d) % n]) for i in range(n)])  59.6 us
    unnamed x122, local copies, waits for them, and re-layouts  24.7 us
    ppermute x23, starting transfers between devices, ring(): lax.ppermute(x, 'ori', [(cycle[i], cycle[(i + d) % n]) for i in range(n)])  24.5 us
    pallas_call x1, Pallas kernels, body(): pl.pallas_call(functools.partial(sums_kernel, n, ori_rows, halves), grid_...  11.9 us
    pallas_call x4, Pallas kernels, group_scores(): pl.pallas_call(functools.partial(score_kernel, wo, ws, [len(k) for k in k...  11 us
    ppermute x4, starting transfers between devices, cross(): return lax.ppermute(x, 'cls', [(i, i ^ 2) for i in range(n_cls)])  5.15 us
  transfers between devices with their start and end apart: 37, of which 17 were waited for; matrix products, arithmetic and copies ran while one was open for 5% of the time, Pallas kernels for 9%

profile of v1, /device:TPU:0, one launch (start us, length us, event | category | flops | bytes accessed | tf_op | source)
XLA Modules:
  0.0 161.1 jit_solution(127926134790032145)
XLA Ops:
  0.7 1.7 %copy-done.3 = bf16[64,20480]{1,0:T(8,128)(2,1)S(1)} copy-done((bf16[64,20480]{1,0:T(8,128)(2,1)S(1)}, bf16[64,20480]{1,0:T(8,128)(2,1)}, u32[]{:S(2)}) %copy-start.3) | copy-done | bytes 2621464
  2.4 0.9 copy-done.45
  5.1 0.8 copy-done.27
  5.9 0.8 copy-done.40
  6.7 0.8 copy.10.prior_ref
  7.4 2.7 %copy-done.2 = bf16[1,144,20480]{2,1,0:T(8,128)(2,1)S(1)} copy-done((bf16[1,144,20480]{2,1,0:T(8,128)(2,1)S(1)}, bf16[1,144,20480]{2,1,0:T(8,128)(2,1)}, u32[]{:S(2)}) %copy-start.2) | copy-done | bytes 5898264
  10.1 0.9 copy-done.47
  11.0 2.9 %prep_projections.1 = (bf16[144,10368]{1,0:T(8,128)(2,1)S(1)}, bf16[144,10368]{1,0:T(8,128)(2,1)S(1)}, f32[144,128]{1,0:T(8,128)S(1)}) custom-call(bf16[144,20480]{1,0:T(8,128)(2,1)S(1)} %bitcast.15, s32[160,128]{1,0:T(8,128)S(1)} %bitcast.17, f32[1,100]{1,0:T(1,128)S(1)} %bitcast.20, f32[144,1]{1,0:T(8,128)S(1)} %copy-done.47), custom_call_target="tpu_custom_call" | custom-call | tf_op jit(solution)/shard_map/prep_projections/pallas_call | solution.py:154
  14.4 2.6 %collective-permute-start = (bf16[64,3200]{1,0:T(8,128)(2,1)S(1)}, bf16[64,3200]{1,0:T(8,128)(2,1)S(1)}, u32[]{:S(2)}, u32[]{:S(2)}) collective-permute-start(bf16[64,3200]{1,0:T(8,128)(2,1)S(1)} %get-tuple-element.36.refs_0_), channel_id=1, source_target_pairs={{0,2},{2,4},{4,6},{6,7},{7,5},{5,3},{3,1},{1,0},{8,10},{10,12},{12... | collective-permute-start | bytes 1228808 | tf_op jit(solution)/shard_map/ppermute | solution.py:380
  17.1 10.0 %collective-permute-done.refs_0_ = bf16[64,3200]{1,0:T(8,128)(2,1)S(1)} collective-permute-done((bf16[64,3200]{1,0:T(8,128)(2,1)S(1)}, bf16[64,3200]{1,0:T(8,128)(2,1)S(1)}, u32[]{:S(2)}, u32[]{:S(2)}) %collective-permute-start) | collective-permute-done | bytes 409632 | tf_op jit(solution)/shard_map/ppermute | solution.py:380
  27.1 1.5 collective-permute-done.1.refs_1_
  28.6 1.6 copy-done
  30.3 1.6 collective-permute-start.5
  31.8 1.6 collective-permute-start.12
  33.9 1.6 collective-permute-start.3
  35.4 0.8 copy-done.6
  36.6 0.8 copy-done.8
  37.4 16.1 %collective-permute-done.3.refs_0_ = bf16[64,3200]{1,0:T(8,128)(2,1)S(1)} collective-permute-done((bf16[64,3200]{1,0:T(8,128)(2,1)S(1)}, bf16[64,3200]{1,0:T(8,128)(2,1)S(1)}, u32[]{:S(2)}, u32[]{:S(2)}) %collective-permute-start.3) | collective-permute-done | bytes 409632 | tf_op jit(solution)/shard_map/ppermute | solution.py:380
  53.5 1.3 collective-permute-done.4.refs_1_
  55.4 1.6 collective-permute-start.13
  57.0 0.8 copy-done.30
  58.3 0.8 copy-done.32
  59.1 0.9 copy-done.22
  60.0 1.6 collective-permute-start.6
  62.0 8.3 %collective-permute-done.13.refs_3_ = bf16[64,4096]{1,0:T(8,128)(2,1)S(1)} collective-permute-done((bf16[64,4096]{1,0:T(8,128)(2,1)S(1)}, bf16[64,4096]{1,0:T(8,128)(2,1)S(1)}, u32[]{:S(2)}, u32[]{:S(2)}) %collective-permute-start.13) | collective-permute-done | bytes 524320 | tf_op jit(solution)/shard_map/ppermute | solution.py:380
  70.3 1.6 collective-permute-start.14
  71.9 0.8 collective-permute-done.17.refs_4_
  73.2 5.9 %collective-permute-done.6.refs_0_ = bf16[64,3200]{1,0:T(8,128)(2,1)S(1)} collective-permute-done((bf16[64,3200]{1,0:T(8,128)(2,1)S(1)}, bf16[64,3200]{1,0:T(8,128)(2,1)S(1)}, u32[]{:S(2)}, u32[]{:S(2)}) %collective-permute-start.6) | collective-permute-done | bytes 409632 | tf_op jit(solution)/shard_map/ppermute | solution.py:380
  79.1 2.4 %collective-permute-done.7.refs_1_ = bf16[64,3200]{1,0:T(8,128)(2,1)S(1)} collective-permute-done((bf16[64,3200]{1,0:T(8,128)(2,1)S(1)}, bf16[64,3200]{1,0:T(8,128)(2,1)S(1)}, u32[]{:S(2)}, u32[]{:S(2)}) %collective-permute-start.7) | collective-permute-done | bytes 409632 | tf_op jit(solution)/shard_map/ppermute | solution.py:380
  81.5 1.0 pack.7
  82.5 1.5 collective-permute-start.20
  84.0 0.9 copy-done.24
  85.4 1.6 collective-permute-start.9
  87.0 6.4 %collective-permute-done.10.refs_1_.refs_2_ = bf16[32,3200]{1,0:T(8,128)(2,1)S(1)} collective-permute-done((bf16[32,3200]{1,0:T(8,128)(2,1)S(1)}, bf16[32,3200]{1,0:T(8,128)(2,1)S(1)}, u32[]{:S(2)}, u32[]{:S(2)}) %collective-permute-start.10) | collective-permute-done | bytes 204832 | tf_op jit(solution)/shard_map/ppermute | solution.py:380
  93.4 0.8 pack.6
  94.2 1.5 collective-permute-start.11
  95.7 0.8 slice.24
  96.5 1.5 collective-permute-start.15
  98.0 0.7 slice.25
  98.8 0.8 copy-done.16
  100.1 1.8 %copy-done.1 = bf16[144,10368]{1,0:T(8,128)(2,1)S(1)} copy-done((bf16[144,10368]{1,0:T(8,128)(2,1)S(1)}, bf16[144,10368]{1,0:T(8,128)(2,1)}, u32[]{:S(2)}) %copy-start.1) | copy-done | bytes 2986008
  102.0 1.0 copy-done.11
  103.0 1.0 copy-done.13
  104.0 1.1 copy-done.25
  105.1 1.0 copy-done.35
  106.2 1.0 copy-done.37
  107.2 3.0 %group_scores.6 = (f32[288,128]{1,0:T(8,128)S(1)}, bf16[128,1280]{1,0:T(8,128)(2,1)}) custom-call(s32[4]{0:T(128)S(1)} %pad_add_fusion.1.where_ref, bf16[144,10368]{1,0:T(8,128)(2,1)S(1)} %get-tuple-element.35.own_ref, bf16[144,10368]{1,0:T(8,128)(2,1)S(1)} %copy-done.1, f32[144,128]{1,0:T(8,128)S(1)} %get-tuple-element.39.bias_ref, ...), custom_call_target="tpu_custom_call" | custom-call | flops 764411904 | bytes 8626176 | tf_op jit(solution)/shard_map/group_scores/pallas_call | solution.py:243
  110.3 2.3 %group_scores.5 = (f32[288,128]{1,0:T(8,128)S(1)}, bf16[128,1280]{1,0:T(8,128)(2,1)S(1)}) custom-call(s32[4]{0:T(128)S(1)} %pad_add_fusion.1.where_ref, bf16[144,10368]{1,0:T(8,128)(2,1)S(1)} %get-tuple-element.35.own_ref, bf16[144,10368]{1,0:T(8,128)(2,1)S(1)} %copy-done.1, f32[144,128]{1,0:T(8,128)S(1)} %get-tuple-element.39.bias_ref, ...), custom_call_target="tpu_custom_call" | custom-call | flops 764411904 | bytes 8626176 | tf_op jit(solution)/shard_map/group_scores/pallas_call | solution.py:243
  113.2 2.9 %group_scores.4 = (f32[288,128]{1,0:T(8,128)S(1)}, bf16[128,1280]{1,0:T(8,128)(2,1)S(1)}) custom-call(s32[4]{0:T(128)S(1)} %pad_add_fusion.1.where_ref, bf16[144,10368]{1,0:T(8,128)(2,1)S(1)} %get-tuple-element.35.own_ref, bf16[144,10368]{1,0:T(8,128)(2,1)S(1)} %copy-done.1, f32[144,128]{1,0:T(8,128)S(1)} %get-tuple-element.39.bias_ref, ...), custom_call_target="tpu_custom_call" | custom-call | flops 764411904 | bytes 8626176 | tf_op jit(solution)/shard_map/group_scores/pallas_call | solution.py:243
  116.5 2.9 %group_scores.7 = (f32[288,128]{1,0:T(8,128)S(1)}, bf16[128,1280]{1,0:T(8,128)(2,1)S(1)}) custom-call(s32[4]{0:T(128)S(1)} %pad_add_fusion.1.where_ref, bf16[144,10368]{1,0:T(8,128)(2,1)S(1)} %get-tuple-element.35.own_ref, bf16[144,10368]{1,0:T(8,128)(2,1)S(1)} %copy-done.1, f32[144,128]{1,0:T(8,128)S(1)} %get-tuple-element.39.bias_ref, ...), custom_call_target="tpu_custom_call" | custom-call | flops 764411904 | bytes 8626176 | tf_op jit(solution)/shard_map/group_scores/pallas_call | solution.py:243
  120.0 0.8 collective-permute-done.24.refs_7_
  121.6 3.2 %collective-permute-done.25.refs_1_ = f32[8,512]{1,0:T(8,128)S(1)} collective-permute-done((f32[8,512]{1,0:T(8,128)S(1)}, f32[8,512]{1,0:T(8,128)S(1)}, u32[]{:S(2)}, u32[]{:S(2)}) %collective-permute-start.25) | collective-permute-done | bytes 16416 | tf_op jit(solution)/shard_map/ppermute | solution.py:435
  125.6 1.5 collective-permute-start.26
  128.9 2.0 %collective-permute-done.26.refs_1_ = bf16[160,512]{1,0:T(8,128)(2,1)S(1)} collective-permute-done((bf16[160,512]{1,0:T(8,128)(2,1)S(1)}, bf16[160,512]{1,0:T(8,128)(2,1)S(1)}, u32[]{:S(2)}, u32[]{:S(2)}) %collective-permute-start.26) | collective-permute-done | bytes 163872 | tf_op jit(solution)/shard_map/ppermute | solution.py:380
  130.9 1.5 collective-permute-start.27
  134.8 1.4 collective-permute-done.27.refs_2_
  136.2 1.5 collective-permute-start.28
  137.7 2.4 %pad_maximum_fusion.refs_8_ = bf16[512,1280]{1,0:T(8,128)(2,1)} fusion(bf16[128,1280]{1,0:T(8,128)(2,1)} %copy-done.44, bf16[128,1280]{1,0:T(8,128)(2,1)} %get-tuple-element.56, bf16[128,1280]{1,0:T(8,128)(2,1)} %copy-done.42, bf16[128,1280]{1,0:T(8,128)(2,1)} %copy-done.43), kind=kLoop, calls=%fused_computation.1 | loop fusion | flops 5242880 | bytes 2621440 | tf_op jit(solution)/shard_map/concatenate | solution.py:457
  140.1 0.7 collective-permute-done.31.refs_6_
  141.5 1.5 collective-permute-start.29
  143.1 1.2 pad_maximum_fusion.1.refs_9_
  144.2 2.4 %collective-permute-done.32.refs_5_ = bf16[160,512]{1,0:T(8,128)(2,1)S(1)} collective-permute-done((bf16[160,512]{1,0:T(8,128)(2,1)S(1)}, bf16[160,512]{1,0:T(8,128)(2,1)S(1)}, u32[]{:S(2)}, u32[]{:S(2)}) %collective-permute-start.32) | collective-permute-done | bytes 163872 | tf_op jit(solution)/shard_map/ppermute | solution.py:380
  148.0 11.9 %class_sums.1 = (bf16[1152,2560]{1,0:T(8,128)(2,1)}, f32[8,64]{1,0:T(8,128)}) custom-call(s32[9]{0:T(128)} %pad_add_fusion.blocks_ref, bf16[160,512]{1,0:T(8,128)(2,1)} %copy-done.26, bf16[160,512]{1,0:T(8,128)(2,1)} %copy-done.52, bf16[160,512]{1,0:T(8,128)(2,1)} %copy-done.54, bf16[160,512]{1,0:T(8,128)(2,1)} %copy-done.56, bf16[160,512]{1,0:T(8,128)(2,1)} %copy-done.58, ...), custom_call_target="tpu_custom_call" | custom-call | tf_op jit(solution)/shard_map/class_sums/pallas_call | solution.py:476
  159.9 1.2 slice_bitcast_fusion
  (159 shorter events, 15.8 us)
Async XLA Ops:
  0.6 6.8 %copy-start.50 = (f32[100]{0:T(128)S(1)}, f32[100]{0:T(128)}, u32[]{:S(2)}) copy-start(f32[100]{0:T(128)} %param.13) | copy-start | bytes 1204
  0.6 6.0 %copy-start.59 = (f32[1,144]{1,0:T(1,128)S(1)}, f32[1,144]{1,0:T(1,128)}, u32[]{:S(2)}) copy-start(f32[1,144]{1,0:T(1,128)} %param.10) | copy-start | bytes 1732
  6.7 10.4 %copy-start.38 = (bf16[64,3200]{1,0:T(8,128)(2,1)}, bf16[64,3200]{1,0:T(8,128)(2,1)S(1)}, u32[]{:S(2)}) copy-start(bf16[64,3200]{1,0:T(8,128)(2,1)S(1)} %get-tuple-element.36.refs_0_) | copy-start | bytes 1228804
  11.0 20.8 %copy-start.28 = (bf16[64,4096]{1,0:T(8,128)(2,1)S(1)}, bf16[64,4096]{1,0:T(8,128)(2,1)}, u32[]{:S(2)}) copy-start(bf16[64,4096]{1,0:T(8,128)(2,1)} %copy-done.27) | copy-start | bytes 1572868
  13.9 14.7 %collective-permute-start.2 = (bf16[144,10368]{1,0:T(8,128)(2,1)S(1)}, bf16[144,10368]{1,0:T(8,128)(2,1)S(1)}, u32[]{:S(2)}, u32[]{:S(2)}) collective-permute-start(bf16[144,10368]{1,0:T(8,128)(2,1)S(1)} %get-tuple-element.37), channel_id=1, source_target_pairs={{0,8},{8,0},{16,24},{24,16},{1,9},{9,1},{17,25},{25,17},{2,10},{10... | collective-permute-start | bytes 8957960 | tf_op jit(solution)/shard_map/ppermute | solution.py:383
  14.4 12.6 %collective-permute-start = (bf16[64,3200]{1,0:T(8,128)(2,1)S(1)}, bf16[64,3200]{1,0:T(8,128)(2,1)S(1)}, u32[]{:S(2)}, u32[]{:S(2)}) collective-permute-start(bf16[64,3200]{1,0:T(8,128)(2,1)S(1)} %get-tuple-element.36.refs_0_), channel_id=1, source_target_pairs={{0,2},{2,4},{4,6},{6,7},{7,5},{5,3},{3,1},{1,0},{8,10},{10,12},{12... | collective-permute-start | bytes 1228808 | tf_op jit(solution)/shard_map/ppermute | solution.py:380
  17.1 11.5 %collective-permute-start.1 = (bf16[64,3200]{1,0:T(8,128)(2,1)S(1)}, bf16[64,3200]{1,0:T(8,128)(2,1)S(1)}, u32[]{:S(2)}, u32[]{:S(2)}) collective-permute-start(bf16[64,3200]{1,0:T(8,128)(2,1)S(1)} %get-tuple-element.36.refs_0_), channel_id=1, source_target_pairs={{0,1},{2,0},{4,2},{6,4},{7,6},{5,7},{3,5},{1,3},{8,9},{10,8},{12,1... | collective-permute-start | bytes 1228808 | tf_op jit(solution)/shard_map/ppermute | solution.py:380
  30.3 28.8 %collective-permute-start.5 = (bf16[128,3072]{1,0:T(8,128)(2,1)S(1)}, bf16[128,3072]{1,0:T(8,128)(2,1)S(1)}, u32[]{:S(2)}, u32[]{:S(2)}) collective-permute-start(bf16[128,3072]{1,0:T(8,128)(2,1)S(1)} %pack.4), channel_id=1, source_target_pairs={{0,16},{8,24},{16,0},{24,8},{1,17},{9,25},{17,1},{25,9},{2,18},{10... | collective-permute-start | bytes 2359304 | tf_op jit(solution)/shard_map/ppermute | solution.py:386
  31.8 23.6 %collective-permute-start.12 = (bf16[64,4096]{1,0:T(8,128)(2,1)S(1)}, bf16[64,4096]{1,0:T(8,128)(2,1)S(1)}, u32[]{:S(2)}, u32[]{:S(2)}) collective-permute-start(bf16[64,4096]{1,0:T(8,128)(2,1)S(1)} %copy-done.28), channel_id=1, source_target_pairs={{0,2},{2,4},{4,6},{6,7},{7,5},{5,3},{3,1},{1,0},{8,10},{10,12},{12... | collective-permute-start | bytes 1572872 | tf_op jit(solution)/shard_map/ppermute | solution.py:380
  33.4 24.4 %collective-permute-start.16 = (bf16[64,4096]{1,0:T(8,128)(2,1)S(1)}, bf16[64,4096]{1,0:T(8,128)(2,1)S(1)}, u32[]{:S(2)}, u32[]{:S(2)}) collective-permute-start(bf16[64,4096]{1,0:T(8,128)(2,1)S(1)} %copy-done.28), channel_id=1, source_target_pairs={{0,1},{2,0},{4,2},{6,4},{7,6},{5,7},{3,5},{1,3},{8,9},{10,8},{12,1... | collective-permute-start | bytes 1572872 | tf_op jit(solution)/shard_map/ppermute | solution.py:380
  33.9 19.6 %collective-permute-start.3 = (bf16[64,3200]{1,0:T(8,128)(2,1)S(1)}, bf16[64,3200]{1,0:T(8,128)(2,1)S(1)}, u32[]{:S(2)}, u32[]{:S(2)}) collective-permute-start(bf16[64,3200]{1,0:T(8,128)(2,1)S(1)} %collective-permute-done.refs_0_), channel_id=1, source_target_pairs={{0,2},{2,4},{4,6},{6,7},{7,5},{5,3},{3,1},{1,0},{8,10},{10,12},{12... | collective-permute-start | bytes 1228808 | tf_op jit(solution)/shard_map/ppermute | solution.py:380
  36.2 18.6 %collective-permute-start.4 = (bf16[64,3200]{1,0:T(8,128)(2,1)S(1)}, bf16[64,3200]{1,0:T(8,128)(2,1)S(1)}, u32[]{:S(2)}, u32[]{:S(2)}) collective-permute-start(bf16[64,3200]{1,0:T(8,128)(2,1)S(1)} %collective-permute-done.1.refs_1_), channel_id=1, source_target_pairs={{0,1},{2,0},{4,2},{6,4},{7,6},{5,7},{3,5},{1,3},{8,9},{10,8},{12,1... | collective-permute-start | bytes 1228808 | tf_op jit(solution)/shard_map/ppermute | solution.py:380
  53.5 43.0 %copy-start.10 = (bf16[64,3200]{1,0:T(8,128)(2,1)}, bf16[64,3200]{1,0:T(8,128)(2,1)S(1)}, u32[]{:S(2)}) copy-start(bf16[64,3200]{1,0:T(8,128)(2,1)S(1)} %collective-permute-done.3.refs_0_) | copy-start | bytes 1228804
  54.8 41.7 %copy-start.12 = (bf16[64,3200]{1,0:T(8,128)(2,1)}, bf16[64,3200]{1,0:T(8,128)(2,1)S(1)}, u32[]{:S(2)}) copy-start(bf16[64,3200]{1,0:T(8,128)(2,1)S(1)} %collective-permute-done.4.refs_1_) | copy-start | bytes 1228804
  54.8 29.2 %collective-permute-start.8 = (bf16[128,3072]{1,0:T(8,128)(2,1)S(1)}, bf16[128,3072]{1,0:T(8,128)(2,1)S(1)}, u32[]{:S(2)}, u32[]{:S(2)}) collective-permute-start(bf16[128,3072]{1,0:T(8,128)(2,1)S(1)} %pack.5), channel_id=1, source_target_pairs={{0,16},{8,24},{16,0},{24,8},{1,17},{9,25},{17,1},{25,9},{2,18},{10... | collective-permute-start | bytes 2359304 | tf_op jit(solution)/shard_map/ppermute | solution.py:386
  55.4 14.9 %collective-permute-start.13 = (bf16[64,4096]{1,0:T(8,128)(2,1)S(1)}, bf16[64,4096]{1,0:T(8,128)(2,1)S(1)}, u32[]{:S(2)}, u32[]{:S(2)}) collective-permute-start(bf16[64,4096]{1,0:T(8,128)(2,1)S(1)} %collective-permute-done.12.refs_3_), channel_id=1, source_target_pairs={{0,2},{2,4},{4,6},{6,7},{7,5},{5,3},{3,1},{1,0},{8,10},{10,12},{12... | collective-permute-start | bytes 1572872 | tf_op jit(solution)/shard_map/ppermute | solution.py:380
  57.8 14.9 %collective-permute-start.17 = (bf16[64,4096]{1,0:T(8,128)(2,1)S(1)}, bf16[64,4096]{1,0:T(8,128)(2,1)S(1)}, u32[]{:S(2)}, u32[]{:S(2)}) collective-permute-start(bf16[64,4096]{1,0:T(8,128)(2,1)S(1)} %collective-permute-done.16.refs_4_), channel_id=1, source_target_pairs={{0,1},{2,0},{4,2},{6,4},{7,6},{5,7},{3,5},{1,3},{8,9},{10,8},{12,1... | collective-permute-start | bytes 1572872 | tf_op jit(solution)/shard_map/ppermute | solution.py:380
  60.0 19.1 %collective-permute-start.6 = (bf16[64,3200]{1,0:T(8,128)(2,1)S(1)}, bf16[64,3200]{1,0:T(8,128)(2,1)S(1)}, u32[]{:S(2)}, u32[]{:S(2)}) collective-permute-start(bf16[64,3200]{1,0:T(8,128)(2,1)S(1)} %collective-permute-done.3.refs_0_), channel_id=1, source_target_pairs={{0,2},{2,4},{4,6},{6,7},{7,5},{5,3},{3,1},{1,0},{8,10},{10,12},{12... | collective-permute-start | bytes 1228808 | tf_op jit(solution)/shard_map/ppermute | solution.py:380
  61.6 19.9 %collective-permute-start.7 = (bf16[64,3200]{1,0:T(8,128)(2,1)S(1)}, bf16[64,3200]{1,0:T(8,128)(2,1)S(1)}, u32[]{:S(2)}, u32[]{:S(2)}) collective-permute-start(bf16[64,3200]{1,0:T(8,128)(2,1)S(1)} %collective-permute-done.4.refs_1_), channel_id=1, source_target_pairs={{0,1},{2,0},{4,2},{6,4},{7,6},{5,7},{3,5},{1,3},{8,9},{10,8},{12,1... | collective-permute-start | bytes 1228808 | tf_op jit(solution)/shard_map/ppermute | solution.py:380
  70.3 29.7 %copy-start.34 = (bf16[64,4096]{1,0:T(8,128)(2,1)}, bf16[64,4096]{1,0:T(8,128)(2,1)S(1)}, u32[]{:S(2)}) copy-start(bf16[64,4096]{1,0:T(8,128)(2,1)S(1)} %collective-permute-done.13.refs_3_) | copy-start | bytes 1572868
  70.3 25.4 %collective-permute-start.14 = (bf16[64,4096]{1,0:T(8,128)(2,1)S(1)}, bf16[64,4096]{1,0:T(8,128)(2,1)S(1)}, u32[]{:S(2)}, u32[]{:S(2)}) collective-permute-start(bf16[64,4096]{1,0:T(8,128)(2,1)S(1)} %collective-permute-done.13.refs_3_), channel_id=1, source_target_pairs={{0,2},{2,4},{4,6},{6,7},{7,5},{5,3},{3,1},{1,0},{8,10},{10,12},{12... | collective-permute-start | bytes 1572872 | tf_op jit(solution)/shard_map/ppermute | solution.py:380
  72.7 27.3 %copy-start.36 = (bf16[64,4096]{1,0:T(8,128)(2,1)}, bf16[64,4096]{1,0:T(8,128)(2,1)S(1)}, u32[]{:S(2)}) copy-start(bf16[64,4096]{1,0:T(8,128)(2,1)S(1)} %collective-permute-done.17.refs_4_) | copy-start | bytes 1572868
  72.7 25.3 %collective-permute-start.18 = (bf16[64,4096]{1,0:T(8,128)(2,1)S(1)}, bf16[64,4096]{1,0:T(8,128)(2,1)S(1)}, u32[]{:S(2)}, u32[]{:S(2)}) collective-permute-start(bf16[64,4096]{1,0:T(8,128)(2,1)S(1)} %collective-permute-done.17.refs_4_), channel_id=1, source_target_pairs={{0,1},{2,0},{4,2},{6,4},{7,6},{5,7},{3,5},{1,3},{8,9},{10,8},{12,1... | collective-permute-start | bytes 1572872 | tf_op jit(solution)/shard_map/ppermute | solution.py:380
  82.5 34.0 %collective-permute-start.20 = (bf16[128,3072]{1,0:T(8,128)(2,1)}, bf16[128,3072]{1,0:T(8,128)(2,1)}, u32[]{:S(2)}, u32[]{:S(2)}) collective-permute-start(bf16[128,3072]{1,0:T(8,128)(2,1)} %pack.7), channel_id=1, source_target_pairs={{0,16},{8,24},{16,0},{24,8},{1,17},{9,25},{17,1},{25,9},{2,18},{10... | collective-permute-start | bytes 2359304 | tf_op jit(solution)/shard_map/ppermute | solution.py:386
  84.9 8.4 %collective-permute-start.10 = (bf16[32,3200]{1,0:T(8,128)(2,1)S(1)}, bf16[32,3200]{1,0:T(8,128)(2,1)S(1)}, u32[]{:S(2)}, u32[]{:S(2)}) collective-permute-start(bf16[32,3200]{1,0:T(8,128)(2,1)S(1)} %slice.23), channel_id=1, source_target_pairs={{0,1},{2,0},{4,2},{6,4},{7,6},{5,7},{3,5},{1,3},{8,9},{10,8},{12,1... | collective-permute-start | bytes 614408 | tf_op jit(solution)/shard_map/ppermute | solution.py:380
  85.4 8.0 %collective-permute-start.9 = (bf16[32,3200]{1,0:T(8,128)(2,1)S(1)}, bf16[32,3200]{1,0:T(8,128)(2,1)S(1)}, u32[]{:S(2)}, u32[]{:S(2)}) collective-permute-start(bf16[32,3200]{1,0:T(8,128)(2,1)S(1)} %slice.22), channel_id=1, source_target_pairs={{0,2},{2,4},{4,6},{6,7},{7,5},{5,3},{3,1},{1,0},{8,10},{10,12},{12... | collective-permute-start | bytes 614408 | tf_op jit(solution)/shard_map/ppermute | solution.py:380
  93.4 5.4 %copy-start.18 = (bf16[32,3200]{1,0:T(8,128)(2,1)}, bf16[32,3200]{1,0:T(8,128)(2,1)S(1)}, u32[]{:S(2)}) copy-start(bf16[32,3200]{1,0:T(8,128)(2,1)S(1)} %collective-permute-done.10.refs_1_.refs_2_) | copy-start | bytes 614404
  93.4 6.7 %copy-start.20 = (bf16[32,3200]{1,0:T(8,128)(2,1)}, bf16[32,3200]{1,0:T(8,128)(2,1)S(1)}, u32[]{:S(2)}) copy-start(bf16[32,3200]{1,0:T(8,128)(2,1)S(1)} %collective-permute-done.9.refs_0_.refs_1_) | copy-start | bytes 614404
  94.2 19.0 %collective-permute-start.11 = (bf16[64,3072]{1,0:T(8,128)(2,1)}, bf16[64,3072]{1,0:T(8,128)(2,1)}, u32[]{:S(2)}, u32[]{:S(2)}) collective-permute-start(bf16[64,3072]{1,0:T(8,128)(2,1)} %pack.6), channel_id=1, source_target_pairs={{0,16},{8,24},{16,0},{24,8},{1,17},{9,25},{17,1},{25,9},{2,18},{10... | collective-permute-start | bytes 1179656 | tf_op jit(solution)/shard_map/ppermute | solution.py:386
  96.5 16.1 %collective-permute-start.15 = (bf16[32,4096]{1,0:T(8,128)(2,1)}, bf16[32,4096]{1,0:T(8,128)(2,1)}, u32[]{:S(2)}, u32[]{:S(2)}) collective-permute-start(bf16[32,4096]{1,0:T(8,128)(2,1)} %slice.24), channel_id=1, source_target_pairs={{0,2},{2,4},{4,6},{6,7},{7,5},{5,3},{3,1},{1,0},{8,10},{10,12},{12... | collective-permute-start | bytes 786440 | tf_op jit(solution)/shard_map/ppermute | solution.py:380
  99.5 13.7 %collective-permute-start.19 = (bf16[32,4096]{1,0:T(8,128)(2,1)}, bf16[32,4096]{1,0:T(8,128)(2,1)}, u32[]{:S(2)}, u32[]{:S(2)}) collective-permute-start(bf16[32,4096]{1,0:T(8,128)(2,1)} %slice.25), channel_id=1, source_target_pairs={{0,1},{2,0},{4,2},{6,4},{7,6},{5,7},{3,5},{1,3},{8,9},{10,8},{12,1... | collective-permute-start | bytes 786440 | tf_op jit(solution)/shard_map/ppermute | solution.py:380
  107.2 3.1 %copy-start.23 = (bf16[128,3072]{1,0:T(8,128)(2,1)S(1)}, bf16[128,3072]{1,0:T(8,128)(2,1)}, u32[]{:S(2)}) copy-start(bf16[128,3072]{1,0:T(8,128)(2,1)} %copy-done.22) | copy-start | bytes 2359300
  107.2 3.1 %copy-start.31 = (bf16[64,4096]{1,0:T(8,128)(2,1)S(1)}, bf16[64,4096]{1,0:T(8,128)(2,1)}, u32[]{:S(2)}) copy-start(bf16[64,4096]{1,0:T(8,128)(2,1)} %copy-done.30) | copy-start | bytes 1572868
  107.2 3.1 %copy-start.33 = (bf16[64,4096]{1,0:T(8,128)(2,1)S(1)}, bf16[64,4096]{1,0:T(8,128)(2,1)}, u32[]{:S(2)}) copy-start(bf16[64,4096]{1,0:T(8,128)(2,1)} %copy-done.32) | copy-start | bytes 1572868
  110.2 9.8 %collective-permute-start.23 = (f32[288,128]{1,0:T(8,128)S(1)}, f32[288,128]{1,0:T(8,128)S(1)}, u32[]{:S(2)}, u32[]{:S(2)}) collective-permute-start(f32[288,128]{1,0:T(8,128)S(1)} %get-tuple-element.50.refs_2_), channel_id=1, source_target_pairs={{0,8},{8,0},{16,24},{24,16},{1,9},{9,1},{17,25},{25,17},{2,10},{10... | collective-permute-start | bytes 442376 | tf_op jit(solution)/shard_map/ppermute | solution.py:383
  112.6 3.5 %copy-start.42 = (bf16[128,1280]{1,0:T(8,128)(2,1)}, bf16[128,1280]{1,0:T(8,128)(2,1)S(1)}, u32[]{:S(2)}) copy-start(bf16[128,1280]{1,0:T(8,128)(2,1)S(1)} %get-tuple-element.55) | copy-start | bytes 983044
  112.6 3.9 %copy-start.5 = (bf16[64,3200]{1,0:T(8,128)(2,1)S(1)}, bf16[64,3200]{1,0:T(8,128)(2,1)}, u32[]{:S(2)}) copy-start(bf16[64,3200]{1,0:T(8,128)(2,1)} %copy-done.4) | copy-start | bytes 1228804
  112.6 3.9 %copy-start.15 = (bf16[64,4096]{1,0:T(8,128)(2,1)S(1)}, bf16[64,4096]{1,0:T(8,128)(2,1)}, u32[]{:S(2)}) copy-start(bf16[64,4096]{1,0:T(8,128)(2,1)} %copy-done.14) | copy-start | bytes 1572868
  112.6 3.9 %copy-start.17 = (bf16[64,4096]{1,0:T(8,128)(2,1)S(1)}, bf16[64,4096]{1,0:T(8,128)(2,1)}, u32[]{:S(2)}) copy-start(bf16[64,4096]{1,0:T(8,128)(2,1)} %copy-done.16) | copy-start | bytes 1572868
  112.7 7.4 %collective-permute-start.22 = (f32[288,128]{1,0:T(8,128)S(1)}, f32[288,128]{1,0:T(8,128)S(1)}, u32[]{:S(2)}, u32[]{:S(2)}) collective-permute-start(f32[288,128]{1,0:T(8,128)S(1)} %get-tuple-element.49.refs_1_), channel_id=1, source_target_pairs={{0,8},{8,0},{16,24},{24,16},{1,9},{9,1},{17,25},{25,17},{2,10},{10... | collective-permute-start | bytes 442376 | tf_op jit(solution)/shard_map/ppermute | solution.py:383
  116.2 3.3 %copy-start.43 = (bf16[128,1280]{1,0:T(8,128)(2,1)}, bf16[128,1280]{1,0:T(8,128)(2,1)S(1)}, u32[]{:S(2)}) copy-start(bf16[128,1280]{1,0:T(8,128)(2,1)S(1)} %get-tuple-element.54) | copy-start | bytes 983044
  116.2 10.9 %copy-start.60 = (s32[8]{0:T(128)S(1)}, s32[8]{0:T(128)}, u32[]{:S(2)}) copy-start(s32[8]{0:T(128)} %constant.57.clone) | copy-start | bytes 100
  116.2 16.2 %copy-start.51 = (s32[8]{0:T(128)S(1)}, s32[8]{0:T(128)}, u32[]{:S(2)}) copy-start(s32[8]{0:T(128)} %constant.58.clone) | copy-start | bytes 100
  116.2 3.8 %collective-permute-start.21 = (f32[288,128]{1,0:T(8,128)S(1)}, f32[288,128]{1,0:T(8,128)S(1)}, u32[]{:S(2)}, u32[]{:S(2)}) collective-permute-start(f32[288,128]{1,0:T(8,128)S(1)} %get-tuple-element.48.refs_0_), channel_id=1, source_target_pairs={{0,8},{8,0},{16,24},{24,16},{1,9},{9,1},{17,25},{25,17},{2,10},{10... | collective-permute-start | bytes 442376 | tf_op jit(solution)/shard_map/ppermute | solution.py:383
  119.4 5.4 %copy-start.44 = (bf16[128,1280]{1,0:T(8,128)(2,1)}, bf16[128,1280]{1,0:T(8,128)(2,1)S(1)}, u32[]{:S(2)}) copy-start(bf16[128,1280]{1,0:T(8,128)(2,1)S(1)} %get-tuple-element.57) | copy-start | bytes 983044
  119.4 1.4 collective-permute-start.24
  119.8 13.9 %collective-permute-start.35 = (bf16[128,1280]{1,0:T(8,128)(2,1)}, bf16[128,1280]{1,0:T(8,128)(2,1)S(1)}, u32[]{:S(2)}, u32[]{:S(2)}) collective-permute-start(bf16[128,1280]{1,0:T(8,128)(2,1)} %get-tuple-element.56), channel_id=1, source_target_pairs={{0,8},{8,0},{16,24},{24,16},{1,9},{9,1},{17,25},{25,17},{2,10},{10... | collective-permute-start | bytes 983048 | tf_op jit(solution)/shard_map/ppermute | solution.py:383
  121.0 3.8 %collective-permute-start.25 = (f32[8,512]{1,0:T(8,128)S(1)}, f32[8,512]{1,0:T(8,128)S(1)}, u32[]{:S(2)}, u32[]{:S(2)}) collective-permute-start(f32[8,512]{1,0:T(8,128)S(1)} %get-tuple-element.53.refs_0_), channel_id=1, source_target_pairs={{0,16},{8,24},{16,0},{24,8},{1,17},{9,25},{17,1},{25,9},{2,18},{10... | collective-permute-start | bytes 49160 | tf_op jit(solution)/shard_map/ppermute | solution.py:435
  125.6 18.7 %copy-start.26 = (bf16[160,512]{1,0:T(8,128)(2,1)}, bf16[160,512]{1,0:T(8,128)(2,1)S(1)}, u32[]{:S(2)}) copy-start(bf16[160,512]{1,0:T(8,128)(2,1)S(1)} %payload.1.refs_0_) | copy-start | bytes 491524
  125.6 5.3 %collective-permute-start.26 = (bf16[160,512]{1,0:T(8,128)(2,1)S(1)}, bf16[160,512]{1,0:T(8,128)(2,1)S(1)}, u32[]{:S(2)}, u32[]{:S(2)}) collective-permute-start(bf16[160,512]{1,0:T(8,128)(2,1)S(1)} %payload.1.refs_0_), channel_id=1, source_target_pairs={{0,2},{2,4},{4,6},{6,7},{7,5},{5,3},{3,1},{1,0},{8,10},{10,12},{12... | collective-permute-start | bytes 491528 | tf_op jit(solution)/shard_map/ppermute | solution.py:380
  128.3 6.0 %collective-permute-start.30 = (bf16[160,512]{1,0:T(8,128)(2,1)S(1)}, bf16[160,512]{1,0:T(8,128)(2,1)S(1)}, u32[]{:S(2)}, u32[]{:S(2)}) collective-permute-start(bf16[160,512]{1,0:T(8,128)(2,1)S(1)} %payload.1.refs_0_), channel_id=1, source_target_pairs={{0,1},{2,0},{4,2},{6,4},{7,6},{5,7},{3,5},{1,3},{8,9},{10,8},{12,1... | collective-permute-start | bytes 491528 | tf_op jit(solution)/shard_map/ppermute | solution.py:380
  130.9 13.3 %copy-start.52 = (bf16[160,512]{1,0:T(8,128)(2,1)}, bf16[160,512]{1,0:T(8,128)(2,1)S(1)}, u32[]{:S(2)}) copy-start(bf16[160,512]{1,0:T(8,128)(2,1)S(1)} %collective-permute-done.26.refs_1_) | copy-start | bytes 491524
  130.9 5.3 %collective-permute-start.27 = (bf16[160,512]{1,0:T(8,128)(2,1)S(1)}, bf16[160,512]{1,0:T(8,128)(2,1)S(1)}, u32[]{:S(2)}, u32[]{:S(2)}) collective-permute-start(bf16[160,512]{1,0:T(8,128)(2,1)S(1)} %collective-permute-done.26.refs_1_), channel_id=1, source_target_pairs={{0,2},{2,4},{4,6},{6,7},{7,5},{5,3},{3,1},{1,0},{8,10},{10,12},{12... | collective-permute-start | bytes 491528 | tf_op jit(solution)/shard_map/ppermute | solution.py:380
  133.1 10.0 %collective-permute-start.34 = (bf16[128,1280]{1,0:T(8,128)(2,1)}, bf16[128,1280]{1,0:T(8,128)(2,1)S(1)}, u32[]{:S(2)}, u32[]{:S(2)}) collective-permute-start(bf16[128,1280]{1,0:T(8,128)(2,1)} %copy-done.42), channel_id=1, source_target_pairs={{0,8},{8,0},{16,24},{24,16},{1,9},{9,1},{17,25},{25,17},{2,10},{10... | collective-permute-start | bytes 983048 | tf_op jit(solution)/shard_map/ppermute | solution.py:383
  133.1 9.9 %collective-permute-start.33 = (bf16[128,1280]{1,0:T(8,128)(2,1)}, bf16[128,1280]{1,0:T(8,128)(2,1)S(1)}, u32[]{:S(2)}, u32[]{:S(2)}) collective-permute-start(bf16[128,1280]{1,0:T(8,128)(2,1)} %copy-done.43), channel_id=1, source_target_pairs={{0,8},{8,0},{16,24},{24,16},{1,9},{9,1},{17,25},{25,17},{2,10},{10... | collective-permute-start | bytes 983048 | tf_op jit(solution)/shard_map/ppermute | solution.py:383
  133.6 9.4 %collective-permute-start.36 = (bf16[128,1280]{1,0:T(8,128)(2,1)}, bf16[128,1280]{1,0:T(8,128)(2,1)S(1)}, u32[]{:S(2)}, u32[]{:S(2)}) collective-permute-start(bf16[128,1280]{1,0:T(8,128)(2,1)} %copy-done.44), channel_id=1, source_target_pairs={{0,8},{8,0},{16,24},{24,16},{1,9},{9,1},{17,25},{25,17},{2,10},{10... | collective-permute-start | bytes 983048 | tf_op jit(solution)/shard_map/ppermute | solution.py:383
  134.3 9.9 %copy-start.53 = (bf16[160,512]{1,0:T(8,128)(2,1)}, bf16[160,512]{1,0:T(8,128)(2,1)S(1)}, u32[]{:S(2)}) copy-start(bf16[160,512]{1,0:T(8,128)(2,1)S(1)} %collective-permute-done.30.refs_7_) | copy-start | bytes 491524
  134.3 6.6 %collective-permute-start.31 = (bf16[160,512]{1,0:T(8,128)(2,1)S(1)}, bf16[160,512]{1,0:T(8,128)(2,1)S(1)}, u32[]{:S(2)}, u32[]{:S(2)}) collective-permute-start(bf16[160,512]{1,0:T(8,128)(2,1)S(1)} %collective-permute-done.30.refs_7_), channel_id=1, source_target_pairs={{0,1},{2,0},{4,2},{6,4},{7,6},{5,7},{3,5},{1,3},{8,9},{10,8},{12,1... | collective-permute-start | bytes 491528 | tf_op jit(solution)/shard_map/ppermute | solution.py:380
  136.2 8.0 %copy-start.54 = (bf16[160,512]{1,0:T(8,128)(2,1)}, bf16[160,512]{1,0:T(8,128)(2,1)S(1)}, u32[]{:S(2)}) copy-start(bf16[160,512]{1,0:T(8,128)(2,1)S(1)} %collective-permute-done.27.refs_2_) | copy-start | bytes 491524
  136.2 5.3 %collective-permute-start.28 = (bf16[160,512]{1,0:T(8,128)(2,1)S(1)}, bf16[160,512]{1,0:T(8,128)(2,1)S(1)}, u32[]{:S(2)}, u32[]{:S(2)}) collective-permute-start(bf16[160,512]{1,0:T(8,128)(2,1)S(1)} %collective-permute-done.27.refs_2_), channel_id=1, source_target_pairs={{0,2},{2,4},{4,6},{6,7},{7,5},{5,3},{3,1},{1,0},{8,10},{10,12},{12... | collective-permute-start | bytes 491528 | tf_op jit(solution)/shard_map/ppermute | solution.py:380
  140.9 6.0 %copy-start.55 = (bf16[160,512]{1,0:T(8,128)(2,1)}, bf16[160,512]{1,0:T(8,128)(2,1)S(1)}, u32[]{:S(2)}) copy-start(bf16[160,512]{1,0:T(8,128)(2,1)S(1)} %collective-permute-done.31.refs_6_) | copy-start | bytes 491524
  140.9 5.8 %collective-permute-start.32 = (bf16[160,512]{1,0:T(8,128)(2,1)S(1)}, bf16[160,512]{1,0:T(8,128)(2,1)S(1)}, u32[]{:S(2)}, u32[]{:S(2)}) collective-permute-start(bf16[160,512]{1,0:T(8,128)(2,1)S(1)} %collective-permute-done.31.refs_6_), channel_id=1, source_target_pairs={{0,1},{2,0},{4,2},{6,4},{7,6},{5,7},{3,5},{1,3},{8,9},{10,8},{12,1... | collective-permute-start | bytes 491528 | tf_op jit(solution)/shard_map/ppermute | solution.py:380
  141.5 5.3 %copy-start.56 = (bf16[160,512]{1,0:T(8,128)(2,1)}, bf16[160,512]{1,0:T(8,128)(2,1)S(1)}, u32[]{:S(2)}) copy-start(bf16[160,512]{1,0:T(8,128)(2,1)S(1)} %collective-permute-done.28.refs_3_) | copy-start | bytes 491524
  141.5 5.3 %collective-permute-start.29 = (bf16[160,512]{1,0:T(8,128)(2,1)S(1)}, bf16[160,512]{1,0:T(8,128)(2,1)S(1)}, u32[]{:S(2)}, u32[]{:S(2)}) collective-permute-start(bf16[160,512]{1,0:T(8,128)(2,1)S(1)} %collective-permute-done.28.refs_3_), channel_id=1, source_target_pairs={{0,2},{2,4},{4,6},{6,7},{7,5},{5,3},{3,1},{1,0},{8,10},{10,12},{12... | collective-permute-start | bytes 491528 | tf_op jit(solution)/shard_map/ppermute | solution.py:380
  (34 other events, 53.8 us)

commit v2 on v1

v2 whole, which is shorter than its diff:
```python
import functools
import math

import jax
import jax.numpy as jnp
from jax import lax
from jax.experimental import pallas as pl
from jax.experimental.pallas import tpu as pltpu
from jax.sharding import PartitionSpec as P

BF16 = jnp.bfloat16
F32 = jnp.float32
MASKED = -1e30
LANES = 128
MIB = 1 << 20
TAIL = 16


def cycle_of(count):
    deep = math.isqrt(count // 2)
    tall = count // deep
    walk = [(z, 0) for z in range(tall)]
    for z in range(tall - 1, -1, -1):
        cols = list(range(1, deep))
        walk += [(z, y) for y in (cols if (tall - 1 - z) % 2 == 0 else cols[::-1])]
    return [z * deep + y for z, y in walk]


def weight_table(index, noise):
    levels = noise.shape[1]
    row = jnp.concatenate([noise, jnp.zeros((1, LANES - levels), F32)], axis=1)
    table = jnp.broadcast_to(row, index.shape)
    return jnp.take_along_axis(table, index, axis=1, mode="promise_in_bounds")


def at(start, size):
    return pl.ds(pl.multiple_of(start, LANES), size)


def image_kernel(n, wo, ws, img_hbm, index_hbm, noise_hbm, sig_hbm, own_ref, oth_ref, shared_ref, w_ref, img, index, noise, sig, sems):
    cls = lax.axis_index("cls")
    core, side = cls % 2, (cls // 2) % 2
    half = 2 * wo + ws
    loads = []
    for i in range(n):
        src = img_hbm.at[:, at((2 * i + core) * half, half)]
        loads.append(pltpu.make_async_copy(src, img.at[:, i * half : (i + 1) * half], sems.at[i]))
    small = [(index_hbm, index), (noise_hbm, noise), (sig_hbm, sig)]
    copies = [pltpu.make_async_copy(src, dst, sems.at[n + i]) for i, (src, dst) in enumerate(small)]
    for copy in copies + loads:
        copy.start()
    for copy in copies:
        copy.wait()
    w_ref[...] = weight_table(index[...], noise[...])
    rows = img.shape[0]
    block = lax.broadcasted_iota(jnp.int32, (LANES, rows), 0)
    listed = block < 0
    for j in range(sig.shape[0]):
        listed = listed | (sig[j : j + 1, :] == block)
    unlisted = jnp.where(listed, 0.0, 1.0).astype(BF16)
    same = lax.broadcasted_iota(jnp.int32, (rows, rows), 0) == lax.broadcasted_iota(jnp.int32, (rows, rows), 1)
    eye = jnp.where(same, 1.0, 0.0).astype(BF16)
    turned = lax.dot_general(eye, unlisted, (((1,), (1,)), ((), ())), preferred_element_type=F32)
    own_ref[:, n * wo :] = turned.astype(BF16)
    for i in range(n):
        loads[i].wait()
        for ref, start, count in (
            (own_ref, side * wo, wo),
            (oth_ref, (1 - side) * wo, wo),
            (shared_ref, 2 * wo, ws),
        ):
            for j in range(0, count, LANES):
                tile = ((2 * i + core) * half + start + j) // LANES
                weight = w_ref[pl.ds(tile, 1), :]
                wide = img[:, at(i * half + start + j, LANES)].astype(F32) * weight
                ref[:, i * count + j : i * count + j + LANES] = wide.astype(BF16)


def prep_images(images, weight_of, significant, core, side, wo, ws, n):
    rows = images.shape[0]
    half = 2 * wo + ws
    if wo % LANES == 0:
        index, noise = weight_of
        sig = significant.T
        out = [jax.ShapeDtypeStruct((rows, w), BF16) for w in (n * wo + LANES, n * wo, n * ws)]
        out.append(jax.ShapeDtypeStruct(index.shape, F32))
        vmem = pl.BlockSpec(memory_space=pltpu.VMEM)
        return pl.pallas_call(
            functools.partial(image_kernel, n, wo, ws),
            in_specs=[pl.BlockSpec(memory_space=pl.ANY)] * 4,
            out_specs=[vmem] * 4,
            out_shape=out,
            scratch_shapes=[
                pltpu.VMEM((rows, n * half), BF16),
                pltpu.VMEM(index.shape, index.dtype),
                pltpu.VMEM(noise.shape, F32),
                pltpu.VMEM(sig.shape, sig.dtype),
                pltpu.SemaphoreType.DMA((n + 3,)),
            ],
            compiler_params=pltpu.CompilerParams(vmem_limit_bytes=61 * MIB),
            name="prep_images",
        )(images, index, noise, sig)
    weight = full_weights(weight_of)
    weighted = (images.astype(F32) * weight).astype(BF16).reshape(rows, n, 2, half)
    mine = lax.dynamic_index_in_dim(weighted, core, 2, keepdims=False)
    own, oth, shared = cut(mine, side, wo)
    lane = jnp.arange(LANES, dtype=jnp.int32)
    listed = jnp.any(significant[:, :, None] == lane[None, None, :], axis=1)
    return jnp.concatenate([own, jnp.where(listed, 0.0, 1.0).astype(BF16)], axis=1), oth, shared, weight


def full_weights(weight_of):
    index, noise = weight_of
    levels = jnp.arange(noise.shape[1], dtype=jnp.int32)
    return jnp.sum(jnp.where(index.reshape(-1, 1) == levels[None, :], noise, 0.0), axis=1)[None, :]


def cut(mine, side, wo):
    rows, n, _ = mine.shape
    own = lax.dynamic_slice_in_dim(mine, side * wo, wo, 2).reshape(rows, n * wo)
    oth = lax.dynamic_slice_in_dim(mine, (1 - side) * wo, wo, 2).reshape(rows, n * wo)
    return own, oth, mine[:, :, 2 * wo :].reshape(rows, -1)


def split_kernel(wo, ws, n, proj_hbm, keep_ref, send_ref, sems):
    half = 2 * wo + ws
    cls, owner = lax.axis_index("cls"), lax.axis_index("ori")
    core, side = cls % 2, (cls // 2) % 2
    copies = []
    for ref, which in ((send_ref, 1 - core), (keep_ref, core)):
        for i in range(n):
            base = (2 * i + which) * half
            for start, spot, count in (
                (base + side * wo, i * wo, wo),
                (base + 2 * wo, n * wo + LANES + i * ws, ws),
                (base + (1 - side) * wo, n * (wo + ws) + LANES + i * wo, wo),
            ):
                src = proj_hbm.at[0, :, at(start, count)]
                copies.append(pltpu.make_async_copy(src, ref.at[:, spot : spot + count], sems.at[len(copies)]))
                copies[-1].start()
    lane = lax.broadcasted_iota(jnp.int32, (keep_ref.shape[0], LANES), 1)
    gate = jnp.where(lane == owner, MASKED, 0.0).astype(BF16)
    keep_ref[:, n * wo : n * wo + LANES] = gate
    send_ref[:, n * wo : n * wo + LANES] = gate
    for copy in copies:
        copy.wait()


def norm_kernel(wo, ws, n, keep_ref, send_ref, prior_ref, w_ref, bias_ref):
    half = 2 * wo + ws
    cls = lax.axis_index("cls")
    core, side = cls % 2, (cls // 2) % 2
    rows = keep_ref.shape[0]
    total = jnp.zeros((rows, LANES), F32)
    for ref, which in ((keep_ref, core), (send_ref, 1 - core)):
        for i in range(n):
            base = (2 * i + which) * half
            for start, spot, count in (
                (base + side * wo, i * wo, wo),
                (base + 2 * wo, n * wo + LANES + i * ws, ws),
                (base + (1 - side) * wo, n * (wo + ws) + LANES + i * wo, wo),
            ):
                for j in range(0, count, LANES):
                    wide = ref[:, spot + j : spot + j + LANES].astype(F32)
                    total = total + wide * wide * w_ref[pl.ds((start + j) // LANES, 1), :]
    half_norm = 0.5 * jnp.sum(total, axis=1, keepdims=True)
    prior = jnp.concatenate([prior_ref[...], jnp.zeros((1, -rows % LANES), F32)], axis=1)
    spread = (rows, prior.shape[1])
    on_line = lax.broadcasted_iota(jnp.int32, spread, 0) == lax.broadcasted_iota(jnp.int32, spread, 1)
    prior = jnp.sum(jnp.where(on_line, prior, 0.0), axis=1, keepdims=True)
    bias_ref[...] = jnp.broadcast_to(prior - half_norm, bias_ref.shape)


def prep_projections(projections, weight, log_prior, core, side, owner, wo, ws, n):
    rows = projections.shape[1]
    half = 2 * wo + ws
    width = n * half + LANES
    if wo % LANES == 0:
        vmem = pl.BlockSpec(memory_space=pltpu.VMEM)
        keep, send = pl.pallas_call(
            functools.partial(split_kernel, wo, ws, n),
            in_specs=[pl.BlockSpec(memory_space=pl.ANY)],
            out_specs=[vmem] * 2,
            out_shape=[jax.ShapeDtypeStruct((rows, width), BF16)] * 2,
            scratch_shapes=[pltpu.SemaphoreType.DMA((6 * n,))],
            compiler_params=pltpu.CompilerParams(vmem_limit_bytes=54 * MIB),
            cost_estimate=pl.CostEstimate(flops=0, bytes_accessed=4 * projections.size, transcendentals=0),
            name="split_projections",
        )(projections)
        bias = pl.pallas_call(
            functools.partial(norm_kernel, wo, ws, n),
            in_specs=[vmem] * 4,
            out_specs=vmem,
            out_shape=jax.ShapeDtypeStruct((rows, LANES), F32),
            compiler_params=pltpu.CompilerParams(vmem_limit_bytes=16 * MIB),
            cost_estimate=pl.CostEstimate(flops=3 * projections.size, bytes_accessed=2 * projections.size, transcendentals=0),
            name="half_norms",
        )(keep, send, log_prior, weight)
        return keep, send, bias
    projection, prior = projections[0], log_prior.reshape(rows, 1)
    half_norm = 0.5 * jnp.sum(jnp.square(projection.astype(F32)) * weight, axis=1, keepdims=True)
    bias = jnp.broadcast_to(prior - half_norm, (rows, LANES))
    lane = jnp.arange(LANES, dtype=jnp.int32)
    gate = jnp.broadcast_to(jnp.where(lane == owner, MASKED, 0.0).astype(BF16)[None, :], (rows, LANES))
    split = projection.reshape(rows, n, 2, half)
    both = []
    for which in (core, 1 - core):
        own, oth, shared = cut(lax.dynamic_index_in_dim(split, which, 2, keepdims=False), side, wo)
        both.append(jnp.concatenate([own, gate, shared, oth], axis=1))
    return both[0], both[1], bias


def pack_kernel(pieces, *refs):
    arrays, outs = refs[: len(refs) - len(pieces)], refs[len(refs) - len(pieces) :]
    for out, places in zip(outs, pieces, strict=True):
        for k, rows, cols, row, col in places:
            size = (rows.stop - rows.start, cols.stop - cols.start)
            out[row : row + size[0], col : col + size[1]] = arrays[k][rows, cols]


def pack(arrays, shapes, pieces):
    vmem = pl.BlockSpec(memory_space=pltpu.VMEM)
    return pl.pallas_call(
        functools.partial(pack_kernel, pieces),
        in_specs=[vmem] * len(arrays),
        out_specs=[vmem] * len(shapes),
        out_shape=[jax.ShapeDtypeStruct(shape, BF16) for shape in shapes],
        compiler_params=pltpu.CompilerParams(vmem_limit_bytes=8 * MIB),
        name="pack",
    )(*arrays)


def score_kernel(wo, ws, kinds, aligned, own_ref, mate_ref, bias_ref, *refs):
    count = 1 + max(k for _, places in kinds for k, _ in places)
    pieces, part_ref = refs[:count], refs[count]
    rows = own_ref.shape[0]
    acc = None
    base = 0
    for width, places in kinds:
        for start in range(0, width, 1024):
            size = min(1024, width - start)
            x = jnp.concatenate([pieces[k][:, c + start : c + start + size] for k, c in places], axis=0)
            cols = slice(base + start, base + start + size)
            p = jnp.concatenate([own_ref[:, cols], mate_ref[:, cols]], axis=0)
            term = lax.dot_general(p, x, (((1,), (1,)), ((), ())), preferred_element_type=F32)
            acc = term if acc is None else acc + term
        base += width
    part_ref[:rows, :] = acc[:rows] + bias_ref[...]
    part_ref[rows:, :] = acc[rows:]
    if aligned:
        side, owner = (lax.axis_index("cls") // 2) % 2, lax.axis_index("ori")
        slice_ref = refs[count + 1]
        for (_, places), spot, size in zip(kinds, (side * wo, 2 * wo, (1 - side) * wo), (wo, ws, wo), strict=True):
            row = 0
            for k, c in places:
                p = pieces[k]
                slice_ref[row : row + p.shape[0], at(spot, size)] = p[:, at(c + owner * size, size)]
                row += p.shape[0]


def group_scores(own, mate, bias, kinds, wo, ws, n):
    aligned = wo % LANES == 0
    rows = own.shape[0]
    half = 2 * wo + ws
    count = sum(p.shape[0] for p, _ in kinds[0])
    out = [jax.ShapeDtypeStruct((2 * rows, count), F32)]
    if aligned:
        out.append(jax.ShapeDtypeStruct((count, half), BF16))
    arrays, numbered = [], []
    for places, width in zip(kinds, (n * wo + LANES, n * ws, n * wo), strict=True):
        numbered.append((width, [(len(arrays) + i, c) for i, (_, c) in enumerate(places)]))
        arrays += [p for p, _ in places]
    vmem = pl.BlockSpec(memory_space=pltpu.VMEM)
    got = pl.pallas_call(
        functools.partial(score_kernel, wo, ws, numbered, aligned),
        in_specs=[vmem] * (3 + len(arrays)),
        out_specs=[vmem] * len(out),
        out_shape=out,
        compiler_params=pltpu.CompilerParams(vmem_limit_bytes=8 * MIB),
        cost_estimate=pl.CostEstimate(
            flops=4 * rows * count * own.shape[1], bytes_accessed=4 * own.size + 2 * count * own.shape[1], transcendentals=0
        ),
        name="group_scores",
    )(own, mate, bias, *arrays)
    if aligned:
        return got
    side, owner = (lax.axis_index("cls") // 2) % 2, lax.axis_index("ori")
    cols = []
    for places, size in zip(kinds, (wo, ws, wo), strict=True):
        cols.append(jnp.concatenate([lax.dynamic_slice_in_dim(p, c + owner * size, size, 1) for p, c in places], axis=0))
    a, c, b = cols
    first, second = jnp.where(side == 0, a, b), jnp.where(side == 0, b, a)
    return got[0], jnp.concatenate([first, second, c], axis=1)


def group_order(n):
    return [(0, n // 2)] + [(d, n - d) for d in range(1, n // 2)]


def stats_kernel(n, *refs):
    groups = n // 2
    parts, recvs = refs[:groups], refs[groups : 2 * groups]
    score_ref, stat_ref = refs[2 * groups :]
    rows = score_ref.shape[0]
    per = parts[0].shape[1] // 2
    for g, pair in enumerate(group_order(n)):
        mine = parts[g][:rows, :] + recvs[g][rows:, :]
        other = parts[g][rows:, :] + recvs[g][:rows, :]
        best = jnp.maximum(jnp.max(mine, axis=0, keepdims=True), jnp.max(other, axis=0, keepdims=True))
        total = jnp.sum(jnp.exp(mine - best), axis=0, keepdims=True) + jnp.sum(jnp.exp(other - best), axis=0, keepdims=True)
        for h, r in enumerate(pair):
            cols, held = slice(r * per, (r + 1) * per), slice(h * per, (h + 1) * per)
            score_ref[:, cols] = mine[:, held]
            stat_ref[0:1, cols] = best[:, held]
            stat_ref[1:2, cols] = total[:, held]
    stat_ref[2:8, :] = jnp.zeros((6, stat_ref.shape[1]), F32)


def payload_kernel(turns, score_ref, *refs):
    stats, out_ref = refs[:turns], refs[turns]
    rows = score_ref.shape[0]
    plane = lax.axis_index("cls") // 2
    best = functools.reduce(jnp.maximum, [s[0:1, :] for s in stats])
    terms = [s[1:2, :] * jnp.exp(s[0:1, :] - best) for s in stats]
    total = None
    for a in range(turns):
        back = lax.rem(plane - a + turns, turns)
        term = sum(jnp.where(back == j, terms[j], 0.0) for j in range(turns))
        total = term if total is None else total + term
    out_ref[:rows, :] = jnp.exp(score_ref[...] - best).astype(BF16)
    left = jnp.concatenate([best, total], axis=0)
    levels = []
    for _ in range(3):
        piece = left.astype(BF16).astype(F32)
        levels.append(piece)
        left = left - piece
    levels.append(jnp.zeros((TAIL - 6, best.shape[1]), F32))
    out_ref[rows:, :] = jnp.concatenate(levels, axis=0).astype(BF16)


def sums_kernel(n, rows, per_half, cycle, *refs):
    owner = lax.axis_index("ori")
    spot = sum(jnp.where(owner == o, cycle.index(o), 0) for o in range(n))
    payloads, refs = refs[:n], refs[n:]
    groups = n // 2
    w_own, w_oth = refs[:groups], refs[groups:-3]
    out_ref, evidence_ref, posterior = refs[-3:]
    step = pl.program_id(0)
    width = payloads[0].shape[1]
    per = width // n

    @pl.when(step == 0)
    def _():
        tops, sums = [], []
        for d in range(n):
            stat = payloads[d][rows:, :].astype(F32)
            stat = jnp.concatenate([stat[0:2] + stat[2:4] + stat[4:6], jnp.zeros((6, width), F32)], axis=0)
            stat = pltpu.roll(stat, per * d, 1) if d else stat
            tops.append(stat[0:1])
            sums.append(stat[1:2])
        best = functools.reduce(jnp.maximum, tops)
        grow = [jnp.exp(t - best) for t in tops]
        total = functools.reduce(lambda a, b: a + b, [s * g for s, g in zip(sums, grow, strict=True)])
        evidence_ref[...] = (best + jnp.log(total))[:, :per]
        for d in range(n):
            wide = payloads[d][:rows, :].astype(F32)
            wide = pltpu.roll(wide, per * d, 1) if d else wide
            back = lax.rem(spot + (n - d), n)
            block = sum(jnp.where(back == p, cycle[p], 0) for p in range(n))
            row = pl.multiple_of(block * rows, 16)
            posterior[pl.ds(row, rows), :] = (wide * (grow[d] / total)).astype(BF16)

    places = {r: (g, h) for g, pair in enumerate(group_order(n)) for h, r in enumerate(pair)}
    first = (step < per_half) == (lax.axis_index("cls") % 2 == 0)
    pieces = []
    for r in range(n):
        g, h = places[r]
        held = slice(h * per, (h + 1) * per)
        pieces.append(jnp.where(first, w_own[g][held, :], w_oth[g][held, :]) if per_half else w_own[g][held, :])
    left = posterior[...]
    if not per_half:
        left = posterior[pl.ds(pl.multiple_of(step * out_ref.shape[0], 16), out_ref.shape[0]), :]
    out_ref[...] = jnp.dot(left, jnp.concatenate(pieces, axis=0), preferred_element_type=F32).astype(BF16)


def tie(*values):
    return lax.optimization_barrier(values)


def body(images, projections, log_prior, significant, shell_index, noise_inv):
    n = lax.axis_size("ori")
    n_cls = lax.axis_size("cls")
    turns = n_cls // 2
    owner = lax.axis_index("ori")
    cls = lax.axis_index("cls")
    core, side = cls % 2, (cls // 2) % 2
    rows, freqs = images.shape
    ori_rows = projections.shape[1]
    half = freqs // n // 2
    wo = 3 * half // 10
    ws = half - 2 * wo
    cycle = cycle_of(n)
    far = n // 2

    def ring(x, d):
        return lax.ppermute(x, "ori", [(cycle[i], cycle[(i + d) % n]) for i in range(n)])

    def swap(x):
        return lax.ppermute(x, "cls", [(i, i ^ 1) for i in range(n_cls)])

    def cross(x):
        return lax.ppermute(x, "cls", [(i, i ^ 2) for i in range(n_cls)])

    weight_of = (shell_index.reshape(freqs // LANES, LANES), noise_inv.reshape(1, -1))
    own, oth, shared, weight = prep_images(images, weight_of, significant, core, side, wo, ws, n)
    projections, own, oth, shared = tie(projections, own, oth, shared)
    keep, send, bias = prep_projections(projections, weight, log_prior, core, side, owner, wo, ws, n)

    cut_at = rows // 2
    every, top, bottom = slice(0, rows), slice(0, cut_at), slice(cut_at, rows)
    plane_w, shared_w = n * wo + LANES, n * ws
    plane_cols, cross_cols = slice(0, plane_w), slice(0, n * wo)
    shared_cols = slice(plane_w, plane_w + shared_w)
    f, b = ring(own, 1), ring(own, -1)
    f, b, shared, send = tie(f, b, shared, send)
    whole = slice(0, shared_w)
    mates = swap(send)
    both, x_in = [None], None
    f2, b2, x_in = pack(
        [f, b, shared],
        [(rows, plane_w + shared_w)] * 2 + [(2 * rows, n * wo)],
        [[(i, every, plane_cols, 0, 0), (2, every, whole, 0, plane_w)] for i in (0, 1)]
        + [[(0, every, cross_cols, 0, 0), (1, every, cross_cols, rows, 0)]],
    )
    both = [(f2, b2)]
    parts, slices = [None] * far, [None] * far
    crossed = [None]
    for s in range(1, far - 1):
        f, b = both[-1]
        f, b, x = ring(f, 1), ring(b, -1), cross(x_in)
        if s == 1:
            f, b, x, mates = tie(f, b, x, mates)
        else:
            f, b, x, parts[s - 1], slices[s - 1] = tie(f, b, x, parts[s - 1], slices[s - 1])
        both.append((f, b))
        crossed.append(x)
        kinds = ([(p, 0) for p in both[s - 1]], [(p, plane_w) for p in both[s]], [(x, 0)])
        parts[s], slices[s] = group_scores(keep, mates, bias, kinds, wo, ws, n)
        if s < far - 2:
            (x_in,) = pack([f, b], [(2 * rows, n * wo)], [[(0, every, cross_cols, 0, 0), (1, every, cross_cols, rows, 0)]])
    x_in, fo, bo, fs, bs = pack(
        [f, b],
        [(2 * rows, n * wo)] + [(cut_at, plane_w)] * 2 + [(rows, shared_w)] * 2,
        [
            [(0, every, cross_cols, 0, 0), (1, every, cross_cols, rows, 0)],
            [(0, top, plane_cols, 0, 0)],
            [(1, bottom, plane_cols, 0, 0)],
            [(0, every, shared_cols, 0, 0)],
            [(1, every, shared_cols, 0, 0)],
        ],
    )
    fo, bo, fs, bs, x = ring(fo, 1), ring(bo, -1), ring(fs, 1), ring(bs, -1), cross(x_in)
    fo, bo, fs, bs, x, parts[far - 2], slices[far - 2] = tie(fo, bo, fs, bs, x, parts[far - 2], slices[far - 2])
    kinds = ([(p, 0) for p in both[far - 2]], [(fs, 0), (bs, 0)], [(x, 0)])
    parts[far - 1], slices[far - 1] = group_scores(keep, mates, bias, kinds, wo, ws, n)
    (x_in,) = pack([fo, bo], [(rows, n * wo)], [[(0, top, cross_cols, 0, 0), (1, top, cross_cols, cut_at, 0)]])
    fs, bs, x = ring(fs[:cut_at], 1), ring(bs[cut_at:], -1), cross(x_in)
    kinds = ([(own, 0), (fo, 0), (bo, 0)], [(shared, 0), (fs, 0), (bs, 0)], [(oth, 0), (x, 0)])
    parts[0], slices[0] = group_scores(keep, mates, bias, kinds, wo, ws, n)
    recvs = [swap(p) for p in parts]
    other_slices = [swap(x) for x in slices]

    vmem = pl.BlockSpec(memory_space=pltpu.VMEM)
    width = n * rows
    scores, stats = pl.pallas_call(
        functools.partial(stats_kernel, n),
        in_specs=[vmem] * (2 * far),
        out_specs=[vmem, vmem],
        out_shape=[jax.ShapeDtypeStruct((ori_rows, width), F32), jax.ShapeDtypeStruct((8, width), F32)],
        compiler_params=pltpu.CompilerParams(vmem_limit_bytes=16 * MIB),
        name="local_stats",
    )(*parts, *recvs)
    all_stats = [stats] + [
        lax.ppermute(stats, "cls", [(i, (i + 2 * j) % n_cls) for i in range(n_cls)]) for j in range(1, turns)
    ]
    payload = pl.pallas_call(
        functools.partial(payload_kernel, turns),
        in_specs=[vmem] * (1 + turns),
        out_specs=vmem,
        out_shape=jax.ShapeDtypeStruct((ori_rows + TAIL, width), BF16),
        compiler_params=pltpu.CompilerParams(vmem_limit_bytes=16 * MIB),
        name="payload",
    )(scores, *all_stats)
    payloads = [payload] + [None] * (n - 1)
    fp = bp = payload
    for d in range(1, far + 1):
        fp = payloads[d] = ring(fp, 1)
        if d < far:
            bp = payloads[n - d] = ring(bp, -1)

    fixed = lambda i: (0, 0)
    per_half = half // 256 if half % 256 == 0 else 0
    if per_half:
        steps = 2 * per_half
        w = slices + other_slices
        w_specs = [pl.BlockSpec((LANES, 256), lambda i: (0, lax.rem(i, per_half)))] * len(w)
        out_spec = pl.BlockSpec((n * ori_rows, 256), lambda i: (0, i))
        grant = 24
    else:
        steps = max(1, n // 2)
        w = [
            jnp.concatenate([jnp.where(core == 0, a, b), jnp.where(core == 0, b, a)], axis=1)
            for a, b in zip(slices, other_slices, strict=True)
        ]
        w_specs = [pl.BlockSpec((LANES, 2 * half), fixed, pipeline_mode=pl.Buffered(1))] * len(w)
        out_spec = pl.BlockSpec((n * ori_rows // steps, 2 * half), lambda i: (i, 0))
        grant = 62
    held_once = pl.BlockSpec(payload.shape, fixed, pipeline_mode=pl.Buffered(1))
    sums, evidence = pl.pallas_call(
        functools.partial(sums_kernel, n, ori_rows, per_half, cycle),
        grid=(steps,),
        in_specs=[held_once] * n + w_specs,
        out_specs=[out_spec, pl.BlockSpec((1, rows), fixed)],
        scratch_shapes=[pltpu.VMEM((n * ori_rows, width), BF16)],
        out_shape=[jax.ShapeDtypeStruct((n * ori_rows, 2 * half), BF16), jax.ShapeDtypeStruct((1, rows), F32)],
        compiler_params=pltpu.CompilerParams(vmem_limit_bytes=grant * MIB),
        name="class_sums",
    )(*payloads, *w)
    return sums[None], evidence.reshape(rows)


def solution(mesh):
    in_specs = (P("ori", None), P("cls", "ori", None), P("cls", "ori"), P("ori", None), P(), P())
    out_specs = (P("cls", None, "ori"), P("ori"))
    return jax.shard_map(body, mesh=mesh, in_specs=in_specs, out_specs=out_specs, check_vma=False)
```

time: 162 us -> 129 us (0.80)
  local copies, waits for them, and re-layouts: 29.4 us -> 1.91 us
  waiting for transfers between devices: 63.7 us -> 70.6 us
  other arithmetic: 4.86 us -> 0 us
  starting transfers between devices: 32.9 us -> 29.1 us
  Pallas kernels: 29.1 us -> 26.4 us
    ppermute x4, waiting for transfers between devices: 0.01 us -> 29 us  [cross(): return lax.ppermute(x, 'cls', [(i, i ^ 2) for i in range(n_cls)])]
    unnamed x122 -> x14, local copies, waits for them, and re-layouts: 24.7 us -> 1.87 us
    ppermute x23 -> x19, waiting for transfers between devices: 59.6 us -> 38 us  [ring(): lax.ppermute(x, 'ori', [(cycle[i], cycle[(i + d) % n]) for i in range(n)])]
    concatenate x3 -> x0, other arithmetic: 4.17 us -> none  [the longest x1 2.41 us: body(): jnp.concatenate(slices, axis=0)]
    ppermute x23 -> x19, starting transfers between devices: 24.5 us -> 21.1 us  [ring(): lax.ppermute(x, 'ori', [(cycle[i], cycle[(i + d) % n]) for i in range(n)])]
    pallas_call x13 -> x14, Pallas kernels: 29.1 us -> 26.4 us  [the longest x1 7.98 us: body(): pl.pallas_call(functools.partial(sums_kernel, n, ori_rows, per_half, cycl...]
  transfers between devices with their start and end apart: 37 -> 33, of which waited for: 17 -> 20; matrix products, arithmetic and copies ran while one was open for 5% -> 0% of each run, Pallas kernels for 9% -> 12%
where the time goes in v2:
time: 129 us
  waiting for transfers between devices  70.6 us (55%)
  starting transfers between devices  29.1 us (23%)
  Pallas kernels  26.4 us (20%)
  local copies, waits for them, and re-layouts  1.91 us (1%)
    ppermute x19, waiting for transfers between devices, ring(): lax.ppermute(x, 'ori', [(cycle[i], cycle[(i + d) % n]) for i in range(n)])  38 us
    ppermute x4, waiting for transfers between devices, cross(): return lax.ppermute(x, 'cls', [(i, i ^ 2) for i in range(n_cls)])  29 us
    ppermute x19, starting transfers between devices, ring(): lax.ppermute(x, 'ori', [(cycle[i], cycle[(i + d) % n]) for i in range(n)])  21.1 us
    pallas_call x1, Pallas kernels, body(): pl.pallas_call(functools.partial(sums_kernel, n, ori_rows, per_half, cycl...  7.98 us
    pallas_call x4, Pallas kernels, group_scores(): pl.pallas_call(functools.partial(score_kernel, wo, ws, numbered, aligned)...  6.98 us
    pallas_call x1, Pallas kernels, prep_projections(): pl.pallas_call(functools.partial(split_kernel, wo, ws, n), in_specs=[pl.B...  5.88 us
    ppermute x4, starting transfers between devices, cross(): return lax.ppermute(x, 'cls', [(i, i ^ 2) for i in range(n_cls)])  5.31 us
    pallas_call x1, Pallas kernels, prep_images(): pl.pallas_call(functools.partial(image_kernel, n, wo, ws), in_specs=[pl.B...  2.67 us
  transfers between devices with their start and end apart: 33, of which 20 were waited for; matrix products, arithmetic and copies ran while one was open for 0% of the time, Pallas kernels for 12%

profile of v2, /device:TPU:0, one launch (start us, length us, event | category | flops | bytes accessed | tf_op | source)
XLA Modules:
  0.0 128.9 jit_solution(8134550197614491573)
XLA Ops:
  0.6 2.7 %prep_images.1 = (bf16[64,3200]{1,0:T(8,128)(2,1)}, bf16[64,3072]{1,0:T(8,128)(2,1)}, bf16[64,4096]{1,0:T(8,128)(2,1)}, f32[160,128]{1,0:T(8,128)}) custom-call(bf16[64,20480]{1,0:T(8,128)(2,1)} %img_hbm.1, s32[160,128]{1,0:T(8,128)} %bitcast.5, f32[1,100]{1,0:T(1,128)} %bitcast.7, s32[4,64]{1,0:T(4,128)} %bitcast.6), custom_call_target="tpu_custom_call" | custom-call | tf_op jit(solution)/shard_map/prep_images/pallas_call | solution.py:88
  3.3 3.0 %collective-permute-start.1 = (bf16[64,3200]{1,0:T(8,128)(2,1)}, bf16[64,3200]{1,0:T(8,128)(2,1)S(1)}, u32[]{:S(2)}, u32[]{:S(2)}) collective-permute-start(bf16[64,3200]{1,0:T(8,128)(2,1)} %get-tuple-element.57.refs_0_), channel_id=1, source_target_pairs={{0,1},{2,0},{4,2},{6,4},{7,6},{5,7},{3,5},{1,3},{8,9},{10,8},{12,1... | collective-permute-start | bytes 1228808 | tf_op jit(solution)/shard_map/ppermute | solution.py:406
  6.3 0.1 collective-permute-start
  6.5 5.9 %split_projections.1 = (bf16[144,10368]{1,0:T(8,128)(2,1)}, bf16[144,10368]{1,0:T(8,128)(2,1)}) custom-call(bf16[1,144,20480]{2,1,0:T(8,128)(2,1)} %proj_hbm), custom_call_target="tpu_custom_call" | custom-call | bytes 11796480 | tf_op jit(solution)/shard_map/split_projections/pallas_call | solution.py:180
  12.4 0.0 copy-start
  12.4 0.0 copy-start.6
  12.4 3.7 %collective-permute-done.1.refs_1_ = bf16[64,3200]{1,0:T(8,128)(2,1)S(1)} collective-permute-done((bf16[64,3200]{1,0:T(8,128)(2,1)}, bf16[64,3200]{1,0:T(8,128)(2,1)S(1)}, u32[]{:S(2)}, u32[]{:S(2)}) %collective-permute-start.1) | collective-permute-done | bytes 409632 | tf_op jit(solution)/shard_map/ppermute | solution.py:406
  16.1 1.4 %collective-permute-done.refs_0_ = bf16[64,3200]{1,0:T(8,128)(2,1)S(1)} collective-permute-done((bf16[64,3200]{1,0:T(8,128)(2,1)}, bf16[64,3200]{1,0:T(8,128)(2,1)S(1)}, u32[]{:S(2)}, u32[]{:S(2)}) %collective-permute-start) | collective-permute-done | bytes 409632 | tf_op jit(solution)/shard_map/ppermute | solution.py:406
  17.5 0.2 pack.4
  17.7 0.5 collective-permute-start.2
  18.1 1.6 %collective-permute-start.3 = (bf16[64,7296]{1,0:T(8,128)(2,1)S(1)}, bf16[64,7296]{1,0:T(8,128)(2,1)S(1)}, u32[]{:S(2)}, u32[]{:S(2)}) collective-permute-start(bf16[64,7296]{1,0:T(8,128)(2,1)S(1)} %get-tuple-element.64.refs_1_), channel_id=1, source_target_pairs={{0,1},{2,0},{4,2},{6,4},{7,6},{5,7},{3,5},{1,3},{8,9},{10,8},{12,1... | collective-permute-start | bytes 2801672 | tf_op jit(solution)/shard_map/ppermute | solution.py:406
  19.7 1.5 %collective-permute-start.4 = (bf16[128,3072]{1,0:T(8,128)(2,1)S(1)}, bf16[128,3072]{1,0:T(8,128)(2,1)S(1)}, u32[]{:S(2)}, u32[]{:S(2)}) collective-permute-start(bf16[128,3072]{1,0:T(8,128)(2,1)S(1)} %get-tuple-element.65), channel_id=1, source_target_pairs={{0,16},{8,24},{16,0},{24,8},{1,17},{9,25},{17,1},{25,9},{2,18},{10... | collective-permute-start | bytes 2359304 | tf_op jit(solution)/shard_map/ppermute | solution.py:412
  21.2 17.9 %collective-permute-done.4.refs_4_ = bf16[128,3072]{1,0:T(8,128)(2,1)S(1)} collective-permute-done((bf16[128,3072]{1,0:T(8,128)(2,1)S(1)}, bf16[128,3072]{1,0:T(8,128)(2,1)S(1)}, u32[]{:S(2)}, u32[]{:S(2)}) %collective-permute-start.4) | collective-permute-done | bytes 786464 | tf_op jit(solution)/shard_map/ppermute | solution.py:412
  39.1 1.7 %collective-permute-done.2.refs_0_.refs_2_ = bf16[64,7296]{1,0:T(8,128)(2,1)S(1)} collective-permute-done((bf16[64,7296]{1,0:T(8,128)(2,1)S(1)}, bf16[64,7296]{1,0:T(8,128)(2,1)S(1)}, u32[]{:S(2)}, u32[]{:S(2)}) %collective-permute-start.2) | collective-permute-done | bytes 933920 | tf_op jit(solution)/shard_map/ppermute | solution.py:406
  40.8 0.1 collective-permute-done.3.refs_1_.refs_3_
  41.0 1.7 %collective-permute-start.6 = (bf16[64,7296]{1,0:T(8,128)(2,1)S(1)}, bf16[64,7296]{1,0:T(8,128)(2,1)S(1)}, u32[]{:S(2)}, u32[]{:S(2)}) collective-permute-start(bf16[64,7296]{1,0:T(8,128)(2,1)S(1)} %collective-permute-done.2.refs_0_.refs_2_), channel_id=1, source_target_pairs={{0,2},{2,4},{4,6},{6,7},{7,5},{5,3},{3,1},{1,0},{8,10},{10,12},{12... | collective-permute-start | bytes 2801672 | tf_op jit(solution)/shard_map/ppermute | solution.py:406
  42.6 0.3 collective-permute-start.7
  43.0 0.1 pack.5
  43.0 1.7 %collective-permute-start.8 = (bf16[128,3072]{1,0:T(8,128)(2,1)S(1)}, bf16[128,3072]{1,0:T(8,128)(2,1)S(1)}, u32[]{:S(2)}, u32[]{:S(2)}) collective-permute-start(bf16[128,3072]{1,0:T(8,128)(2,1)S(1)} %pack.5), channel_id=1, source_target_pairs={{0,16},{8,24},{16,0},{24,8},{1,17},{9,25},{17,1},{25,9},{2,18},{10... | collective-permute-start | bytes 2359304 | tf_op jit(solution)/shard_map/ppermute | solution.py:412
  44.7 1.8 %copy-done.1 = bf16[144,10368]{1,0:T(8,128)(2,1)S(1)} copy-done((bf16[144,10368]{1,0:T(8,128)(2,1)S(1)}, bf16[144,10368]{1,0:T(8,128)(2,1)}, u32[]{:S(2)}) %copy-start.1) | copy-done | bytes 2986008
  46.5 2.2 %half_norms.1.bias_ref = f32[144,128]{1,0:T(8,128)S(1)} custom-call(bf16[144,10368]{1,0:T(8,128)(2,1)S(1)} %copy-done, bf16[144,10368]{1,0:T(8,128)(2,1)S(1)} %copy-done.1, f32[1,144]{1,0:T(1,128)S(1)} %copy-done.6, f32[160,128]{1,0:T(8,128)S(1)} %copy-done.5), custom_call_target="tpu_custom_call" | custom-call | flops 8847360 | bytes 5898240 | tf_op jit(solution)/shard_map/half_norms/pallas_call | solution.py:190
  48.7 1.7 %group_scores.4 = (f32[288,128]{1,0:T(8,128)S(1)}, bf16[128,1280]{1,0:T(8,128)(2,1)S(1)}) custom-call(bf16[144,10368]{1,0:T(8,128)(2,1)S(1)} %copy-done, bf16[144,10368]{1,0:T(8,128)(2,1)S(1)} %collective-permute-done.5.mate_ref, f32[144,128]{1,0:T(8,128)S(1)} %half_norms.1.bias_ref, bf16[64,7296]{1,0:T(8,128)(2,1)S(1)} %get-tuple-element.63.refs_0_, ...), custom_call_target="tpu_custom_call" | custom-call | flops 764411904 | bytes 8626176 | tf_op jit(solution)/shard_map/group_scores/pallas_call | solution.py:274
  50.5 11.1 %collective-permute-done.8.refs_4_ = bf16[128,3072]{1,0:T(8,128)(2,1)S(1)} collective-permute-done((bf16[128,3072]{1,0:T(8,128)(2,1)S(1)}, bf16[128,3072]{1,0:T(8,128)(2,1)S(1)}, u32[]{:S(2)}, u32[]{:S(2)}) %collective-permute-start.8) | collective-permute-done | bytes 786464 | tf_op jit(solution)/shard_map/ppermute | solution.py:412
  61.6 1.6 %collective-permute-done.6.refs_0_.refs_2_ = bf16[64,7296]{1,0:T(8,128)(2,1)S(1)} collective-permute-done((bf16[64,7296]{1,0:T(8,128)(2,1)S(1)}, bf16[64,7296]{1,0:T(8,128)(2,1)S(1)}, u32[]{:S(2)}, u32[]{:S(2)}) %collective-permute-start.6) | collective-permute-done | bytes 933920 | tf_op jit(solution)/shard_map/ppermute | solution.py:406
  63.2 1.2 collective-permute-done.7.refs_1_.refs_3_
  64.4 0.1 pack.6
  64.5 1.6 %collective-permute-start.13 = (bf16[128,3072]{1,0:T(8,128)(2,1)S(1)}, bf16[128,3072]{1,0:T(8,128)(2,1)S(1)}, u32[]{:S(2)}, u32[]{:S(2)}) collective-permute-start(bf16[128,3072]{1,0:T(8,128)(2,1)S(1)} %get-tuple-element.80), channel_id=1, source_target_pairs={{0,16},{8,24},{16,0},{24,8},{1,17},{9,25},{17,1},{25,9},{2,18},{10... | collective-permute-start | bytes 2359304 | tf_op jit(solution)/shard_map/ppermute | solution.py:412
  66.1 1.6 %collective-permute-start.11 = (bf16[64,4096]{1,0:T(8,128)(2,1)S(1)}, bf16[64,4096]{1,0:T(8,128)(2,1)S(1)}, u32[]{:S(2)}, u32[]{:S(2)}) collective-permute-start(bf16[64,4096]{1,0:T(8,128)(2,1)S(1)} %get-tuple-element.78), channel_id=1, source_target_pairs={{0,2},{2,4},{4,6},{6,7},{7,5},{5,3},{3,1},{1,0},{8,10},{10,12},{12... | collective-permute-start | bytes 1572872 | tf_op jit(solution)/shard_map/ppermute | solution.py:406
  67.7 0.4 collective-permute-start.12
  68.1 1.6 %collective-permute-start.9 = (bf16[32,3200]{1,0:T(8,128)(2,1)S(1)}, bf16[32,3200]{1,0:T(8,128)(2,1)S(1)}, u32[]{:S(2)}, u32[]{:S(2)}) collective-permute-start(bf16[32,3200]{1,0:T(8,128)(2,1)S(1)} %get-tuple-element.76), channel_id=1, source_target_pairs={{0,2},{2,4},{4,6},{6,7},{7,5},{5,3},{3,1},{1,0},{8,10},{10,12},{12... | collective-permute-start | bytes 614408 | tf_op jit(solution)/shard_map/ppermute | solution.py:406
  69.7 0.4 collective-permute-start.10
  70.1 1.7 %group_scores.5 = (f32[288,128]{1,0:T(8,128)S(1)}, bf16[128,1280]{1,0:T(8,128)(2,1)S(1)}) custom-call(bf16[144,10368]{1,0:T(8,128)(2,1)S(1)} %copy-done, bf16[144,10368]{1,0:T(8,128)(2,1)S(1)} %collective-permute-done.5.mate_ref, f32[144,128]{1,0:T(8,128)S(1)} %half_norms.1.bias_ref, bf16[64,7296]{1,0:T(8,128)(2,1)S(1)} %collective-permute-done.2.refs_0_.refs_2_, ...), custom_call_target="tpu_custom_call" | custom-call | flops 764411904 | bytes 8626176 | tf_op jit(solution)/shard_map/group_scores/pallas_call | solution.py:274
  71.9 10.3 %collective-permute-done.9.refs_0_.refs_1_ = bf16[32,3200]{1,0:T(8,128)(2,1)S(1)} collective-permute-done((bf16[32,3200]{1,0:T(8,128)(2,1)S(1)}, bf16[32,3200]{1,0:T(8,128)(2,1)S(1)}, u32[]{:S(2)}, u32[]{:S(2)}) %collective-permute-start.9) | collective-permute-done | bytes 204832 | tf_op jit(solution)/shard_map/ppermute | solution.py:406
  82.2 1.3 %collective-permute-done.10.refs_1_.refs_2_ = bf16[32,3200]{1,0:T(8,128)(2,1)S(1)} collective-permute-done((bf16[32,3200]{1,0:T(8,128)(2,1)S(1)}, bf16[32,3200]{1,0:T(8,128)(2,1)S(1)}, u32[]{:S(2)}, u32[]{:S(2)}) %collective-permute-start.10) | collective-permute-done | bytes 204832 | tf_op jit(solution)/shard_map/ppermute | solution.py:406
  83.6 0.6 collective-permute-start.16
  84.2 1.6 %collective-permute-start.14 = (bf16[32,4096]{1,0:T(8,128)(2,1)S(1)}, bf16[32,4096]{1,0:T(8,128)(2,1)S(1)}, u32[]{:S(2)}, u32[]{:S(2)}) collective-permute-start(bf16[32,4096]{1,0:T(8,128)(2,1)S(1)} %slice.6), channel_id=1, source_target_pairs={{0,2},{2,4},{4,6},{6,7},{7,5},{5,3},{3,1},{1,0},{8,10},{10,12},{12... | collective-permute-start | bytes 786440 | tf_op jit(solution)/shard_map/ppermute | solution.py:406
  85.9 0.5 collective-permute-start.15
  86.4 1.8 %group_scores.7 = (f32[288,128]{1,0:T(8,128)S(1)}, bf16[128,1280]{1,0:T(8,128)(2,1)S(1)}) custom-call(bf16[144,10368]{1,0:T(8,128)(2,1)S(1)} %copy-done, bf16[144,10368]{1,0:T(8,128)(2,1)S(1)} %collective-permute-done.5.mate_ref, f32[144,128]{1,0:T(8,128)S(1)} %half_norms.1.bias_ref, bf16[64,7296]{1,0:T(8,128)(2,1)S(1)} %collective-permute-done.6.refs_0_.refs_2_, ...), custom_call_target="tpu_custom_call" | custom-call | flops 764411904 | bytes 8626176 | tf_op jit(solution)/shard_map/group_scores/pallas_call | solution.py:274
  88.1 0.6 collective-permute-start.20
  88.7 1.9 %collective-permute-done.14.refs_4_ = bf16[32,4096]{1,0:T(8,128)(2,1)S(1)} collective-permute-done((bf16[32,4096]{1,0:T(8,128)(2,1)S(1)}, bf16[32,4096]{1,0:T(8,128)(2,1)S(1)}, u32[]{:S(2)}, u32[]{:S(2)}) %collective-permute-start.14) | collective-permute-done | bytes 262176 | tf_op jit(solution)/shard_map/ppermute | solution.py:406
  90.6 1.7 %collective-permute-done.15.refs_5_ = bf16[32,4096]{1,0:T(8,128)(2,1)S(1)} collective-permute-done((bf16[32,4096]{1,0:T(8,128)(2,1)S(1)}, bf16[32,4096]{1,0:T(8,128)(2,1)S(1)}, u32[]{:S(2)}, u32[]{:S(2)}) %collective-permute-start.15) | collective-permute-done | bytes 262176 | tf_op jit(solution)/shard_map/ppermute | solution.py:406
  92.3 1.7 %group_scores.6 = (f32[288,128]{1,0:T(8,128)S(1)}, bf16[128,1280]{1,0:T(8,128)(2,1)S(1)}) custom-call(bf16[144,10368]{1,0:T(8,128)(2,1)S(1)} %copy-done, bf16[144,10368]{1,0:T(8,128)(2,1)S(1)} %collective-permute-done.5.mate_ref, f32[144,128]{1,0:T(8,128)S(1)} %half_norms.1.bias_ref, bf16[64,3200]{1,0:T(8,128)(2,1)S(1)} %copy-done.3, ...), custom_call_target="tpu_custom_call" | custom-call | flops 764411904 | bytes 8626176 | tf_op jit(solution)/shard_map/group_scores/pallas_call | solution.py:274
  94.0 0.1 collective-permute-start.17
  94.1 1.3 %collective-permute-done.17.refs_4_ = f32[288,128]{1,0:T(8,128)S(1)} collective-permute-done((f32[288,128]{1,0:T(8,128)S(1)}, f32[288,128]{1,0:T(8,128)S(1)}, u32[]{:S(2)}, u32[]{:S(2)}) %collective-permute-start.17) | collective-permute-done | bytes 147488 | tf_op jit(solution)/shard_map/ppermute | solution.py:409
  95.5 0.3 local_stats.1
  95.8 1.5 %collective-permute-start.21 = (f32[8,512]{1,0:T(8,128)S(1)}, f32[8,512]{1,0:T(8,128)S(1)}, u32[]{:S(2)}, u32[]{:S(2)}) collective-permute-start(f32[8,512]{1,0:T(8,128)S(1)} %get-tuple-element.95.refs_0_), channel_id=1, source_target_pairs={{0,16},{8,24},{16,0},{24,8},{1,17},{9,25},{17,1},{25,9},{2,18},{10... | collective-permute-start | bytes 49160 | tf_op jit(solution)/shard_map/ppermute | solution.py:484
  97.3 2.2 %collective-permute-done.21.refs_1_ = f32[8,512]{1,0:T(8,128)S(1)} collective-permute-done((f32[8,512]{1,0:T(8,128)S(1)}, f32[8,512]{1,0:T(8,128)S(1)}, u32[]{:S(2)}, u32[]{:S(2)}) %collective-permute-start.21) | collective-permute-done | bytes 16416 | tf_op jit(solution)/shard_map/ppermute | solution.py:484
  99.5 0.1 payload.1.refs_0_
  99.6 1.6 %collective-permute-start.22 = (bf16[160,512]{1,0:T(8,128)(2,1)S(1)}, bf16[160,512]{1,0:T(8,128)(2,1)S(1)}, u32[]{:S(2)}, u32[]{:S(2)}) collective-permute-start(bf16[160,512]{1,0:T(8,128)(2,1)S(1)} %payload.1.refs_0_), channel_id=1, source_target_pairs={{0,2},{2,4},{4,6},{6,7},{7,5},{5,3},{3,1},{1,0},{8,10},{10,12},{12... | collective-permute-start | bytes 491528 | tf_op jit(solution)/shard_map/ppermute | solution.py:406
  101.2 0.5 collective-permute-start.26
  101.7 3.3 %collective-permute-done.22.refs_1_ = bf16[160,512]{1,0:T(8,128)(2,1)S(1)} collective-permute-done((bf16[160,512]{1,0:T(8,128)(2,1)S(1)}, bf16[160,512]{1,0:T(8,128)(2,1)S(1)}, u32[]{:S(2)}, u32[]{:S(2)}) %collective-permute-start.22) | collective-permute-done | bytes 163872 | tf_op jit(solution)/shard_map/ppermute | solution.py:406
  105.0 1.5 %collective-permute-start.23 = (bf16[160,512]{1,0:T(8,128)(2,1)S(1)}, bf16[160,512]{1,0:T(8,128)(2,1)S(1)}, u32[]{:S(2)}, u32[]{:S(2)}) collective-permute-start(bf16[160,512]{1,0:T(8,128)(2,1)S(1)} %collective-permute-done.22.refs_1_), channel_id=1, source_target_pairs={{0,2},{2,4},{4,6},{6,7},{7,5},{5,3},{3,1},{1,0},{8,10},{10,12},{12... | collective-permute-start | bytes 491528 | tf_op jit(solution)/shard_map/ppermute | solution.py:406
  106.5 0.5 collective-permute-start.31
  107.0 0.0 collective-permute-start.29
  107.0 0.6 collective-permute-start.27
  107.6 2.7 %collective-permute-done.23.refs_2_ = bf16[160,512]{1,0:T(8,128)(2,1)S(1)} collective-permute-done((bf16[160,512]{1,0:T(8,128)(2,1)S(1)}, bf16[160,512]{1,0:T(8,128)(2,1)S(1)}, u32[]{:S(2)}, u32[]{:S(2)}) %collective-permute-start.23) | collective-permute-done | bytes 163872 | tf_op jit(solution)/shard_map/ppermute | solution.py:406
  110.3 1.5 %collective-permute-start.24 = (bf16[160,512]{1,0:T(8,128)(2,1)S(1)}, bf16[160,512]{1,0:T(8,128)(2,1)S(1)}, u32[]{:S(2)}, u32[]{:S(2)}) collective-permute-start(bf16[160,512]{1,0:T(8,128)(2,1)S(1)} %collective-permute-done.23.refs_2_), channel_id=1, source_target_pairs={{0,2},{2,4},{4,6},{6,7},{7,5},{5,3},{3,1},{1,0},{8,10},{10,12},{12... | collective-permute-start | bytes 491528 | tf_op jit(solution)/shard_map/ppermute | solution.py:406
  111.8 1.8 %collective-permute-done.27.refs_6_ = bf16[160,512]{1,0:T(8,128)(2,1)S(1)} collective-permute-done((bf16[160,512]{1,0:T(8,128)(2,1)S(1)}, bf16[160,512]{1,0:T(8,128)(2,1)S(1)}, u32[]{:S(2)}, u32[]{:S(2)}) %collective-permute-start.27) | collective-permute-done | bytes 163872 | tf_op jit(solution)/shard_map/ppermute | solution.py:406
  113.6 0.5 collective-permute-start.28
  114.1 1.5 %collective-permute-done.24.refs_3_ = bf16[160,512]{1,0:T(8,128)(2,1)S(1)} collective-permute-done((bf16[160,512]{1,0:T(8,128)(2,1)S(1)}, bf16[160,512]{1,0:T(8,128)(2,1)S(1)}, u32[]{:S(2)}, u32[]{:S(2)}) %collective-permute-start.24) | collective-permute-done | bytes 163872 | tf_op jit(solution)/shard_map/ppermute | solution.py:406
  115.6 1.5 %collective-permute-start.25 = (bf16[160,512]{1,0:T(8,128)(2,1)S(1)}, bf16[160,512]{1,0:T(8,128)(2,1)S(1)}, u32[]{:S(2)}, u32[]{:S(2)}) collective-permute-start(bf16[160,512]{1,0:T(8,128)(2,1)S(1)} %collective-permute-done.24.refs_3_), channel_id=1, source_target_pairs={{0,2},{2,4},{4,6},{6,7},{7,5},{5,3},{3,1},{1,0},{8,10},{10,12},{12... | collective-permute-start | bytes 491528 | tf_op jit(solution)/shard_map/ppermute | solution.py:406
  117.2 2.3 %collective-permute-done.28.refs_5_ = bf16[160,512]{1,0:T(8,128)(2,1)S(1)} collective-permute-done((bf16[160,512]{1,0:T(8,128)(2,1)S(1)}, bf16[160,512]{1,0:T(8,128)(2,1)S(1)}, u32[]{:S(2)}, u32[]{:S(2)}) %collective-permute-start.28) | collective-permute-done | bytes 163872 | tf_op jit(solution)/shard_map/ppermute | solution.py:406
  119.4 1.5 %collective-permute-done.25.refs_4_ = bf16[160,512]{1,0:T(8,128)(2,1)S(1)} collective-permute-done((bf16[160,512]{1,0:T(8,128)(2,1)S(1)}, bf16[160,512]{1,0:T(8,128)(2,1)S(1)}, u32[]{:S(2)}, u32[]{:S(2)}) %collective-permute-start.25) | collective-permute-done | bytes 163872 | tf_op jit(solution)/shard_map/ppermute | solution.py:406
  120.9 8.0 %class_sums.1 = (bf16[1152,2560]{1,0:T(8,128)(2,1)}, f32[1,64]{1,0:T(1,128)}) custom-call(bf16[160,512]{1,0:T(8,128)(2,1)S(1)} %payload.1.refs_0_, bf16[160,512]{1,0:T(8,128)(2,1)S(1)} %collective-permute-done.22.refs_1_, bf16[160,512]{1,0:T(8,128)(2,1)S(1)} %collective-permute-done.23.refs_2_, bf16[160,512]{1,0:T(8,128)(2,1)S(1)} %collective-permute-done.24.refs_3_, ...), custom_call_target="tpu_custom_call" | custom-call | tf_op jit(solution)/shard_map/class_sums/pallas_call | solution.py:519
  (32 shorter events, 0.1 us)
Async XLA Ops:
  3.3 14.2 %copy-start.2 = (bf16[64,4096]{1,0:T(8,128)(2,1)S(1)}, bf16[64,4096]{1,0:T(8,128)(2,1)}, u32[]{:S(2)}) copy-start(bf16[64,4096]{1,0:T(8,128)(2,1)} %get-tuple-element.62.refs_2_.refs_3_) | copy-start | bytes 1572868
  3.3 12.8 %collective-permute-start.1 = (bf16[64,3200]{1,0:T(8,128)(2,1)}, bf16[64,3200]{1,0:T(8,128)(2,1)S(1)}, u32[]{:S(2)}, u32[]{:S(2)}) collective-permute-start(bf16[64,3200]{1,0:T(8,128)(2,1)} %get-tuple-element.57.refs_0_), channel_id=1, source_target_pairs={{0,1},{2,0},{4,2},{6,4},{7,6},{5,7},{3,5},{1,3},{8,9},{10,8},{12,1... | collective-permute-start | bytes 1228808 | tf_op jit(solution)/shard_map/ppermute | solution.py:406
  6.3 11.1 %collective-permute-start = (bf16[64,3200]{1,0:T(8,128)(2,1)}, bf16[64,3200]{1,0:T(8,128)(2,1)S(1)}, u32[]{:S(2)}, u32[]{:S(2)}) collective-permute-start(bf16[64,3200]{1,0:T(8,128)(2,1)} %get-tuple-element.57.refs_0_), channel_id=1, source_target_pairs={{0,2},{2,4},{4,6},{6,7},{7,5},{5,3},{3,1},{1,0},{8,10},{10,12},{12... | collective-permute-start | bytes 1228808 | tf_op jit(solution)/shard_map/ppermute | solution.py:406
  12.4 32.3 %copy-start = (bf16[144,10368]{1,0:T(8,128)(2,1)S(1)}, bf16[144,10368]{1,0:T(8,128)(2,1)}, u32[]{:S(2)}) copy-start(bf16[144,10368]{1,0:T(8,128)(2,1)} %get-tuple-element.56.keep_ref.own_ref) | copy-start | bytes 8957956
  12.4 32.3 %copy-start.5 = (f32[160,128]{1,0:T(8,128)S(1)}, f32[160,128]{1,0:T(8,128)}, u32[]{:S(2)}) copy-start(f32[160,128]{1,0:T(8,128)} %get-tuple-element.68.w_ref) | copy-start | bytes 245764
  12.4 32.3 %copy-start.6 = (f32[1,144]{1,0:T(1,128)S(1)}, f32[1,144]{1,0:T(1,128)}, u32[]{:S(2)}) copy-start(f32[1,144]{1,0:T(1,128)} %prior_ref.1) | copy-start | bytes 1732
  17.5 23.5 %collective-permute-start.5 = (bf16[144,10368]{1,0:T(8,128)(2,1)}, bf16[144,10368]{1,0:T(8,128)(2,1)S(1)}, u32[]{:S(2)}, u32[]{:S(2)}) collective-permute-start(bf16[144,10368]{1,0:T(8,128)(2,1)} %get-tuple-element.66.send_ref), channel_id=1, source_target_pairs={{0,8},{8,0},{16,24},{24,16},{1,9},{9,1},{17,25},{25,17},{2,10},{10... | collective-permute-start | bytes 8957960 | tf_op jit(solution)/shard_map/ppermute | solution.py:409
  17.7 23.2 %collective-permute-start.2 = (bf16[64,7296]{1,0:T(8,128)(2,1)S(1)}, bf16[64,7296]{1,0:T(8,128)(2,1)S(1)}, u32[]{:S(2)}, u32[]{:S(2)}) collective-permute-start(bf16[64,7296]{1,0:T(8,128)(2,1)S(1)} %get-tuple-element.63.refs_0_), channel_id=1, source_target_pairs={{0,2},{2,4},{4,6},{6,7},{7,5},{5,3},{3,1},{1,0},{8,10},{10,12},{12... | collective-permute-start | bytes 2801672 | tf_op jit(solution)/shard_map/ppermute | solution.py:406
  18.1 22.8 %collective-permute-start.3 = (bf16[64,7296]{1,0:T(8,128)(2,1)S(1)}, bf16[64,7296]{1,0:T(8,128)(2,1)S(1)}, u32[]{:S(2)}, u32[]{:S(2)}) collective-permute-start(bf16[64,7296]{1,0:T(8,128)(2,1)S(1)} %get-tuple-element.64.refs_1_), channel_id=1, source_target_pairs={{0,1},{2,0},{4,2},{6,4},{7,6},{5,7},{3,5},{1,3},{8,9},{10,8},{12,1... | collective-permute-start | bytes 2801672 | tf_op jit(solution)/shard_map/ppermute | solution.py:406
  19.7 19.4 %collective-permute-start.4 = (bf16[128,3072]{1,0:T(8,128)(2,1)S(1)}, bf16[128,3072]{1,0:T(8,128)(2,1)S(1)}, u32[]{:S(2)}, u32[]{:S(2)}) collective-permute-start(bf16[128,3072]{1,0:T(8,128)(2,1)S(1)} %get-tuple-element.65), channel_id=1, source_target_pairs={{0,16},{8,24},{16,0},{24,8},{1,17},{9,25},{17,1},{25,9},{2,18},{10... | collective-permute-start | bytes 2359304 | tf_op jit(solution)/shard_map/ppermute | solution.py:412
  41.0 22.2 %collective-permute-start.6 = (bf16[64,7296]{1,0:T(8,128)(2,1)S(1)}, bf16[64,7296]{1,0:T(8,128)(2,1)S(1)}, u32[]{:S(2)}, u32[]{:S(2)}) collective-permute-start(bf16[64,7296]{1,0:T(8,128)(2,1)S(1)} %collective-permute-done.2.refs_0_.refs_2_), channel_id=1, source_target_pairs={{0,2},{2,4},{4,6},{6,7},{7,5},{5,3},{3,1},{1,0},{8,10},{10,12},{12... | collective-permute-start | bytes 2801672 | tf_op jit(solution)/shard_map/ppermute | solution.py:406
  42.6 21.7 %collective-permute-start.7 = (bf16[64,7296]{1,0:T(8,128)(2,1)S(1)}, bf16[64,7296]{1,0:T(8,128)(2,1)S(1)}, u32[]{:S(2)}, u32[]{:S(2)}) collective-permute-start(bf16[64,7296]{1,0:T(8,128)(2,1)S(1)} %collective-permute-done.3.refs_1_.refs_3_), channel_id=1, source_target_pairs={{0,1},{2,0},{4,2},{6,4},{7,6},{5,7},{3,5},{1,3},{8,9},{10,8},{12,1... | collective-permute-start | bytes 2801672 | tf_op jit(solution)/shard_map/ppermute | solution.py:406
  43.0 18.6 %collective-permute-start.8 = (bf16[128,3072]{1,0:T(8,128)(2,1)S(1)}, bf16[128,3072]{1,0:T(8,128)(2,1)S(1)}, u32[]{:S(2)}, u32[]{:S(2)}) collective-permute-start(bf16[128,3072]{1,0:T(8,128)(2,1)S(1)} %pack.5), channel_id=1, source_target_pairs={{0,16},{8,24},{16,0},{24,8},{1,17},{9,25},{17,1},{25,9},{2,18},{10... | collective-permute-start | bytes 2359304 | tf_op jit(solution)/shard_map/ppermute | solution.py:412
  44.7 1.8 %copy-start.1 = (bf16[144,10368]{1,0:T(8,128)(2,1)S(1)}, bf16[144,10368]{1,0:T(8,128)(2,1)}, u32[]{:S(2)}) copy-start(bf16[144,10368]{1,0:T(8,128)(2,1)} %get-tuple-element.66.send_ref) | copy-start | bytes 8957956
  64.5 19.0 %collective-permute-start.13 = (bf16[128,3072]{1,0:T(8,128)(2,1)S(1)}, bf16[128,3072]{1,0:T(8,128)(2,1)S(1)}, u32[]{:S(2)}, u32[]{:S(2)}) collective-permute-start(bf16[128,3072]{1,0:T(8,128)(2,1)S(1)} %get-tuple-element.80), channel_id=1, source_target_pairs={{0,16},{8,24},{16,0},{24,8},{1,17},{9,25},{17,1},{25,9},{2,18},{10... | collective-permute-start | bytes 2359304 | tf_op jit(solution)/shard_map/ppermute | solution.py:412
  66.1 17.4 %collective-permute-start.11 = (bf16[64,4096]{1,0:T(8,128)(2,1)S(1)}, bf16[64,4096]{1,0:T(8,128)(2,1)S(1)}, u32[]{:S(2)}, u32[]{:S(2)}) collective-permute-start(bf16[64,4096]{1,0:T(8,128)(2,1)S(1)} %get-tuple-element.78), channel_id=1, source_target_pairs={{0,2},{2,4},{4,6},{6,7},{7,5},{5,3},{3,1},{1,0},{8,10},{10,12},{12... | collective-permute-start | bytes 1572872 | tf_op jit(solution)/shard_map/ppermute | solution.py:406
  67.7 15.9 %collective-permute-start.12 = (bf16[64,4096]{1,0:T(8,128)(2,1)S(1)}, bf16[64,4096]{1,0:T(8,128)(2,1)S(1)}, u32[]{:S(2)}, u32[]{:S(2)}) collective-permute-start(bf16[64,4096]{1,0:T(8,128)(2,1)S(1)} %get-tuple-element.79), channel_id=1, source_target_pairs={{0,1},{2,0},{4,2},{6,4},{7,6},{5,7},{3,5},{1,3},{8,9},{10,8},{12,1... | collective-permute-start | bytes 1572872 | tf_op jit(solution)/shard_map/ppermute | solution.py:406
  68.1 14.1 %collective-permute-start.9 = (bf16[32,3200]{1,0:T(8,128)(2,1)S(1)}, bf16[32,3200]{1,0:T(8,128)(2,1)S(1)}, u32[]{:S(2)}, u32[]{:S(2)}) collective-permute-start(bf16[32,3200]{1,0:T(8,128)(2,1)S(1)} %get-tuple-element.76), channel_id=1, source_target_pairs={{0,2},{2,4},{4,6},{6,7},{7,5},{5,3},{3,1},{1,0},{8,10},{10,12},{12... | collective-permute-start | bytes 614408 | tf_op jit(solution)/shard_map/ppermute | solution.py:406
  69.7 13.8 %collective-permute-start.10 = (bf16[32,3200]{1,0:T(8,128)(2,1)S(1)}, bf16[32,3200]{1,0:T(8,128)(2,1)S(1)}, u32[]{:S(2)}, u32[]{:S(2)}) collective-permute-start(bf16[32,3200]{1,0:T(8,128)(2,1)S(1)} %get-tuple-element.77), channel_id=1, source_target_pairs={{0,1},{2,0},{4,2},{6,4},{7,6},{5,7},{3,5},{1,3},{8,9},{10,8},{12,1... | collective-permute-start | bytes 614408 | tf_op jit(solution)/shard_map/ppermute | solution.py:406
  83.6 8.7 %collective-permute-start.16 = (bf16[64,3072]{1,0:T(8,128)(2,1)S(1)}, bf16[64,3072]{1,0:T(8,128)(2,1)S(1)}, u32[]{:S(2)}, u32[]{:S(2)}) collective-permute-start(bf16[64,3072]{1,0:T(8,128)(2,1)S(1)} %pack.7), channel_id=1, source_target_pairs={{0,16},{8,24},{16,0},{24,8},{1,17},{9,25},{17,1},{25,9},{2,18},{10... | collective-permute-start | bytes 1179656 | tf_op jit(solution)/shard_map/ppermute | solution.py:412
  84.2 6.4 %collective-permute-start.14 = (bf16[32,4096]{1,0:T(8,128)(2,1)S(1)}, bf16[32,4096]{1,0:T(8,128)(2,1)S(1)}, u32[]{:S(2)}, u32[]{:S(2)}) collective-permute-start(bf16[32,4096]{1,0:T(8,128)(2,1)S(1)} %slice.6), channel_id=1, source_target_pairs={{0,2},{2,4},{4,6},{6,7},{7,5},{5,3},{3,1},{1,0},{8,10},{10,12},{12... | collective-permute-start | bytes 786440 | tf_op jit(solution)/shard_map/ppermute | solution.py:406
  85.8 6.5 %copy-start.3 = (bf16[64,3200]{1,0:T(8,128)(2,1)S(1)}, bf16[64,3200]{1,0:T(8,128)(2,1)}, u32[]{:S(2)}) copy-start(bf16[64,3200]{1,0:T(8,128)(2,1)} %get-tuple-element.57.refs_0_) | copy-start | bytes 1228804
  85.8 6.4 %copy-start.4 = (bf16[64,3072]{1,0:T(8,128)(2,1)S(1)}, bf16[64,3072]{1,0:T(8,128)(2,1)}, u32[]{:S(2)}) copy-start(bf16[64,3072]{1,0:T(8,128)(2,1)} %get-tuple-element.88.refs_6_) | copy-start | bytes 1179652
  85.9 6.4 %collective-permute-start.15 = (bf16[32,4096]{1,0:T(8,128)(2,1)S(1)}, bf16[32,4096]{1,0:T(8,128)(2,1)S(1)}, u32[]{:S(2)}, u32[]{:S(2)}) collective-permute-start(bf16[32,4096]{1,0:T(8,128)(2,1)S(1)} %slice.7), channel_id=1, source_target_pairs={{0,1},{2,0},{4,2},{6,4},{7,6},{5,7},{3,5},{1,3},{8,9},{10,8},{12,1... | collective-permute-start | bytes 786440 | tf_op jit(solution)/shard_map/ppermute | solution.py:406
  86.4 7.8 %collective-permute-start.18 = (f32[288,128]{1,0:T(8,128)S(1)}, f32[288,128]{1,0:T(8,128)S(1)}, u32[]{:S(2)}, u32[]{:S(2)}) collective-permute-start(f32[288,128]{1,0:T(8,128)S(1)} %get-tuple-element.90.refs_1_), channel_id=1, source_target_pairs={{0,8},{8,0},{16,24},{24,16},{1,9},{9,1},{17,25},{25,17},{2,10},{10... | collective-permute-start | bytes 442376 | tf_op jit(solution)/shard_map/ppermute | solution.py:409
  88.1 6.0 %collective-permute-start.20 = (f32[288,128]{1,0:T(8,128)S(1)}, f32[288,128]{1,0:T(8,128)S(1)}, u32[]{:S(2)}, u32[]{:S(2)}) collective-permute-start(f32[288,128]{1,0:T(8,128)S(1)} %get-tuple-element.93.refs_3_), channel_id=1, source_target_pairs={{0,8},{8,0},{16,24},{24,16},{1,9},{9,1},{17,25},{25,17},{2,10},{10... | collective-permute-start | bytes 442376 | tf_op jit(solution)/shard_map/ppermute | solution.py:409
  90.6 3.5 %collective-permute-start.19 = (f32[288,128]{1,0:T(8,128)S(1)}, f32[288,128]{1,0:T(8,128)S(1)}, u32[]{:S(2)}, u32[]{:S(2)}) collective-permute-start(f32[288,128]{1,0:T(8,128)S(1)} %get-tuple-element.91.refs_2_), channel_id=1, source_target_pairs={{0,8},{8,0},{16,24},{24,16},{1,9},{9,1},{17,25},{25,17},{2,10},{10... | collective-permute-start | bytes 442376 | tf_op jit(solution)/shard_map/ppermute | solution.py:409
  94.0 1.4 %collective-permute-start.17 = (f32[288,128]{1,0:T(8,128)S(1)}, f32[288,128]{1,0:T(8,128)S(1)}, u32[]{:S(2)}, u32[]{:S(2)}) collective-permute-start(f32[288,128]{1,0:T(8,128)S(1)} %get-tuple-element.89.refs_0_), channel_id=1, source_target_pairs={{0,8},{8,0},{16,24},{24,16},{1,9},{9,1},{17,25},{25,17},{2,10},{10... | collective-permute-start | bytes 442376 | tf_op jit(solution)/shard_map/ppermute | solution.py:409
  95.8 3.8 %collective-permute-start.21 = (f32[8,512]{1,0:T(8,128)S(1)}, f32[8,512]{1,0:T(8,128)S(1)}, u32[]{:S(2)}, u32[]{:S(2)}) collective-permute-start(f32[8,512]{1,0:T(8,128)S(1)} %get-tuple-element.95.refs_0_), channel_id=1, source_target_pairs={{0,16},{8,24},{16,0},{24,8},{1,17},{9,25},{17,1},{25,9},{2,18},{10... | collective-permute-start | bytes 49160 | tf_op jit(solution)/shard_map/ppermute | solution.py:484
  97.3 9.7 %collective-permute-start.30 = (bf16[128,1280]{1,0:T(8,128)(2,1)S(1)}, bf16[128,1280]{1,0:T(8,128)(2,1)S(1)}, u32[]{:S(2)}, u32[]{:S(2)}) collective-permute-start(bf16[128,1280]{1,0:T(8,128)(2,1)S(1)} %get-tuple-element.97.refs_9_), channel_id=1, source_target_pairs={{0,8},{8,0},{16,24},{24,16},{1,9},{9,1},{17,25},{25,17},{2,10},{10... | collective-permute-start | bytes 983048 | tf_op jit(solution)/shard_map/ppermute | solution.py:409
  99.6 5.4 %collective-permute-start.22 = (bf16[160,512]{1,0:T(8,128)(2,1)S(1)}, bf16[160,512]{1,0:T(8,128)(2,1)S(1)}, u32[]{:S(2)}, u32[]{:S(2)}) collective-permute-start(bf16[160,512]{1,0:T(8,128)(2,1)S(1)} %payload.1.refs_0_), channel_id=1, source_target_pairs={{0,2},{2,4},{4,6},{6,7},{7,5},{5,3},{3,1},{1,0},{8,10},{10,12},{12... | collective-permute-start | bytes 491528 | tf_op jit(solution)/shard_map/ppermute | solution.py:406
  101.2 5.8 %collective-permute-start.26 = (bf16[160,512]{1,0:T(8,128)(2,1)S(1)}, bf16[160,512]{1,0:T(8,128)(2,1)S(1)}, u32[]{:S(2)}, u32[]{:S(2)}) collective-permute-start(bf16[160,512]{1,0:T(8,128)(2,1)S(1)} %payload.1.refs_0_), channel_id=1, source_target_pairs={{0,1},{2,0},{4,2},{6,4},{7,6},{5,7},{3,5},{1,3},{8,9},{10,8},{12,1... | collective-permute-start | bytes 491528 | tf_op jit(solution)/shard_map/ppermute | solution.py:406
  105.0 5.3 %collective-permute-start.23 = (bf16[160,512]{1,0:T(8,128)(2,1)S(1)}, bf16[160,512]{1,0:T(8,128)(2,1)S(1)}, u32[]{:S(2)}, u32[]{:S(2)}) collective-permute-start(bf16[160,512]{1,0:T(8,128)(2,1)S(1)} %collective-permute-done.22.refs_1_), channel_id=1, source_target_pairs={{0,2},{2,4},{4,6},{6,7},{7,5},{5,3},{3,1},{1,0},{8,10},{10,12},{12... | collective-permute-start | bytes 491528 | tf_op jit(solution)/shard_map/ppermute | solution.py:406
  106.5 10.6 %collective-permute-start.32 = (bf16[128,1280]{1,0:T(8,128)(2,1)S(1)}, bf16[128,1280]{1,0:T(8,128)(2,1)S(1)}, u32[]{:S(2)}, u32[]{:S(2)}) collective-permute-start(bf16[128,1280]{1,0:T(8,128)(2,1)S(1)} %get-tuple-element.99.refs_11_), channel_id=1, source_target_pairs={{0,8},{8,0},{16,24},{24,16},{1,9},{9,1},{17,25},{25,17},{2,10},{10... | collective-permute-start | bytes 983048 | tf_op jit(solution)/shard_map/ppermute | solution.py:409
  106.5 10.6 %collective-permute-start.31 = (bf16[128,1280]{1,0:T(8,128)(2,1)S(1)}, bf16[128,1280]{1,0:T(8,128)(2,1)S(1)}, u32[]{:S(2)}, u32[]{:S(2)}) collective-permute-start(bf16[128,1280]{1,0:T(8,128)(2,1)S(1)} %get-tuple-element.98.refs_10_), channel_id=1, source_target_pairs={{0,8},{8,0},{16,24},{24,16},{1,9},{9,1},{17,25},{25,17},{2,10},{10... | collective-permute-start | bytes 983048 | tf_op jit(solution)/shard_map/ppermute | solution.py:409
  107.0 10.1 %collective-permute-start.29 = (bf16[128,1280]{1,0:T(8,128)(2,1)S(1)}, bf16[128,1280]{1,0:T(8,128)(2,1)S(1)}, u32[]{:S(2)}, u32[]{:S(2)}) collective-permute-start(bf16[128,1280]{1,0:T(8,128)(2,1)S(1)} %get-tuple-element.96.refs_8_), channel_id=1, source_target_pairs={{0,8},{8,0},{16,24},{24,16},{1,9},{9,1},{17,25},{25,17},{2,10},{10... | collective-permute-start | bytes 983048 | tf_op jit(solution)/shard_map/ppermute | solution.py:409
  107.0 6.6 %collective-permute-start.27 = (bf16[160,512]{1,0:T(8,128)(2,1)S(1)}, bf16[160,512]{1,0:T(8,128)(2,1)S(1)}, u32[]{:S(2)}, u32[]{:S(2)}) collective-permute-start(bf16[160,512]{1,0:T(8,128)(2,1)S(1)} %collective-permute-done.26.refs_7_), channel_id=1, source_target_pairs={{0,1},{2,0},{4,2},{6,4},{7,6},{5,7},{3,5},{1,3},{8,9},{10,8},{12,1... | collective-permute-start | bytes 491528 | tf_op jit(solution)/shard_map/ppermute | solution.py:406
  110.3 5.3 %collective-permute-start.24 = (bf16[160,512]{1,0:T(8,128)(2,1)S(1)}, bf16[160,512]{1,0:T(8,128)(2,1)S(1)}, u32[]{:S(2)}, u32[]{:S(2)}) collective-permute-start(bf16[160,512]{1,0:T(8,128)(2,1)S(1)} %collective-permute-done.23.refs_2_), channel_id=1, source_target_pairs={{0,2},{2,4},{4,6},{6,7},{7,5},{5,3},{3,1},{1,0},{8,10},{10,12},{12... | collective-permute-start | bytes 491528 | tf_op jit(solution)/shard_map/ppermute | solution.py:406
  113.6 5.8 %collective-permute-start.28 = (bf16[160,512]{1,0:T(8,128)(2,1)S(1)}, bf16[160,512]{1,0:T(8,128)(2,1)S(1)}, u32[]{:S(2)}, u32[]{:S(2)}) collective-permute-start(bf16[160,512]{1,0:T(8,128)(2,1)S(1)} %collective-permute-done.27.refs_6_), channel_id=1, source_target_pairs={{0,1},{2,0},{4,2},{6,4},{7,6},{5,7},{3,5},{1,3},{8,9},{10,8},{12,1... | collective-permute-start | bytes 491528 | tf_op jit(solution)/shard_map/ppermute | solution.py:406
  115.6 5.3 %collective-permute-start.25 = (bf16[160,512]{1,0:T(8,128)(2,1)S(1)}, bf16[160,512]{1,0:T(8,128)(2,1)S(1)}, u32[]{:S(2)}, u32[]{:S(2)}) collective-permute-start(bf16[160,512]{1,0:T(8,128)(2,1)S(1)} %collective-permute-done.24.refs_3_), channel_id=1, source_target_pairs={{0,2},{2,4},{4,6},{6,7},{7,5},{5,3},{3,1},{1,0},{8,10},{10,12},{12... | collective-permute-start | bytes 491528 | tf_op jit(solution)/shard_map/ppermute | solution.py:406

commit v3 on v2

--- a/solution.py
+++ b/solution.py
@@ -14,6 +14,7 @@
 LANES = 128
 MIB = 1 << 20
 TAIL = 16
+COLS = 1280
 
 
 def cycle_of(count):
@@ -493,19 +494,19 @@
     )(scores, *all_stats)
     payloads = [payload] + [None] * (n - 1)
     fp = bp = payload
-    for d in range(1, far + 1):
+    payloads[far] = ring(payload, far)
+    for d in range(1, far):
         fp = payloads[d] = ring(fp, 1)
-        if d < far:
-            bp = payloads[n - d] = ring(bp, -1)
+        bp = payloads[n - d] = ring(bp, -1)
 
     fixed = lambda i: (0, 0)
-    per_half = half // 256 if half % 256 == 0 else 0
+    per_half = half // COLS if half % COLS == 0 else 0
     if per_half:
         steps = 2 * per_half
         w = slices + other_slices
-        w_specs = [pl.BlockSpec((LANES, 256), lambda i: (0, lax.rem(i, per_half)))] * len(w)
-        out_spec = pl.BlockSpec((n * ori_rows, 256), lambda i: (0, i))
-        grant = 24
+        w_specs = [pl.BlockSpec((LANES, COLS), lambda i: (0, lax.rem(i, per_half)))] * len(w)
+        out_spec = pl.BlockSpec((n * ori_rows, COLS), lambda i: (0, i))
+        grant = 40
     else:
         steps = max(1, n // 2)
         w = [

time: 129 us -> 126 us (0.977)
  waiting for transfers between devices: 70.6 us -> 67.1 us
  starting transfers between devices: 29.1 us -> 31.6 us
  Pallas kernels: 26.4 us -> 24 us
    ppermute x19, waiting for transfers between devices: 38 us -> 34.9 us  [ring(): lax.ppermute(x, 'ori', [(cycle[i], cycle[(i + d) % n]) for i in range(n)])]
    pallas_call x1, Pallas kernels: 7.98 us -> 5.51 us  [body(): pl.pallas_call(functools.partial(sums_kernel, n, ori_rows, per_half, cycl...]
    ppermute x19, starting transfers between devices: 21.1 us -> 23.1 us  [ring(): lax.ppermute(x, 'ori', [(cycle[i], cycle[(i + d) % n]) for i in range(n)])]
  transfers between devices with their start and end apart: 33 -> 33, of which waited for: 20 -> 18; matrix products, arithmetic and copies ran while one was open for 0% -> 0% of each run, Pallas kernels for 12% -> 12%
where the time goes in v3:
time: 126 us; the launch traced here: 125 us
  waiting for transfers between devices  67.1 us (53%)
  starting transfers between devices  31.6 us (25%)
  Pallas kernels  24 us (19%)
  local copies, waits for them, and re-layouts  1.91 us (2%)
    ppermute x19, waiting for transfers between devices, ring(): lax.ppermute(x, 'ori', [(cycle[i], cycle[(i + d) % n]) for i in range(n)])  34.9 us
    ppermute x4, waiting for transfers between devices, cross(): return lax.ppermute(x, 'cls', [(i, i ^ 2) for i in range(n_cls)])  29 us
    ppermute x19, starting transfers between devices, ring(): lax.ppermute(x, 'ori', [(cycle[i], cycle[(i + d) % n]) for i in range(n)])  23.1 us
    pallas_call x4, Pallas kernels, group_scores(): pl.pallas_call(functools.partial(score_kernel, wo, ws, numbered, aligned)...  6.98 us
    pallas_call x1, Pallas kernels, prep_projections(): pl.pallas_call(functools.partial(split_kernel, wo, ws, n), in_specs=[pl.B...  5.88 us
    pallas_call x1, Pallas kernels, body(): pl.pallas_call(functools.partial(sums_kernel, n, ori_rows, per_half, cycl...  5.51 us
    ppermute x4, starting transfers between devices, cross(): return lax.ppermute(x, 'cls', [(i, i ^ 2) for i in range(n_cls)])  5.31 us
    pallas_call x1, Pallas kernels, prep_images(): pl.pallas_call(functools.partial(image_kernel, n, wo, ws), in_specs=[pl.B...  2.67 us
  transfers between devices with their start and end apart: 33, of which 18 were waited for; matrix products, arithmetic and copies ran while one was open for 0% of the time, Pallas kernels for 12%

profile of v3, /device:TPU:0, one launch (start us, length us, event | category | flops | bytes accessed | tf_op | source)
XLA Modules:
  0.0 125.4 jit_solution(17677493609811335071)
XLA Ops:
  0.6 2.7 %prep_images.1 = (bf16[64,3200]{1,0:T(8,128)(2,1)}, bf16[64,3072]{1,0:T(8,128)(2,1)}, bf16[64,4096]{1,0:T(8,128)(2,1)}, f32[160,128]{1,0:T(8,128)}) custom-call(bf16[64,20480]{1,0:T(8,128)(2,1)} %img_hbm.1, s32[160,128]{1,0:T(8,128)} %bitcast.5, f32[1,100]{1,0:T(1,128)} %bitcast.7, s32[4,64]{1,0:T(4,128)} %bitcast.6), custom_call_target="tpu_custom_call" | custom-call | tf_op jit(solution)/shard_map/prep_images/pallas_call | solution.py:89
  3.3 3.0 %collective-permute-start.1 = (bf16[64,3200]{1,0:T(8,128)(2,1)}, bf16[64,3200]{1,0:T(8,128)(2,1)S(1)}, u32[]{:S(2)}, u32[]{:S(2)}) collective-permute-start(bf16[64,3200]{1,0:T(8,128)(2,1)} %get-tuple-element.57.refs_0_), channel_id=1, source_target_pairs={{0,1},{2,0},{4,2},{6,4},{7,6},{5,7},{3,5},{1,3},{8,9},{10,8},{12,1... | collective-permute-start | bytes 1228808 | tf_op jit(solution)/shard_map/ppermute | solution.py:407
  6.3 0.1 collective-permute-start
  6.5 5.9 %split_projections.1 = (bf16[144,10368]{1,0:T(8,128)(2,1)}, bf16[144,10368]{1,0:T(8,128)(2,1)}) custom-call(bf16[1,144,20480]{2,1,0:T(8,128)(2,1)} %proj_hbm), custom_call_target="tpu_custom_call" | custom-call | bytes 11796480 | tf_op jit(solution)/shard_map/split_projections/pallas_call | solution.py:181
  12.4 0.0 copy-start
  12.4 0.0 copy-start.6
  12.4 3.7 %collective-permute-done.1.refs_1_ = bf16[64,3200]{1,0:T(8,128)(2,1)S(1)} collective-permute-done((bf16[64,3200]{1,0:T(8,128)(2,1)}, bf16[64,3200]{1,0:T(8,128)(2,1)S(1)}, u32[]{:S(2)}, u32[]{:S(2)}) %collective-permute-start.1) | collective-permute-done | bytes 409632 | tf_op jit(solution)/shard_map/ppermute | solution.py:407
  16.1 1.4 %collective-permute-done.refs_0_ = bf16[64,3200]{1,0:T(8,128)(2,1)S(1)} collective-permute-done((bf16[64,3200]{1,0:T(8,128)(2,1)}, bf16[64,3200]{1,0:T(8,128)(2,1)S(1)}, u32[]{:S(2)}, u32[]{:S(2)}) %collective-permute-start) | collective-permute-done | bytes 409632 | tf_op jit(solution)/shard_map/ppermute | solution.py:407
  17.5 0.2 pack.4
  17.7 0.5 collective-permute-start.2
  18.1 1.6 %collective-permute-start.3 = (bf16[64,7296]{1,0:T(8,128)(2,1)S(1)}, bf16[64,7296]{1,0:T(8,128)(2,1)S(1)}, u32[]{:S(2)}, u32[]{:S(2)}) collective-permute-start(bf16[64,7296]{1,0:T(8,128)(2,1)S(1)} %get-tuple-element.64.refs_1_), channel_id=1, source_target_pairs={{0,1},{2,0},{4,2},{6,4},{7,6},{5,7},{3,5},{1,3},{8,9},{10,8},{12,1... | collective-permute-start | bytes 2801672 | tf_op jit(solution)/shard_map/ppermute | solution.py:407
  19.7 1.5 %collective-permute-start.4 = (bf16[128,3072]{1,0:T(8,128)(2,1)S(1)}, bf16[128,3072]{1,0:T(8,128)(2,1)S(1)}, u32[]{:S(2)}, u32[]{:S(2)}) collective-permute-start(bf16[128,3072]{1,0:T(8,128)(2,1)S(1)} %get-tuple-element.65), channel_id=1, source_target_pairs={{0,16},{8,24},{16,0},{24,8},{1,17},{9,25},{17,1},{25,9},{2,18},{10... | collective-permute-start | bytes 2359304 | tf_op jit(solution)/shard_map/ppermute | solution.py:413
  21.2 17.9 %collective-permute-done.4.refs_4_ = bf16[128,3072]{1,0:T(8,128)(2,1)S(1)} collective-permute-done((bf16[128,3072]{1,0:T(8,128)(2,1)S(1)}, bf16[128,3072]{1,0:T(8,128)(2,1)S(1)}, u32[]{:S(2)}, u32[]{:S(2)}) %collective-permute-start.4) | collective-permute-done | bytes 786464 | tf_op jit(solution)/shard_map/ppermute | solution.py:413
  39.1 1.7 %collective-permute-done.2.refs_0_.refs_2_ = bf16[64,7296]{1,0:T(8,128)(2,1)S(1)} collective-permute-done((bf16[64,7296]{1,0:T(8,128)(2,1)S(1)}, bf16[64,7296]{1,0:T(8,128)(2,1)S(1)}, u32[]{:S(2)}, u32[]{:S(2)}) %collective-permute-start.2) | collective-permute-done | bytes 933920 | tf_op jit(solution)/shard_map/ppermute | solution.py:407
  40.8 0.1 collective-permute-done.3.refs_1_.refs_3_
  41.0 1.7 %collective-permute-start.6 = (bf16[64,7296]{1,0:T(8,128)(2,1)S(1)}, bf16[64,7296]{1,0:T(8,128)(2,1)S(1)}, u32[]{:S(2)}, u32[]{:S(2)}) collective-permute-start(bf16[64,7296]{1,0:T(8,128)(2,1)S(1)} %collective-permute-done.2.refs_0_.refs_2_), channel_id=1, source_target_pairs={{0,2},{2,4},{4,6},{6,7},{7,5},{5,3},{3,1},{1,0},{8,10},{10,12},{12... | collective-permute-start | bytes 2801672 | tf_op jit(solution)/shard_map/ppermute | solution.py:407
  42.6 0.3 collective-permute-start.7
  43.0 0.1 pack.5
  43.0 1.7 %collective-permute-start.8 = (bf16[128,3072]{1,0:T(8,128)(2,1)S(1)}, bf16[128,3072]{1,0:T(8,128)(2,1)S(1)}, u32[]{:S(2)}, u32[]{:S(2)}) collective-permute-start(bf16[128,3072]{1,0:T(8,128)(2,1)S(1)} %pack.5), channel_id=1, source_target_pairs={{0,16},{8,24},{16,0},{24,8},{1,17},{9,25},{17,1},{25,9},{2,18},{10... | collective-permute-start | bytes 2359304 | tf_op jit(solution)/shard_map/ppermute | solution.py:413
  44.7 1.8 %copy-done.1 = bf16[144,10368]{1,0:T(8,128)(2,1)S(1)} copy-done((bf16[144,10368]{1,0:T(8,128)(2,1)S(1)}, bf16[144,10368]{1,0:T(8,128)(2,1)}, u32[]{:S(2)}) %copy-start.1) | copy-done | bytes 2986008
  46.5 2.2 %half_norms.1.bias_ref = f32[144,128]{1,0:T(8,128)S(1)} custom-call(bf16[144,10368]{1,0:T(8,128)(2,1)S(1)} %copy-done, bf16[144,10368]{1,0:T(8,128)(2,1)S(1)} %copy-done.1, f32[1,144]{1,0:T(1,128)S(1)} %copy-done.6, f32[160,128]{1,0:T(8,128)S(1)} %copy-done.5), custom_call_target="tpu_custom_call" | custom-call | flops 8847360 | bytes 5898240 | tf_op jit(solution)/shard_map/half_norms/pallas_call | solution.py:191
  48.7 1.7 %group_scores.4 = (f32[288,128]{1,0:T(8,128)S(1)}, bf16[128,1280]{1,0:T(8,128)(2,1)S(1)}) custom-call(bf16[144,10368]{1,0:T(8,128)(2,1)S(1)} %copy-done, bf16[144,10368]{1,0:T(8,128)(2,1)S(1)} %collective-permute-done.5.mate_ref, f32[144,128]{1,0:T(8,128)S(1)} %half_norms.1.bias_ref, bf16[64,7296]{1,0:T(8,128)(2,1)S(1)} %get-tuple-element.63.refs_0_, ...), custom_call_target="tpu_custom_call" | custom-call | flops 764411904 | bytes 8626176 | tf_op jit(solution)/shard_map/group_scores/pallas_call | solution.py:275
  50.5 11.1 %collective-permute-done.8.refs_4_ = bf16[128,3072]{1,0:T(8,128)(2,1)S(1)} collective-permute-done((bf16[128,3072]{1,0:T(8,128)(2,1)S(1)}, bf16[128,3072]{1,0:T(8,128)(2,1)S(1)}, u32[]{:S(2)}, u32[]{:S(2)}) %collective-permute-start.8) | collective-permute-done | bytes 786464 | tf_op jit(solution)/shard_map/ppermute | solution.py:413
  61.6 1.6 %collective-permute-done.6.refs_0_.refs_2_ = bf16[64,7296]{1,0:T(8,128)(2,1)S(1)} collective-permute-done((bf16[64,7296]{1,0:T(8,128)(2,1)S(1)}, bf16[64,7296]{1,0:T(8,128)(2,1)S(1)}, u32[]{:S(2)}, u32[]{:S(2)}) %collective-permute-start.6) | collective-permute-done | bytes 933920 | tf_op jit(solution)/shard_map/ppermute | solution.py:407
  63.2 1.2 collective-permute-done.7.refs_1_.refs_3_
  64.4 0.1 pack.6
  64.5 1.6 %collective-permute-start.13 = (bf16[128,3072]{1,0:T(8,128)(2,1)S(1)}, bf16[128,3072]{1,0:T(8,128)(2,1)S(1)}, u32[]{:S(2)}, u32[]{:S(2)}) collective-permute-start(bf16[128,3072]{1,0:T(8,128)(2,1)S(1)} %get-tuple-element.80), channel_id=1, source_target_pairs={{0,16},{8,24},{16,0},{24,8},{1,17},{9,25},{17,1},{25,9},{2,18},{10... | collective-permute-start | bytes 2359304 | tf_op jit(solution)/shard_map/ppermute | solution.py:413
  66.1 1.6 %collective-permute-start.11 = (bf16[64,4096]{1,0:T(8,128)(2,1)S(1)}, bf16[64,4096]{1,0:T(8,128)(2,1)S(1)}, u32[]{:S(2)}, u32[]{:S(2)}) collective-permute-start(bf16[64,4096]{1,0:T(8,128)(2,1)S(1)} %get-tuple-element.78), channel_id=1, source_target_pairs={{0,2},{2,4},{4,6},{6,7},{7,5},{5,3},{3,1},{1,0},{8,10},{10,12},{12... | collective-permute-start | bytes 1572872 | tf_op jit(solution)/shard_map/ppermute | solution.py:407
  67.7 0.4 collective-permute-start.12
  68.1 1.6 %collective-permute-start.9 = (bf16[32,3200]{1,0:T(8,128)(2,1)S(1)}, bf16[32,3200]{1,0:T(8,128)(2,1)S(1)}, u32[]{:S(2)}, u32[]{:S(2)}) collective-permute-start(bf16[32,3200]{1,0:T(8,128)(2,1)S(1)} %get-tuple-element.76), channel_id=1, source_target_pairs={{0,2},{2,4},{4,6},{6,7},{7,5},{5,3},{3,1},{1,0},{8,10},{10,12},{12... | collective-permute-start | bytes 614408 | tf_op jit(solution)/shard_map/ppermute | solution.py:407
  69.7 0.4 collective-permute-start.10
  70.1 1.7 %group_scores.5 = (f32[288,128]{1,0:T(8,128)S(1)}, bf16[128,1280]{1,0:T(8,128)(2,1)S(1)}) custom-call(bf16[144,10368]{1,0:T(8,128)(2,1)S(1)} %copy-done, bf16[144,10368]{1,0:T(8,128)(2,1)S(1)} %collective-permute-done.5.mate_ref, f32[144,128]{1,0:T(8,128)S(1)} %half_norms.1.bias_ref, bf16[64,7296]{1,0:T(8,128)(2,1)S(1)} %collective-permute-done.2.refs_0_.refs_2_, ...), custom_call_target="tpu_custom_call" | custom-call | flops 764411904 | bytes 8626176 | tf_op jit(solution)/shard_map/group_scores/pallas_call | solution.py:275
  71.9 10.3 %collective-permute-done.9.refs_0_.refs_1_ = bf16[32,3200]{1,0:T(8,128)(2,1)S(1)} collective-permute-done((bf16[32,3200]{1,0:T(8,128)(2,1)S(1)}, bf16[32,3200]{1,0:T(8,128)(2,1)S(1)}, u32[]{:S(2)}, u32[]{:S(2)}) %collective-permute-start.9) | collective-permute-done | bytes 204832 | tf_op jit(solution)/shard_map/ppermute | solution.py:407
  82.2 1.3 %collective-permute-done.10.refs_1_.refs_2_ = bf16[32,3200]{1,0:T(8,128)(2,1)S(1)} collective-permute-done((bf16[32,3200]{1,0:T(8,128)(2,1)S(1)}, bf16[32,3200]{1,0:T(8,128)(2,1)S(1)}, u32[]{:S(2)}, u32[]{:S(2)}) %collective-permute-start.10) | collective-permute-done | bytes 204832 | tf_op jit(solution)/shard_map/ppermute | solution.py:407
  83.5 0.0 collective-permute-done.11.refs_2_
  83.5 0.0 collective-permute-done.12.refs_3_
  83.6 0.6 collective-permute-start.16
  84.2 1.6 %collective-permute-start.14 = (bf16[32,4096]{1,0:T(8,128)(2,1)S(1)}, bf16[32,4096]{1,0:T(8,128)(2,1)S(1)}, u32[]{:S(2)}, u32[]{:S(2)}) collective-permute-start(bf16[32,4096]{1,0:T(8,128)(2,1)S(1)} %slice.6), channel_id=1, source_target_pairs={{0,2},{2,4},{4,6},{6,7},{7,5},{5,3},{3,1},{1,0},{8,10},{10,12},{12... | collective-permute-start | bytes 786440 | tf_op jit(solution)/shard_map/ppermute | solution.py:407
  85.9 0.5 collective-permute-start.15
  86.4 1.8 %group_scores.7 = (f32[288,128]{1,0:T(8,128)S(1)}, bf16[128,1280]{1,0:T(8,128)(2,1)S(1)}) custom-call(bf16[144,10368]{1,0:T(8,128)(2,1)S(1)} %copy-done, bf16[144,10368]{1,0:T(8,128)(2,1)S(1)} %collective-permute-done.5.mate_ref, f32[144,128]{1,0:T(8,128)S(1)} %half_norms.1.bias_ref, bf16[64,7296]{1,0:T(8,128)(2,1)S(1)} %collective-permute-done.6.refs_0_.refs_2_, ...), custom_call_target="tpu_custom_call" | custom-call | flops 764411904 | bytes 8626176 | tf_op jit(solution)/shard_map/group_scores/pallas_call | solution.py:275
  88.1 0.6 collective-permute-start.20
  88.7 1.9 %collective-permute-done.14.refs_4_ = bf16[32,4096]{1,0:T(8,128)(2,1)S(1)} collective-permute-done((bf16[32,4096]{1,0:T(8,128)(2,1)S(1)}, bf16[32,4096]{1,0:T(8,128)(2,1)S(1)}, u32[]{:S(2)}, u32[]{:S(2)}) %collective-permute-start.14) | collective-permute-done | bytes 262176 | tf_op jit(solution)/shard_map/ppermute | solution.py:407
  90.6 0.0 collective-permute-start.19
  90.6 1.7 %collective-permute-done.15.refs_5_ = bf16[32,4096]{1,0:T(8,128)(2,1)S(1)} collective-permute-done((bf16[32,4096]{1,0:T(8,128)(2,1)S(1)}, bf16[32,4096]{1,0:T(8,128)(2,1)S(1)}, u32[]{:S(2)}, u32[]{:S(2)}) %collective-permute-start.15) | collective-permute-done | bytes 262176 | tf_op jit(solution)/shard_map/ppermute | solution.py:407
  92.3 1.7 %group_scores.6 = (f32[288,128]{1,0:T(8,128)S(1)}, bf16[128,1280]{1,0:T(8,128)(2,1)S(1)}) custom-call(bf16[144,10368]{1,0:T(8,128)(2,1)S(1)} %copy-done, bf16[144,10368]{1,0:T(8,128)(2,1)S(1)} %collective-permute-done.5.mate_ref, f32[144,128]{1,0:T(8,128)S(1)} %half_norms.1.bias_ref, bf16[64,3200]{1,0:T(8,128)(2,1)S(1)} %copy-done.3, ...), custom_call_target="tpu_custom_call" | custom-call | flops 764411904 | bytes 8626176 | tf_op jit(solution)/shard_map/group_scores/pallas_call | solution.py:275
  94.0 0.1 collective-permute-start.17
  94.1 0.5 collective-permute-start.30
  94.6 0.8 collective-permute-done.17.refs_4_
  95.5 0.3 local_stats.1
  95.7 1.5 %collective-permute-start.21 = (f32[8,512]{1,0:T(8,128)S(1)}, f32[8,512]{1,0:T(8,128)S(1)}, u32[]{:S(2)}, u32[]{:S(2)}) collective-permute-start(f32[8,512]{1,0:T(8,128)S(1)} %get-tuple-element.95.refs_0_), channel_id=1, source_target_pairs={{0,16},{8,24},{16,0},{24,8},{1,17},{9,25},{17,1},{25,9},{2,18},{10... | collective-permute-start | bytes 49160 | tf_op jit(solution)/shard_map/ppermute | solution.py:485
  97.3 2.2 %collective-permute-done.21.refs_1_ = f32[8,512]{1,0:T(8,128)S(1)} collective-permute-done((f32[8,512]{1,0:T(8,128)S(1)}, f32[8,512]{1,0:T(8,128)S(1)}, u32[]{:S(2)}, u32[]{:S(2)}) %collective-permute-start.21) | collective-permute-done | bytes 16416 | tf_op jit(solution)/shard_map/ppermute | solution.py:485
  99.5 0.1 payload.1.refs_0_
  99.6 0.5 collective-permute-start.26
  100.1 1.6 %collective-permute-start.22 = (bf16[160,512]{1,0:T(8,128)(2,1)S(1)}, bf16[160,512]{1,0:T(8,128)(2,1)S(1)}, u32[]{:S(2)}, u32[]{:S(2)}) collective-permute-start(bf16[160,512]{1,0:T(8,128)(2,1)S(1)} %payload.1.refs_0_), channel_id=1, source_target_pairs={{0,2},{2,4},{4,6},{6,7},{7,5},{5,3},{3,1},{1,0},{8,10},{10,12},{12... | collective-permute-start | bytes 491528 | tf_op jit(solution)/shard_map/ppermute | solution.py:407
  101.7 0.5 collective-permute-start.29
  102.2 2.8 %collective-permute-done.26.refs_7_ = bf16[160,512]{1,0:T(8,128)(2,1)S(1)} collective-permute-done((bf16[160,512]{1,0:T(8,128)(2,1)S(1)}, bf16[160,512]{1,0:T(8,128)(2,1)S(1)}, u32[]{:S(2)}, u32[]{:S(2)}) %collective-permute-start.26) | collective-permute-done | bytes 163872 | tf_op jit(solution)/shard_map/ppermute | solution.py:407
  105.0 0.5 collective-permute-start.27
  105.4 1.6 %collective-permute-start.23 = (bf16[160,512]{1,0:T(8,128)(2,1)S(1)}, bf16[160,512]{1,0:T(8,128)(2,1)S(1)}, u32[]{:S(2)}, u32[]{:S(2)}) collective-permute-start(bf16[160,512]{1,0:T(8,128)(2,1)S(1)} %collective-permute-done.22.refs_1_), channel_id=1, source_target_pairs={{0,2},{2,4},{4,6},{6,7},{7,5},{5,3},{3,1},{1,0},{8,10},{10,12},{12... | collective-permute-start | bytes 491528 | tf_op jit(solution)/shard_map/ppermute | solution.py:407
  107.0 2.4 %collective-permute-start.25 = (bf16[160,512]{1,0:T(8,128)(2,1)S(1)}, bf16[160,512]{1,0:T(8,128)(2,1)S(1)}, u32[]{:S(2)}, u32[]{:S(2)}) collective-permute-start(bf16[160,512]{1,0:T(8,128)(2,1)S(1)} %payload.1.refs_0_), channel_id=1, source_target_pairs={{0,7},{2,5},{4,3},{6,1},{7,0},{5,2},{3,4},{1,6},{8,15},{10,13},{12... | collective-permute-start | bytes 491528 | tf_op jit(solution)/shard_map/ppermute | solution.py:407
  109.4 4.0 %collective-permute-done.27.refs_6_ = bf16[160,512]{1,0:T(8,128)(2,1)S(1)} collective-permute-done((bf16[160,512]{1,0:T(8,128)(2,1)S(1)}, bf16[160,512]{1,0:T(8,128)(2,1)S(1)}, u32[]{:S(2)}, u32[]{:S(2)}) %collective-permute-start.27) | collective-permute-done | bytes 163872 | tf_op jit(solution)/shard_map/ppermute | solution.py:407
  113.4 3.2 %collective-permute-start.24 = (bf16[160,512]{1,0:T(8,128)(2,1)S(1)}, bf16[160,512]{1,0:T(8,128)(2,1)S(1)}, u32[]{:S(2)}, u32[]{:S(2)}) collective-permute-start(bf16[160,512]{1,0:T(8,128)(2,1)S(1)} %collective-permute-done.23.refs_2_), channel_id=1, source_target_pairs={{0,2},{2,4},{4,6},{6,7},{7,5},{5,3},{3,1},{1,0},{8,10},{10,12},{12... | collective-permute-start | bytes 491528 | tf_op jit(solution)/shard_map/ppermute | solution.py:407
  116.6 0.5 collective-permute-done.25.refs_4_
  117.0 2.8 %collective-permute-done.28.refs_5_ = bf16[160,512]{1,0:T(8,128)(2,1)S(1)} collective-permute-done((bf16[160,512]{1,0:T(8,128)(2,1)S(1)}, bf16[160,512]{1,0:T(8,128)(2,1)S(1)}, u32[]{:S(2)}, u32[]{:S(2)}) %collective-permute-start.28) | collective-permute-done | bytes 163872 | tf_op jit(solution)/shard_map/ppermute | solution.py:407
  119.8 5.5 %class_sums.1 = (bf16[1152,2560]{1,0:T(8,128)(2,1)}, f32[1,64]{1,0:T(1,128)}) custom-call(bf16[160,512]{1,0:T(8,128)(2,1)S(1)} %payload.1.refs_0_, bf16[160,512]{1,0:T(8,128)(2,1)S(1)} %collective-permute-done.22.refs_1_, bf16[160,512]{1,0:T(8,128)(2,1)S(1)} %collective-permute-done.23.refs_2_, bf16[160,512]{1,0:T(8,128)(2,1)S(1)} %collective-permute-done.24.refs_3_, ...), custom_call_target="tpu_custom_call" | custom-call | tf_op jit(solution)/shard_map/class_sums/pallas_call | solution.py:520
  (32 shorter events, 0.1 us)
Async XLA Ops:
  3.3 14.2 %copy-start.2 = (bf16[64,4096]{1,0:T(8,128)(2,1)S(1)}, bf16[64,4096]{1,0:T(8,128)(2,1)}, u32[]{:S(2)}) copy-start(bf16[64,4096]{1,0:T(8,128)(2,1)} %get-tuple-element.62.refs_2_.refs_3_) | copy-start | bytes 1572868
  3.3 12.8 %collective-permute-start.1 = (bf16[64,3200]{1,0:T(8,128)(2,1)}, bf16[64,3200]{1,0:T(8,128)(2,1)S(1)}, u32[]{:S(2)}, u32[]{:S(2)}) collective-permute-start(bf16[64,3200]{1,0:T(8,128)(2,1)} %get-tuple-element.57.refs_0_), channel_id=1, source_target_pairs={{0,1},{2,0},{4,2},{6,4},{7,6},{5,7},{3,5},{1,3},{8,9},{10,8},{12,1... | collective-permute-start | bytes 1228808 | tf_op jit(solution)/shard_map/ppermute | solution.py:407
  6.3 11.1 %collective-permute-start = (bf16[64,3200]{1,0:T(8,128)(2,1)}, bf16[64,3200]{1,0:T(8,128)(2,1)S(1)}, u32[]{:S(2)}, u32[]{:S(2)}) collective-permute-start(bf16[64,3200]{1,0:T(8,128)(2,1)} %get-tuple-element.57.refs_0_), channel_id=1, source_target_pairs={{0,2},{2,4},{4,6},{6,7},{7,5},{5,3},{3,1},{1,0},{8,10},{10,12},{12... | collective-permute-start | bytes 1228808 | tf_op jit(solution)/shard_map/ppermute | solution.py:407
  12.4 32.3 %copy-start = (bf16[144,10368]{1,0:T(8,128)(2,1)S(1)}, bf16[144,10368]{1,0:T(8,128)(2,1)}, u32[]{:S(2)}) copy-start(bf16[144,10368]{1,0:T(8,128)(2,1)} %get-tuple-element.56.keep_ref.own_ref) | copy-start | bytes 8957956
  12.4 32.3 %copy-start.5 = (f32[160,128]{1,0:T(8,128)S(1)}, f32[160,128]{1,0:T(8,128)}, u32[]{:S(2)}) copy-start(f32[160,128]{1,0:T(8,128)} %get-tuple-element.68.w_ref) | copy-start | bytes 245764
  12.4 32.3 %copy-start.6 = (f32[1,144]{1,0:T(1,128)S(1)}, f32[1,144]{1,0:T(1,128)}, u32[]{:S(2)}) copy-start(f32[1,144]{1,0:T(1,128)} %prior_ref.1) | copy-start | bytes 1732
  17.5 23.5 %collective-permute-start.5 = (bf16[144,10368]{1,0:T(8,128)(2,1)}, bf16[144,10368]{1,0:T(8,128)(2,1)S(1)}, u32[]{:S(2)}, u32[]{:S(2)}) collective-permute-start(bf16[144,10368]{1,0:T(8,128)(2,1)} %get-tuple-element.66.send_ref), channel_id=1, source_target_pairs={{0,8},{8,0},{16,24},{24,16},{1,9},{9,1},{17,25},{25,17},{2,10},{10... | collective-permute-start | bytes 8957960 | tf_op jit(solution)/shard_map/ppermute | solution.py:410
  17.7 23.2 %collective-permute-start.2 = (bf16[64,7296]{1,0:T(8,128)(2,1)S(1)}, bf16[64,7296]{1,0:T(8,128)(2,1)S(1)}, u32[]{:S(2)}, u32[]{:S(2)}) collective-permute-start(bf16[64,7296]{1,0:T(8,128)(2,1)S(1)} %get-tuple-element.63.refs_0_), channel_id=1, source_target_pairs={{0,2},{2,4},{4,6},{6,7},{7,5},{5,3},{3,1},{1,0},{8,10},{10,12},{12... | collective-permute-start | bytes 2801672 | tf_op jit(solution)/shard_map/ppermute | solution.py:407
  18.1 22.8 %collective-permute-start.3 = (bf16[64,7296]{1,0:T(8,128)(2,1)S(1)}, bf16[64,7296]{1,0:T(8,128)(2,1)S(1)}, u32[]{:S(2)}, u32[]{:S(2)}) collective-permute-start(bf16[64,7296]{1,0:T(8,128)(2,1)S(1)} %get-tuple-element.64.refs_1_), channel_id=1, source_target_pairs={{0,1},{2,0},{4,2},{6,4},{7,6},{5,7},{3,5},{1,3},{8,9},{10,8},{12,1... | collective-permute-start | bytes 2801672 | tf_op jit(solution)/shard_map/ppermute | solution.py:407
  19.7 19.4 %collective-permute-start.4 = (bf16[128,3072]{1,0:T(8,128)(2,1)S(1)}, bf16[128,3072]{1,0:T(8,128)(2,1)S(1)}, u32[]{:S(2)}, u32[]{:S(2)}) collective-permute-start(bf16[128,3072]{1,0:T(8,128)(2,1)S(1)} %get-tuple-element.65), channel_id=1, source_target_pairs={{0,16},{8,24},{16,0},{24,8},{1,17},{9,25},{17,1},{25,9},{2,18},{10... | collective-permute-start | bytes 2359304 | tf_op jit(solution)/shard_map/ppermute | solution.py:413
  41.0 22.2 %collective-permute-start.6 = (bf16[64,7296]{1,0:T(8,128)(2,1)S(1)}, bf16[64,7296]{1,0:T(8,128)(2,1)S(1)}, u32[]{:S(2)}, u32[]{:S(2)}) collective-permute-start(bf16[64,7296]{1,0:T(8,128)(2,1)S(1)} %collective-permute-done.2.refs_0_.refs_2_), channel_id=1, source_target_pairs={{0,2},{2,4},{4,6},{6,7},{7,5},{5,3},{3,1},{1,0},{8,10},{10,12},{12... | collective-permute-start | bytes 2801672 | tf_op jit(solution)/shard_map/ppermute | solution.py:407
  42.6 21.7 %collective-permute-start.7 = (bf16[64,7296]{1,0:T(8,128)(2,1)S(1)}, bf16[64,7296]{1,0:T(8,128)(2,1)S(1)}, u32[]{:S(2)}, u32[]{:S(2)}) collective-permute-start(bf16[64,7296]{1,0:T(8,128)(2,1)S(1)} %collective-permute-done.3.refs_1_.refs_3_), channel_id=1, source_target_pairs={{0,1},{2,0},{4,2},{6,4},{7,6},{5,7},{3,5},{1,3},{8,9},{10,8},{12,1... | collective-permute-start | bytes 2801672 | tf_op jit(solution)/shard_map/ppermute | solution.py:407
  43.0 18.6 %collective-permute-start.8 = (bf16[128,3072]{1,0:T(8,128)(2,1)S(1)}, bf16[128,3072]{1,0:T(8,128)(2,1)S(1)}, u32[]{:S(2)}, u32[]{:S(2)}) collective-permute-start(bf16[128,3072]{1,0:T(8,128)(2,1)S(1)} %pack.5), channel_id=1, source_target_pairs={{0,16},{8,24},{16,0},{24,8},{1,17},{9,25},{17,1},{25,9},{2,18},{10... | collective-permute-start | bytes 2359304 | tf_op jit(solution)/shard_map/ppermute | solution.py:413
  44.7 1.8 %copy-start.1 = (bf16[144,10368]{1,0:T(8,128)(2,1)S(1)}, bf16[144,10368]{1,0:T(8,128)(2,1)}, u32[]{:S(2)}) copy-start(bf16[144,10368]{1,0:T(8,128)(2,1)} %get-tuple-element.66.send_ref) | copy-start | bytes 8957956
  64.5 19.0 %collective-permute-start.13 = (bf16[128,3072]{1,0:T(8,128)(2,1)S(1)}, bf16[128,3072]{1,0:T(8,128)(2,1)S(1)}, u32[]{:S(2)}, u32[]{:S(2)}) collective-permute-start(bf16[128,3072]{1,0:T(8,128)(2,1)S(1)} %get-tuple-element.80), channel_id=1, source_target_pairs={{0,16},{8,24},{16,0},{24,8},{1,17},{9,25},{17,1},{25,9},{2,18},{10... | collective-permute-start | bytes 2359304 | tf_op jit(solution)/shard_map/ppermute | solution.py:413
  66.1 17.4 %collective-permute-start.11 = (bf16[64,4096]{1,0:T(8,128)(2,1)S(1)}, bf16[64,4096]{1,0:T(8,128)(2,1)S(1)}, u32[]{:S(2)}, u32[]{:S(2)}) collective-permute-start(bf16[64,4096]{1,0:T(8,128)(2,1)S(1)} %get-tuple-element.78), channel_id=1, source_target_pairs={{0,2},{2,4},{4,6},{6,7},{7,5},{5,3},{3,1},{1,0},{8,10},{10,12},{12... | collective-permute-start | bytes 1572872 | tf_op jit(solution)/shard_map/ppermute | solution.py:407
  67.7 15.9 %collective-permute-start.12 = (bf16[64,4096]{1,0:T(8,128)(2,1)S(1)}, bf16[64,4096]{1,0:T(8,128)(2,1)S(1)}, u32[]{:S(2)}, u32[]{:S(2)}) collective-permute-start(bf16[64,4096]{1,0:T(8,128)(2,1)S(1)} %get-tuple-element.79), channel_id=1, source_target_pairs={{0,1},{2,0},{4,2},{6,4},{7,6},{5,7},{3,5},{1,3},{8,9},{10,8},{12,1... | collective-permute-start | bytes 1572872 | tf_op jit(solution)/shard_map/ppermute | solution.py:407
  68.1 14.1 %collective-permute-start.9 = (bf16[32,3200]{1,0:T(8,128)(2,1)S(1)}, bf16[32,3200]{1,0:T(8,128)(2,1)S(1)}, u32[]{:S(2)}, u32[]{:S(2)}) collective-permute-start(bf16[32,3200]{1,0:T(8,128)(2,1)S(1)} %get-tuple-element.76), channel_id=1, source_target_pairs={{0,2},{2,4},{4,6},{6,7},{7,5},{5,3},{3,1},{1,0},{8,10},{10,12},{12... | collective-permute-start | bytes 614408 | tf_op jit(solution)/shard_map/ppermute | solution.py:407
  69.7 13.8 %collective-permute-start.10 = (bf16[32,3200]{1,0:T(8,128)(2,1)S(1)}, bf16[32,3200]{1,0:T(8,128)(2,1)S(1)}, u32[]{:S(2)}, u32[]{:S(2)}) collective-permute-start(bf16[32,3200]{1,0:T(8,128)(2,1)S(1)} %get-tuple-element.77), channel_id=1, source_target_pairs={{0,1},{2,0},{4,2},{6,4},{7,6},{5,7},{3,5},{1,3},{8,9},{10,8},{12,1... | collective-permute-start | bytes 614408 | tf_op jit(solution)/shard_map/ppermute | solution.py:407
  83.6 8.7 %collective-permute-start.16 = (bf16[64,3072]{1,0:T(8,128)(2,1)S(1)}, bf16[64,3072]{1,0:T(8,128)(2,1)S(1)}, u32[]{:S(2)}, u32[]{:S(2)}) collective-permute-start(bf16[64,3072]{1,0:T(8,128)(2,1)S(1)} %pack.7), channel_id=1, source_target_pairs={{0,16},{8,24},{16,0},{24,8},{1,17},{9,25},{17,1},{25,9},{2,18},{10... | collective-permute-start | bytes 1179656 | tf_op jit(solution)/shard_map/ppermute | solution.py:413
  84.2 6.4 %collective-permute-start.14 = (bf16[32,4096]{1,0:T(8,128)(2,1)S(1)}, bf16[32,4096]{1,0:T(8,128)(2,1)S(1)}, u32[]{:S(2)}, u32[]{:S(2)}) collective-permute-start(bf16[32,4096]{1,0:T(8,128)(2,1)S(1)} %slice.6), channel_id=1, source_target_pairs={{0,2},{2,4},{4,6},{6,7},{7,5},{5,3},{3,1},{1,0},{8,10},{10,12},{12... | collective-permute-start | bytes 786440 | tf_op jit(solution)/shard_map/ppermute | solution.py:407
  85.8 6.5 %copy-start.3 = (bf16[64,3200]{1,0:T(8,128)(2,1)S(1)}, bf16[64,3200]{1,0:T(8,128)(2,1)}, u32[]{:S(2)}) copy-start(bf16[64,3200]{1,0:T(8,128)(2,1)} %get-tuple-element.57.refs_0_) | copy-start | bytes 1228804
  85.8 6.4 %copy-start.4 = (bf16[64,3072]{1,0:T(8,128)(2,1)S(1)}, bf16[64,3072]{1,0:T(8,128)(2,1)}, u32[]{:S(2)}) copy-start(bf16[64,3072]{1,0:T(8,128)(2,1)} %get-tuple-element.88.refs_6_) | copy-start | bytes 1179652
  85.9 6.4 %collective-permute-start.15 = (bf16[32,4096]{1,0:T(8,128)(2,1)S(1)}, bf16[32,4096]{1,0:T(8,128)(2,1)S(1)}, u32[]{:S(2)}, u32[]{:S(2)}) collective-permute-start(bf16[32,4096]{1,0:T(8,128)(2,1)S(1)} %slice.7), channel_id=1, source_target_pairs={{0,1},{2,0},{4,2},{6,4},{7,6},{5,7},{3,5},{1,3},{8,9},{10,8},{12,1... | collective-permute-start | bytes 786440 | tf_op jit(solution)/shard_map/ppermute | solution.py:407
  86.4 8.3 %collective-permute-start.18 = (f32[288,128]{1,0:T(8,128)S(1)}, f32[288,128]{1,0:T(8,128)S(1)}, u32[]{:S(2)}, u32[]{:S(2)}) collective-permute-start(f32[288,128]{1,0:T(8,128)S(1)} %get-tuple-element.90.refs_1_), channel_id=1, source_target_pairs={{0,8},{8,0},{16,24},{24,16},{1,9},{9,1},{17,25},{25,17},{2,10},{10... | collective-permute-start | bytes 442376 | tf_op jit(solution)/shard_map/ppermute | solution.py:410
  88.1 6.5 %collective-permute-start.20 = (f32[288,128]{1,0:T(8,128)S(1)}, f32[288,128]{1,0:T(8,128)S(1)}, u32[]{:S(2)}, u32[]{:S(2)}) collective-permute-start(f32[288,128]{1,0:T(8,128)S(1)} %get-tuple-element.93.refs_3_), channel_id=1, source_target_pairs={{0,8},{8,0},{16,24},{24,16},{1,9},{9,1},{17,25},{25,17},{2,10},{10... | collective-permute-start | bytes 442376 | tf_op jit(solution)/shard_map/ppermute | solution.py:410
  90.6 4.0 %collective-permute-start.19 = (f32[288,128]{1,0:T(8,128)S(1)}, f32[288,128]{1,0:T(8,128)S(1)}, u32[]{:S(2)}, u32[]{:S(2)}) collective-permute-start(f32[288,128]{1,0:T(8,128)S(1)} %get-tuple-element.91.refs_2_), channel_id=1, source_target_pairs={{0,8},{8,0},{16,24},{24,16},{1,9},{9,1},{17,25},{25,17},{2,10},{10... | collective-permute-start | bytes 442376 | tf_op jit(solution)/shard_map/ppermute | solution.py:410
  94.0 1.4 %collective-permute-start.17 = (f32[288,128]{1,0:T(8,128)S(1)}, f32[288,128]{1,0:T(8,128)S(1)}, u32[]{:S(2)}, u32[]{:S(2)}) collective-permute-start(f32[288,128]{1,0:T(8,128)S(1)} %get-tuple-element.89.refs_0_), channel_id=1, source_target_pairs={{0,8},{8,0},{16,24},{24,16},{1,9},{9,1},{17,25},{25,17},{2,10},{10... | collective-permute-start | bytes 442376 | tf_op jit(solution)/shard_map/ppermute | solution.py:410
  94.1 7.6 %collective-permute-start.30 = (bf16[128,1280]{1,0:T(8,128)(2,1)S(1)}, bf16[128,1280]{1,0:T(8,128)(2,1)S(1)}, u32[]{:S(2)}, u32[]{:S(2)}) collective-permute-start(bf16[128,1280]{1,0:T(8,128)(2,1)S(1)} %get-tuple-element.97.refs_9_), channel_id=1, source_target_pairs={{0,8},{8,0},{16,24},{24,16},{1,9},{9,1},{17,25},{25,17},{2,10},{10... | collective-permute-start | bytes 983048 | tf_op jit(solution)/shard_map/ppermute | solution.py:410
  95.7 3.8 %collective-permute-start.21 = (f32[8,512]{1,0:T(8,128)S(1)}, f32[8,512]{1,0:T(8,128)S(1)}, u32[]{:S(2)}, u32[]{:S(2)}) collective-permute-start(f32[8,512]{1,0:T(8,128)S(1)} %get-tuple-element.95.refs_0_), channel_id=1, source_target_pairs={{0,16},{8,24},{16,0},{24,8},{1,17},{9,25},{17,1},{25,9},{2,18},{10... | collective-permute-start | bytes 49160 | tf_op jit(solution)/shard_map/ppermute | solution.py:485
  97.3 9.7 %collective-permute-start.32 = (bf16[128,1280]{1,0:T(8,128)(2,1)S(1)}, bf16[128,1280]{1,0:T(8,128)(2,1)S(1)}, u32[]{:S(2)}, u32[]{:S(2)}) collective-permute-start(bf16[128,1280]{1,0:T(8,128)(2,1)S(1)} %get-tuple-element.99.refs_11_), channel_id=1, source_target_pairs={{0,8},{8,0},{16,24},{24,16},{1,9},{9,1},{17,25},{25,17},{2,10},{10... | collective-permute-start | bytes 983048 | tf_op jit(solution)/shard_map/ppermute | solution.py:410
  99.6 5.4 %collective-permute-start.26 = (bf16[160,512]{1,0:T(8,128)(2,1)S(1)}, bf16[160,512]{1,0:T(8,128)(2,1)S(1)}, u32[]{:S(2)}, u32[]{:S(2)}) collective-permute-start(bf16[160,512]{1,0:T(8,128)(2,1)S(1)} %payload.1.refs_0_), channel_id=1, source_target_pairs={{0,1},{2,0},{4,2},{6,4},{7,6},{5,7},{3,5},{1,3},{8,9},{10,8},{12,1... | collective-permute-start | bytes 491528 | tf_op jit(solution)/shard_map/ppermute | solution.py:407
  100.1 5.3 %collective-permute-start.22 = (bf16[160,512]{1,0:T(8,128)(2,1)S(1)}, bf16[160,512]{1,0:T(8,128)(2,1)S(1)}, u32[]{:S(2)}, u32[]{:S(2)}) collective-permute-start(bf16[160,512]{1,0:T(8,128)(2,1)S(1)} %payload.1.refs_0_), channel_id=1, source_target_pairs={{0,2},{2,4},{4,6},{6,7},{7,5},{5,3},{3,1},{1,0},{8,10},{10,12},{12... | collective-permute-start | bytes 491528 | tf_op jit(solution)/shard_map/ppermute | solution.py:407
  101.7 14.9 %collective-permute-start.31 = (bf16[128,1280]{1,0:T(8,128)(2,1)S(1)}, bf16[128,1280]{1,0:T(8,128)(2,1)S(1)}, u32[]{:S(2)}, u32[]{:S(2)}) collective-permute-start(bf16[128,1280]{1,0:T(8,128)(2,1)S(1)} %get-tuple-element.98.refs_10_), channel_id=1, source_target_pairs={{0,8},{8,0},{16,24},{24,16},{1,9},{9,1},{17,25},{25,17},{2,10},{10... | collective-permute-start | bytes 983048 | tf_op jit(solution)/shard_map/ppermute | solution.py:410
  101.7 15.4 %collective-permute-start.29 = (bf16[128,1280]{1,0:T(8,128)(2,1)S(1)}, bf16[128,1280]{1,0:T(8,128)(2,1)S(1)}, u32[]{:S(2)}, u32[]{:S(2)}) collective-permute-start(bf16[128,1280]{1,0:T(8,128)(2,1)S(1)} %get-tuple-element.96.refs_8_), channel_id=1, source_target_pairs={{0,8},{8,0},{16,24},{24,16},{1,9},{9,1},{17,25},{25,17},{2,10},{10... | collective-permute-start | bytes 983048 | tf_op jit(solution)/shard_map/ppermute | solution.py:410
  105.0 8.4 %collective-permute-start.27 = (bf16[160,512]{1,0:T(8,128)(2,1)S(1)}, bf16[160,512]{1,0:T(8,128)(2,1)S(1)}, u32[]{:S(2)}, u32[]{:S(2)}) collective-permute-start(bf16[160,512]{1,0:T(8,128)(2,1)S(1)} %collective-permute-done.26.refs_7_), channel_id=1, source_target_pairs={{0,1},{2,0},{4,2},{6,4},{7,6},{5,7},{3,5},{1,3},{8,9},{10,8},{12,1... | collective-permute-start | bytes 491528 | tf_op jit(solution)/shard_map/ppermute | solution.py:407
  105.4 7.9 %collective-permute-start.23 = (bf16[160,512]{1,0:T(8,128)(2,1)S(1)}, bf16[160,512]{1,0:T(8,128)(2,1)S(1)}, u32[]{:S(2)}, u32[]{:S(2)}) collective-permute-start(bf16[160,512]{1,0:T(8,128)(2,1)S(1)} %collective-permute-done.22.refs_1_), channel_id=1, source_target_pairs={{0,2},{2,4},{4,6},{6,7},{7,5},{5,3},{3,1},{1,0},{8,10},{10,12},{12... | collective-permute-start | bytes 491528 | tf_op jit(solution)/shard_map/ppermute | solution.py:407
  107.0 10.0 %collective-permute-start.25 = (bf16[160,512]{1,0:T(8,128)(2,1)S(1)}, bf16[160,512]{1,0:T(8,128)(2,1)S(1)}, u32[]{:S(2)}, u32[]{:S(2)}) collective-permute-start(bf16[160,512]{1,0:T(8,128)(2,1)S(1)} %payload.1.refs_0_), channel_id=1, source_target_pairs={{0,7},{2,5},{4,3},{6,1},{7,0},{5,2},{3,4},{1,6},{8,15},{10,13},{12... | collective-permute-start | bytes 491528 | tf_op jit(solution)/shard_map/ppermute | solution.py:407
  113.4 6.5 %collective-permute-start.28 = (bf16[160,512]{1,0:T(8,128)(2,1)S(1)}, bf16[160,512]{1,0:T(8,128)(2,1)S(1)}, u32[]{:S(2)}, u32[]{:S(2)}) collective-permute-start(bf16[160,512]{1,0:T(8,128)(2,1)S(1)} %collective-permute-done.27.refs_6_), channel_id=1, source_target_pairs={{0,1},{2,0},{4,2},{6,4},{7,6},{5,7},{3,5},{1,3},{8,9},{10,8},{12,1... | collective-permute-start | bytes 491528 | tf_op jit(solution)/shard_map/ppermute | solution.py:407
  113.4 6.5 %collective-permute-start.24 = (bf16[160,512]{1,0:T(8,128)(2,1)S(1)}, bf16[160,512]{1,0:T(8,128)(2,1)S(1)}, u32[]{:S(2)}, u32[]{:S(2)}) collective-permute-start(bf16[160,512]{1,0:T(8,128)(2,1)S(1)} %collective-permute-done.23.refs_2_), channel_id=1, source_target_pairs={{0,2},{2,4},{4,6},{6,7},{7,5},{5,3},{3,1},{1,0},{8,10},{10,12},{12... | collective-permute-start | bytes 491528 | tf_op jit(solution)/shard_map/ppermute | solution.py:407

commit v4 on v3

--- a/solution.py
+++ b/solution.py
@@ -14,7 +14,7 @@
 LANES = 128
 MIB = 1 << 20
 TAIL = 16
-COLS = 1280
+CHUNKS = 4
 
 
 def cycle_of(count):
@@ -38,16 +38,27 @@
     return pl.ds(pl.multiple_of(start, LANES), size)
 
 
-def image_kernel(n, wo, ws, img_hbm, index_hbm, noise_hbm, sig_hbm, own_ref, oth_ref, shared_ref, w_ref, img, index, noise, sig, sems):
+def weigh(n, half, pieces, img, w_ref):
+    core = lax.axis_index("cls") % 2
+    for i in range(n):
+        yield i
+        for ref, first, start, count in pieces:
+            for j in range(0, count, LANES):
+                weight = w_ref[pl.ds(((2 * i + core) * half + start + j) // LANES, 1), :]
+                wide = img[:, at(first + i * count + j, LANES)].astype(F32) * weight
+                ref[:, i * count + j : i * count + j + LANES] = wide.astype(BF16)
+
+
+def own_kernel(n, wo, ws, img_hbm, index_hbm, noise_hbm, sig_hbm, own_ref, w_ref, img, index, noise, sig, sems):
     cls = lax.axis_index("cls")
     core, side = cls % 2, (cls // 2) % 2
     half = 2 * wo + ws
+    small = [(index_hbm, index), (noise_hbm, noise), (sig_hbm, sig)]
+    copies = [pltpu.make_async_copy(src, dst, sems.at[n + i]) for i, (src, dst) in enumerate(small)]
     loads = []
     for i in range(n):
-        src = img_hbm.at[:, at((2 * i + core) * half, half)]
-        loads.append(pltpu.make_async_copy(src, img.at[:, i * half : (i + 1) * half], sems.at[i]))
-    small = [(index_hbm, index), (noise_hbm, noise), (sig_hbm, sig)]
-    copies = [pltpu.make_async_copy(src, dst, sems.at[n + i]) for i, (src, dst) in enumerate(small)]
+        src = img_hbm.at[:, at((2 * i + core) * half + side * wo, wo)]
+        loads.append(pltpu.make_async_copy(src, img.at[:, i * wo : (i + 1) * wo], sems.at[i]))
     for copy in copies + loads:
         copy.start()
     for copy in copies:
@@ -63,18 +74,25 @@
     eye = jnp.where(same, 1.0, 0.0).astype(BF16)
     turned = lax.dot_general(eye, unlisted, (((1,), (1,)), ((), ())), preferred_element_type=F32)
     own_ref[:, n * wo :] = turned.astype(BF16)
+    for i in weigh(n, half, [(own_ref, 0, side * wo, wo)], img, w_ref):
+        loads[i].wait()
+
+
+def rest_kernel(n, wo, ws, img_hbm, w_ref, oth_ref, shared_ref, img, sems):
+    cls = lax.axis_index("cls")
+    core, side = cls % 2, (cls // 2) % 2
+    half = 2 * wo + ws
+    loads = []
     for i in range(n):
-        loads[i].wait()
-        for ref, start, count in (
-            (own_ref, side * wo, wo),
-            (oth_ref, (1 - side) * wo, wo),
-            (shared_ref, 2 * wo, ws),
-        ):
-            for j in range(0, count, LANES):
-                tile = ((2 * i + core) * half + start + j) // LANES
-                weight = w_ref[pl.ds(tile, 1), :]
-                wide = img[:, at(i * half + start + j, LANES)].astype(F32) * weight
-                ref[:, i * count + j : i * count + j + LANES] = wide.astype(BF16)
+        base = (2 * i + core) * half
+        for k, start, first, count in ((0, (1 - side) * wo, i * wo, wo), (1, 2 * wo, n * wo + i * ws, ws)):
+            src = img_hbm.at[:, at(base + start, count)]
+            loads.append(pltpu.make_async_copy(src, img.at[:, first : first + count], sems.at[2 * i + k]))
+            loads[-1].start()
+    pieces = [(oth_ref, 0, (1 - side) * wo, wo), (shared_ref, n * wo, 2 * wo, ws)]
+    for i in weigh(n, half, pieces, img, w_ref):
+        loads[2 * i].wait()
+        loads[2 * i + 1].wait()
 
 
 def prep_images(images, weight_of, significant, core, side, wo, ws, n):
@@ -83,24 +101,32 @@
     if wo % LANES == 0:
         index, noise = weight_of
         sig = significant.T
-        out = [jax.ShapeDtypeStruct((rows, w), BF16) for w in (n * wo + LANES, n * wo, n * ws)]
-        out.append(jax.ShapeDtypeStruct(index.shape, F32))
-        vmem = pl.BlockSpec(memory_space=pltpu.VMEM)
-        return pl.pallas_call(
-            functools.partial(image_kernel, n, wo, ws),
-            in_specs=[pl.BlockSpec(memory_space=pl.ANY)] * 4,
-            out_specs=[vmem] * 4,
-            out_shape=out,
+        vmem, somewhere = pl.BlockSpec(memory_space=pltpu.VMEM), pl.BlockSpec(memory_space=pl.ANY)
+        own, weight = pl.pallas_call(
+            functools.partial(own_kernel, n, wo, ws),
+            in_specs=[somewhere] * 4,
+            out_specs=[vmem] * 2,
+            out_shape=[jax.ShapeDtypeStruct((rows, n * wo + LANES), BF16), jax.ShapeDtypeStruct(index.shape, F32)],
             scratch_shapes=[
-                pltpu.VMEM((rows, n * half), BF16),
+                pltpu.VMEM((rows, n * wo), BF16),
                 pltpu.VMEM(index.shape, index.dtype),
                 pltpu.VMEM(noise.shape, F32),
                 pltpu.VMEM(sig.shape, sig.dtype),
                 pltpu.SemaphoreType.DMA((n + 3,)),
             ],
             compiler_params=pltpu.CompilerParams(vmem_limit_bytes=61 * MIB),
-            name="prep_images",
+            name="prep_own_plane",
         )(images, index, noise, sig)
+        oth, shared = pl.pallas_call(
+            functools.partial(rest_kernel, n, wo, ws),
+            in_specs=[somewhere, vmem],
+            out_specs=[vmem] * 2,
+            out_shape=[jax.ShapeDtypeStruct((rows, n * wo), BF16), jax.ShapeDtypeStruct((rows, n * ws), BF16)],
+            scratch_shapes=[pltpu.VMEM((rows, n * (wo + ws)), BF16), pltpu.SemaphoreType.DMA((2 * n,))],
+            compiler_params=pltpu.CompilerParams(vmem_limit_bytes=58 * MIB),
+            name="prep_rest",
+        )(images, weight)
+        return own, oth, shared, weight
     weight = full_weights(weight_of)
     weighted = (images.astype(F32) * weight).astype(BF16).reshape(rows, n, 2, half)
     mine = lax.dynamic_index_in_dim(weighted, core, 2, keepdims=False)
@@ -339,49 +365,71 @@
     out_ref[rows:, :] = jnp.concatenate(levels, axis=0).astype(BF16)
 
 
-def sums_kernel(n, rows, per_half, cycle, *refs):
+def scale_posteriors(n, rows, cycle, payloads, posterior, evidence_ref):
     owner = lax.axis_index("ori")
     spot = sum(jnp.where(owner == o, cycle.index(o), 0) for o in range(n))
+    width = payloads[0].shape[1]
+    per = width // n
+    tops, sums = [], []
+    for d in range(n):
+        stat = payloads[d][rows:, :].astype(F32)
+        stat = jnp.concatenate([stat[0:2] + stat[2:4] + stat[4:6], jnp.zeros((6, width), F32)], axis=0)
+        stat = pltpu.roll(stat, per * d, 1) if d else stat
+        tops.append(stat[0:1])
+        sums.append(stat[1:2])
+    best = functools.reduce(jnp.maximum, tops)
+    grow = [jnp.exp(t - best) for t in tops]
+    total = functools.reduce(lambda a, b: a + b, [s * g for s, g in zip(sums, grow, strict=True)])
+    evidence_ref[...] = (best + jnp.log(total))[:, :per]
+    for d in range(n):
+        wide = payloads[d][:rows, :].astype(F32)
+        wide = pltpu.roll(wide, per * d, 1) if d else wide
+        back = lax.rem(spot + (n - d), n)
+        block = sum(jnp.where(back == p, cycle[p], 0) for p in range(n))
+        row = pl.multiple_of(block * rows, 16)
+        posterior[pl.ds(row, rows), :] = (wide * (grow[d] / total)).astype(BF16)
+
+
+def images_in_order(n, w):
+    per = w[0].shape[0] // 2
+    places = {r: (g, h) for g, pair in enumerate(group_order(n)) for h, r in enumerate(pair)}
+    return jnp.concatenate([w[places[r][0]][places[r][1] * per : (places[r][1] + 1) * per, :] for r in range(n)], axis=0)
+
+
+def stream_kernel(n, rows, cycle, *refs):
     payloads, refs = refs[:n], refs[n:]
     groups = n // 2
-    w_own, w_oth = refs[:groups], refs[groups:-3]
-    out_ref, evidence_ref, posterior = refs[-3:]
+    halves = (refs[:groups], refs[groups : 2 * groups])
+    out_hbm, evidence_ref, posterior, held, sems = refs[2 * groups :]
+    scale_posteriors(n, rows, cycle, payloads, posterior, evidence_ref)
+    core = lax.axis_index("cls") % 2
+    half = held.shape[1] // 2
+    tall = held.shape[0] // CHUNKS
+    copies = []
+    for h, w in enumerate(halves):
+        which = core if h == 0 else 1 - core
+        right = images_in_order(n, w)
+        for c in range(CHUNKS):
+            part, cols = slice(c * tall, (c + 1) * tall), slice(h * half, (h + 1) * half)
+            held[part, cols] = jnp.dot(posterior[part, :], right, preferred_element_type=F32).astype(BF16)
+            target = out_hbm.at[part, at(which * half, half)]
+            copies.append(pltpu.make_async_copy(held.at[part, cols], target, sems.at[len(copies)]))
+            copies[-1].start()
+    for copy in copies:
+        copy.wait()
+
+
+def sums_kernel(n, rows, cycle, *refs):
+    payloads, refs = refs[:n], refs[n:]
+    w, (out_ref, evidence_ref, posterior) = refs[:-3], refs[-3:]
     step = pl.program_id(0)
-    width = payloads[0].shape[1]
-    per = width // n
 
     @pl.when(step == 0)
     def _():
-        tops, sums = [], []
-        for d in range(n):
-            stat = payloads[d][rows:, :].astype(F32)
-            stat = jnp.concatenate([stat[0:2] + stat[2:4] + stat[4:6], jnp.zeros((6, width), F32)], axis=0)
-            stat = pltpu.roll(stat, per * d, 1) if d else stat
-            tops.append(stat[0:1])
-            sums.append(stat[1:2])
-        best = functools.reduce(jnp.maximum, tops)
-        grow = [jnp.exp(t - best) for t in tops]
-        total = functools.reduce(lambda a, b: a + b, [s * g for s, g in zip(sums, grow, strict=True)])
-        evidence_ref[...] = (best + jnp.log(total))[:, :per]
-        for d in range(n):
-            wide = payloads[d][:rows, :].astype(F32)
-            wide = pltpu.roll(wide, per * d, 1) if d else wide
-            back = lax.rem(spot + (n - d), n)
-            block = sum(jnp.where(back == p, cycle[p], 0) for p in range(n))
-            row = pl.multiple_of(block * rows, 16)
-            posterior[pl.ds(row, rows), :] = (wide * (grow[d] / total)).astype(BF16)
-
-    places = {r: (g, h) for g, pair in enumerate(group_order(n)) for h, r in enumerate(pair)}
-    first = (step < per_half) == (lax.axis_index("cls") % 2 == 0)
-    pieces = []
-    for r in range(n):
-        g, h = places[r]
-        held = slice(h * per, (h + 1) * per)
-        pieces.append(jnp.where(first, w_own[g][held, :], w_oth[g][held, :]) if per_half else w_own[g][held, :])
-    left = posterior[...]
-    if not per_half:
-        left = posterior[pl.ds(pl.multiple_of(step * out_ref.shape[0], 16), out_ref.shape[0]), :]
-    out_ref[...] = jnp.dot(left, jnp.concatenate(pieces, axis=0), preferred_element_type=F32).astype(BF16)
+        scale_posteriors(n, rows, cycle, payloads, posterior, evidence_ref)
+
+    left = posterior[pl.ds(pl.multiple_of(step * out_ref.shape[0], 16), out_ref.shape[0]), :]
+    out_ref[...] = jnp.dot(left, images_in_order(n, w), preferred_element_type=F32).astype(BF16)
 
 
 def tie(*values):
@@ -414,7 +462,7 @@
 
     weight_of = (shell_index.reshape(freqs // LANES, LANES), noise_inv.reshape(1, -1))
     own, oth, shared, weight = prep_images(images, weight_of, significant, core, side, wo, ws, n)
-    projections, own, oth, shared = tie(projections, own, oth, shared)
+    projections, own = tie(projections, own)
     keep, send, bias = prep_projections(projections, weight, log_prior, core, side, owner, wo, ws, n)
 
     cut_at = rows // 2
@@ -499,32 +547,35 @@
         fp = payloads[d] = ring(fp, 1)
         bp = payloads[n - d] = ring(bp, -1)
 
+    out_shape = [jax.ShapeDtypeStruct((n * ori_rows, 2 * half), BF16), jax.ShapeDtypeStruct((1, rows), F32)]
+    posterior = pltpu.VMEM((n * ori_rows, width), BF16)
+    if half % LANES == 0:
+        w = slices + other_slices
+        sums, evidence = pl.pallas_call(
+            functools.partial(stream_kernel, n, ori_rows, cycle),
+            in_specs=[vmem] * (n + len(w)),
+            out_specs=[pl.BlockSpec(memory_space=pl.ANY), vmem],
+            out_shape=out_shape,
+            scratch_shapes=[posterior, pltpu.VMEM(out_shape[0].shape, BF16), pltpu.SemaphoreType.DMA((2 * CHUNKS,))],
+            compiler_params=pltpu.CompilerParams(vmem_limit_bytes=32 * MIB),
+            name="class_sums",
+        )(*payloads, *w)
+        return sums[None], evidence.reshape(rows)
     fixed = lambda i: (0, 0)
-    per_half = half // COLS if half % COLS == 0 else 0
-    if per_half:
-        steps = 2 * per_half
-        w = slices + other_slices
-        w_specs = [pl.BlockSpec((LANES, COLS), lambda i: (0, lax.rem(i, per_half)))] * len(w)
-        out_spec = pl.BlockSpec((n * ori_rows, COLS), lambda i: (0, i))
-        grant = 40
-    else:
-        steps = max(1, n // 2)
-        w = [
-            jnp.concatenate([jnp.where(core == 0, a, b), jnp.where(core == 0, b, a)], axis=1)
-            for a, b in zip(slices, other_slices, strict=True)
-        ]
-        w_specs = [pl.BlockSpec((LANES, 2 * half), fixed, pipeline_mode=pl.Buffered(1))] * len(w)
-        out_spec = pl.BlockSpec((n * ori_rows // steps, 2 * half), lambda i: (i, 0))
-        grant = 62
-    held_once = pl.BlockSpec(payload.shape, fixed, pipeline_mode=pl.Buffered(1))
+    steps = max(1, n // 2)
+    w = [
+        jnp.concatenate([jnp.where(core == 0, a, b), jnp.where(core == 0, b, a)], axis=1)
+        for a, b in zip(slices, other_slices, strict=True)
+    ]
+    once = lambda x: pl.BlockSpec(x.shape, fixed, pipeline_mode=pl.Buffered(1))
     sums, evidence = pl.pallas_call(
-        functools.partial(sums_kernel, n, ori_rows, per_half, cycle),
+        functools.partial(sums_kernel, n, ori_rows, cycle),
         grid=(steps,),
-        in_specs=[held_once] * n + w_specs,
-        out_specs=[out_spec, pl.BlockSpec((1, rows), fixed)],
-        scratch_shapes=[pltpu.VMEM((n * ori_rows, width), BF16)],
-        out_shape=[jax.ShapeDtypeStruct((n * ori_rows, 2 * half), BF16), jax.ShapeDtypeStruct((1, rows), F32)],
-        compiler_params=pltpu.CompilerParams(vmem_limit_bytes=grant * MIB),
+        in_specs=[once(x) for x in payloads + w],
+        out_specs=[pl.BlockSpec((n * ori_rows // steps, 2 * half), lambda i: (i, 0)), pl.BlockSpec((1, rows), fixed)],
+        out_shape=out_shape,
+        scratch_shapes=[posterior],
+        compiler_params=pltpu.CompilerParams(vmem_limit_bytes=62 * MIB),
         name="class_sums",
     )(*payloads, *w)
     return sums[None], evidence.reshape(rows)

time: 126 us -> 125 us (level)
  waiting for transfers between devices: 67.1 us -> 63.9 us
  Pallas kernels: 24 us -> 26.2 us
    ppermute x19, waiting for transfers between devices: 34.9 us -> 31.7 us  [ring(): lax.ppermute(x, 'ori', [(cycle[i], cycle[(i + d) % n]) for i in range(n)])]
    pallas_call x2 -> x3, Pallas kernels: 8.18 us -> 10.4 us  [the longest x1 5.17 us: body(): pl.pallas_call(functools.partial(stream_kernel, n, ori_rows, cycle), in_s...]
  transfers between devices with their start and end apart: 33 -> 33, of which waited for: 18 -> 18; matrix products, arithmetic and copies ran while one was open for 0% -> 0% of each run, Pallas kernels for 12% -> 15%
where the time goes in v4:
time: 125 us
  waiting for transfers between devices  63.9 us (51%)
  starting transfers between devices  31.6 us (25%)
  Pallas kernels  26.2 us (21%)
  local copies, waits for them, and re-layouts  1.91 us (2%)
    ppermute x19, waiting for transfers between devices, ring(): lax.ppermute(x, 'ori', [(cycle[i], cycle[(i + d) % n]) for i in range(n)])  31.7 us
    ppermute x4, waiting for transfers between devices, cross(): return lax.ppermute(x, 'cls', [(i, i ^ 2) for i in range(n_cls)])  29 us
    ppermute x19, starting transfers between devices, ring(): lax.ppermute(x, 'ori', [(cycle[i], cycle[(i + d) % n]) for i in range(n)])  23.1 us
    pallas_call x4, Pallas kernels, group_scores(): pl.pallas_call(functools.partial(score_kernel, wo, ws, numbered, aligned)...  6.98 us
    pallas_call x1, Pallas kernels, prep_projections(): pl.pallas_call(functools.partial(split_kernel, wo, ws, n), in_specs=[pl.B...  5.9 us
    ppermute x4, starting transfers between devices, cross(): return lax.ppermute(x, 'cls', [(i, i ^ 2) for i in range(n_cls)])  5.31 us
    pallas_call x1, Pallas kernels, body(): pl.pallas_call(functools.partial(stream_kernel, n, ori_rows, cycle), in_s...  5.17 us
    pallas_call x1, Pallas kernels, prep_images(): pl.pallas_call(functools.partial(rest_kernel, n, wo, ws), in_specs=[somew...  3.21 us
  transfers between devices with their start and end apart: 33, of which 18 were waited for; matrix products, arithmetic and copies ran while one was open for 0% of the time, Pallas kernels for 15%

profile of v4, /device:TPU:0, one launch (start us, length us, event | category | flops | bytes accessed | tf_op | source)
XLA Modules:
  0.0 124.5 jit_solution(4406908991109455561)
XLA Ops:
  0.6 2.0 %prep_own_plane.1 = (bf16[64,3200]{1,0:T(8,128)(2,1)}, f32[160,128]{1,0:T(8,128)}) custom-call(bf16[64,20480]{1,0:T(8,128)(2,1)} %img_hbm.3, s32[160,128]{1,0:T(8,128)} %bitcast.5, f32[1,100]{1,0:T(1,128)} %bitcast.7, s32[4,64]{1,0:T(4,128)} %bitcast.6), custom_call_target="tpu_custom_call" | custom-call | tf_op jit(solution)/shard_map/prep_own_plane/pallas_call | solution.py:105
  2.7 3.0 %collective-permute-start.1 = (bf16[64,3200]{1,0:T(8,128)(2,1)}, bf16[64,3200]{1,0:T(8,128)(2,1)S(1)}, u32[]{:S(2)}, u32[]{:S(2)}) collective-permute-start(bf16[64,3200]{1,0:T(8,128)(2,1)} %get-tuple-element.53.refs_0_), channel_id=1, source_target_pairs={{0,1},{2,0},{4,2},{6,4},{7,6},{5,7},{3,5},{1,3},{8,9},{10,8},{12,1... | collective-permute-start | bytes 1228808 | tf_op jit(solution)/shard_map/ppermute | solution.py:455
  5.7 0.1 collective-permute-start
  5.8 3.2 %prep_rest.1 = (bf16[64,3072]{1,0:T(8,128)(2,1)}, bf16[64,4096]{1,0:T(8,128)(2,1)}) custom-call(bf16[64,20480]{1,0:T(8,128)(2,1)} %img_hbm.3, f32[160,128]{1,0:T(8,128)} %get-tuple-element.54.w_ref), custom_call_target="tpu_custom_call" | custom-call | tf_op jit(solution)/shard_map/prep_rest/pallas_call | solution.py:120
  9.1 5.9 %split_projections.1 = (bf16[144,10368]{1,0:T(8,128)(2,1)}, bf16[144,10368]{1,0:T(8,128)(2,1)}) custom-call(bf16[1,144,20480]{2,1,0:T(8,128)(2,1)} %proj_hbm), custom_call_target="tpu_custom_call" | custom-call | bytes 11796480 | tf_op jit(solution)/shard_map/split_projections/pallas_call | solution.py:207
  15.0 0.0 copy-start
  15.0 0.0 copy-start.6
  15.0 0.4 collective-permute-done.1.refs_1_
  15.4 1.4 %collective-permute-done.refs_0_ = bf16[64,3200]{1,0:T(8,128)(2,1)S(1)} collective-permute-done((bf16[64,3200]{1,0:T(8,128)(2,1)}, bf16[64,3200]{1,0:T(8,128)(2,1)S(1)}, u32[]{:S(2)}, u32[]{:S(2)}) %collective-permute-start) | collective-permute-done | bytes 409632 | tf_op jit(solution)/shard_map/ppermute | solution.py:455
  16.8 0.0 collective-permute-start.5
  16.8 0.2 pack.4
  17.0 0.5 collective-permute-start.2
  17.5 1.6 %collective-permute-start.3 = (bf16[64,7296]{1,0:T(8,128)(2,1)S(1)}, bf16[64,7296]{1,0:T(8,128)(2,1)S(1)}, u32[]{:S(2)}, u32[]{:S(2)}) collective-permute-start(bf16[64,7296]{1,0:T(8,128)(2,1)S(1)} %get-tuple-element.61.refs_1_), channel_id=1, source_target_pairs={{0,1},{2,0},{4,2},{6,4},{7,6},{5,7},{3,5},{1,3},{8,9},{10,8},{12,1... | collective-permute-start | bytes 2801672 | tf_op jit(solution)/shard_map/ppermute | solution.py:455
  19.1 1.5 %collective-permute-start.4 = (bf16[128,3072]{1,0:T(8,128)(2,1)S(1)}, bf16[128,3072]{1,0:T(8,128)(2,1)S(1)}, u32[]{:S(2)}, u32[]{:S(2)}) collective-permute-start(bf16[128,3072]{1,0:T(8,128)(2,1)S(1)} %get-tuple-element.62), channel_id=1, source_target_pairs={{0,16},{8,24},{16,0},{24,8},{1,17},{9,25},{17,1},{25,9},{2,18},{10... | collective-permute-start | bytes 2359304 | tf_op jit(solution)/shard_map/ppermute | solution.py:461
  20.6 17.9 %collective-permute-done.4.refs_4_ = bf16[128,3072]{1,0:T(8,128)(2,1)S(1)} collective-permute-done((bf16[128,3072]{1,0:T(8,128)(2,1)S(1)}, bf16[128,3072]{1,0:T(8,128)(2,1)S(1)}, u32[]{:S(2)}, u32[]{:S(2)}) %collective-permute-start.4) | collective-permute-done | bytes 786464 | tf_op jit(solution)/shard_map/ppermute | solution.py:461
  38.5 1.7 %collective-permute-done.2.refs_0_.refs_2_ = bf16[64,7296]{1,0:T(8,128)(2,1)S(1)} collective-permute-done((bf16[64,7296]{1,0:T(8,128)(2,1)S(1)}, bf16[64,7296]{1,0:T(8,128)(2,1)S(1)}, u32[]{:S(2)}, u32[]{:S(2)}) %collective-permute-start.2) | collective-permute-done | bytes 933920 | tf_op jit(solution)/shard_map/ppermute | solution.py:455
  40.2 0.1 collective-permute-done.3.refs_1_.refs_3_
  40.3 1.7 %collective-permute-start.6 = (bf16[64,7296]{1,0:T(8,128)(2,1)S(1)}, bf16[64,7296]{1,0:T(8,128)(2,1)S(1)}, u32[]{:S(2)}, u32[]{:S(2)}) collective-permute-start(bf16[64,7296]{1,0:T(8,128)(2,1)S(1)} %collective-permute-done.2.refs_0_.refs_2_), channel_id=1, source_target_pairs={{0,2},{2,4},{4,6},{6,7},{7,5},{5,3},{3,1},{1,0},{8,10},{10,12},{12... | collective-permute-start | bytes 2801672 | tf_op jit(solution)/shard_map/ppermute | solution.py:455
  42.0 0.3 collective-permute-start.7
  42.3 0.1 pack.5
  42.4 1.7 %collective-permute-start.8 = (bf16[128,3072]{1,0:T(8,128)(2,1)S(1)}, bf16[128,3072]{1,0:T(8,128)(2,1)S(1)}, u32[]{:S(2)}, u32[]{:S(2)}) collective-permute-start(bf16[128,3072]{1,0:T(8,128)(2,1)S(1)} %pack.5), channel_id=1, source_target_pairs={{0,16},{8,24},{16,0},{24,8},{1,17},{9,25},{17,1},{25,9},{2,18},{10... | collective-permute-start | bytes 2359304 | tf_op jit(solution)/shard_map/ppermute | solution.py:461
  44.1 1.8 %copy-done.1 = bf16[144,10368]{1,0:T(8,128)(2,1)S(1)} copy-done((bf16[144,10368]{1,0:T(8,128)(2,1)S(1)}, bf16[144,10368]{1,0:T(8,128)(2,1)}, u32[]{:S(2)}) %copy-start.1) | copy-done | bytes 2986008
  45.9 2.2 %half_norms.1.bias_ref = f32[144,128]{1,0:T(8,128)S(1)} custom-call(bf16[144,10368]{1,0:T(8,128)(2,1)S(1)} %copy-done, bf16[144,10368]{1,0:T(8,128)(2,1)S(1)} %copy-done.1, f32[1,144]{1,0:T(1,128)S(1)} %copy-done.6, f32[160,128]{1,0:T(8,128)S(1)} %copy-done.5), custom_call_target="tpu_custom_call" | custom-call | flops 8847360 | bytes 5898240 | tf_op jit(solution)/shard_map/half_norms/pallas_call | solution.py:217
  48.1 1.7 %group_scores.4 = (f32[288,128]{1,0:T(8,128)S(1)}, bf16[128,1280]{1,0:T(8,128)(2,1)S(1)}) custom-call(bf16[144,10368]{1,0:T(8,128)(2,1)S(1)} %copy-done, bf16[144,10368]{1,0:T(8,128)(2,1)S(1)} %collective-permute-done.5.mate_ref, f32[144,128]{1,0:T(8,128)S(1)} %half_norms.1.bias_ref, bf16[64,7296]{1,0:T(8,128)(2,1)S(1)} %get-tuple-element.60.refs_0_, ...), custom_call_target="tpu_custom_call" | custom-call | flops 764411904 | bytes 8626176 | tf_op jit(solution)/shard_map/group_scores/pallas_call | solution.py:301
  49.9 11.1 %collective-permute-done.8.refs_4_ = bf16[128,3072]{1,0:T(8,128)(2,1)S(1)} collective-permute-done((bf16[128,3072]{1,0:T(8,128)(2,1)S(1)}, bf16[128,3072]{1,0:T(8,128)(2,1)S(1)}, u32[]{:S(2)}, u32[]{:S(2)}) %collective-permute-start.8) | collective-permute-done | bytes 786464 | tf_op jit(solution)/shard_map/ppermute | solution.py:461
  61.0 1.6 %collective-permute-done.6.refs_0_.refs_2_ = bf16[64,7296]{1,0:T(8,128)(2,1)S(1)} collective-permute-done((bf16[64,7296]{1,0:T(8,128)(2,1)S(1)}, bf16[64,7296]{1,0:T(8,128)(2,1)S(1)}, u32[]{:S(2)}, u32[]{:S(2)}) %collective-permute-start.6) | collective-permute-done | bytes 933920 | tf_op jit(solution)/shard_map/ppermute | solution.py:455
  62.5 1.2 collective-permute-done.7.refs_1_.refs_3_
  63.7 0.1 pack.6
  63.9 1.6 %collective-permute-start.13 = (bf16[128,3072]{1,0:T(8,128)(2,1)S(1)}, bf16[128,3072]{1,0:T(8,128)(2,1)S(1)}, u32[]{:S(2)}, u32[]{:S(2)}) collective-permute-start(bf16[128,3072]{1,0:T(8,128)(2,1)S(1)} %get-tuple-element.76), channel_id=1, source_target_pairs={{0,16},{8,24},{16,0},{24,8},{1,17},{9,25},{17,1},{25,9},{2,18},{10... | collective-permute-start | bytes 2359304 | tf_op jit(solution)/shard_map/ppermute | solution.py:461
  65.4 1.6 %collective-permute-start.11 = (bf16[64,4096]{1,0:T(8,128)(2,1)S(1)}, bf16[64,4096]{1,0:T(8,128)(2,1)S(1)}, u32[]{:S(2)}, u32[]{:S(2)}) collective-permute-start(bf16[64,4096]{1,0:T(8,128)(2,1)S(1)} %get-tuple-element.74), channel_id=1, source_target_pairs={{0,2},{2,4},{4,6},{6,7},{7,5},{5,3},{3,1},{1,0},{8,10},{10,12},{12... | collective-permute-start | bytes 1572872 | tf_op jit(solution)/shard_map/ppermute | solution.py:455
  67.0 0.4 collective-permute-start.12
  67.5 1.6 %collective-permute-start.9 = (bf16[32,3200]{1,0:T(8,128)(2,1)S(1)}, bf16[32,3200]{1,0:T(8,128)(2,1)S(1)}, u32[]{:S(2)}, u32[]{:S(2)}) collective-permute-start(bf16[32,3200]{1,0:T(8,128)(2,1)S(1)} %get-tuple-element.72), channel_id=1, source_target_pairs={{0,2},{2,4},{4,6},{6,7},{7,5},{5,3},{3,1},{1,0},{8,10},{10,12},{12... | collective-permute-start | bytes 614408 | tf_op jit(solution)/shard_map/ppermute | solution.py:455
  69.0 0.4 collective-permute-start.10
  69.5 1.7 %group_scores.5 = (f32[288,128]{1,0:T(8,128)S(1)}, bf16[128,1280]{1,0:T(8,128)(2,1)S(1)}) custom-call(bf16[144,10368]{1,0:T(8,128)(2,1)S(1)} %copy-done, bf16[144,10368]{1,0:T(8,128)(2,1)S(1)} %collective-permute-done.5.mate_ref, f32[144,128]{1,0:T(8,128)S(1)} %half_norms.1.bias_ref, bf16[64,7296]{1,0:T(8,128)(2,1)S(1)} %collective-permute-done.2.refs_0_.refs_2_, ...), custom_call_target="tpu_custom_call" | custom-call | flops 764411904 | bytes 8626176 | tf_op jit(solution)/shard_map/group_scores/pallas_call | solution.py:301
  71.2 10.3 %collective-permute-done.9.refs_0_.refs_1_ = bf16[32,3200]{1,0:T(8,128)(2,1)S(1)} collective-permute-done((bf16[32,3200]{1,0:T(8,128)(2,1)S(1)}, bf16[32,3200]{1,0:T(8,128)(2,1)S(1)}, u32[]{:S(2)}, u32[]{:S(2)}) %collective-permute-start.9) | collective-permute-done | bytes 204832 | tf_op jit(solution)/shard_map/ppermute | solution.py:455
  81.6 1.3 %collective-permute-done.10.refs_1_.refs_2_ = bf16[32,3200]{1,0:T(8,128)(2,1)S(1)} collective-permute-done((bf16[32,3200]{1,0:T(8,128)(2,1)S(1)}, bf16[32,3200]{1,0:T(8,128)(2,1)S(1)}, u32[]{:S(2)}, u32[]{:S(2)}) %collective-permute-start.10) | collective-permute-done | bytes 204832 | tf_op jit(solution)/shard_map/ppermute | solution.py:455
  82.9 0.6 collective-permute-start.16
  83.6 1.6 %collective-permute-start.14 = (bf16[32,4096]{1,0:T(8,128)(2,1)S(1)}, bf16[32,4096]{1,0:T(8,128)(2,1)S(1)}, u32[]{:S(2)}, u32[]{:S(2)}) collective-permute-start(bf16[32,4096]{1,0:T(8,128)(2,1)S(1)} %slice.6), channel_id=1, source_target_pairs={{0,2},{2,4},{4,6},{6,7},{7,5},{5,3},{3,1},{1,0},{8,10},{10,12},{12... | collective-permute-start | bytes 786440 | tf_op jit(solution)/shard_map/ppermute | solution.py:455
  85.2 0.5 collective-permute-start.15
  85.7 1.8 %group_scores.7 = (f32[288,128]{1,0:T(8,128)S(1)}, bf16[128,1280]{1,0:T(8,128)(2,1)S(1)}) custom-call(bf16[144,10368]{1,0:T(8,128)(2,1)S(1)} %copy-done, bf16[144,10368]{1,0:T(8,128)(2,1)S(1)} %collective-permute-done.5.mate_ref, f32[144,128]{1,0:T(8,128)S(1)} %half_norms.1.bias_ref, bf16[64,7296]{1,0:T(8,128)(2,1)S(1)} %collective-permute-done.6.refs_0_.refs_2_, ...), custom_call_target="tpu_custom_call" | custom-call | flops 764411904 | bytes 8626176 | tf_op jit(solution)/shard_map/group_scores/pallas_call | solution.py:301
  87.5 0.6 collective-permute-start.20
  88.1 1.9 %collective-permute-done.14.refs_4_ = bf16[32,4096]{1,0:T(8,128)(2,1)S(1)} collective-permute-done((bf16[32,4096]{1,0:T(8,128)(2,1)S(1)}, bf16[32,4096]{1,0:T(8,128)(2,1)S(1)}, u32[]{:S(2)}, u32[]{:S(2)}) %collective-permute-start.14) | collective-permute-done | bytes 262176 | tf_op jit(solution)/shard_map/ppermute | solution.py:455
  90.0 1.7 %collective-permute-done.15.refs_5_ = bf16[32,4096]{1,0:T(8,128)(2,1)S(1)} collective-permute-done((bf16[32,4096]{1,0:T(8,128)(2,1)S(1)}, bf16[32,4096]{1,0:T(8,128)(2,1)S(1)}, u32[]{:S(2)}, u32[]{:S(2)}) %collective-permute-start.15) | collective-permute-done | bytes 262176 | tf_op jit(solution)/shard_map/ppermute | solution.py:455
  91.7 1.7 %group_scores.6 = (f32[288,128]{1,0:T(8,128)S(1)}, bf16[128,1280]{1,0:T(8,128)(2,1)S(1)}) custom-call(bf16[144,10368]{1,0:T(8,128)(2,1)S(1)} %copy-done, bf16[144,10368]{1,0:T(8,128)(2,1)S(1)} %collective-permute-done.5.mate_ref, f32[144,128]{1,0:T(8,128)S(1)} %half_norms.1.bias_ref, bf16[64,3200]{1,0:T(8,128)(2,1)S(1)} %copy-done.3, ...), custom_call_target="tpu_custom_call" | custom-call | flops 764411904 | bytes 8626176 | tf_op jit(solution)/shard_map/group_scores/pallas_call | solution.py:301
  93.4 0.1 collective-permute-start.17
  93.5 0.5 collective-permute-start.30
  94.0 0.8 collective-permute-done.17.refs_4_
  94.8 0.3 local_stats.1
  95.1 1.5 %collective-permute-start.21 = (f32[8,512]{1,0:T(8,128)S(1)}, f32[8,512]{1,0:T(8,128)S(1)}, u32[]{:S(2)}, u32[]{:S(2)}) collective-permute-start(f32[8,512]{1,0:T(8,128)S(1)} %get-tuple-element.91.refs_0_), channel_id=1, source_target_pairs={{0,16},{8,24},{16,0},{24,8},{1,17},{9,25},{17,1},{25,9},{2,18},{10... | collective-permute-start | bytes 49160 | tf_op jit(solution)/shard_map/ppermute | solution.py:533
  96.7 2.2 %collective-permute-done.21.refs_1_ = f32[8,512]{1,0:T(8,128)S(1)} collective-permute-done((f32[8,512]{1,0:T(8,128)S(1)}, f32[8,512]{1,0:T(8,128)S(1)}, u32[]{:S(2)}, u32[]{:S(2)}) %collective-permute-start.21) | collective-permute-done | bytes 16416 | tf_op jit(solution)/shard_map/ppermute | solution.py:533
  98.9 0.1 payload.1.refs_0_
  99.0 0.5 collective-permute-start.26
  99.5 1.6 %collective-permute-start.22 = (bf16[160,512]{1,0:T(8,128)(2,1)S(1)}, bf16[160,512]{1,0:T(8,128)(2,1)S(1)}, u32[]{:S(2)}, u32[]{:S(2)}) collective-permute-start(bf16[160,512]{1,0:T(8,128)(2,1)S(1)} %payload.1.refs_0_), channel_id=1, source_target_pairs={{0,2},{2,4},{4,6},{6,7},{7,5},{5,3},{3,1},{1,0},{8,10},{10,12},{12... | collective-permute-start | bytes 491528 | tf_op jit(solution)/shard_map/ppermute | solution.py:455
  101.1 0.5 collective-permute-start.29
  101.6 2.8 %collective-permute-done.26.refs_7_ = bf16[160,512]{1,0:T(8,128)(2,1)S(1)} collective-permute-done((bf16[160,512]{1,0:T(8,128)(2,1)S(1)}, bf16[160,512]{1,0:T(8,128)(2,1)S(1)}, u32[]{:S(2)}, u32[]{:S(2)}) %collective-permute-start.26) | collective-permute-done | bytes 163872 | tf_op jit(solution)/shard_map/ppermute | solution.py:455
  104.3 0.5 collective-permute-start.27
  104.8 1.6 %collective-permute-start.23 = (bf16[160,512]{1,0:T(8,128)(2,1)S(1)}, bf16[160,512]{1,0:T(8,128)(2,1)S(1)}, u32[]{:S(2)}, u32[]{:S(2)}) collective-permute-start(bf16[160,512]{1,0:T(8,128)(2,1)S(1)} %collective-permute-done.22.refs_1_), channel_id=1, source_target_pairs={{0,2},{2,4},{4,6},{6,7},{7,5},{5,3},{3,1},{1,0},{8,10},{10,12},{12... | collective-permute-start | bytes 491528 | tf_op jit(solution)/shard_map/ppermute | solution.py:455
  106.4 2.4 %collective-permute-start.25 = (bf16[160,512]{1,0:T(8,128)(2,1)S(1)}, bf16[160,512]{1,0:T(8,128)(2,1)S(1)}, u32[]{:S(2)}, u32[]{:S(2)}) collective-permute-start(bf16[160,512]{1,0:T(8,128)(2,1)S(1)} %payload.1.refs_0_), channel_id=1, source_target_pairs={{0,7},{2,5},{4,3},{6,1},{7,0},{5,2},{3,4},{1,6},{8,15},{10,13},{12... | collective-permute-start | bytes 491528 | tf_op jit(solution)/shard_map/ppermute | solution.py:455
  108.8 4.0 %collective-permute-done.27.refs_6_ = bf16[160,512]{1,0:T(8,128)(2,1)S(1)} collective-permute-done((bf16[160,512]{1,0:T(8,128)(2,1)S(1)}, bf16[160,512]{1,0:T(8,128)(2,1)S(1)}, u32[]{:S(2)}, u32[]{:S(2)}) %collective-permute-start.27) | collective-permute-done | bytes 163872 | tf_op jit(solution)/shard_map/ppermute | solution.py:455
  112.7 0.0 collective-permute-start.28
  112.8 3.2 %collective-permute-start.24 = (bf16[160,512]{1,0:T(8,128)(2,1)S(1)}, bf16[160,512]{1,0:T(8,128)(2,1)S(1)}, u32[]{:S(2)}, u32[]{:S(2)}) collective-permute-start(bf16[160,512]{1,0:T(8,128)(2,1)S(1)} %collective-permute-done.23.refs_2_), channel_id=1, source_target_pairs={{0,2},{2,4},{4,6},{6,7},{7,5},{5,3},{3,1},{1,0},{8,10},{10,12},{12... | collective-permute-start | bytes 491528 | tf_op jit(solution)/shard_map/ppermute | solution.py:455
  115.9 0.5 collective-permute-done.25.refs_4_
  116.4 2.8 %collective-permute-done.28.refs_5_ = bf16[160,512]{1,0:T(8,128)(2,1)S(1)} collective-permute-done((bf16[160,512]{1,0:T(8,128)(2,1)S(1)}, bf16[160,512]{1,0:T(8,128)(2,1)S(1)}, u32[]{:S(2)}, u32[]{:S(2)}) %collective-permute-start.28) | collective-permute-done | bytes 163872 | tf_op jit(solution)/shard_map/ppermute | solution.py:455
  119.2 5.2 %class_sums.1 = (bf16[1152,2560]{1,0:T(8,128)(2,1)}, f32[1,64]{1,0:T(1,128)}) custom-call(bf16[160,512]{1,0:T(8,128)(2,1)S(1)} %payload.1.refs_0_, bf16[160,512]{1,0:T(8,128)(2,1)S(1)} %collective-permute-done.22.refs_1_, bf16[160,512]{1,0:T(8,128)(2,1)S(1)} %collective-permute-done.23.refs_2_, bf16[160,512]{1,0:T(8,128)(2,1)S(1)} %collective-permute-done.24.refs_3_, ...), custom_call_target="tpu_custom_call" | custom-call | tf_op jit(solution)/shard_map/class_sums/pallas_call | solution.py:554
  (33 shorter events, 0.1 us)
Async XLA Ops:
  2.7 12.8 %collective-permute-start.1 = (bf16[64,3200]{1,0:T(8,128)(2,1)}, bf16[64,3200]{1,0:T(8,128)(2,1)S(1)}, u32[]{:S(2)}, u32[]{:S(2)}) collective-permute-start(bf16[64,3200]{1,0:T(8,128)(2,1)} %get-tuple-element.53.refs_0_), channel_id=1, source_target_pairs={{0,1},{2,0},{4,2},{6,4},{7,6},{5,7},{3,5},{1,3},{8,9},{10,8},{12,1... | collective-permute-start | bytes 1228808 | tf_op jit(solution)/shard_map/ppermute | solution.py:455
  5.7 11.1 %collective-permute-start = (bf16[64,3200]{1,0:T(8,128)(2,1)}, bf16[64,3200]{1,0:T(8,128)(2,1)S(1)}, u32[]{:S(2)}, u32[]{:S(2)}) collective-permute-start(bf16[64,3200]{1,0:T(8,128)(2,1)} %get-tuple-element.53.refs_0_), channel_id=1, source_target_pairs={{0,2},{2,4},{4,6},{6,7},{7,5},{5,3},{3,1},{1,0},{8,10},{10,12},{12... | collective-permute-start | bytes 1228808 | tf_op jit(solution)/shard_map/ppermute | solution.py:455
  9.0 7.8 %copy-start.2 = (bf16[64,4096]{1,0:T(8,128)(2,1)S(1)}, bf16[64,4096]{1,0:T(8,128)(2,1)}, u32[]{:S(2)}) copy-start(bf16[64,4096]{1,0:T(8,128)(2,1)} %get-tuple-element.59.refs_2_.refs_3_) | copy-start | bytes 1572868
  15.0 29.1 %copy-start = (bf16[144,10368]{1,0:T(8,128)(2,1)S(1)}, bf16[144,10368]{1,0:T(8,128)(2,1)}, u32[]{:S(2)}) copy-start(bf16[144,10368]{1,0:T(8,128)(2,1)} %get-tuple-element.52.keep_ref.own_ref) | copy-start | bytes 8957956
  15.0 29.1 %copy-start.5 = (f32[160,128]{1,0:T(8,128)S(1)}, f32[160,128]{1,0:T(8,128)}, u32[]{:S(2)}) copy-start(f32[160,128]{1,0:T(8,128)} %get-tuple-element.54.w_ref) | copy-start | bytes 245764
  15.0 29.1 %copy-start.6 = (f32[1,144]{1,0:T(1,128)S(1)}, f32[1,144]{1,0:T(1,128)}, u32[]{:S(2)}) copy-start(f32[1,144]{1,0:T(1,128)} %prior_ref.1) | copy-start | bytes 1732
  16.8 23.5 %collective-permute-start.5 = (bf16[144,10368]{1,0:T(8,128)(2,1)}, bf16[144,10368]{1,0:T(8,128)(2,1)S(1)}, u32[]{:S(2)}, u32[]{:S(2)}) collective-permute-start(bf16[144,10368]{1,0:T(8,128)(2,1)} %get-tuple-element.63.send_ref), channel_id=1, source_target_pairs={{0,8},{8,0},{16,24},{24,16},{1,9},{9,1},{17,25},{25,17},{2,10},{10... | collective-permute-start | bytes 8957960 | tf_op jit(solution)/shard_map/ppermute | solution.py:458
  17.0 23.2 %collective-permute-start.2 = (bf16[64,7296]{1,0:T(8,128)(2,1)S(1)}, bf16[64,7296]{1,0:T(8,128)(2,1)S(1)}, u32[]{:S(2)}, u32[]{:S(2)}) collective-permute-start(bf16[64,7296]{1,0:T(8,128)(2,1)S(1)} %get-tuple-element.60.refs_0_), channel_id=1, source_target_pairs={{0,2},{2,4},{4,6},{6,7},{7,5},{5,3},{3,1},{1,0},{8,10},{10,12},{12... | collective-permute-start | bytes 2801672 | tf_op jit(solution)/shard_map/ppermute | solution.py:455
  17.5 22.8 %collective-permute-start.3 = (bf16[64,7296]{1,0:T(8,128)(2,1)S(1)}, bf16[64,7296]{1,0:T(8,128)(2,1)S(1)}, u32[]{:S(2)}, u32[]{:S(2)}) collective-permute-start(bf16[64,7296]{1,0:T(8,128)(2,1)S(1)} %get-tuple-element.61.refs_1_), channel_id=1, source_target_pairs={{0,1},{2,0},{4,2},{6,4},{7,6},{5,7},{3,5},{1,3},{8,9},{10,8},{12,1... | collective-permute-start | bytes 2801672 | tf_op jit(solution)/shard_map/ppermute | solution.py:455
  19.1 19.4 %collective-permute-start.4 = (bf16[128,3072]{1,0:T(8,128)(2,1)S(1)}, bf16[128,3072]{1,0:T(8,128)(2,1)S(1)}, u32[]{:S(2)}, u32[]{:S(2)}) collective-permute-start(bf16[128,3072]{1,0:T(8,128)(2,1)S(1)} %get-tuple-element.62), channel_id=1, source_target_pairs={{0,16},{8,24},{16,0},{24,8},{1,17},{9,25},{17,1},{25,9},{2,18},{10... | collective-permute-start | bytes 2359304 | tf_op jit(solution)/shard_map/ppermute | solution.py:461
  40.3 22.2 %collective-permute-start.6 = (bf16[64,7296]{1,0:T(8,128)(2,1)S(1)}, bf16[64,7296]{1,0:T(8,128)(2,1)S(1)}, u32[]{:S(2)}, u32[]{:S(2)}) collective-permute-start(bf16[64,7296]{1,0:T(8,128)(2,1)S(1)} %collective-permute-done.2.refs_0_.refs_2_), channel_id=1, source_target_pairs={{0,2},{2,4},{4,6},{6,7},{7,5},{5,3},{3,1},{1,0},{8,10},{10,12},{12... | collective-permute-start | bytes 2801672 | tf_op jit(solution)/shard_map/ppermute | solution.py:455
  42.0 21.7 %collective-permute-start.7 = (bf16[64,7296]{1,0:T(8,128)(2,1)S(1)}, bf16[64,7296]{1,0:T(8,128)(2,1)S(1)}, u32[]{:S(2)}, u32[]{:S(2)}) collective-permute-start(bf16[64,7296]{1,0:T(8,128)(2,1)S(1)} %collective-permute-done.3.refs_1_.refs_3_), channel_id=1, source_target_pairs={{0,1},{2,0},{4,2},{6,4},{7,6},{5,7},{3,5},{1,3},{8,9},{10,8},{12,1... | collective-permute-start | bytes 2801672 | tf_op jit(solution)/shard_map/ppermute | solution.py:455
  42.4 18.6 %collective-permute-start.8 = (bf16[128,3072]{1,0:T(8,128)(2,1)S(1)}, bf16[128,3072]{1,0:T(8,128)(2,1)S(1)}, u32[]{:S(2)}, u32[]{:S(2)}) collective-permute-start(bf16[128,3072]{1,0:T(8,128)(2,1)S(1)} %pack.5), channel_id=1, source_target_pairs={{0,16},{8,24},{16,0},{24,8},{1,17},{9,25},{17,1},{25,9},{2,18},{10... | collective-permute-start | bytes 2359304 | tf_op jit(solution)/shard_map/ppermute | solution.py:461
  44.1 1.8 %copy-start.1 = (bf16[144,10368]{1,0:T(8,128)(2,1)S(1)}, bf16[144,10368]{1,0:T(8,128)(2,1)}, u32[]{:S(2)}) copy-start(bf16[144,10368]{1,0:T(8,128)(2,1)} %get-tuple-element.63.send_ref) | copy-start | bytes 8957956
  63.9 19.0 %collective-permute-start.13 = (bf16[128,3072]{1,0:T(8,128)(2,1)S(1)}, bf16[128,3072]{1,0:T(8,128)(2,1)S(1)}, u32[]{:S(2)}, u32[]{:S(2)}) collective-permute-start(bf16[128,3072]{1,0:T(8,128)(2,1)S(1)} %get-tuple-element.76), channel_id=1, source_target_pairs={{0,16},{8,24},{16,0},{24,8},{1,17},{9,25},{17,1},{25,9},{2,18},{10... | collective-permute-start | bytes 2359304 | tf_op jit(solution)/shard_map/ppermute | solution.py:461
  65.4 17.4 %collective-permute-start.11 = (bf16[64,4096]{1,0:T(8,128)(2,1)S(1)}, bf16[64,4096]{1,0:T(8,128)(2,1)S(1)}, u32[]{:S(2)}, u32[]{:S(2)}) collective-permute-start(bf16[64,4096]{1,0:T(8,128)(2,1)S(1)} %get-tuple-element.74), channel_id=1, source_target_pairs={{0,2},{2,4},{4,6},{6,7},{7,5},{5,3},{3,1},{1,0},{8,10},{10,12},{12... | collective-permute-start | bytes 1572872 | tf_op jit(solution)/shard_map/ppermute | solution.py:455
  67.0 15.9 %collective-permute-start.12 = (bf16[64,4096]{1,0:T(8,128)(2,1)S(1)}, bf16[64,4096]{1,0:T(8,128)(2,1)S(1)}, u32[]{:S(2)}, u32[]{:S(2)}) collective-permute-start(bf16[64,4096]{1,0:T(8,128)(2,1)S(1)} %get-tuple-element.75), channel_id=1, source_target_pairs={{0,1},{2,0},{4,2},{6,4},{7,6},{5,7},{3,5},{1,3},{8,9},{10,8},{12,1... | collective-permute-start | bytes 1572872 | tf_op jit(solution)/shard_map/ppermute | solution.py:455
  67.5 14.1 %collective-permute-start.9 = (bf16[32,3200]{1,0:T(8,128)(2,1)S(1)}, bf16[32,3200]{1,0:T(8,128)(2,1)S(1)}, u32[]{:S(2)}, u32[]{:S(2)}) collective-permute-start(bf16[32,3200]{1,0:T(8,128)(2,1)S(1)} %get-tuple-element.72), channel_id=1, source_target_pairs={{0,2},{2,4},{4,6},{6,7},{7,5},{5,3},{3,1},{1,0},{8,10},{10,12},{12... | collective-permute-start | bytes 614408 | tf_op jit(solution)/shard_map/ppermute | solution.py:455
  69.0 13.8 %collective-permute-start.10 = (bf16[32,3200]{1,0:T(8,128)(2,1)S(1)}, bf16[32,3200]{1,0:T(8,128)(2,1)S(1)}, u32[]{:S(2)}, u32[]{:S(2)}) collective-permute-start(bf16[32,3200]{1,0:T(8,128)(2,1)S(1)} %get-tuple-element.73), channel_id=1, source_target_pairs={{0,1},{2,0},{4,2},{6,4},{7,6},{5,7},{3,5},{1,3},{8,9},{10,8},{12,1... | collective-permute-start | bytes 614408 | tf_op jit(solution)/shard_map/ppermute | solution.py:455
  82.9 8.7 %collective-permute-start.16 = (bf16[64,3072]{1,0:T(8,128)(2,1)S(1)}, bf16[64,3072]{1,0:T(8,128)(2,1)S(1)}, u32[]{:S(2)}, u32[]{:S(2)}) collective-permute-start(bf16[64,3072]{1,0:T(8,128)(2,1)S(1)} %pack.7), channel_id=1, source_target_pairs={{0,16},{8,24},{16,0},{24,8},{1,17},{9,25},{17,1},{25,9},{2,18},{10... | collective-permute-start | bytes 1179656 | tf_op jit(solution)/shard_map/ppermute | solution.py:461
  83.6 6.4 %collective-permute-start.14 = (bf16[32,4096]{1,0:T(8,128)(2,1)S(1)}, bf16[32,4096]{1,0:T(8,128)(2,1)S(1)}, u32[]{:S(2)}, u32[]{:S(2)}) collective-permute-start(bf16[32,4096]{1,0:T(8,128)(2,1)S(1)} %slice.6), channel_id=1, source_target_pairs={{0,2},{2,4},{4,6},{6,7},{7,5},{5,3},{3,1},{1,0},{8,10},{10,12},{12... | collective-permute-start | bytes 786440 | tf_op jit(solution)/shard_map/ppermute | solution.py:455
  85.2 6.5 %copy-start.3 = (bf16[64,3200]{1,0:T(8,128)(2,1)S(1)}, bf16[64,3200]{1,0:T(8,128)(2,1)}, u32[]{:S(2)}) copy-start(bf16[64,3200]{1,0:T(8,128)(2,1)} %get-tuple-element.53.refs_0_) | copy-start | bytes 1228804
  85.2 6.4 %copy-start.4 = (bf16[64,3072]{1,0:T(8,128)(2,1)S(1)}, bf16[64,3072]{1,0:T(8,128)(2,1)}, u32[]{:S(2)}) copy-start(bf16[64,3072]{1,0:T(8,128)(2,1)} %get-tuple-element.84.refs_6_) | copy-start | bytes 1179652
  85.2 6.4 %collective-permute-start.15 = (bf16[32,4096]{1,0:T(8,128)(2,1)S(1)}, bf16[32,4096]{1,0:T(8,128)(2,1)S(1)}, u32[]{:S(2)}, u32[]{:S(2)}) collective-permute-start(bf16[32,4096]{1,0:T(8,128)(2,1)S(1)} %slice.7), channel_id=1, source_target_pairs={{0,1},{2,0},{4,2},{6,4},{7,6},{5,7},{3,5},{1,3},{8,9},{10,8},{12,1... | collective-permute-start | bytes 786440 | tf_op jit(solution)/shard_map/ppermute | solution.py:455
  85.7 8.3 %collective-permute-start.18 = (f32[288,128]{1,0:T(8,128)S(1)}, f32[288,128]{1,0:T(8,128)S(1)}, u32[]{:S(2)}, u32[]{:S(2)}) collective-permute-start(f32[288,128]{1,0:T(8,128)S(1)} %get-tuple-element.86.refs_1_), channel_id=1, source_target_pairs={{0,8},{8,0},{16,24},{24,16},{1,9},{9,1},{17,25},{25,17},{2,10},{10... | collective-permute-start | bytes 442376 | tf_op jit(solution)/shard_map/ppermute | solution.py:458
  87.5 6.5 %collective-permute-start.20 = (f32[288,128]{1,0:T(8,128)S(1)}, f32[288,128]{1,0:T(8,128)S(1)}, u32[]{:S(2)}, u32[]{:S(2)}) collective-permute-start(f32[288,128]{1,0:T(8,128)S(1)} %get-tuple-element.89.refs_3_), channel_id=1, source_target_pairs={{0,8},{8,0},{16,24},{24,16},{1,9},{9,1},{17,25},{25,17},{2,10},{10... | collective-permute-start | bytes 442376 | tf_op jit(solution)/shard_map/ppermute | solution.py:458
  90.0 4.0 %collective-permute-start.19 = (f32[288,128]{1,0:T(8,128)S(1)}, f32[288,128]{1,0:T(8,128)S(1)}, u32[]{:S(2)}, u32[]{:S(2)}) collective-permute-start(f32[288,128]{1,0:T(8,128)S(1)} %get-tuple-element.87.refs_2_), channel_id=1, source_target_pairs={{0,8},{8,0},{16,24},{24,16},{1,9},{9,1},{17,25},{25,17},{2,10},{10... | collective-permute-start | bytes 442376 | tf_op jit(solution)/shard_map/ppermute | solution.py:458
  93.4 1.4 %collective-permute-start.17 = (f32[288,128]{1,0:T(8,128)S(1)}, f32[288,128]{1,0:T(8,128)S(1)}, u32[]{:S(2)}, u32[]{:S(2)}) collective-permute-start(f32[288,128]{1,0:T(8,128)S(1)} %get-tuple-element.85.refs_0_), channel_id=1, source_target_pairs={{0,8},{8,0},{16,24},{24,16},{1,9},{9,1},{17,25},{25,17},{2,10},{10... | collective-permute-start | bytes 442376 | tf_op jit(solution)/shard_map/ppermute | solution.py:458
  93.5 7.6 %collective-permute-start.30 = (bf16[128,1280]{1,0:T(8,128)(2,1)S(1)}, bf16[128,1280]{1,0:T(8,128)(2,1)S(1)}, u32[]{:S(2)}, u32[]{:S(2)}) collective-permute-start(bf16[128,1280]{1,0:T(8,128)(2,1)S(1)} %get-tuple-element.93.refs_9_), channel_id=1, source_target_pairs={{0,8},{8,0},{16,24},{24,16},{1,9},{9,1},{17,25},{25,17},{2,10},{10... | collective-permute-start | bytes 983048 | tf_op jit(solution)/shard_map/ppermute | solution.py:458
  95.1 3.8 %collective-permute-start.21 = (f32[8,512]{1,0:T(8,128)S(1)}, f32[8,512]{1,0:T(8,128)S(1)}, u32[]{:S(2)}, u32[]{:S(2)}) collective-permute-start(f32[8,512]{1,0:T(8,128)S(1)} %get-tuple-element.91.refs_0_), channel_id=1, source_target_pairs={{0,16},{8,24},{16,0},{24,8},{1,17},{9,25},{17,1},{25,9},{2,18},{10... | collective-permute-start | bytes 49160 | tf_op jit(solution)/shard_map/ppermute | solution.py:533
  96.7 9.7 %collective-permute-start.32 = (bf16[128,1280]{1,0:T(8,128)(2,1)S(1)}, bf16[128,1280]{1,0:T(8,128)(2,1)S(1)}, u32[]{:S(2)}, u32[]{:S(2)}) collective-permute-start(bf16[128,1280]{1,0:T(8,128)(2,1)S(1)} %get-tuple-element.95.refs_11_), channel_id=1, source_target_pairs={{0,8},{8,0},{16,24},{24,16},{1,9},{9,1},{17,25},{25,17},{2,10},{10... | collective-permute-start | bytes 983048 | tf_op jit(solution)/shard_map/ppermute | solution.py:458
  99.0 5.4 %collective-permute-start.26 = (bf16[160,512]{1,0:T(8,128)(2,1)S(1)}, bf16[160,512]{1,0:T(8,128)(2,1)S(1)}, u32[]{:S(2)}, u32[]{:S(2)}) collective-permute-start(bf16[160,512]{1,0:T(8,128)(2,1)S(1)} %payload.1.refs_0_), channel_id=1, source_target_pairs={{0,1},{2,0},{4,2},{6,4},{7,6},{5,7},{3,5},{1,3},{8,9},{10,8},{12,1... | collective-permute-start | bytes 491528 | tf_op jit(solution)/shard_map/ppermute | solution.py:455
  99.5 5.3 %collective-permute-start.22 = (bf16[160,512]{1,0:T(8,128)(2,1)S(1)}, bf16[160,512]{1,0:T(8,128)(2,1)S(1)}, u32[]{:S(2)}, u32[]{:S(2)}) collective-permute-start(bf16[160,512]{1,0:T(8,128)(2,1)S(1)} %payload.1.refs_0_), channel_id=1, source_target_pairs={{0,2},{2,4},{4,6},{6,7},{7,5},{5,3},{3,1},{1,0},{8,10},{10,12},{12... | collective-permute-start | bytes 491528 | tf_op jit(solution)/shard_map/ppermute | solution.py:455
  101.0 14.9 %collective-permute-start.31 = (bf16[128,1280]{1,0:T(8,128)(2,1)S(1)}, bf16[128,1280]{1,0:T(8,128)(2,1)S(1)}, u32[]{:S(2)}, u32[]{:S(2)}) collective-permute-start(bf16[128,1280]{1,0:T(8,128)(2,1)S(1)} %get-tuple-element.94.refs_10_), channel_id=1, source_target_pairs={{0,8},{8,0},{16,24},{24,16},{1,9},{9,1},{17,25},{25,17},{2,10},{10... | collective-permute-start | bytes 983048 | tf_op jit(solution)/shard_map/ppermute | solution.py:458
  101.1 15.4 %collective-permute-start.29 = (bf16[128,1280]{1,0:T(8,128)(2,1)S(1)}, bf16[128,1280]{1,0:T(8,128)(2,1)S(1)}, u32[]{:S(2)}, u32[]{:S(2)}) collective-permute-start(bf16[128,1280]{1,0:T(8,128)(2,1)S(1)} %get-tuple-element.92.refs_8_), channel_id=1, source_target_pairs={{0,8},{8,0},{16,24},{24,16},{1,9},{9,1},{17,25},{25,17},{2,10},{10... | collective-permute-start | bytes 983048 | tf_op jit(solution)/shard_map/ppermute | solution.py:458
  104.3 8.4 %collective-permute-start.27 = (bf16[160,512]{1,0:T(8,128)(2,1)S(1)}, bf16[160,512]{1,0:T(8,128)(2,1)S(1)}, u32[]{:S(2)}, u32[]{:S(2)}) collective-permute-start(bf16[160,512]{1,0:T(8,128)(2,1)S(1)} %collective-permute-done.26.refs_7_), channel_id=1, source_target_pairs={{0,1},{2,0},{4,2},{6,4},{7,6},{5,7},{3,5},{1,3},{8,9},{10,8},{12,1... | collective-permute-start | bytes 491528 | tf_op jit(solution)/shard_map/ppermute | solution.py:455
  104.8 8.0 %collective-permute-start.23 = (bf16[160,512]{1,0:T(8,128)(2,1)S(1)}, bf16[160,512]{1,0:T(8,128)(2,1)S(1)}, u32[]{:S(2)}, u32[]{:S(2)}) collective-permute-start(bf16[160,512]{1,0:T(8,128)(2,1)S(1)} %collective-permute-done.22.refs_1_), channel_id=1, source_target_pairs={{0,2},{2,4},{4,6},{6,7},{7,5},{5,3},{3,1},{1,0},{8,10},{10,12},{12... | collective-permute-start | bytes 491528 | tf_op jit(solution)/shard_map/ppermute | solution.py:455
  106.4 10.0 %collective-permute-start.25 = (bf16[160,512]{1,0:T(8,128)(2,1)S(1)}, bf16[160,512]{1,0:T(8,128)(2,1)S(1)}, u32[]{:S(2)}, u32[]{:S(2)}) collective-permute-start(bf16[160,512]{1,0:T(8,128)(2,1)S(1)} %payload.1.refs_0_), channel_id=1, source_target_pairs={{0,7},{2,5},{4,3},{6,1},{7,0},{5,2},{3,4},{1,6},{8,15},{10,13},{12... | collective-permute-start | bytes 491528 | tf_op jit(solution)/shard_map/ppermute | solution.py:455
  112.7 6.5 %collective-permute-start.28 = (bf16[160,512]{1,0:T(8,128)(2,1)S(1)}, bf16[160,512]{1,0:T(8,128)(2,1)S(1)}, u32[]{:S(2)}, u32[]{:S(2)}) collective-permute-start(bf16[160,512]{1,0:T(8,128)(2,1)S(1)} %collective-permute-done.27.refs_6_), channel_id=1, source_target_pairs={{0,1},{2,0},{4,2},{6,4},{7,6},{5,7},{3,5},{1,3},{8,9},{10,8},{12,1... | collective-permute-start | bytes 491528 | tf_op jit(solution)/shard_map/ppermute | solution.py:455
  112.8 6.5 %collective-permute-start.24 = (bf16[160,512]{1,0:T(8,128)(2,1)S(1)}, bf16[160,512]{1,0:T(8,128)(2,1)S(1)}, u32[]{:S(2)}, u32[]{:S(2)}) collective-permute-start(bf16[160,512]{1,0:T(8,128)(2,1)S(1)} %collective-permute-done.23.refs_2_), channel_id=1, source_target_pairs={{0,2},{2,4},{4,6},{6,7},{7,5},{5,3},{3,1},{1,0},{8,10},{10,12},{12... | collective-permute-start | bytes 491528 | tf_op jit(solution)/shard_map/ppermute | solution.py:455

commit v5 on v4

--- a/solution.py
+++ b/solution.py
@@ -257,13 +257,41 @@
     )(*arrays)
 
 
-def score_kernel(wo, ws, kinds, aligned, own_ref, mate_ref, bias_ref, *refs):
-    count = 1 + max(k for _, places in kinds for k, _ in places)
+def plane_kernel(own_ref, mate_ref, bias_ref, *refs):
+    part_ref = refs[-1]
+    rows = own_ref.shape[0]
+    acc = None
+    for start in range(0, refs[0].shape[1], 1024):
+        cols = slice(start, min(start + 1024, refs[0].shape[1]))
+        x = jnp.concatenate([p[:, cols] for p in refs[:-1]], axis=0)
+        p = jnp.concatenate([own_ref[:, cols], mate_ref[:, cols]], axis=0)
+        term = lax.dot_general(p, x, (((1,), (1,)), ((), ())), preferred_element_type=F32)
+        acc = term if acc is None else acc + term
+    part_ref[:rows, :] = acc[:rows] + bias_ref[...]
+    part_ref[rows:, :] = acc[rows:]
+
+
+def plane_scores(own, mate, bias, pieces):
+    vmem = pl.BlockSpec(memory_space=pltpu.VMEM)
+    rows, count, depth = own.shape[0], sum(p.shape[0] for p in pieces), pieces[0].shape[1]
+    return pl.pallas_call(
+        plane_kernel,
+        in_specs=[vmem] * (3 + len(pieces)),
+        out_specs=vmem,
+        out_shape=jax.ShapeDtypeStruct((2 * rows, count), F32),
+        compiler_params=pltpu.CompilerParams(vmem_limit_bytes=8 * MIB),
+        cost_estimate=pl.CostEstimate(flops=4 * rows * count * depth, bytes_accessed=4 * rows * depth, transcendentals=0),
+        name="plane_scores",
+    )(own, mate, bias, *pieces)
+
+
+def score_kernel(wo, ws, kinds, aligned, begun, own_ref, mate_ref, bias_ref, *refs):
+    count = 1 + max(k for kind in kinds for _, places in kind for k, _ in places)
     pieces, part_ref = refs[:count], refs[count]
     rows = own_ref.shape[0]
-    acc = None
-    base = 0
-    for width, places in kinds:
+    acc = bias_ref[...] if begun else None
+    base = sum(width for width, _ in kinds[0]) if begun else 0
+    for width, places in [segment for kind in kinds[int(begun) :] for segment in kind]:
         for start in range(0, width, 1024):
             size = min(1024, width - start)
             x = jnp.concatenate([pieces[k][:, c + start : c + start + size] for k, c in places], axis=0)
@@ -272,34 +300,49 @@
             term = lax.dot_general(p, x, (((1,), (1,)), ((), ())), preferred_element_type=F32)
             acc = term if acc is None else acc + term
         base += width
-    part_ref[:rows, :] = acc[:rows] + bias_ref[...]
+    part_ref[:rows, :] = acc[:rows] if begun else acc[:rows] + bias_ref[...]
     part_ref[rows:, :] = acc[rows:]
     if aligned:
         side, owner = (lax.axis_index("cls") // 2) % 2, lax.axis_index("ori")
         slice_ref = refs[count + 1]
-        for (_, places), spot, size in zip(kinds, (side * wo, 2 * wo, (1 - side) * wo), (wo, ws, wo), strict=True):
+        for kind, spot, size in zip(kinds, (side * wo, 2 * wo, (1 - side) * wo), (wo, ws, wo), strict=True):
             row = 0
-            for k, c in places:
-                p = pieces[k]
-                slice_ref[row : row + p.shape[0], at(spot, size)] = p[:, at(c + owner * size, size)]
-                row += p.shape[0]
-
-
-def group_scores(own, mate, bias, kinds, wo, ws, n):
+            for i in range(len(kind[0][1])):
+                k, c = kind[0][1][i]
+                high = pieces[k].shape[0]
+                own_part = kind[0][0] // size
+                if len(kind) == 1 or kind[1][1][i][0] == k:
+                    tile = pieces[k][:, at(c + owner * size, size)]
+                else:
+                    k2, c2 = kind[1][1][i]
+                    first = pieces[k][:, at(c + jnp.minimum(owner, own_part - 1) * size, size)]
+                    second = pieces[k2][:, at(c2 + jnp.maximum(owner - own_part, 0) * size, size)]
+                    tile = jnp.where(owner < own_part, first, second)
+                slice_ref[row : row + high, at(spot, size)] = tile
+                row += high
+
+
+def group_scores(own, mate, bias, kinds, wo, ws, begun=False):
     aligned = wo % LANES == 0
     rows = own.shape[0]
     half = 2 * wo + ws
-    count = sum(p.shape[0] for p, _ in kinds[0])
+    count = sum(p.shape[0] for p, _ in kinds[0][0][1])
     out = [jax.ShapeDtypeStruct((2 * rows, count), F32)]
     if aligned:
         out.append(jax.ShapeDtypeStruct((count, half), BF16))
     arrays, numbered = [], []
-    for places, width in zip(kinds, (n * wo + LANES, n * ws, n * wo), strict=True):
-        numbered.append((width, [(len(arrays) + i, c) for i, (_, c) in enumerate(places)]))
-        arrays += [p for p, _ in places]
+    for kind in kinds:
+        numbered.append([])
+        for width, places in kind:
+            named = []
+            for p, c in places:
+                if not any(p is q for q in arrays):
+                    arrays.append(p)
+                named.append(([p is q for q in arrays].index(True), c))
+            numbered[-1].append((width, named))
     vmem = pl.BlockSpec(memory_space=pltpu.VMEM)
     got = pl.pallas_call(
-        functools.partial(score_kernel, wo, ws, numbered, aligned),
+        functools.partial(score_kernel, wo, ws, numbered, aligned, begun),
         in_specs=[vmem] * (3 + len(arrays)),
         out_specs=[vmem] * len(out),
         out_shape=out,
@@ -313,8 +356,10 @@
         return got
     side, owner = (lax.axis_index("cls") // 2) % 2, lax.axis_index("ori")
     cols = []
-    for places, size in zip(kinds, (wo, ws, wo), strict=True):
-        cols.append(jnp.concatenate([lax.dynamic_slice_in_dim(p, c + owner * size, size, 1) for p, c in places], axis=0))
+    for kind, size in zip(kinds, (wo, ws, wo), strict=True):
+        sources = zip(*[[p[:, c : c + width] for p, c in places] for width, places in kind], strict=True)
+        rows_of = [jnp.concatenate(parts, axis=1) for parts in sources]
+        cols.append(jnp.concatenate([lax.dynamic_slice_in_dim(p, owner * size, size, 1) for p in rows_of], axis=0))
     a, c, b = cols
     first, second = jnp.where(side == 0, a, b), jnp.where(side == 0, b, a)
     return got[0], jnp.concatenate([first, second, c], axis=1)
@@ -465,8 +510,7 @@
     projections, own = tie(projections, own)
     keep, send, bias = prep_projections(projections, weight, log_prior, core, side, owner, wo, ws, n)
 
-    cut_at = rows // 2
-    every, top, bottom = slice(0, rows), slice(0, cut_at), slice(cut_at, rows)
+    every = slice(0, rows)
     plane_w, shared_w = n * wo + LANES, n * ws
     plane_cols, cross_cols = slice(0, plane_w), slice(0, n * wo)
     shared_cols = slice(plane_w, plane_w + shared_w)
@@ -493,29 +537,52 @@
             f, b, x, parts[s - 1], slices[s - 1] = tie(f, b, x, parts[s - 1], slices[s - 1])
         both.append((f, b))
         crossed.append(x)
-        kinds = ([(p, 0) for p in both[s - 1]], [(p, plane_w) for p in both[s]], [(x, 0)])
-        parts[s], slices[s] = group_scores(keep, mates, bias, kinds, wo, ws, n)
+        kinds = (
+            [(plane_w, [(p, 0) for p in both[s - 1]])],
+            [(shared_w, [(p, plane_w) for p in both[s]])],
+            [(n * wo, [(x, 0)])],
+        )
+        parts[s], slices[s] = group_scores(keep, mates, bias, kinds, wo, ws)
         if s < far - 2:
             (x_in,) = pack([f, b], [(2 * rows, n * wo)], [[(0, every, cross_cols, 0, 0), (1, every, cross_cols, rows, 0)]])
-    x_in, fo, bo, fs, bs = pack(
+    half_o, half_s = n // 2 * wo, n // 2 * ws
+    rest_o = plane_w - half_o
+    x_in, f, b = pack(
         [f, b],
-        [(2 * rows, n * wo)] + [(cut_at, plane_w)] * 2 + [(rows, shared_w)] * 2,
+        [(2 * rows, n * wo), (rows, half_o + shared_w), (rows, rest_o + shared_w)],
         [
             [(0, every, cross_cols, 0, 0), (1, every, cross_cols, rows, 0)],
-            [(0, top, plane_cols, 0, 0)],
-            [(1, bottom, plane_cols, 0, 0)],
-            [(0, every, shared_cols, 0, 0)],
-            [(1, every, shared_cols, 0, 0)],
+            [(0, every, slice(0, half_o), 0, 0), (0, every, shared_cols, 0, half_o)],
+            [(1, every, slice(half_o, plane_w), 0, 0), (1, every, shared_cols, 0, rest_o)],
         ],
     )
-    fo, bo, fs, bs, x = ring(fo, 1), ring(bo, -1), ring(fs, 1), ring(bs, -1), cross(x_in)
-    fo, bo, fs, bs, x, parts[far - 2], slices[far - 2] = tie(fo, bo, fs, bs, x, parts[far - 2], slices[far - 2])
-    kinds = ([(p, 0) for p in both[far - 2]], [(fs, 0), (bs, 0)], [(x, 0)])
-    parts[far - 1], slices[far - 1] = group_scores(keep, mates, bias, kinds, wo, ws, n)
-    (x_in,) = pack([fo, bo], [(rows, n * wo)], [[(0, top, cross_cols, 0, 0), (1, top, cross_cols, cut_at, 0)]])
-    fs, bs, x = ring(fs[:cut_at], 1), ring(bs[cut_at:], -1), cross(x_in)
-    kinds = ([(own, 0), (fo, 0), (bo, 0)], [(shared, 0), (fs, 0), (bs, 0)], [(oth, 0), (x, 0)])
-    parts[0], slices[0] = group_scores(keep, mates, bias, kinds, wo, ws, n)
+    f, b, x = ring(f, 1), ring(b, -1), cross(x_in)
+    f, b, x, parts[far - 2], slices[far - 2] = tie(f, b, x, parts[far - 2], slices[far - 2])
+    kinds = (
+        [(plane_w, [(p, 0) for p in both[far - 2]])],
+        [(shared_w, [(f, half_o), (b, rest_o)])],
+        [(n * wo, [(x, 0)])],
+    )
+    parts[far - 1], slices[far - 1] = group_scores(keep, mates, bias, kinds, wo, ws)
+    x_in, last, f, b = pack(
+        [f, b],
+        [(rows, n * wo), (rows, plane_w), (rows, half_s), (rows, half_s)],
+        [
+            [(0, every, slice(0, half_o), 0, 0), (1, every, slice(0, n * wo - half_o), 0, half_o)],
+            [(0, every, slice(0, half_o), 0, 0), (1, every, slice(0, rest_o), 0, half_o)],
+            [(0, every, slice(half_o, half_o + half_s), 0, 0)],
+            [(1, every, slice(rest_o + half_s, rest_o + shared_w), 0, 0)],
+        ],
+    )
+    f, b, x = ring(f, 1), ring(b, -1), cross(x_in)
+    begun = plane_scores(keep, mates, bias, [own, last])
+    f, b, x, begun = tie(f, b, x, begun)
+    kinds = (
+        [(plane_w, [(own, 0), (last, 0)])],
+        [(half_s, [(shared, 0), (f, 0)]), (half_s, [(shared, half_s), (b, 0)])],
+        [(n * wo, [(oth, 0), (x, 0)])],
+    )
+    parts[0], slices[0] = group_scores(keep, mates, begun, kinds, wo, ws, True)
     recvs = [swap(p) for p in parts]
     other_slices = [swap(x) for x in slices]
 

time: 125 us -> 124 us (level)
    ppermute x19 -> x17, starting transfers between devices: 23.1 us -> 22.2 us  [ring(): lax.ppermute(x, 'ori', [(cycle[i], cycle[(i + d) % n]) for i in range(n)])]
    ppermute x19 -> x17, waiting for transfers between devices: 31.7 us -> 31.3 us  [ring(): lax.ppermute(x, 'ori', [(cycle[i], cycle[(i + d) % n]) for i in range(n)])]
    pallas_call x4 -> x5, Pallas kernels: 6.98 us -> 7.11 us  [the longest x4 6.47 us: group_scores(): pl.pallas_call(functools.partial(score_kernel, wo, ws, numbered, aligned,...]
  transfers between devices with their start and end apart: 33 -> 31, of which waited for: 18 -> 17; matrix products, arithmetic and copies ran while one was open for 0% -> 0% of each run, Pallas kernels for 15% -> 15%
where the time goes in v5:
time: 124 us
  waiting for transfers between devices  64.2 us (52%)
  starting transfers between devices  30.5 us (25%)
  Pallas kernels  26.4 us (21%)
  local copies, waits for them, and re-layouts  1.87 us (2%)
    ppermute x17, waiting for transfers between devices, ring(): lax.ppermute(x, 'ori', [(cycle[i], cycle[(i + d) % n]) for i in range(n)])  31.3 us
    ppermute x4, waiting for transfers between devices, cross(): return lax.ppermute(x, 'cls', [(i, i ^ 2) for i in range(n_cls)])  29 us
    ppermute x17, starting transfers between devices, ring(): lax.ppermute(x, 'ori', [(cycle[i], cycle[(i + d) % n]) for i in range(n)])  22.2 us
    pallas_call x4, Pallas kernels, group_scores(): pl.pallas_call(functools.partial(score_kernel, wo, ws, numbered, aligned,...  6.47 us
    ppermute x4, starting transfers between devices, cross(): return lax.ppermute(x, 'cls', [(i, i ^ 2) for i in range(n_cls)])  5.91 us
    pallas_call x1, Pallas kernels, prep_projections(): pl.pallas_call(functools.partial(split_kernel, wo, ws, n), in_specs=[pl.B...  5.89 us
    pallas_call x1, Pallas kernels, body(): pl.pallas_call(functools.partial(stream_kernel, n, ori_rows, cycle), in_s...  5.17 us
    pallas_call x1, Pallas kernels, prep_images(): pl.pallas_call(functools.partial(rest_kernel, n, wo, ws), in_specs=[somew...  3.19 us
  transfers between devices with their start and end apart: 31, of which 17 were waited for; matrix products, arithmetic and copies ran while one was open for 0% of the time, Pallas kernels for 15%

profile of v5, /device:TPU:0, one launch (start us, length us, event | category | flops | bytes accessed | tf_op | source)
XLA Modules:
  0.0 123.9 jit_solution(2028562081396154970)
XLA Ops:
  0.6 2.1 %prep_own_plane.1 = (bf16[64,3200]{1,0:T(8,128)(2,1)}, f32[160,128]{1,0:T(8,128)}) custom-call(bf16[64,20480]{1,0:T(8,128)(2,1)} %img_hbm.3, s32[160,128]{1,0:T(8,128)} %bitcast.5, f32[1,100]{1,0:T(1,128)} %bitcast.7, s32[4,64]{1,0:T(4,128)} %bitcast.6), custom_call_target="tpu_custom_call" | custom-call | tf_op jit(solution)/shard_map/prep_own_plane/pallas_call | solution.py:105
  2.7 3.0 %collective-permute-start.1 = (bf16[64,3200]{1,0:T(8,128)(2,1)}, bf16[64,3200]{1,0:T(8,128)(2,1)S(1)}, u32[]{:S(2)}, u32[]{:S(2)}) collective-permute-start(bf16[64,3200]{1,0:T(8,128)(2,1)} %get-tuple-element.57.refs_0_), channel_id=1, source_target_pairs={{0,1},{2,0},{4,2},{6,4},{7,6},{5,7},{3,5},{1,3},{8,9},{10,8},{12,1... | collective-permute-start | bytes 1228808 | tf_op jit(solution)/shard_map/ppermute | solution.py:500
  5.7 0.1 collective-permute-start
  5.8 3.2 %prep_rest.1 = (bf16[64,3072]{1,0:T(8,128)(2,1)}, bf16[64,4096]{1,0:T(8,128)(2,1)}) custom-call(bf16[64,20480]{1,0:T(8,128)(2,1)} %img_hbm.3, f32[160,128]{1,0:T(8,128)} %get-tuple-element.58.w_ref), custom_call_target="tpu_custom_call" | custom-call | tf_op jit(solution)/shard_map/prep_rest/pallas_call | solution.py:120
  9.0 5.9 %split_projections.1 = (bf16[144,10368]{1,0:T(8,128)(2,1)}, bf16[144,10368]{1,0:T(8,128)(2,1)}) custom-call(bf16[1,144,20480]{2,1,0:T(8,128)(2,1)} %proj_hbm), custom_call_target="tpu_custom_call" | custom-call | bytes 11796480 | tf_op jit(solution)/shard_map/split_projections/pallas_call | solution.py:207
  14.9 0.0 copy-start
  15.0 0.0 copy-start.6
  15.0 0.5 collective-permute-done.1.refs_1_
  15.4 1.4 %collective-permute-done.refs_0_ = bf16[64,3200]{1,0:T(8,128)(2,1)S(1)} collective-permute-done((bf16[64,3200]{1,0:T(8,128)(2,1)}, bf16[64,3200]{1,0:T(8,128)(2,1)S(1)}, u32[]{:S(2)}, u32[]{:S(2)}) %collective-permute-start) | collective-permute-done | bytes 409632 | tf_op jit(solution)/shard_map/ppermute | solution.py:500
  16.9 0.2 pack.4
  17.0 0.5 collective-permute-start.2
  17.5 1.6 %collective-permute-start.3 = (bf16[64,7296]{1,0:T(8,128)(2,1)S(1)}, bf16[64,7296]{1,0:T(8,128)(2,1)S(1)}, u32[]{:S(2)}, u32[]{:S(2)}) collective-permute-start(bf16[64,7296]{1,0:T(8,128)(2,1)S(1)} %get-tuple-element.65.refs_1_), channel_id=1, source_target_pairs={{0,1},{2,0},{4,2},{6,4},{7,6},{5,7},{3,5},{1,3},{8,9},{10,8},{12,1... | collective-permute-start | bytes 2801672 | tf_op jit(solution)/shard_map/ppermute | solution.py:500
  19.1 1.5 %collective-permute-start.4 = (bf16[128,3072]{1,0:T(8,128)(2,1)S(1)}, bf16[128,3072]{1,0:T(8,128)(2,1)S(1)}, u32[]{:S(2)}, u32[]{:S(2)}) collective-permute-start(bf16[128,3072]{1,0:T(8,128)(2,1)S(1)} %get-tuple-element.66), channel_id=1, source_target_pairs={{0,16},{8,24},{16,0},{24,8},{1,17},{9,25},{17,1},{25,9},{2,18},{10... | collective-permute-start | bytes 2359304 | tf_op jit(solution)/shard_map/ppermute | solution.py:506
  20.6 17.9 %collective-permute-done.4.refs_4_ = bf16[128,3072]{1,0:T(8,128)(2,1)S(1)} collective-permute-done((bf16[128,3072]{1,0:T(8,128)(2,1)S(1)}, bf16[128,3072]{1,0:T(8,128)(2,1)S(1)}, u32[]{:S(2)}, u32[]{:S(2)}) %collective-permute-start.4) | collective-permute-done | bytes 786464 | tf_op jit(solution)/shard_map/ppermute | solution.py:506
  38.5 1.7 %collective-permute-done.2.refs_0_.refs_2_ = bf16[64,7296]{1,0:T(8,128)(2,1)S(1)} collective-permute-done((bf16[64,7296]{1,0:T(8,128)(2,1)S(1)}, bf16[64,7296]{1,0:T(8,128)(2,1)S(1)}, u32[]{:S(2)}, u32[]{:S(2)}) %collective-permute-start.2) | collective-permute-done | bytes 933920 | tf_op jit(solution)/shard_map/ppermute | solution.py:500
  40.2 0.1 collective-permute-done.3.refs_1_.refs_3_
  40.3 1.7 %collective-permute-start.6 = (bf16[64,7296]{1,0:T(8,128)(2,1)S(1)}, bf16[64,7296]{1,0:T(8,128)(2,1)S(1)}, u32[]{:S(2)}, u32[]{:S(2)}) collective-permute-start(bf16[64,7296]{1,0:T(8,128)(2,1)S(1)} %collective-permute-done.2.refs_0_.refs_2_), channel_id=1, source_target_pairs={{0,2},{2,4},{4,6},{6,7},{7,5},{5,3},{3,1},{1,0},{8,10},{10,12},{12... | collective-permute-start | bytes 2801672 | tf_op jit(solution)/shard_map/ppermute | solution.py:500
  42.0 0.3 collective-permute-start.7
  42.4 0.1 pack.5
  42.4 1.7 %collective-permute-start.8 = (bf16[128,3072]{1,0:T(8,128)(2,1)S(1)}, bf16[128,3072]{1,0:T(8,128)(2,1)S(1)}, u32[]{:S(2)}, u32[]{:S(2)}) collective-permute-start(bf16[128,3072]{1,0:T(8,128)(2,1)S(1)} %pack.5), channel_id=1, source_target_pairs={{0,16},{8,24},{16,0},{24,8},{1,17},{9,25},{17,1},{25,9},{2,18},{10... | collective-permute-start | bytes 2359304 | tf_op jit(solution)/shard_map/ppermute | solution.py:506
  44.1 1.8 %copy-done.1 = bf16[144,10368]{1,0:T(8,128)(2,1)S(1)} copy-done((bf16[144,10368]{1,0:T(8,128)(2,1)S(1)}, bf16[144,10368]{1,0:T(8,128)(2,1)}, u32[]{:S(2)}) %copy-start.1) | copy-done | bytes 2986008
  45.9 2.2 %half_norms.1.bias_ref = f32[144,128]{1,0:T(8,128)S(1)} custom-call(bf16[144,10368]{1,0:T(8,128)(2,1)S(1)} %copy-done, bf16[144,10368]{1,0:T(8,128)(2,1)S(1)} %copy-done.1, f32[1,144]{1,0:T(1,128)S(1)} %copy-done.6, f32[160,128]{1,0:T(8,128)S(1)} %copy-done.5), custom_call_target="tpu_custom_call" | custom-call | flops 8847360 | bytes 5898240 | tf_op jit(solution)/shard_map/half_norms/pallas_call | solution.py:217
  48.1 1.7 %group_scores.4 = (f32[288,128]{1,0:T(8,128)S(1)}, bf16[128,1280]{1,0:T(8,128)(2,1)S(1)}) custom-call(bf16[144,10368]{1,0:T(8,128)(2,1)S(1)} %copy-done, bf16[144,10368]{1,0:T(8,128)(2,1)S(1)} %collective-permute-done.5.mate_ref, f32[144,128]{1,0:T(8,128)S(1)} %half_norms.1.bias_ref, bf16[64,7296]{1,0:T(8,128)(2,1)S(1)} %get-tuple-element.64.refs_0_, ...), custom_call_target="tpu_custom_call" | custom-call | flops 764411904 | bytes 8626176 | tf_op jit(solution)/shard_map/group_scores/pallas_call | solution.py:344
  49.9 11.1 %collective-permute-done.8.refs_4_ = bf16[128,3072]{1,0:T(8,128)(2,1)S(1)} collective-permute-done((bf16[128,3072]{1,0:T(8,128)(2,1)S(1)}, bf16[128,3072]{1,0:T(8,128)(2,1)S(1)}, u32[]{:S(2)}, u32[]{:S(2)}) %collective-permute-start.8) | collective-permute-done | bytes 786464 | tf_op jit(solution)/shard_map/ppermute | solution.py:506
  61.0 1.6 %collective-permute-done.6.refs_0_.refs_2_ = bf16[64,7296]{1,0:T(8,128)(2,1)S(1)} collective-permute-done((bf16[64,7296]{1,0:T(8,128)(2,1)S(1)}, bf16[64,7296]{1,0:T(8,128)(2,1)S(1)}, u32[]{:S(2)}, u32[]{:S(2)}) %collective-permute-start.6) | collective-permute-done | bytes 933920 | tf_op jit(solution)/shard_map/ppermute | solution.py:500
  62.5 1.2 collective-permute-done.7.refs_1_.refs_3_
  63.7 0.1 pack.6
  63.9 1.6 %collective-permute-start.11 = (bf16[128,3072]{1,0:T(8,128)(2,1)S(1)}, bf16[128,3072]{1,0:T(8,128)(2,1)S(1)}, u32[]{:S(2)}, u32[]{:S(2)}) collective-permute-start(bf16[128,3072]{1,0:T(8,128)(2,1)S(1)} %get-tuple-element.78), channel_id=1, source_target_pairs={{0,16},{8,24},{16,0},{24,8},{1,17},{9,25},{17,1},{25,9},{2,18},{10... | collective-permute-start | bytes 2359304 | tf_op jit(solution)/shard_map/ppermute | solution.py:506
  65.5 0.5 collective-permute-start.10
  66.0 1.5 %collective-permute-start.9 = (bf16[64,5632]{1,0:T(8,128)(2,1)S(1)}, bf16[64,5632]{1,0:T(8,128)(2,1)S(1)}, u32[]{:S(2)}, u32[]{:S(2)}) collective-permute-start(bf16[64,5632]{1,0:T(8,128)(2,1)S(1)} %get-tuple-element.76), channel_id=1, source_target_pairs={{0,2},{2,4},{4,6},{6,7},{7,5},{5,3},{3,1},{1,0},{8,10},{10,12},{12... | collective-permute-start | bytes 2162696 | tf_op jit(solution)/shard_map/ppermute | solution.py:500
  67.5 1.7 %group_scores.5 = (f32[288,128]{1,0:T(8,128)S(1)}, bf16[128,1280]{1,0:T(8,128)(2,1)S(1)}) custom-call(bf16[144,10368]{1,0:T(8,128)(2,1)S(1)} %copy-done, bf16[144,10368]{1,0:T(8,128)(2,1)S(1)} %collective-permute-done.5.mate_ref, f32[144,128]{1,0:T(8,128)S(1)} %half_norms.1.bias_ref, bf16[64,7296]{1,0:T(8,128)(2,1)S(1)} %collective-permute-done.2.refs_0_.refs_2_, ...), custom_call_target="tpu_custom_call" | custom-call | flops 764411904 | bytes 8626176 | tf_op jit(solution)/shard_map/group_scores/pallas_call | solution.py:344
  69.2 12.7 %collective-permute-done.9.refs_0_.refs_2_ = bf16[64,5632]{1,0:T(8,128)(2,1)S(1)} collective-permute-done((bf16[64,5632]{1,0:T(8,128)(2,1)S(1)}, bf16[64,5632]{1,0:T(8,128)(2,1)S(1)}, u32[]{:S(2)}, u32[]{:S(2)}) %collective-permute-start.9) | collective-permute-done | bytes 720928 | tf_op jit(solution)/shard_map/ppermute | solution.py:500
  82.0 0.1 pack.7
  82.1 1.2 collective-permute-start.14
  83.3 1.6 %collective-permute-start.12 = (bf16[64,2048]{1,0:T(8,128)(2,1)S(1)}, bf16[64,2048]{1,0:T(8,128)(2,1)S(1)}, u32[]{:S(2)}, u32[]{:S(2)}) collective-permute-start(bf16[64,2048]{1,0:T(8,128)(2,1)S(1)} %get-tuple-element.84), channel_id=1, source_target_pairs={{0,2},{2,4},{4,6},{6,7},{7,5},{5,3},{3,1},{1,0},{8,10},{10,12},{12... | collective-permute-start | bytes 786440 | tf_op jit(solution)/shard_map/ppermute | solution.py:500
  84.8 0.4 collective-permute-start.13
  85.3 0.0 collective-permute-start.16
  85.3 1.7 %group_scores.7 = (f32[288,128]{1,0:T(8,128)S(1)}, bf16[128,1280]{1,0:T(8,128)(2,1)S(1)}) custom-call(bf16[144,10368]{1,0:T(8,128)(2,1)S(1)} %copy-done, bf16[144,10368]{1,0:T(8,128)(2,1)S(1)} %collective-permute-done.5.mate_ref, f32[144,128]{1,0:T(8,128)S(1)} %half_norms.1.bias_ref, bf16[64,7296]{1,0:T(8,128)(2,1)S(1)} %collective-permute-done.6.refs_0_.refs_2_, ...), custom_call_target="tpu_custom_call" | custom-call | flops 764411904 | bytes 8626176 | tf_op jit(solution)/shard_map/group_scores/pallas_call | solution.py:344
  87.0 0.6 collective-permute-start.18
  87.6 0.6 plane_scores.1.bias_ref
  88.3 1.4 %collective-permute-done.12.refs_3_ = bf16[64,2048]{1,0:T(8,128)(2,1)S(1)} collective-permute-done((bf16[64,2048]{1,0:T(8,128)(2,1)S(1)}, bf16[64,2048]{1,0:T(8,128)(2,1)S(1)}, u32[]{:S(2)}, u32[]{:S(2)}) %collective-permute-start.12) | collective-permute-done | bytes 262176 | tf_op jit(solution)/shard_map/ppermute | solution.py:500
  89.6 0.0 collective-permute-start.17
  89.6 1.6 %collective-permute-done.13.refs_4_ = bf16[64,2048]{1,0:T(8,128)(2,1)S(1)} collective-permute-done((bf16[64,2048]{1,0:T(8,128)(2,1)S(1)}, bf16[64,2048]{1,0:T(8,128)(2,1)S(1)}, u32[]{:S(2)}, u32[]{:S(2)}) %collective-permute-start.13) | collective-permute-done | bytes 262176 | tf_op jit(solution)/shard_map/ppermute | solution.py:500
  91.2 0.0 collective-permute-done.14.refs_6_
  91.2 1.2 group_scores.6
  92.5 0.1 collective-permute-start.15
  92.5 0.5 collective-permute-start.28
  93.1 0.8 collective-permute-done.15.refs_4_
  93.9 0.3 local_stats.1
  94.2 0.7 collective-permute-start.19
  94.9 3.0 %collective-permute-done.19.refs_1_ = f32[8,512]{1,0:T(8,128)S(1)} collective-permute-done((f32[8,512]{1,0:T(8,128)S(1)}, f32[8,512]{1,0:T(8,128)S(1)}, u32[]{:S(2)}, u32[]{:S(2)}) %collective-permute-start.19) | collective-permute-done | bytes 16416 | tf_op jit(solution)/shard_map/ppermute | solution.py:600
  98.0 0.1 payload.1.refs_0_
  98.0 0.6 collective-permute-start.24
  98.6 1.5 %collective-permute-start.20 = (bf16[160,512]{1,0:T(8,128)(2,1)S(1)}, bf16[160,512]{1,0:T(8,128)(2,1)S(1)}, u32[]{:S(2)}, u32[]{:S(2)}) collective-permute-start(bf16[160,512]{1,0:T(8,128)(2,1)S(1)} %payload.1.refs_0_), channel_id=1, source_target_pairs={{0,2},{2,4},{4,6},{6,7},{7,5},{5,3},{3,1},{1,0},{8,10},{10,12},{12... | collective-permute-start | bytes 491528 | tf_op jit(solution)/shard_map/ppermute | solution.py:500
  100.1 0.5 collective-permute-start.27
  100.6 2.8 %collective-permute-done.24.refs_7_ = bf16[160,512]{1,0:T(8,128)(2,1)S(1)} collective-permute-done((bf16[160,512]{1,0:T(8,128)(2,1)S(1)}, bf16[160,512]{1,0:T(8,128)(2,1)S(1)}, u32[]{:S(2)}, u32[]{:S(2)}) %collective-permute-start.24) | collective-permute-done | bytes 163872 | tf_op jit(solution)/shard_map/ppermute | solution.py:500
  103.4 0.5 collective-permute-start.25
  103.9 1.5 %collective-permute-start.21 = (bf16[160,512]{1,0:T(8,128)(2,1)S(1)}, bf16[160,512]{1,0:T(8,128)(2,1)S(1)}, u32[]{:S(2)}, u32[]{:S(2)}) collective-permute-start(bf16[160,512]{1,0:T(8,128)(2,1)S(1)} %collective-permute-done.20.refs_1_), channel_id=1, source_target_pairs={{0,2},{2,4},{4,6},{6,7},{7,5},{5,3},{3,1},{1,0},{8,10},{10,12},{12... | collective-permute-start | bytes 491528 | tf_op jit(solution)/shard_map/ppermute | solution.py:500
  105.4 2.9 %collective-permute-start.23 = (bf16[160,512]{1,0:T(8,128)(2,1)S(1)}, bf16[160,512]{1,0:T(8,128)(2,1)S(1)}, u32[]{:S(2)}, u32[]{:S(2)}) collective-permute-start(bf16[160,512]{1,0:T(8,128)(2,1)S(1)} %payload.1.refs_0_), channel_id=1, source_target_pairs={{0,7},{2,5},{4,3},{6,1},{7,0},{5,2},{3,4},{1,6},{8,15},{10,13},{12... | collective-permute-start | bytes 491528 | tf_op jit(solution)/shard_map/ppermute | solution.py:500
  108.3 3.1 %collective-permute-done.25.refs_6_ = bf16[160,512]{1,0:T(8,128)(2,1)S(1)} collective-permute-done((bf16[160,512]{1,0:T(8,128)(2,1)S(1)}, bf16[160,512]{1,0:T(8,128)(2,1)S(1)}, u32[]{:S(2)}, u32[]{:S(2)}) %collective-permute-start.25) | collective-permute-done | bytes 163872 | tf_op jit(solution)/shard_map/ppermute | solution.py:500
  111.4 3.9 %collective-permute-start.22 = (bf16[160,512]{1,0:T(8,128)(2,1)S(1)}, bf16[160,512]{1,0:T(8,128)(2,1)S(1)}, u32[]{:S(2)}, u32[]{:S(2)}) collective-permute-start(bf16[160,512]{1,0:T(8,128)(2,1)S(1)} %collective-permute-done.21.refs_2_), channel_id=1, source_target_pairs={{0,2},{2,4},{4,6},{6,7},{7,5},{5,3},{3,1},{1,0},{8,10},{10,12},{12... | collective-permute-start | bytes 491528 | tf_op jit(solution)/shard_map/ppermute | solution.py:500
  115.3 0.3 collective-permute-done.23.refs_4_
  115.7 2.9 %collective-permute-done.26.refs_5_ = bf16[160,512]{1,0:T(8,128)(2,1)S(1)} collective-permute-done((bf16[160,512]{1,0:T(8,128)(2,1)S(1)}, bf16[160,512]{1,0:T(8,128)(2,1)S(1)}, u32[]{:S(2)}, u32[]{:S(2)}) %collective-permute-start.26) | collective-permute-done | bytes 163872 | tf_op jit(solution)/shard_map/ppermute | solution.py:500
  118.6 5.2 %class_sums.1 = (bf16[1152,2560]{1,0:T(8,128)(2,1)}, f32[1,64]{1,0:T(1,128)}) custom-call(bf16[160,512]{1,0:T(8,128)(2,1)S(1)} %payload.1.refs_0_, bf16[160,512]{1,0:T(8,128)(2,1)S(1)} %collective-permute-done.20.refs_1_, bf16[160,512]{1,0:T(8,128)(2,1)S(1)} %collective-permute-done.21.refs_2_, bf16[160,512]{1,0:T(8,128)(2,1)S(1)} %collective-permute-done.22.refs_3_, ...), custom_call_target="tpu_custom_call" | custom-call | tf_op jit(solution)/shard_map/class_sums/pallas_call | solution.py:621
  (28 shorter events, 0.1 us)
Async XLA Ops:
  2.7 12.8 %collective-permute-start.1 = (bf16[64,3200]{1,0:T(8,128)(2,1)}, bf16[64,3200]{1,0:T(8,128)(2,1)S(1)}, u32[]{:S(2)}, u32[]{:S(2)}) collective-permute-start(bf16[64,3200]{1,0:T(8,128)(2,1)} %get-tuple-element.57.refs_0_), channel_id=1, source_target_pairs={{0,1},{2,0},{4,2},{6,4},{7,6},{5,7},{3,5},{1,3},{8,9},{10,8},{12,1... | collective-permute-start | bytes 1228808 | tf_op jit(solution)/shard_map/ppermute | solution.py:500
  5.7 11.1 %collective-permute-start = (bf16[64,3200]{1,0:T(8,128)(2,1)}, bf16[64,3200]{1,0:T(8,128)(2,1)S(1)}, u32[]{:S(2)}, u32[]{:S(2)}) collective-permute-start(bf16[64,3200]{1,0:T(8,128)(2,1)} %get-tuple-element.57.refs_0_), channel_id=1, source_target_pairs={{0,2},{2,4},{4,6},{6,7},{7,5},{5,3},{3,1},{1,0},{8,10},{10,12},{12... | collective-permute-start | bytes 1228808 | tf_op jit(solution)/shard_map/ppermute | solution.py:500
  9.0 7.8 %copy-start.2 = (bf16[64,4096]{1,0:T(8,128)(2,1)S(1)}, bf16[64,4096]{1,0:T(8,128)(2,1)}, u32[]{:S(2)}) copy-start(bf16[64,4096]{1,0:T(8,128)(2,1)} %get-tuple-element.63.refs_2_) | copy-start | bytes 1572868
  14.9 29.1 %copy-start = (bf16[144,10368]{1,0:T(8,128)(2,1)S(1)}, bf16[144,10368]{1,0:T(8,128)(2,1)}, u32[]{:S(2)}) copy-start(bf16[144,10368]{1,0:T(8,128)(2,1)} %get-tuple-element.56.keep_ref.own_ref) | copy-start | bytes 8957956
  15.0 29.1 %copy-start.5 = (f32[160,128]{1,0:T(8,128)S(1)}, f32[160,128]{1,0:T(8,128)}, u32[]{:S(2)}) copy-start(f32[160,128]{1,0:T(8,128)} %get-tuple-element.58.w_ref) | copy-start | bytes 245764
  15.0 29.1 %copy-start.6 = (f32[1,144]{1,0:T(1,128)S(1)}, f32[1,144]{1,0:T(1,128)}, u32[]{:S(2)}) copy-start(f32[1,144]{1,0:T(1,128)} %prior_ref.1) | copy-start | bytes 1732
  16.9 23.5 %collective-permute-start.5 = (bf16[144,10368]{1,0:T(8,128)(2,1)}, bf16[144,10368]{1,0:T(8,128)(2,1)S(1)}, u32[]{:S(2)}, u32[]{:S(2)}) collective-permute-start(bf16[144,10368]{1,0:T(8,128)(2,1)} %get-tuple-element.67.send_ref), channel_id=1, source_target_pairs={{0,8},{8,0},{16,24},{24,16},{1,9},{9,1},{17,25},{25,17},{2,10},{10... | collective-permute-start | bytes 8957960 | tf_op jit(solution)/shard_map/ppermute | solution.py:503
  17.0 23.2 %collective-permute-start.2 = (bf16[64,7296]{1,0:T(8,128)(2,1)S(1)}, bf16[64,7296]{1,0:T(8,128)(2,1)S(1)}, u32[]{:S(2)}, u32[]{:S(2)}) collective-permute-start(bf16[64,7296]{1,0:T(8,128)(2,1)S(1)} %get-tuple-element.64.refs_0_), channel_id=1, source_target_pairs={{0,2},{2,4},{4,6},{6,7},{7,5},{5,3},{3,1},{1,0},{8,10},{10,12},{12... | collective-permute-start | bytes 2801672 | tf_op jit(solution)/shard_map/ppermute | solution.py:500
  17.5 22.8 %collective-permute-start.3 = (bf16[64,7296]{1,0:T(8,128)(2,1)S(1)}, bf16[64,7296]{1,0:T(8,128)(2,1)S(1)}, u32[]{:S(2)}, u32[]{:S(2)}) collective-permute-start(bf16[64,7296]{1,0:T(8,128)(2,1)S(1)} %get-tuple-element.65.refs_1_), channel_id=1, source_target_pairs={{0,1},{2,0},{4,2},{6,4},{7,6},{5,7},{3,5},{1,3},{8,9},{10,8},{12,1... | collective-permute-start | bytes 2801672 | tf_op jit(solution)/shard_map/ppermute | solution.py:500
  19.1 19.4 %collective-permute-start.4 = (bf16[128,3072]{1,0:T(8,128)(2,1)S(1)}, bf16[128,3072]{1,0:T(8,128)(2,1)S(1)}, u32[]{:S(2)}, u32[]{:S(2)}) collective-permute-start(bf16[128,3072]{1,0:T(8,128)(2,1)S(1)} %get-tuple-element.66), channel_id=1, source_target_pairs={{0,16},{8,24},{16,0},{24,8},{1,17},{9,25},{17,1},{25,9},{2,18},{10... | collective-permute-start | bytes 2359304 | tf_op jit(solution)/shard_map/ppermute | solution.py:506
  40.3 22.2 %collective-permute-start.6 = (bf16[64,7296]{1,0:T(8,128)(2,1)S(1)}, bf16[64,7296]{1,0:T(8,128)(2,1)S(1)}, u32[]{:S(2)}, u32[]{:S(2)}) collective-permute-start(bf16[64,7296]{1,0:T(8,128)(2,1)S(1)} %collective-permute-done.2.refs_0_.refs_2_), channel_id=1, source_target_pairs={{0,2},{2,4},{4,6},{6,7},{7,5},{5,3},{3,1},{1,0},{8,10},{10,12},{12... | collective-permute-start | bytes 2801672 | tf_op jit(solution)/shard_map/ppermute | solution.py:500
  42.0 21.7 %collective-permute-start.7 = (bf16[64,7296]{1,0:T(8,128)(2,1)S(1)}, bf16[64,7296]{1,0:T(8,128)(2,1)S(1)}, u32[]{:S(2)}, u32[]{:S(2)}) collective-permute-start(bf16[64,7296]{1,0:T(8,128)(2,1)S(1)} %collective-permute-done.3.refs_1_.refs_3_), channel_id=1, source_target_pairs={{0,1},{2,0},{4,2},{6,4},{7,6},{5,7},{3,5},{1,3},{8,9},{10,8},{12,1... | collective-permute-start | bytes 2801672 | tf_op jit(solution)/shard_map/ppermute | solution.py:500
  42.4 18.6 %collective-permute-start.8 = (bf16[128,3072]{1,0:T(8,128)(2,1)S(1)}, bf16[128,3072]{1,0:T(8,128)(2,1)S(1)}, u32[]{:S(2)}, u32[]{:S(2)}) collective-permute-start(bf16[128,3072]{1,0:T(8,128)(2,1)S(1)} %pack.5), channel_id=1, source_target_pairs={{0,16},{8,24},{16,0},{24,8},{1,17},{9,25},{17,1},{25,9},{2,18},{10... | collective-permute-start | bytes 2359304 | tf_op jit(solution)/shard_map/ppermute | solution.py:506
  44.1 1.8 %copy-start.1 = (bf16[144,10368]{1,0:T(8,128)(2,1)S(1)}, bf16[144,10368]{1,0:T(8,128)(2,1)}, u32[]{:S(2)}) copy-start(bf16[144,10368]{1,0:T(8,128)(2,1)} %get-tuple-element.67.send_ref) | copy-start | bytes 8957956
  63.9 18.1 %collective-permute-start.11 = (bf16[128,3072]{1,0:T(8,128)(2,1)S(1)}, bf16[128,3072]{1,0:T(8,128)(2,1)S(1)}, u32[]{:S(2)}, u32[]{:S(2)}) collective-permute-start(bf16[128,3072]{1,0:T(8,128)(2,1)S(1)} %get-tuple-element.78), channel_id=1, source_target_pairs={{0,16},{8,24},{16,0},{24,8},{1,17},{9,25},{17,1},{25,9},{2,18},{10... | collective-permute-start | bytes 2359304 | tf_op jit(solution)/shard_map/ppermute | solution.py:506
  65.5 16.5 %collective-permute-start.10 = (bf16[64,5760]{1,0:T(8,128)(2,1)S(1)}, bf16[64,5760]{1,0:T(8,128)(2,1)S(1)}, u32[]{:S(2)}, u32[]{:S(2)}) collective-permute-start(bf16[64,5760]{1,0:T(8,128)(2,1)S(1)} %get-tuple-element.77), channel_id=1, source_target_pairs={{0,1},{2,0},{4,2},{6,4},{7,6},{5,7},{3,5},{1,3},{8,9},{10,8},{12,1... | collective-permute-start | bytes 2211848 | tf_op jit(solution)/shard_map/ppermute | solution.py:500
  66.0 16.0 %collective-permute-start.9 = (bf16[64,5632]{1,0:T(8,128)(2,1)S(1)}, bf16[64,5632]{1,0:T(8,128)(2,1)S(1)}, u32[]{:S(2)}, u32[]{:S(2)}) collective-permute-start(bf16[64,5632]{1,0:T(8,128)(2,1)S(1)} %get-tuple-element.76), channel_id=1, source_target_pairs={{0,2},{2,4},{4,6},{6,7},{7,5},{5,3},{3,1},{1,0},{8,10},{10,12},{12... | collective-permute-start | bytes 2162696 | tf_op jit(solution)/shard_map/ppermute | solution.py:500
  82.1 9.2 %collective-permute-start.14 = (bf16[64,3072]{1,0:T(8,128)(2,1)S(1)}, bf16[64,3072]{1,0:T(8,128)(2,1)S(1)}, u32[]{:S(2)}, u32[]{:S(2)}) collective-permute-start(bf16[64,3072]{1,0:T(8,128)(2,1)S(1)} %get-tuple-element.86), channel_id=1, source_target_pairs={{0,16},{8,24},{16,0},{24,8},{1,17},{9,25},{17,1},{25,9},{2,18},{10... | collective-permute-start | bytes 1179656 | tf_op jit(solution)/shard_map/ppermute | solution.py:506
  83.3 6.4 %collective-permute-start.12 = (bf16[64,2048]{1,0:T(8,128)(2,1)S(1)}, bf16[64,2048]{1,0:T(8,128)(2,1)S(1)}, u32[]{:S(2)}, u32[]{:S(2)}) collective-permute-start(bf16[64,2048]{1,0:T(8,128)(2,1)S(1)} %get-tuple-element.84), channel_id=1, source_target_pairs={{0,2},{2,4},{4,6},{6,7},{7,5},{5,3},{3,1},{1,0},{8,10},{10,12},{12... | collective-permute-start | bytes 786440 | tf_op jit(solution)/shard_map/ppermute | solution.py:500
  84.8 2.8 %copy-start.3 = (bf16[64,3200]{1,0:T(8,128)(2,1)S(1)}, bf16[64,3200]{1,0:T(8,128)(2,1)}, u32[]{:S(2)}) copy-start(bf16[64,3200]{1,0:T(8,128)(2,1)} %get-tuple-element.57.refs_0_) | copy-start | bytes 1228804
  84.8 6.4 %collective-permute-start.13 = (bf16[64,2048]{1,0:T(8,128)(2,1)S(1)}, bf16[64,2048]{1,0:T(8,128)(2,1)S(1)}, u32[]{:S(2)}, u32[]{:S(2)}) collective-permute-start(bf16[64,2048]{1,0:T(8,128)(2,1)S(1)} %get-tuple-element.85), channel_id=1, source_target_pairs={{0,1},{2,0},{4,2},{6,4},{7,6},{5,7},{3,5},{1,3},{8,9},{10,8},{12,1... | collective-permute-start | bytes 786440 | tf_op jit(solution)/shard_map/ppermute | solution.py:500
  85.3 7.8 %collective-permute-start.16 = (f32[288,128]{1,0:T(8,128)S(1)}, f32[288,128]{1,0:T(8,128)S(1)}, u32[]{:S(2)}, u32[]{:S(2)}) collective-permute-start(f32[288,128]{1,0:T(8,128)S(1)} %get-tuple-element.94.refs_1_), channel_id=1, source_target_pairs={{0,8},{8,0},{16,24},{24,16},{1,9},{9,1},{17,25},{25,17},{2,10},{10... | collective-permute-start | bytes 442376 | tf_op jit(solution)/shard_map/ppermute | solution.py:503
  87.0 6.0 %collective-permute-start.18 = (f32[288,128]{1,0:T(8,128)S(1)}, f32[288,128]{1,0:T(8,128)S(1)}, u32[]{:S(2)}, u32[]{:S(2)}) collective-permute-start(f32[288,128]{1,0:T(8,128)S(1)} %get-tuple-element.97.refs_3_), channel_id=1, source_target_pairs={{0,8},{8,0},{16,24},{24,16},{1,9},{9,1},{17,25},{25,17},{2,10},{10... | collective-permute-start | bytes 442376 | tf_op jit(solution)/shard_map/ppermute | solution.py:503
  87.6 3.6 %copy-start.4 = (bf16[64,3072]{1,0:T(8,128)(2,1)S(1)}, bf16[64,3072]{1,0:T(8,128)(2,1)}, u32[]{:S(2)}) copy-start(bf16[64,3072]{1,0:T(8,128)(2,1)} %get-tuple-element.91.refs_5_) | copy-start | bytes 1179652
  89.6 3.4 %collective-permute-start.17 = (f32[288,128]{1,0:T(8,128)S(1)}, f32[288,128]{1,0:T(8,128)S(1)}, u32[]{:S(2)}, u32[]{:S(2)}) collective-permute-start(f32[288,128]{1,0:T(8,128)S(1)} %get-tuple-element.95.refs_2_), channel_id=1, source_target_pairs={{0,8},{8,0},{16,24},{24,16},{1,9},{9,1},{17,25},{25,17},{2,10},{10... | collective-permute-start | bytes 442376 | tf_op jit(solution)/shard_map/ppermute | solution.py:503
  92.5 1.4 %collective-permute-start.15 = (f32[288,128]{1,0:T(8,128)S(1)}, f32[288,128]{1,0:T(8,128)S(1)}, u32[]{:S(2)}, u32[]{:S(2)}) collective-permute-start(f32[288,128]{1,0:T(8,128)S(1)} %get-tuple-element.93.refs_0_), channel_id=1, source_target_pairs={{0,8},{8,0},{16,24},{24,16},{1,9},{9,1},{17,25},{25,17},{2,10},{10... | collective-permute-start | bytes 442376 | tf_op jit(solution)/shard_map/ppermute | solution.py:503
  92.5 7.6 %collective-permute-start.28 = (bf16[128,1280]{1,0:T(8,128)(2,1)S(1)}, bf16[128,1280]{1,0:T(8,128)(2,1)S(1)}, u32[]{:S(2)}, u32[]{:S(2)}) collective-permute-start(bf16[128,1280]{1,0:T(8,128)(2,1)S(1)} %get-tuple-element.101.refs_9_), channel_id=1, source_target_pairs={{0,8},{8,0},{16,24},{24,16},{1,9},{9,1},{17,25},{25,17},{2,10},{10... | collective-permute-start | bytes 983048 | tf_op jit(solution)/shard_map/ppermute | solution.py:503
  94.2 3.8 %collective-permute-start.19 = (f32[8,512]{1,0:T(8,128)S(1)}, f32[8,512]{1,0:T(8,128)S(1)}, u32[]{:S(2)}, u32[]{:S(2)}) collective-permute-start(f32[8,512]{1,0:T(8,128)S(1)} %get-tuple-element.99.refs_0_), channel_id=1, source_target_pairs={{0,16},{8,24},{16,0},{24,8},{1,17},{9,25},{17,1},{25,9},{2,18},{10... | collective-permute-start | bytes 49160 | tf_op jit(solution)/shard_map/ppermute | solution.py:600
  94.9 10.5 %collective-permute-start.30 = (bf16[128,1280]{1,0:T(8,128)(2,1)S(1)}, bf16[128,1280]{1,0:T(8,128)(2,1)S(1)}, u32[]{:S(2)}, u32[]{:S(2)}) collective-permute-start(bf16[128,1280]{1,0:T(8,128)(2,1)S(1)} %get-tuple-element.103.refs_11_), channel_id=1, source_target_pairs={{0,8},{8,0},{16,24},{24,16},{1,9},{9,1},{17,25},{25,17},{2,10},{10... | collective-permute-start | bytes 983048 | tf_op jit(solution)/shard_map/ppermute | solution.py:503
  98.0 5.4 %collective-permute-start.24 = (bf16[160,512]{1,0:T(8,128)(2,1)S(1)}, bf16[160,512]{1,0:T(8,128)(2,1)S(1)}, u32[]{:S(2)}, u32[]{:S(2)}) collective-permute-start(bf16[160,512]{1,0:T(8,128)(2,1)S(1)} %payload.1.refs_0_), channel_id=1, source_target_pairs={{0,1},{2,0},{4,2},{6,4},{7,6},{5,7},{3,5},{1,3},{8,9},{10,8},{12,1... | collective-permute-start | bytes 491528 | tf_op jit(solution)/shard_map/ppermute | solution.py:500
  98.6 5.3 %collective-permute-start.20 = (bf16[160,512]{1,0:T(8,128)(2,1)S(1)}, bf16[160,512]{1,0:T(8,128)(2,1)S(1)}, u32[]{:S(2)}, u32[]{:S(2)}) collective-permute-start(bf16[160,512]{1,0:T(8,128)(2,1)S(1)} %payload.1.refs_0_), channel_id=1, source_target_pairs={{0,2},{2,4},{4,6},{6,7},{7,5},{5,3},{3,1},{1,0},{8,10},{10,12},{12... | collective-permute-start | bytes 491528 | tf_op jit(solution)/shard_map/ppermute | solution.py:500
  100.1 15.2 %collective-permute-start.29 = (bf16[128,1280]{1,0:T(8,128)(2,1)S(1)}, bf16[128,1280]{1,0:T(8,128)(2,1)S(1)}, u32[]{:S(2)}, u32[]{:S(2)}) collective-permute-start(bf16[128,1280]{1,0:T(8,128)(2,1)S(1)} %get-tuple-element.102.refs_10_), channel_id=1, source_target_pairs={{0,8},{8,0},{16,24},{24,16},{1,9},{9,1},{17,25},{25,17},{2,10},{10... | collective-permute-start | bytes 983048 | tf_op jit(solution)/shard_map/ppermute | solution.py:503
  100.1 15.5 %collective-permute-start.27 = (bf16[128,1280]{1,0:T(8,128)(2,1)S(1)}, bf16[128,1280]{1,0:T(8,128)(2,1)S(1)}, u32[]{:S(2)}, u32[]{:S(2)}) collective-permute-start(bf16[128,1280]{1,0:T(8,128)(2,1)S(1)} %get-tuple-element.100.refs_8_), channel_id=1, source_target_pairs={{0,8},{8,0},{16,24},{24,16},{1,9},{9,1},{17,25},{25,17},{2,10},{10... | collective-permute-start | bytes 983048 | tf_op jit(solution)/shard_map/ppermute | solution.py:503
  103.4 8.0 %collective-permute-start.25 = (bf16[160,512]{1,0:T(8,128)(2,1)S(1)}, bf16[160,512]{1,0:T(8,128)(2,1)S(1)}, u32[]{:S(2)}, u32[]{:S(2)}) collective-permute-start(bf16[160,512]{1,0:T(8,128)(2,1)S(1)} %collective-permute-done.24.refs_7_), channel_id=1, source_target_pairs={{0,1},{2,0},{4,2},{6,4},{7,6},{5,7},{3,5},{1,3},{8,9},{10,8},{12,1... | collective-permute-start | bytes 491528 | tf_op jit(solution)/shard_map/ppermute | solution.py:500
  103.9 7.5 %collective-permute-start.21 = (bf16[160,512]{1,0:T(8,128)(2,1)S(1)}, bf16[160,512]{1,0:T(8,128)(2,1)S(1)}, u32[]{:S(2)}, u32[]{:S(2)}) collective-permute-start(bf16[160,512]{1,0:T(8,128)(2,1)S(1)} %collective-permute-done.20.refs_1_), channel_id=1, source_target_pairs={{0,2},{2,4},{4,6},{6,7},{7,5},{5,3},{3,1},{1,0},{8,10},{10,12},{12... | collective-permute-start | bytes 491528 | tf_op jit(solution)/shard_map/ppermute | solution.py:500
  105.4 10.2 %collective-permute-start.23 = (bf16[160,512]{1,0:T(8,128)(2,1)S(1)}, bf16[160,512]{1,0:T(8,128)(2,1)S(1)}, u32[]{:S(2)}, u32[]{:S(2)}) collective-permute-start(bf16[160,512]{1,0:T(8,128)(2,1)S(1)} %payload.1.refs_0_), channel_id=1, source_target_pairs={{0,7},{2,5},{4,3},{6,1},{7,0},{5,2},{3,4},{1,6},{8,15},{10,13},{12... | collective-permute-start | bytes 491528 | tf_op jit(solution)/shard_map/ppermute | solution.py:500
  111.4 7.2 %collective-permute-start.26 = (bf16[160,512]{1,0:T(8,128)(2,1)S(1)}, bf16[160,512]{1,0:T(8,128)(2,1)S(1)}, u32[]{:S(2)}, u32[]{:S(2)}) collective-permute-start(bf16[160,512]{1,0:T(8,128)(2,1)S(1)} %collective-permute-done.25.refs_6_), channel_id=1, source_target_pairs={{0,1},{2,0},{4,2},{6,4},{7,6},{5,7},{3,5},{1,3},{8,9},{10,8},{12,1... | collective-permute-start | bytes 491528 | tf_op jit(solution)/shard_map/ppermute | solution.py:500
  111.4 7.2 %collective-permute-start.22 = (bf16[160,512]{1,0:T(8,128)(2,1)S(1)}, bf16[160,512]{1,0:T(8,128)(2,1)S(1)}, u32[]{:S(2)}, u32[]{:S(2)}) collective-permute-start(bf16[160,512]{1,0:T(8,128)(2,1)S(1)} %collective-permute-done.21.refs_2_), channel_id=1, source_target_pairs={{0,2},{2,4},{4,6},{6,7},{7,5},{5,3},{3,1},{1,0},{8,10},{10,12},{12... | collective-permute-start | bytes 491528 | tf_op jit(solution)/shard_map/ppermute | solution.py:500

commit v6 on v5

--- a/solution.py
+++ b/solution.py
@@ -410,6 +410,15 @@
     out_ref[rows:, :] = jnp.concatenate(levels, axis=0).astype(BF16)
 
 
+def payload_rows(n, payloads, d, held):
+    if d == n // 2:
+        row = jnp.concatenate([ref[held, :] for ref in payloads[n - 1 :]], axis=1)
+    else:
+        row = payloads[d - int(d > n // 2)][held, :]
+    row = row.astype(F32)
+    return pltpu.roll(row, row.shape[1] // n * d, 1) if d else row
+
+
 def scale_posteriors(n, rows, cycle, payloads, posterior, evidence_ref):
     owner = lax.axis_index("ori")
     spot = sum(jnp.where(owner == o, cycle.index(o), 0) for o in range(n))
@@ -417,9 +426,8 @@
     per = width // n
     tops, sums = [], []
     for d in range(n):
-        stat = payloads[d][rows:, :].astype(F32)
-        stat = jnp.concatenate([stat[0:2] + stat[2:4] + stat[4:6], jnp.zeros((6, width), F32)], axis=0)
-        stat = pltpu.roll(stat, per * d, 1) if d else stat
+        stat = payload_rows(n, payloads, d, slice(rows, rows + TAIL))
+        stat = stat[0:2] + stat[2:4] + stat[4:6]
         tops.append(stat[0:1])
         sums.append(stat[1:2])
     best = functools.reduce(jnp.maximum, tops)
@@ -427,8 +435,7 @@
     total = functools.reduce(lambda a, b: a + b, [s * g for s, g in zip(sums, grow, strict=True)])
     evidence_ref[...] = (best + jnp.log(total))[:, :per]
     for d in range(n):
-        wide = payloads[d][:rows, :].astype(F32)
-        wide = pltpu.roll(wide, per * d, 1) if d else wide
+        wide = payload_rows(n, payloads, d, slice(0, rows))
         back = lax.rem(spot + (n - d), n)
         block = sum(jnp.where(back == p, cycle[p], 0) for p in range(n))
         row = pl.multiple_of(block * rows, 16)
@@ -442,7 +449,7 @@
 
 
 def stream_kernel(n, rows, cycle, *refs):
-    payloads, refs = refs[:n], refs[n:]
+    payloads, refs = refs[: n + 1], refs[n + 1 :]
     groups = n // 2
     halves = (refs[:groups], refs[groups : 2 * groups])
     out_hbm, evidence_ref, posterior, held, sems = refs[2 * groups :]
@@ -465,7 +472,7 @@
 
 
 def sums_kernel(n, rows, cycle, *refs):
-    payloads, refs = refs[:n], refs[n:]
+    payloads, refs = refs[: n + 1], refs[n + 1 :]
     w, (out_ref, evidence_ref, posterior) = refs[:-3], refs[-3:]
     step = pl.program_id(0)
 
@@ -545,7 +552,7 @@
         parts[s], slices[s] = group_scores(keep, mates, bias, kinds, wo, ws)
         if s < far - 2:
             (x_in,) = pack([f, b], [(2 * rows, n * wo)], [[(0, every, cross_cols, 0, 0), (1, every, cross_cols, rows, 0)]])
-    half_o, half_s = n // 2 * wo, n // 2 * ws
+    half_o, half_s = (n // 2 + 2) * wo, n // 2 * ws
     rest_o = plane_w - half_o
     x_in, f, b = pack(
         [f, b],
@@ -609,10 +616,14 @@
     )(scores, *all_stats)
     payloads = [payload] + [None] * (n - 1)
     fp = bp = payload
-    payloads[far] = ring(payload, far)
     for d in range(1, far):
         fp = payloads[d] = ring(fp, 1)
         bp = payloads[n - d] = ring(bp, -1)
+    tall, half_w = ori_rows + TAIL, width // 2
+    every_row = slice(0, tall)
+    (fp,) = pack([payloads[far - 2]], [(tall, half_w)], [[(0, every_row, slice(0, half_w), 0, 0)]])
+    (bp,) = pack([payloads[far + 2]], [(tall, half_w)], [[(0, every_row, slice(half_w, width), 0, 0)]])
+    payloads = payloads[:far] + payloads[far + 1 :] + [ring(fp, 2), ring(bp, -2)]
 
     out_shape = [jax.ShapeDtypeStruct((n * ori_rows, 2 * half), BF16), jax.ShapeDtypeStruct((1, rows), F32)]
     posterior = pltpu.VMEM((n * ori_rows, width), BF16)
@@ -620,7 +631,7 @@
         w = slices + other_slices
         sums, evidence = pl.pallas_call(
             functools.partial(stream_kernel, n, ori_rows, cycle),
-            in_specs=[vmem] * (n + len(w)),
+            in_specs=[vmem] * (len(payloads) + len(w)),
             out_specs=[pl.BlockSpec(memory_space=pl.ANY), vmem],
             out_shape=out_shape,
             scratch_shapes=[posterior, pltpu.VMEM(out_shape[0].shape, BF16), pltpu.SemaphoreType.DMA((2 * CHUNKS,))],

time: 124 us -> 124 us (level)
  starting transfers between devices: 30.5 us -> 28.6 us
  waiting for transfers between devices: 64.2 us -> 66.1 us
    ppermute x4, waiting for transfers between devices: 29 us -> 31.1 us  [cross(): return lax.ppermute(x, 'cls', [(i, i ^ 2) for i in range(n_cls)])]
    ppermute x17 -> x18, starting transfers between devices: 22.2 us -> 20.1 us  [ring(): lax.ppermute(x, 'ori', [(cycle[i], cycle[(i + d) % n]) for i in range(n)])]
    ppermute x17 -> x18, waiting for transfers between devices: 31.3 us -> 30.9 us  [ring(): lax.ppermute(x, 'ori', [(cycle[i], cycle[(i + d) % n]) for i in range(n)])]
  transfers between devices with their start and end apart: 31 -> 32, of which waited for: 17 -> 19; matrix products, arithmetic and copies ran while one was open for 0% -> 0% of each run, Pallas kernels for 15% -> 15%
where the time goes in v6:
time: 124 us
  waiting for transfers between devices  66.1 us (53%)
  starting transfers between devices  28.6 us (23%)
  Pallas kernels  26.4 us (21%)
  local copies, waits for them, and re-layouts  1.87 us (2%)
    ppermute x4, waiting for transfers between devices, cross(): return lax.ppermute(x, 'cls', [(i, i ^ 2) for i in range(n_cls)])  31.1 us
    ppermute x18, waiting for transfers between devices, ring(): lax.ppermute(x, 'ori', [(cycle[i], cycle[(i + d) % n]) for i in range(n)])  30.9 us
    ppermute x18, starting transfers between devices, ring(): lax.ppermute(x, 'ori', [(cycle[i], cycle[(i + d) % n]) for i in range(n)])  20.1 us
    pallas_call x4, Pallas kernels, group_scores(): pl.pallas_call(functools.partial(score_kernel, wo, ws, numbered, aligned,...  6.47 us
    ppermute x4, starting transfers between devices, cross(): return lax.ppermute(x, 'cls', [(i, i ^ 2) for i in range(n_cls)])  6.2 us
    pallas_call x1, Pallas kernels, prep_projections(): pl.pallas_call(functools.partial(split_kernel, wo, ws, n), in_specs=[pl.B...  5.9 us
    pallas_call x1, Pallas kernels, body(): pl.pallas_call(functools.partial(stream_kernel, n, ori_rows, cycle), in_s...  5.17 us
    pallas_call x1, Pallas kernels, prep_images(): pl.pallas_call(functools.partial(rest_kernel, n, wo, ws), in_specs=[somew...  3.21 us
  transfers between devices with their start and end apart: 32, of which 19 were waited for; matrix products, arithmetic and copies ran while one was open for 0% of the time, Pallas kernels for 15%

profile of v6, /device:TPU:0, one launch (start us, length us, event | category | flops | bytes accessed | tf_op | source)
XLA Modules:
  0.0 123.9 jit_solution(17085269904271595892)
XLA Ops:
  0.6 2.0 %prep_own_plane.1 = (bf16[64,3200]{1,0:T(8,128)(2,1)}, f32[160,128]{1,0:T(8,128)}) custom-call(bf16[64,20480]{1,0:T(8,128)(2,1)} %img_hbm.3, s32[160,128]{1,0:T(8,128)} %bitcast.5, f32[1,100]{1,0:T(1,128)} %bitcast.7, s32[4,64]{1,0:T(4,128)} %bitcast.6), custom_call_target="tpu_custom_call" | custom-call | tf_op jit(solution)/shard_map/prep_own_plane/pallas_call | solution.py:105
  2.7 3.0 %collective-permute-start.1 = (bf16[64,3200]{1,0:T(8,128)(2,1)}, bf16[64,3200]{1,0:T(8,128)(2,1)S(1)}, u32[]{:S(2)}, u32[]{:S(2)}) collective-permute-start(bf16[64,3200]{1,0:T(8,128)(2,1)} %get-tuple-element.57.refs_0_), channel_id=1, source_target_pairs={{0,1},{2,0},{4,2},{6,4},{7,6},{5,7},{3,5},{1,3},{8,9},{10,8},{12,1... | collective-permute-start | bytes 1228808 | tf_op jit(solution)/shard_map/ppermute | solution.py:507
  5.7 0.1 collective-permute-start
  5.8 3.2 %prep_rest.1 = (bf16[64,3072]{1,0:T(8,128)(2,1)}, bf16[64,4096]{1,0:T(8,128)(2,1)}) custom-call(bf16[64,20480]{1,0:T(8,128)(2,1)} %img_hbm.3, f32[160,128]{1,0:T(8,128)} %get-tuple-element.58.w_ref), custom_call_target="tpu_custom_call" | custom-call | tf_op jit(solution)/shard_map/prep_rest/pallas_call | solution.py:120
  9.1 5.9 %split_projections.1 = (bf16[144,10368]{1,0:T(8,128)(2,1)}, bf16[144,10368]{1,0:T(8,128)(2,1)}) custom-call(bf16[1,144,20480]{2,1,0:T(8,128)(2,1)} %proj_hbm), custom_call_target="tpu_custom_call" | custom-call | bytes 11796480 | tf_op jit(solution)/shard_map/split_projections/pallas_call | solution.py:207
  15.0 0.0 copy-start
  15.0 0.4 collective-permute-done.1.refs_1_
  15.4 1.4 %collective-permute-done.refs_0_ = bf16[64,3200]{1,0:T(8,128)(2,1)S(1)} collective-permute-done((bf16[64,3200]{1,0:T(8,128)(2,1)}, bf16[64,3200]{1,0:T(8,128)(2,1)S(1)}, u32[]{:S(2)}, u32[]{:S(2)}) %collective-permute-start) | collective-permute-done | bytes 409632 | tf_op jit(solution)/shard_map/ppermute | solution.py:507
  16.8 0.2 pack.6
  17.0 0.5 collective-permute-start.2
  17.5 1.6 %collective-permute-start.3 = (bf16[64,7296]{1,0:T(8,128)(2,1)S(1)}, bf16[64,7296]{1,0:T(8,128)(2,1)S(1)}, u32[]{:S(2)}, u32[]{:S(2)}) collective-permute-start(bf16[64,7296]{1,0:T(8,128)(2,1)S(1)} %get-tuple-element.65.refs_1_), channel_id=1, source_target_pairs={{0,1},{2,0},{4,2},{6,4},{7,6},{5,7},{3,5},{1,3},{8,9},{10,8},{12,1... | collective-permute-start | bytes 2801672 | tf_op jit(solution)/shard_map/ppermute | solution.py:507
  19.1 1.5 %collective-permute-start.4 = (bf16[128,3072]{1,0:T(8,128)(2,1)S(1)}, bf16[128,3072]{1,0:T(8,128)(2,1)S(1)}, u32[]{:S(2)}, u32[]{:S(2)}) collective-permute-start(bf16[128,3072]{1,0:T(8,128)(2,1)S(1)} %get-tuple-element.66), channel_id=1, source_target_pairs={{0,16},{8,24},{16,0},{24,8},{1,17},{9,25},{17,1},{25,9},{2,18},{10... | collective-permute-start | bytes 2359304 | tf_op jit(solution)/shard_map/ppermute | solution.py:513
  20.6 17.9 %collective-permute-done.4.refs_4_ = bf16[128,3072]{1,0:T(8,128)(2,1)S(1)} collective-permute-done((bf16[128,3072]{1,0:T(8,128)(2,1)S(1)}, bf16[128,3072]{1,0:T(8,128)(2,1)S(1)}, u32[]{:S(2)}, u32[]{:S(2)}) %collective-permute-start.4) | collective-permute-done | bytes 786464 | tf_op jit(solution)/shard_map/ppermute | solution.py:513
  38.5 1.7 %collective-permute-done.2.refs_0_.refs_2_ = bf16[64,7296]{1,0:T(8,128)(2,1)S(1)} collective-permute-done((bf16[64,7296]{1,0:T(8,128)(2,1)S(1)}, bf16[64,7296]{1,0:T(8,128)(2,1)S(1)}, u32[]{:S(2)}, u32[]{:S(2)}) %collective-permute-start.2) | collective-permute-done | bytes 933920 | tf_op jit(solution)/shard_map/ppermute | solution.py:507
  40.2 0.1 collective-permute-done.3.refs_1_.refs_3_
  40.3 1.7 %collective-permute-start.6 = (bf16[64,7296]{1,0:T(8,128)(2,1)S(1)}, bf16[64,7296]{1,0:T(8,128)(2,1)S(1)}, u32[]{:S(2)}, u32[]{:S(2)}) collective-permute-start(bf16[64,7296]{1,0:T(8,128)(2,1)S(1)} %collective-permute-done.2.refs_0_.refs_2_), channel_id=1, source_target_pairs={{0,2},{2,4},{4,6},{6,7},{7,5},{5,3},{3,1},{1,0},{8,10},{10,12},{12... | collective-permute-start | bytes 2801672 | tf_op jit(solution)/shard_map/ppermute | solution.py:507
  42.0 0.3 collective-permute-start.7
  42.3 0.1 pack.7
  42.4 1.7 %collective-permute-start.8 = (bf16[128,3072]{1,0:T(8,128)(2,1)S(1)}, bf16[128,3072]{1,0:T(8,128)(2,1)S(1)}, u32[]{:S(2)}, u32[]{:S(2)}) collective-permute-start(bf16[128,3072]{1,0:T(8,128)(2,1)S(1)} %pack.7), channel_id=1, source_target_pairs={{0,16},{8,24},{16,0},{24,8},{1,17},{9,25},{17,1},{25,9},{2,18},{10... | collective-permute-start | bytes 2359304 | tf_op jit(solution)/shard_map/ppermute | solution.py:513
  44.1 1.8 %copy-done.1 = bf16[144,10368]{1,0:T(8,128)(2,1)S(1)} copy-done((bf16[144,10368]{1,0:T(8,128)(2,1)S(1)}, bf16[144,10368]{1,0:T(8,128)(2,1)}, u32[]{:S(2)}) %copy-start.1) | copy-done | bytes 2986008
  45.9 2.2 %half_norms.1.bias_ref = f32[144,128]{1,0:T(8,128)S(1)} custom-call(bf16[144,10368]{1,0:T(8,128)(2,1)S(1)} %copy-done, bf16[144,10368]{1,0:T(8,128)(2,1)S(1)} %copy-done.1, f32[1,144]{1,0:T(1,128)S(1)} %copy-done.6, f32[160,128]{1,0:T(8,128)S(1)} %copy-done.5), custom_call_target="tpu_custom_call" | custom-call | flops 8847360 | bytes 5898240 | tf_op jit(solution)/shard_map/half_norms/pallas_call | solution.py:217
  48.1 1.7 %group_scores.4 = (f32[288,128]{1,0:T(8,128)S(1)}, bf16[128,1280]{1,0:T(8,128)(2,1)S(1)}) custom-call(bf16[144,10368]{1,0:T(8,128)(2,1)S(1)} %copy-done, bf16[144,10368]{1,0:T(8,128)(2,1)S(1)} %collective-permute-done.5.mate_ref, f32[144,128]{1,0:T(8,128)S(1)} %half_norms.1.bias_ref, bf16[64,7296]{1,0:T(8,128)(2,1)S(1)} %get-tuple-element.64.refs_0_, ...), custom_call_target="tpu_custom_call" | custom-call | flops 764411904 | bytes 8626176 | tf_op jit(solution)/shard_map/group_scores/pallas_call | solution.py:344
  49.9 11.1 %collective-permute-done.8.refs_4_ = bf16[128,3072]{1,0:T(8,128)(2,1)S(1)} collective-permute-done((bf16[128,3072]{1,0:T(8,128)(2,1)S(1)}, bf16[128,3072]{1,0:T(8,128)(2,1)S(1)}, u32[]{:S(2)}, u32[]{:S(2)}) %collective-permute-start.8) | collective-permute-done | bytes 786464 | tf_op jit(solution)/shard_map/ppermute | solution.py:513
  61.0 1.6 %collective-permute-done.6.refs_0_.refs_2_ = bf16[64,7296]{1,0:T(8,128)(2,1)S(1)} collective-permute-done((bf16[64,7296]{1,0:T(8,128)(2,1)S(1)}, bf16[64,7296]{1,0:T(8,128)(2,1)S(1)}, u32[]{:S(2)}, u32[]{:S(2)}) %collective-permute-start.6) | collective-permute-done | bytes 933920 | tf_op jit(solution)/shard_map/ppermute | solution.py:507
  62.5 1.2 collective-permute-done.7.refs_1_.refs_3_
  63.7 0.1 pack.8
  63.9 1.6 %collective-permute-start.9 = (bf16[64,6400]{1,0:T(8,128)(2,1)S(1)}, bf16[64,6400]{1,0:T(8,128)(2,1)S(1)}, u32[]{:S(2)}, u32[]{:S(2)}) collective-permute-start(bf16[64,6400]{1,0:T(8,128)(2,1)S(1)} %get-tuple-element.76), channel_id=1, source_target_pairs={{0,2},{2,4},{4,6},{6,7},{7,5},{5,3},{3,1},{1,0},{8,10},{10,12},{12... | collective-permute-start | bytes 2457608 | tf_op jit(solution)/shard_map/ppermute | solution.py:507
  65.5 1.5 %collective-permute-start.11 = (bf16[128,3072]{1,0:T(8,128)(2,1)S(1)}, bf16[128,3072]{1,0:T(8,128)(2,1)S(1)}, u32[]{:S(2)}, u32[]{:S(2)}) collective-permute-start(bf16[128,3072]{1,0:T(8,128)(2,1)S(1)} %get-tuple-element.78), channel_id=1, source_target_pairs={{0,16},{8,24},{16,0},{24,8},{1,17},{9,25},{17,1},{25,9},{2,18},{10... | collective-permute-start | bytes 2359304 | tf_op jit(solution)/shard_map/ppermute | solution.py:513
  67.0 0.4 collective-permute-start.10
  67.5 1.7 %group_scores.5 = (f32[288,128]{1,0:T(8,128)S(1)}, bf16[128,1280]{1,0:T(8,128)(2,1)S(1)}) custom-call(bf16[144,10368]{1,0:T(8,128)(2,1)S(1)} %copy-done, bf16[144,10368]{1,0:T(8,128)(2,1)S(1)} %collective-permute-done.5.mate_ref, f32[144,128]{1,0:T(8,128)S(1)} %half_norms.1.bias_ref, bf16[64,7296]{1,0:T(8,128)(2,1)S(1)} %collective-permute-done.2.refs_0_.refs_2_, ...), custom_call_target="tpu_custom_call" | custom-call | flops 764411904 | bytes 8626176 | tf_op jit(solution)/shard_map/group_scores/pallas_call | solution.py:344
  69.2 11.7 %collective-permute-done.10.refs_1_.refs_3_ = bf16[64,4992]{1,0:T(8,128)(2,1)S(1)} collective-permute-done((bf16[64,4992]{1,0:T(8,128)(2,1)S(1)}, bf16[64,4992]{1,0:T(8,128)(2,1)S(1)}, u32[]{:S(2)}, u32[]{:S(2)}) %collective-permute-start.10) | collective-permute-done | bytes 639008 | tf_op jit(solution)/shard_map/ppermute | solution.py:507
  80.9 2.1 %collective-permute-done.11.refs_4_ = bf16[128,3072]{1,0:T(8,128)(2,1)S(1)} collective-permute-done((bf16[128,3072]{1,0:T(8,128)(2,1)S(1)}, bf16[128,3072]{1,0:T(8,128)(2,1)S(1)}, u32[]{:S(2)}, u32[]{:S(2)}) %collective-permute-start.11) | collective-permute-done | bytes 786464 | tf_op jit(solution)/shard_map/ppermute | solution.py:513
  83.1 0.1 pack.9
  83.2 1.6 %collective-permute-start.14 = (bf16[64,3072]{1,0:T(8,128)(2,1)S(1)}, bf16[64,3072]{1,0:T(8,128)(2,1)S(1)}, u32[]{:S(2)}, u32[]{:S(2)}) collective-permute-start(bf16[64,3072]{1,0:T(8,128)(2,1)S(1)} %get-tuple-element.86), channel_id=1, source_target_pairs={{0,16},{8,24},{16,0},{24,8},{1,17},{9,25},{17,1},{25,9},{2,18},{10... | collective-permute-start | bytes 1179656 | tf_op jit(solution)/shard_map/ppermute | solution.py:513
  84.7 1.6 %collective-permute-start.12 = (bf16[64,2048]{1,0:T(8,128)(2,1)S(1)}, bf16[64,2048]{1,0:T(8,128)(2,1)S(1)}, u32[]{:S(2)}, u32[]{:S(2)}) collective-permute-start(bf16[64,2048]{1,0:T(8,128)(2,1)S(1)} %get-tuple-element.84), channel_id=1, source_target_pairs={{0,2},{2,4},{4,6},{6,7},{7,5},{5,3},{3,1},{1,0},{8,10},{10,12},{12... | collective-permute-start | bytes 786440 | tf_op jit(solution)/shard_map/ppermute | solution.py:507
  86.3 0.4 collective-permute-start.13
  86.7 1.7 %group_scores.7 = (f32[288,128]{1,0:T(8,128)S(1)}, bf16[128,1280]{1,0:T(8,128)(2,1)S(1)}) custom-call(bf16[144,10368]{1,0:T(8,128)(2,1)S(1)} %copy-done, bf16[144,10368]{1,0:T(8,128)(2,1)S(1)} %collective-permute-done.5.mate_ref, f32[144,128]{1,0:T(8,128)S(1)} %half_norms.1.bias_ref, bf16[64,7296]{1,0:T(8,128)(2,1)S(1)} %collective-permute-done.6.refs_0_.refs_2_, ...), custom_call_target="tpu_custom_call" | custom-call | flops 764411904 | bytes 8626176 | tf_op jit(solution)/shard_map/group_scores/pallas_call | solution.py:344
  88.5 0.6 collective-permute-start.18
  89.1 0.6 plane_scores.1.bias_ref
  89.7 1.4 %collective-permute-done.12.refs_3_ = bf16[64,2048]{1,0:T(8,128)(2,1)S(1)} collective-permute-done((bf16[64,2048]{1,0:T(8,128)(2,1)S(1)}, bf16[64,2048]{1,0:T(8,128)(2,1)S(1)}, u32[]{:S(2)}, u32[]{:S(2)}) %collective-permute-start.12) | collective-permute-done | bytes 262176 | tf_op jit(solution)/shard_map/ppermute | solution.py:507
  91.1 1.6 %collective-permute-done.13.refs_4_ = bf16[64,2048]{1,0:T(8,128)(2,1)S(1)} collective-permute-done((bf16[64,2048]{1,0:T(8,128)(2,1)S(1)}, bf16[64,2048]{1,0:T(8,128)(2,1)S(1)}, u32[]{:S(2)}, u32[]{:S(2)}) %collective-permute-start.13) | collective-permute-done | bytes 262176 | tf_op jit(solution)/shard_map/ppermute | solution.py:507
  92.7 1.2 group_scores.6
  93.9 0.1 collective-permute-start.15
  94.0 0.5 collective-permute-start.29
  94.5 0.8 collective-permute-done.15.refs_4_
  95.3 0.3 local_stats.1
  95.6 0.6 collective-permute-start.19
  96.2 3.2 %collective-permute-done.19.refs_1_ = f32[8,512]{1,0:T(8,128)S(1)} collective-permute-done((f32[8,512]{1,0:T(8,128)S(1)}, f32[8,512]{1,0:T(8,128)S(1)}, u32[]{:S(2)}, u32[]{:S(2)}) %collective-permute-start.19) | collective-permute-done | bytes 16416 | tf_op jit(solution)/shard_map/ppermute | solution.py:607
  99.4 0.1 payload.1.refs_0_
  99.5 0.5 collective-permute-start.23
  100.0 1.6 %collective-permute-start.20 = (bf16[160,512]{1,0:T(8,128)(2,1)S(1)}, bf16[160,512]{1,0:T(8,128)(2,1)S(1)}, u32[]{:S(2)}, u32[]{:S(2)}) collective-permute-start(bf16[160,512]{1,0:T(8,128)(2,1)S(1)} %payload.1.refs_0_), channel_id=1, source_target_pairs={{0,2},{2,4},{4,6},{6,7},{7,5},{5,3},{3,1},{1,0},{8,10},{10,12},{12... | collective-permute-start | bytes 491528 | tf_op jit(solution)/shard_map/ppermute | solution.py:507
  101.6 0.5 collective-permute-start.30
  102.1 2.8 %collective-permute-done.23.refs_6_ = bf16[160,512]{1,0:T(8,128)(2,1)S(1)} collective-permute-done((bf16[160,512]{1,0:T(8,128)(2,1)S(1)}, bf16[160,512]{1,0:T(8,128)(2,1)S(1)}, u32[]{:S(2)}, u32[]{:S(2)}) %collective-permute-start.23) | collective-permute-done | bytes 163872 | tf_op jit(solution)/shard_map/ppermute | solution.py:507
  104.8 0.5 collective-permute-start.24
  105.3 1.6 %collective-permute-start.21 = (bf16[160,512]{1,0:T(8,128)(2,1)S(1)}, bf16[160,512]{1,0:T(8,128)(2,1)S(1)}, u32[]{:S(2)}, u32[]{:S(2)}) collective-permute-start(bf16[160,512]{1,0:T(8,128)(2,1)S(1)} %collective-permute-done.20.refs_1_), channel_id=1, source_target_pairs={{0,2},{2,4},{4,6},{6,7},{7,5},{5,3},{3,1},{1,0},{8,10},{10,12},{12... | collective-permute-start | bytes 491528 | tf_op jit(solution)/shard_map/ppermute | solution.py:507
  106.9 4.0 %collective-permute-done.24.refs_0_.refs_5_ = bf16[160,512]{1,0:T(8,128)(2,1)S(1)} collective-permute-done((bf16[160,512]{1,0:T(8,128)(2,1)S(1)}, bf16[160,512]{1,0:T(8,128)(2,1)S(1)}, u32[]{:S(2)}, u32[]{:S(2)}) %collective-permute-start.24) | collective-permute-done | bytes 163872 | tf_op jit(solution)/shard_map/ppermute | solution.py:507
  110.9 0.5 collective-permute-start.25
  111.3 0.3 collective-permute-done.21.refs_0_.refs_2_
  111.6 1.3 %collective-permute-start.22 = (bf16[160,512]{1,0:T(8,128)(2,1)S(1)}, bf16[160,512]{1,0:T(8,128)(2,1)S(1)}, u32[]{:S(2)}, u32[]{:S(2)}) collective-permute-start(bf16[160,512]{1,0:T(8,128)(2,1)S(1)} %collective-permute-done.21.refs_0_.refs_2_), channel_id=1, source_target_pairs={{0,2},{2,4},{4,6},{6,7},{7,5},{5,3},{3,1},{1,0},{8,10},{10,12},{12... | collective-permute-start | bytes 491528 | tf_op jit(solution)/shard_map/ppermute | solution.py:507
  112.9 0.3 collective-permute-start.27
  113.2 2.7 %collective-permute-start.26 = (bf16[160,256]{1,0:T(8,128)(2,1)S(1)}, bf16[160,256]{1,0:T(8,128)(2,1)S(1)}, u32[]{:S(2)}, u32[]{:S(2)}) collective-permute-start(bf16[160,256]{1,0:T(8,128)(2,1)S(1)} %pack.10), channel_id=1, source_target_pairs={{0,4},{2,6},{4,7},{6,5},{7,3},{5,1},{3,0},{1,2},{8,12},{10,14},{12... | collective-permute-start | bytes 245768 | tf_op jit(solution)/shard_map/ppermute | solution.py:507
  115.9 2.5 %collective-permute-done.27.refs_8_ = bf16[160,256]{1,0:T(8,128)(2,1)S(1)} collective-permute-done((bf16[160,256]{1,0:T(8,128)(2,1)S(1)}, bf16[160,256]{1,0:T(8,128)(2,1)S(1)}, u32[]{:S(2)}, u32[]{:S(2)}) %collective-permute-start.27) | collective-permute-done | bytes 81952 | tf_op jit(solution)/shard_map/ppermute | solution.py:507
  118.4 0.2 collective-permute-done.26.refs_7_
  118.6 5.2 %class_sums.1 = (bf16[1152,2560]{1,0:T(8,128)(2,1)}, f32[1,64]{1,0:T(1,128)}) custom-call(bf16[160,512]{1,0:T(8,128)(2,1)S(1)} %payload.1.refs_0_, bf16[160,512]{1,0:T(8,128)(2,1)S(1)} %collective-permute-done.20.refs_1_, bf16[160,512]{1,0:T(8,128)(2,1)S(1)} %collective-permute-done.21.refs_0_.refs_2_, bf16[160,512]{1,0:T(8,128)(2,1)S(1)} %collective-permute-done.22.refs_3_, ...), custom_call_target="tpu_custom_call" | custom-call | tf_op jit(solution)/shard_map/class_sums/pallas_call | solution.py:632
  (32 shorter events, 0.1 us)
Async XLA Ops:
  2.7 12.8 %collective-permute-start.1 = (bf16[64,3200]{1,0:T(8,128)(2,1)}, bf16[64,3200]{1,0:T(8,128)(2,1)S(1)}, u32[]{:S(2)}, u32[]{:S(2)}) collective-permute-start(bf16[64,3200]{1,0:T(8,128)(2,1)} %get-tuple-element.57.refs_0_), channel_id=1, source_target_pairs={{0,1},{2,0},{4,2},{6,4},{7,6},{5,7},{3,5},{1,3},{8,9},{10,8},{12,1... | collective-permute-start | bytes 1228808 | tf_op jit(solution)/shard_map/ppermute | solution.py:507
  5.7 11.1 %collective-permute-start = (bf16[64,3200]{1,0:T(8,128)(2,1)}, bf16[64,3200]{1,0:T(8,128)(2,1)S(1)}, u32[]{:S(2)}, u32[]{:S(2)}) collective-permute-start(bf16[64,3200]{1,0:T(8,128)(2,1)} %get-tuple-element.57.refs_0_), channel_id=1, source_target_pairs={{0,2},{2,4},{4,6},{6,7},{7,5},{5,3},{3,1},{1,0},{8,10},{10,12},{12... | collective-permute-start | bytes 1228808 | tf_op jit(solution)/shard_map/ppermute | solution.py:507
  9.0 7.8 %copy-start.2 = (bf16[64,4096]{1,0:T(8,128)(2,1)S(1)}, bf16[64,4096]{1,0:T(8,128)(2,1)}, u32[]{:S(2)}) copy-start(bf16[64,4096]{1,0:T(8,128)(2,1)} %get-tuple-element.63.refs_2_) | copy-start | bytes 1572868
  15.0 29.1 %copy-start = (bf16[144,10368]{1,0:T(8,128)(2,1)S(1)}, bf16[144,10368]{1,0:T(8,128)(2,1)}, u32[]{:S(2)}) copy-start(bf16[144,10368]{1,0:T(8,128)(2,1)} %get-tuple-element.56.keep_ref.own_ref) | copy-start | bytes 8957956
  15.0 29.1 %copy-start.5 = (f32[160,128]{1,0:T(8,128)S(1)}, f32[160,128]{1,0:T(8,128)}, u32[]{:S(2)}) copy-start(f32[160,128]{1,0:T(8,128)} %get-tuple-element.58.w_ref) | copy-start | bytes 245764
  15.0 29.1 %copy-start.6 = (f32[1,144]{1,0:T(1,128)S(1)}, f32[1,144]{1,0:T(1,128)}, u32[]{:S(2)}) copy-start(f32[1,144]{1,0:T(1,128)} %prior_ref.1) | copy-start | bytes 1732
  16.8 23.5 %collective-permute-start.5 = (bf16[144,10368]{1,0:T(8,128)(2,1)}, bf16[144,10368]{1,0:T(8,128)(2,1)S(1)}, u32[]{:S(2)}, u32[]{:S(2)}) collective-permute-start(bf16[144,10368]{1,0:T(8,128)(2,1)} %get-tuple-element.67.send_ref), channel_id=1, source_target_pairs={{0,8},{8,0},{16,24},{24,16},{1,9},{9,1},{17,25},{25,17},{2,10},{10... | collective-permute-start | bytes 8957960 | tf_op jit(solution)/shard_map/ppermute | solution.py:510
  17.0 23.2 %collective-permute-start.2 = (bf16[64,7296]{1,0:T(8,128)(2,1)S(1)}, bf16[64,7296]{1,0:T(8,128)(2,1)S(1)}, u32[]{:S(2)}, u32[]{:S(2)}) collective-permute-start(bf16[64,7296]{1,0:T(8,128)(2,1)S(1)} %get-tuple-element.64.refs_0_), channel_id=1, source_target_pairs={{0,2},{2,4},{4,6},{6,7},{7,5},{5,3},{3,1},{1,0},{8,10},{10,12},{12... | collective-permute-start | bytes 2801672 | tf_op jit(solution)/shard_map/ppermute | solution.py:507
  17.5 22.8 %collective-permute-start.3 = (bf16[64,7296]{1,0:T(8,128)(2,1)S(1)}, bf16[64,7296]{1,0:T(8,128)(2,1)S(1)}, u32[]{:S(2)}, u32[]{:S(2)}) collective-permute-start(bf16[64,7296]{1,0:T(8,128)(2,1)S(1)} %get-tuple-element.65.refs_1_), channel_id=1, source_target_pairs={{0,1},{2,0},{4,2},{6,4},{7,6},{5,7},{3,5},{1,3},{8,9},{10,8},{12,1... | collective-permute-start | bytes 2801672 | tf_op jit(solution)/shard_map/ppermute | solution.py:507
  19.1 19.4 %collective-permute-start.4 = (bf16[128,3072]{1,0:T(8,128)(2,1)S(1)}, bf16[128,3072]{1,0:T(8,128)(2,1)S(1)}, u32[]{:S(2)}, u32[]{:S(2)}) collective-permute-start(bf16[128,3072]{1,0:T(8,128)(2,1)S(1)} %get-tuple-element.66), channel_id=1, source_target_pairs={{0,16},{8,24},{16,0},{24,8},{1,17},{9,25},{17,1},{25,9},{2,18},{10... | collective-permute-start | bytes 2359304 | tf_op jit(solution)/shard_map/ppermute | solution.py:513
  40.3 22.2 %collective-permute-start.6 = (bf16[64,7296]{1,0:T(8,128)(2,1)S(1)}, bf16[64,7296]{1,0:T(8,128)(2,1)S(1)}, u32[]{:S(2)}, u32[]{:S(2)}) collective-permute-start(bf16[64,7296]{1,0:T(8,128)(2,1)S(1)} %collective-permute-done.2.refs_0_.refs_2_), channel_id=1, source_target_pairs={{0,2},{2,4},{4,6},{6,7},{7,5},{5,3},{3,1},{1,0},{8,10},{10,12},{12... | collective-permute-start | bytes 2801672 | tf_op jit(solution)/shard_map/ppermute | solution.py:507
  42.0 21.7 %collective-permute-start.7 = (bf16[64,7296]{1,0:T(8,128)(2,1)S(1)}, bf16[64,7296]{1,0:T(8,128)(2,1)S(1)}, u32[]{:S(2)}, u32[]{:S(2)}) collective-permute-start(bf16[64,7296]{1,0:T(8,128)(2,1)S(1)} %collective-permute-done.3.refs_1_.refs_3_), channel_id=1, source_target_pairs={{0,1},{2,0},{4,2},{6,4},{7,6},{5,7},{3,5},{1,3},{8,9},{10,8},{12,1... | collective-permute-start | bytes 2801672 | tf_op jit(solution)/shard_map/ppermute | solution.py:507
  42.4 18.6 %collective-permute-start.8 = (bf16[128,3072]{1,0:T(8,128)(2,1)S(1)}, bf16[128,3072]{1,0:T(8,128)(2,1)S(1)}, u32[]{:S(2)}, u32[]{:S(2)}) collective-permute-start(bf16[128,3072]{1,0:T(8,128)(2,1)S(1)} %pack.7), channel_id=1, source_target_pairs={{0,16},{8,24},{16,0},{24,8},{1,17},{9,25},{17,1},{25,9},{2,18},{10... | collective-permute-start | bytes 2359304 | tf_op jit(solution)/shard_map/ppermute | solution.py:513
  44.1 1.8 %copy-start.1 = (bf16[144,10368]{1,0:T(8,128)(2,1)S(1)}, bf16[144,10368]{1,0:T(8,128)(2,1)}, u32[]{:S(2)}) copy-start(bf16[144,10368]{1,0:T(8,128)(2,1)} %get-tuple-element.67.send_ref) | copy-start | bytes 8957956
  63.9 19.2 %collective-permute-start.9 = (bf16[64,6400]{1,0:T(8,128)(2,1)S(1)}, bf16[64,6400]{1,0:T(8,128)(2,1)S(1)}, u32[]{:S(2)}, u32[]{:S(2)}) collective-permute-start(bf16[64,6400]{1,0:T(8,128)(2,1)S(1)} %get-tuple-element.76), channel_id=1, source_target_pairs={{0,2},{2,4},{4,6},{6,7},{7,5},{5,3},{3,1},{1,0},{8,10},{10,12},{12... | collective-permute-start | bytes 2457608 | tf_op jit(solution)/shard_map/ppermute | solution.py:507
  65.5 17.5 %collective-permute-start.11 = (bf16[128,3072]{1,0:T(8,128)(2,1)S(1)}, bf16[128,3072]{1,0:T(8,128)(2,1)S(1)}, u32[]{:S(2)}, u32[]{:S(2)}) collective-permute-start(bf16[128,3072]{1,0:T(8,128)(2,1)S(1)} %get-tuple-element.78), channel_id=1, source_target_pairs={{0,16},{8,24},{16,0},{24,8},{1,17},{9,25},{17,1},{25,9},{2,18},{10... | collective-permute-start | bytes 2359304 | tf_op jit(solution)/shard_map/ppermute | solution.py:513
  67.0 13.9 %collective-permute-start.10 = (bf16[64,4992]{1,0:T(8,128)(2,1)S(1)}, bf16[64,4992]{1,0:T(8,128)(2,1)S(1)}, u32[]{:S(2)}, u32[]{:S(2)}) collective-permute-start(bf16[64,4992]{1,0:T(8,128)(2,1)S(1)} %get-tuple-element.77), channel_id=1, source_target_pairs={{0,1},{2,0},{4,2},{6,4},{7,6},{5,7},{3,5},{1,3},{8,9},{10,8},{12,1... | collective-permute-start | bytes 1916936 | tf_op jit(solution)/shard_map/ppermute | solution.py:507
  83.2 9.5 %collective-permute-start.14 = (bf16[64,3072]{1,0:T(8,128)(2,1)S(1)}, bf16[64,3072]{1,0:T(8,128)(2,1)S(1)}, u32[]{:S(2)}, u32[]{:S(2)}) collective-permute-start(bf16[64,3072]{1,0:T(8,128)(2,1)S(1)} %get-tuple-element.86), channel_id=1, source_target_pairs={{0,16},{8,24},{16,0},{24,8},{1,17},{9,25},{17,1},{25,9},{2,18},{10... | collective-permute-start | bytes 1179656 | tf_op jit(solution)/shard_map/ppermute | solution.py:513
  84.7 6.4 %collective-permute-start.12 = (bf16[64,2048]{1,0:T(8,128)(2,1)S(1)}, bf16[64,2048]{1,0:T(8,128)(2,1)S(1)}, u32[]{:S(2)}, u32[]{:S(2)}) collective-permute-start(bf16[64,2048]{1,0:T(8,128)(2,1)S(1)} %get-tuple-element.84), channel_id=1, source_target_pairs={{0,2},{2,4},{4,6},{6,7},{7,5},{5,3},{3,1},{1,0},{8,10},{10,12},{12... | collective-permute-start | bytes 786440 | tf_op jit(solution)/shard_map/ppermute | solution.py:507
  86.3 2.8 %copy-start.3 = (bf16[64,3200]{1,0:T(8,128)(2,1)S(1)}, bf16[64,3200]{1,0:T(8,128)(2,1)}, u32[]{:S(2)}) copy-start(bf16[64,3200]{1,0:T(8,128)(2,1)} %get-tuple-element.57.refs_0_) | copy-start | bytes 1228804
  86.3 6.4 %collective-permute-start.13 = (bf16[64,2048]{1,0:T(8,128)(2,1)S(1)}, bf16[64,2048]{1,0:T(8,128)(2,1)S(1)}, u32[]{:S(2)}, u32[]{:S(2)}) collective-permute-start(bf16[64,2048]{1,0:T(8,128)(2,1)S(1)} %get-tuple-element.85), channel_id=1, source_target_pairs={{0,1},{2,0},{4,2},{6,4},{7,6},{5,7},{3,5},{1,3},{8,9},{10,8},{12,1... | collective-permute-start | bytes 786440 | tf_op jit(solution)/shard_map/ppermute | solution.py:507
  86.7 7.8 %collective-permute-start.16 = (f32[288,128]{1,0:T(8,128)S(1)}, f32[288,128]{1,0:T(8,128)S(1)}, u32[]{:S(2)}, u32[]{:S(2)}) collective-permute-start(f32[288,128]{1,0:T(8,128)S(1)} %get-tuple-element.94.refs_1_), channel_id=1, source_target_pairs={{0,8},{8,0},{16,24},{24,16},{1,9},{9,1},{17,25},{25,17},{2,10},{10... | collective-permute-start | bytes 442376 | tf_op jit(solution)/shard_map/ppermute | solution.py:510
  88.5 6.0 %collective-permute-start.18 = (f32[288,128]{1,0:T(8,128)S(1)}, f32[288,128]{1,0:T(8,128)S(1)}, u32[]{:S(2)}, u32[]{:S(2)}) collective-permute-start(f32[288,128]{1,0:T(8,128)S(1)} %get-tuple-element.97.refs_3_), channel_id=1, source_target_pairs={{0,8},{8,0},{16,24},{24,16},{1,9},{9,1},{17,25},{25,17},{2,10},{10... | collective-permute-start | bytes 442376 | tf_op jit(solution)/shard_map/ppermute | solution.py:510
  89.1 3.6 %copy-start.4 = (bf16[64,3072]{1,0:T(8,128)(2,1)S(1)}, bf16[64,3072]{1,0:T(8,128)(2,1)}, u32[]{:S(2)}) copy-start(bf16[64,3072]{1,0:T(8,128)(2,1)} %get-tuple-element.91.refs_5_) | copy-start | bytes 1179652
  91.1 3.4 %collective-permute-start.17 = (f32[288,128]{1,0:T(8,128)S(1)}, f32[288,128]{1,0:T(8,128)S(1)}, u32[]{:S(2)}, u32[]{:S(2)}) collective-permute-start(f32[288,128]{1,0:T(8,128)S(1)} %get-tuple-element.95.refs_2_), channel_id=1, source_target_pairs={{0,8},{8,0},{16,24},{24,16},{1,9},{9,1},{17,25},{25,17},{2,10},{10... | collective-permute-start | bytes 442376 | tf_op jit(solution)/shard_map/ppermute | solution.py:510
  93.9 1.4 %collective-permute-start.15 = (f32[288,128]{1,0:T(8,128)S(1)}, f32[288,128]{1,0:T(8,128)S(1)}, u32[]{:S(2)}, u32[]{:S(2)}) collective-permute-start(f32[288,128]{1,0:T(8,128)S(1)} %get-tuple-element.93.refs_0_), channel_id=1, source_target_pairs={{0,8},{8,0},{16,24},{24,16},{1,9},{9,1},{17,25},{25,17},{2,10},{10... | collective-permute-start | bytes 442376 | tf_op jit(solution)/shard_map/ppermute | solution.py:510
  94.0 8.1 %collective-permute-start.29 = (bf16[128,1280]{1,0:T(8,128)(2,1)S(1)}, bf16[128,1280]{1,0:T(8,128)(2,1)S(1)}, u32[]{:S(2)}, u32[]{:S(2)}) collective-permute-start(bf16[128,1280]{1,0:T(8,128)(2,1)S(1)} %get-tuple-element.101.refs_10_), channel_id=1, source_target_pairs={{0,8},{8,0},{16,24},{24,16},{1,9},{9,1},{17,25},{25,17},{2,10},{10... | collective-permute-start | bytes 983048 | tf_op jit(solution)/shard_map/ppermute | solution.py:510
  95.6 3.8 %collective-permute-start.19 = (f32[8,512]{1,0:T(8,128)S(1)}, f32[8,512]{1,0:T(8,128)S(1)}, u32[]{:S(2)}, u32[]{:S(2)}) collective-permute-start(f32[8,512]{1,0:T(8,128)S(1)} %get-tuple-element.99.refs_0_), channel_id=1, source_target_pairs={{0,16},{8,24},{16,0},{24,8},{1,17},{9,25},{17,1},{25,9},{2,18},{10... | collective-permute-start | bytes 49160 | tf_op jit(solution)/shard_map/ppermute | solution.py:607
  99.5 5.4 %collective-permute-start.23 = (bf16[160,512]{1,0:T(8,128)(2,1)S(1)}, bf16[160,512]{1,0:T(8,128)(2,1)S(1)}, u32[]{:S(2)}, u32[]{:S(2)}) collective-permute-start(bf16[160,512]{1,0:T(8,128)(2,1)S(1)} %payload.1.refs_0_), channel_id=1, source_target_pairs={{0,1},{2,0},{4,2},{6,4},{7,6},{5,7},{3,5},{1,3},{8,9},{10,8},{12,1... | collective-permute-start | bytes 491528 | tf_op jit(solution)/shard_map/ppermute | solution.py:507
  100.0 5.3 %collective-permute-start.20 = (bf16[160,512]{1,0:T(8,128)(2,1)S(1)}, bf16[160,512]{1,0:T(8,128)(2,1)S(1)}, u32[]{:S(2)}, u32[]{:S(2)}) collective-permute-start(bf16[160,512]{1,0:T(8,128)(2,1)S(1)} %payload.1.refs_0_), channel_id=1, source_target_pairs={{0,2},{2,4},{4,6},{6,7},{7,5},{5,3},{3,1},{1,0},{8,10},{10,12},{12... | collective-permute-start | bytes 491528 | tf_op jit(solution)/shard_map/ppermute | solution.py:507
  101.5 11.4 %collective-permute-start.31 = (bf16[128,1280]{1,0:T(8,128)(2,1)S(1)}, bf16[128,1280]{1,0:T(8,128)(2,1)S(1)}, u32[]{:S(2)}, u32[]{:S(2)}) collective-permute-start(bf16[128,1280]{1,0:T(8,128)(2,1)S(1)} %get-tuple-element.103.refs_12_), channel_id=1, source_target_pairs={{0,8},{8,0},{16,24},{24,16},{1,9},{9,1},{17,25},{25,17},{2,10},{10... | collective-permute-start | bytes 983048 | tf_op jit(solution)/shard_map/ppermute | solution.py:510
  101.6 11.6 %collective-permute-start.30 = (bf16[128,1280]{1,0:T(8,128)(2,1)S(1)}, bf16[128,1280]{1,0:T(8,128)(2,1)S(1)}, u32[]{:S(2)}, u32[]{:S(2)}) collective-permute-start(bf16[128,1280]{1,0:T(8,128)(2,1)S(1)} %get-tuple-element.102.refs_11_), channel_id=1, source_target_pairs={{0,8},{8,0},{16,24},{24,16},{1,9},{9,1},{17,25},{25,17},{2,10},{10... | collective-permute-start | bytes 983048 | tf_op jit(solution)/shard_map/ppermute | solution.py:510
  102.1 13.8 %collective-permute-start.28 = (bf16[128,1280]{1,0:T(8,128)(2,1)S(1)}, bf16[128,1280]{1,0:T(8,128)(2,1)S(1)}, u32[]{:S(2)}, u32[]{:S(2)}) collective-permute-start(bf16[128,1280]{1,0:T(8,128)(2,1)S(1)} %get-tuple-element.100.refs_9_), channel_id=1, source_target_pairs={{0,8},{8,0},{16,24},{24,16},{1,9},{9,1},{17,25},{25,17},{2,10},{10... | collective-permute-start | bytes 983048 | tf_op jit(solution)/shard_map/ppermute | solution.py:510
  104.8 6.0 %collective-permute-start.24 = (bf16[160,512]{1,0:T(8,128)(2,1)S(1)}, bf16[160,512]{1,0:T(8,128)(2,1)S(1)}, u32[]{:S(2)}, u32[]{:S(2)}) collective-permute-start(bf16[160,512]{1,0:T(8,128)(2,1)S(1)} %collective-permute-done.23.refs_6_), channel_id=1, source_target_pairs={{0,1},{2,0},{4,2},{6,4},{7,6},{5,7},{3,5},{1,3},{8,9},{10,8},{12,1... | collective-permute-start | bytes 491528 | tf_op jit(solution)/shard_map/ppermute | solution.py:507
  105.3 6.3 %collective-permute-start.21 = (bf16[160,512]{1,0:T(8,128)(2,1)S(1)}, bf16[160,512]{1,0:T(8,128)(2,1)S(1)}, u32[]{:S(2)}, u32[]{:S(2)}) collective-permute-start(bf16[160,512]{1,0:T(8,128)(2,1)S(1)} %collective-permute-done.20.refs_1_), channel_id=1, source_target_pairs={{0,2},{2,4},{4,6},{6,7},{7,5},{5,3},{3,1},{1,0},{8,10},{10,12},{12... | collective-permute-start | bytes 491528 | tf_op jit(solution)/shard_map/ppermute | solution.py:507
  110.9 7.7 %collective-permute-start.25 = (bf16[160,512]{1,0:T(8,128)(2,1)S(1)}, bf16[160,512]{1,0:T(8,128)(2,1)S(1)}, u32[]{:S(2)}, u32[]{:S(2)}) collective-permute-start(bf16[160,512]{1,0:T(8,128)(2,1)S(1)} %collective-permute-done.24.refs_0_.refs_5_), channel_id=1, source_target_pairs={{0,1},{2,0},{4,2},{6,4},{7,6},{5,7},{3,5},{1,3},{8,9},{10,8},{12,1... | collective-permute-start | bytes 491528 | tf_op jit(solution)/shard_map/ppermute | solution.py:507
  111.6 6.9 %collective-permute-start.22 = (bf16[160,512]{1,0:T(8,128)(2,1)S(1)}, bf16[160,512]{1,0:T(8,128)(2,1)S(1)}, u32[]{:S(2)}, u32[]{:S(2)}) collective-permute-start(bf16[160,512]{1,0:T(8,128)(2,1)S(1)} %collective-permute-done.21.refs_0_.refs_2_), channel_id=1, source_target_pairs={{0,2},{2,4},{4,6},{6,7},{7,5},{5,3},{3,1},{1,0},{8,10},{10,12},{12... | collective-permute-start | bytes 491528 | tf_op jit(solution)/shard_map/ppermute | solution.py:507
  112.9 5.5 %collective-permute-start.27 = (bf16[160,256]{1,0:T(8,128)(2,1)S(1)}, bf16[160,256]{1,0:T(8,128)(2,1)S(1)}, u32[]{:S(2)}, u32[]{:S(2)}) collective-permute-start(bf16[160,256]{1,0:T(8,128)(2,1)S(1)} %pack.11), channel_id=1, source_target_pairs={{0,3},{2,1},{4,0},{6,2},{7,4},{5,6},{3,7},{1,5},{8,11},{10,9},{12,... | collective-permute-start | bytes 245768 | tf_op jit(solution)/shard_map/ppermute | solution.py:507
  113.2 5.4 %collective-permute-start.26 = (bf16[160,256]{1,0:T(8,128)(2,1)S(1)}, bf16[160,256]{1,0:T(8,128)(2,1)S(1)}, u32[]{:S(2)}, u32[]{:S(2)}) collective-permute-start(bf16[160,256]{1,0:T(8,128)(2,1)S(1)} %pack.10), channel_id=1, source_target_pairs={{0,4},{2,6},{4,7},{6,5},{7,3},{5,1},{3,0},{1,2},{8,12},{10,14},{12... | collective-permute-start | bytes 245768 | tf_op jit(solution)/shard_map/ppermute | solution.py:507

commit v7 on v5

--- a/solution.py
+++ b/solution.py
@@ -117,16 +117,7 @@
             compiler_params=pltpu.CompilerParams(vmem_limit_bytes=61 * MIB),
             name="prep_own_plane",
         )(images, index, noise, sig)
-        oth, shared = pl.pallas_call(
-            functools.partial(rest_kernel, n, wo, ws),
-            in_specs=[somewhere, vmem],
-            out_specs=[vmem] * 2,
-            out_shape=[jax.ShapeDtypeStruct((rows, n * wo), BF16), jax.ShapeDtypeStruct((rows, n * ws), BF16)],
-            scratch_shapes=[pltpu.VMEM((rows, n * (wo + ws)), BF16), pltpu.SemaphoreType.DMA((2 * n,))],
-            compiler_params=pltpu.CompilerParams(vmem_limit_bytes=58 * MIB),
-            name="prep_rest",
-        )(images, weight)
-        return own, oth, shared, weight
+        return own, None, None, weight
     weight = full_weights(weight_of)
     weighted = (images.astype(F32) * weight).astype(BF16).reshape(rows, n, 2, half)
     mine = lax.dynamic_index_in_dim(weighted, core, 2, keepdims=False)
@@ -149,7 +140,7 @@
     return own, oth, mine[:, :, 2 * wo :].reshape(rows, -1)
 
 
-def split_kernel(wo, ws, n, proj_hbm, keep_ref, send_ref, sems):
+def split_kernel(wo, ws, n, proj_hbm, keep_ref, send_ref, sems, meanwhile):
     half = 2 * wo + ws
     cls, owner = lax.axis_index("cls"), lax.axis_index("ori")
     core, side = cls % 2, (cls // 2) % 2
@@ -169,8 +160,13 @@
     gate = jnp.where(lane == owner, MASKED, 0.0).astype(BF16)
     keep_ref[:, n * wo : n * wo + LANES] = gate
     send_ref[:, n * wo : n * wo + LANES] = gate
+    meanwhile()
     for copy in copies:
         copy.wait()
+
+
+def prep_kernel(n, wo, ws, img_hbm, proj_hbm, w_ref, oth_ref, shared_ref, keep_ref, send_ref, img, img_sems, sems):
+    split_kernel(wo, ws, n, proj_hbm, keep_ref, send_ref, sems, lambda: rest_kernel(n, wo, ws, img_hbm, w_ref, oth_ref, shared_ref, img, img_sems))
 
 
 def norm_kernel(wo, ws, n, keep_ref, send_ref, prior_ref, w_ref, bias_ref):
@@ -198,22 +194,29 @@
     bias_ref[...] = jnp.broadcast_to(prior - half_norm, bias_ref.shape)
 
 
-def prep_projections(projections, weight, log_prior, core, side, owner, wo, ws, n):
+def prep_projections(images, projections, weight, log_prior, core, side, owner, wo, ws, n):
     rows = projections.shape[1]
     half = 2 * wo + ws
     width = n * half + LANES
     if wo % LANES == 0:
         vmem = pl.BlockSpec(memory_space=pltpu.VMEM)
-        keep, send = pl.pallas_call(
-            functools.partial(split_kernel, wo, ws, n),
-            in_specs=[pl.BlockSpec(memory_space=pl.ANY)],
-            out_specs=[vmem] * 2,
-            out_shape=[jax.ShapeDtypeStruct((rows, width), BF16)] * 2,
-            scratch_shapes=[pltpu.SemaphoreType.DMA((6 * n,))],
+        somewhere = pl.BlockSpec(memory_space=pl.ANY)
+        pixels = images.shape[0]
+        oth, shared, keep, send = pl.pallas_call(
+            functools.partial(prep_kernel, n, wo, ws),
+            in_specs=[somewhere, somewhere, vmem],
+            out_specs=[vmem] * 4,
+            out_shape=[jax.ShapeDtypeStruct((pixels, n * w), BF16) for w in (wo, ws)]
+            + [jax.ShapeDtypeStruct((rows, width), BF16)] * 2,
+            scratch_shapes=[
+                pltpu.VMEM((pixels, n * (wo + ws)), BF16),
+                pltpu.SemaphoreType.DMA((2 * n,)),
+                pltpu.SemaphoreType.DMA((6 * n,)),
+            ],
             compiler_params=pltpu.CompilerParams(vmem_limit_bytes=54 * MIB),
             cost_estimate=pl.CostEstimate(flops=0, bytes_accessed=4 * projections.size, transcendentals=0),
-            name="split_projections",
-        )(projections)
+            name="prep_rest",
+        )(images, projections, weight)
         bias = pl.pallas_call(
             functools.partial(norm_kernel, wo, ws, n),
             in_specs=[vmem] * 4,
@@ -223,7 +226,7 @@
             cost_estimate=pl.CostEstimate(flops=3 * projections.size, bytes_accessed=2 * projections.size, transcendentals=0),
             name="half_norms",
         )(keep, send, log_prior, weight)
-        return keep, send, bias
+        return oth, shared, keep, send, bias
     projection, prior = projections[0], log_prior.reshape(rows, 1)
     half_norm = 0.5 * jnp.sum(jnp.square(projection.astype(F32)) * weight, axis=1, keepdims=True)
     bias = jnp.broadcast_to(prior - half_norm, (rows, LANES))
@@ -234,7 +237,7 @@
     for which in (core, 1 - core):
         own, oth, shared = cut(lax.dynamic_index_in_dim(split, which, 2, keepdims=False), side, wo)
         both.append(jnp.concatenate([own, gate, shared, oth], axis=1))
-    return both[0], both[1], bias
+    return None, None, both[0], both[1], bias
 
 
 def pack_kernel(pieces, *refs):
@@ -508,7 +511,9 @@
     weight_of = (shell_index.reshape(freqs // LANES, LANES), noise_inv.reshape(1, -1))
     own, oth, shared, weight = prep_images(images, weight_of, significant, core, side, wo, ws, n)
     projections, own = tie(projections, own)
-    keep, send, bias = prep_projections(projections, weight, log_prior, core, side, owner, wo, ws, n)
+    rest_o, rest_s, keep, send, bias = prep_projections(images, projections, weight, log_prior, core, side, owner, wo, ws, n)
+    if oth is None:
+        oth, shared = rest_o, rest_s
 
     every = slice(0, rows)
     plane_w, shared_w = n * wo + LANES, n * ws

time: 124 us -> 125 us (level)
  waiting for transfers between devices: 64.2 us -> 65.8 us
  Pallas kernels: 26.4 us -> 24.9 us
    ppermute x17, waiting for transfers between devices: 31.3 us -> 32.8 us  [ring(): lax.ppermute(x, 'ori', [(cycle[i], cycle[(i + d) % n]) for i in range(n)])]
    pallas_call x2 -> x1, Pallas kernels: 9.09 us -> 7.6 us  [prep_projections(): pl.pallas_call(functools.partial(prep_kernel, n, wo, ws), in_specs=[somew...]
    unnamed x14 -> x16, local copies, waits for them, and re-layouts: 1.87 us -> 2.91 us
  transfers between devices with their start and end apart: 31 -> 31, of which waited for: 17 -> 17; matrix products, arithmetic and copies ran while one was open for 0% -> 0% of each run, Pallas kernels for 15% -> 14%
where the time goes in v7:
time: 125 us
  waiting for transfers between devices  65.8 us (53%)
  starting transfers between devices  30.5 us (24%)
  Pallas kernels  24.9 us (20%)
  local copies, waits for them, and re-layouts  2.91 us (2%)
    ppermute x17, waiting for transfers between devices, ring(): lax.ppermute(x, 'ori', [(cycle[i], cycle[(i + d) % n]) for i in range(n)])  32.8 us
    ppermute x4, waiting for transfers between devices, cross(): return lax.ppermute(x, 'cls', [(i, i ^ 2) for i in range(n_cls)])  29 us
    ppermute x17, starting transfers between devices, ring(): lax.ppermute(x, 'ori', [(cycle[i], cycle[(i + d) % n]) for i in range(n)])  22.1 us
    pallas_call x1, Pallas kernels, prep_projections(): pl.pallas_call(functools.partial(prep_kernel, n, wo, ws), in_specs=[somew...  7.6 us
    pallas_call x4, Pallas kernels, group_scores(): pl.pallas_call(functools.partial(score_kernel, wo, ws, numbered, aligned,...  6.45 us
    ppermute x4, starting transfers between devices, cross(): return lax.ppermute(x, 'cls', [(i, i ^ 2) for i in range(n_cls)])  5.91 us
    pallas_call x1, Pallas kernels, body(): pl.pallas_call(functools.partial(stream_kernel, n, ori_rows, cycle), in_s...  5.17 us
    ppermute x1, waiting for transfers between devices, body(): lax.ppermute(stats, 'cls', [(i, (i + 2 * j) % n_cls) for i in range(n_cls)])  3.04 us
  transfers between devices with their start and end apart: 31, of which 17 were waited for; matrix products, arithmetic and copies ran while one was open for 0% of the time, Pallas kernels for 14%

profile of v7, /device:TPU:0, one launch (start us, length us, event | category | flops | bytes accessed | tf_op | source)
XLA Modules:
  0.0 125.0 jit_solution(6880546127718614229)
XLA Ops:
  0.6 2.0 %prep_own_plane.1 = (bf16[64,3200]{1,0:T(8,128)(2,1)}, f32[160,128]{1,0:T(8,128)}) custom-call(bf16[64,20480]{1,0:T(8,128)(2,1)} %img_hbm.3, s32[160,128]{1,0:T(8,128)} %bitcast.5, f32[1,100]{1,0:T(1,128)} %bitcast.7, s32[4,64]{1,0:T(4,128)} %bitcast.6), custom_call_target="tpu_custom_call" | custom-call | tf_op jit(solution)/shard_map/prep_own_plane/pallas_call | solution.py:105
  2.7 3.0 %collective-permute-start.1 = (bf16[64,3200]{1,0:T(8,128)(2,1)}, bf16[64,3200]{1,0:T(8,128)(2,1)S(1)}, u32[]{:S(2)}, u32[]{:S(2)}) collective-permute-start(bf16[64,3200]{1,0:T(8,128)(2,1)} %get-tuple-element.58.refs_0_), channel_id=1, source_target_pairs={{0,1},{2,0},{4,2},{6,4},{7,6},{5,7},{3,5},{1,3},{8,9},{10,8},{12,1... | collective-permute-start | bytes 1228808 | tf_op jit(solution)/shard_map/ppermute | solution.py:503
  5.7 0.1 collective-permute-start
  5.8 7.6 %prep_rest.1 = (bf16[64,3072]{1,0:T(8,128)(2,1)}, bf16[64,4096]{1,0:T(8,128)(2,1)}, bf16[144,10368]{1,0:T(8,128)(2,1)}, bf16[144,10368]{1,0:T(8,128)(2,1)}) custom-call(bf16[64,20480]{1,0:T(8,128)(2,1)} %img_hbm.3, bf16[1,144,20480]{2,1,0:T(8,128)(2,1)} %proj_hbm, f32[160,128]{1,0:T(8,128)} %get-tuple-element.56.w_ref), custom_call_target="tpu_custom_call" | custom-call | bytes 11796480 | tf_op jit(solution)/shard_map/prep_rest/pallas_call | solution.py:205
  13.4 0.0 copy-start
  13.4 2.0 %collective-permute-done.1.refs_1_ = bf16[64,3200]{1,0:T(8,128)(2,1)S(1)} collective-permute-done((bf16[64,3200]{1,0:T(8,128)(2,1)}, bf16[64,3200]{1,0:T(8,128)(2,1)S(1)}, u32[]{:S(2)}, u32[]{:S(2)}) %collective-permute-start.1) | collective-permute-done | bytes 409632 | tf_op jit(solution)/shard_map/ppermute | solution.py:503
  15.4 1.4 %collective-permute-done.refs_0_ = bf16[64,3200]{1,0:T(8,128)(2,1)S(1)} collective-permute-done((bf16[64,3200]{1,0:T(8,128)(2,1)}, bf16[64,3200]{1,0:T(8,128)(2,1)S(1)}, u32[]{:S(2)}, u32[]{:S(2)}) %collective-permute-start) | collective-permute-done | bytes 409632 | tf_op jit(solution)/shard_map/ppermute | solution.py:503
  16.8 0.0 collective-permute-start.5
  16.8 1.0 copy-done.2
  17.9 0.2 pack.4
  18.1 0.5 collective-permute-start.2
  18.5 1.6 %collective-permute-start.3 = (bf16[64,7296]{1,0:T(8,128)(2,1)S(1)}, bf16[64,7296]{1,0:T(8,128)(2,1)S(1)}, u32[]{:S(2)}, u32[]{:S(2)}) collective-permute-start(bf16[64,7296]{1,0:T(8,128)(2,1)S(1)} %get-tuple-element.65.refs_1_), channel_id=1, source_target_pairs={{0,1},{2,0},{4,2},{6,4},{7,6},{5,7},{3,5},{1,3},{8,9},{10,8},{12,1... | collective-permute-start | bytes 2801672 | tf_op jit(solution)/shard_map/ppermute | solution.py:503
  20.1 1.5 %collective-permute-start.4 = (bf16[128,3072]{1,0:T(8,128)(2,1)S(1)}, bf16[128,3072]{1,0:T(8,128)(2,1)S(1)}, u32[]{:S(2)}, u32[]{:S(2)}) collective-permute-start(bf16[128,3072]{1,0:T(8,128)(2,1)S(1)} %get-tuple-element.66), channel_id=1, source_target_pairs={{0,16},{8,24},{16,0},{24,8},{1,17},{9,25},{17,1},{25,9},{2,18},{10... | collective-permute-start | bytes 2359304 | tf_op jit(solution)/shard_map/ppermute | solution.py:509
  21.6 17.9 %collective-permute-done.4.refs_4_ = bf16[128,3072]{1,0:T(8,128)(2,1)S(1)} collective-permute-done((bf16[128,3072]{1,0:T(8,128)(2,1)S(1)}, bf16[128,3072]{1,0:T(8,128)(2,1)S(1)}, u32[]{:S(2)}, u32[]{:S(2)}) %collective-permute-start.4) | collective-permute-done | bytes 786464 | tf_op jit(solution)/shard_map/ppermute | solution.py:509
  39.5 1.7 %collective-permute-done.2.refs_0_.refs_2_ = bf16[64,7296]{1,0:T(8,128)(2,1)S(1)} collective-permute-done((bf16[64,7296]{1,0:T(8,128)(2,1)S(1)}, bf16[64,7296]{1,0:T(8,128)(2,1)S(1)}, u32[]{:S(2)}, u32[]{:S(2)}) %collective-permute-start.2) | collective-permute-done | bytes 933920 | tf_op jit(solution)/shard_map/ppermute | solution.py:503
  41.2 0.1 collective-permute-done.3.refs_1_.refs_3_
  41.3 0.0 collective-permute-done.5.mate_ref
  41.4 1.7 %collective-permute-start.6 = (bf16[64,7296]{1,0:T(8,128)(2,1)S(1)}, bf16[64,7296]{1,0:T(8,128)(2,1)S(1)}, u32[]{:S(2)}, u32[]{:S(2)}) collective-permute-start(bf16[64,7296]{1,0:T(8,128)(2,1)S(1)} %collective-permute-done.2.refs_0_.refs_2_), channel_id=1, source_target_pairs={{0,2},{2,4},{4,6},{6,7},{7,5},{5,3},{3,1},{1,0},{8,10},{10,12},{12... | collective-permute-start | bytes 2801672 | tf_op jit(solution)/shard_map/ppermute | solution.py:503
  43.0 0.3 collective-permute-start.7
  43.4 0.1 pack.5
  43.4 1.7 %collective-permute-start.8 = (bf16[128,3072]{1,0:T(8,128)(2,1)S(1)}, bf16[128,3072]{1,0:T(8,128)(2,1)S(1)}, u32[]{:S(2)}, u32[]{:S(2)}) collective-permute-start(bf16[128,3072]{1,0:T(8,128)(2,1)S(1)} %pack.5), channel_id=1, source_target_pairs={{0,16},{8,24},{16,0},{24,8},{1,17},{9,25},{17,1},{25,9},{2,18},{10... | collective-permute-start | bytes 2359304 | tf_op jit(solution)/shard_map/ppermute | solution.py:509
  45.1 1.8 %copy-done.1 = bf16[144,10368]{1,0:T(8,128)(2,1)S(1)} copy-done((bf16[144,10368]{1,0:T(8,128)(2,1)S(1)}, bf16[144,10368]{1,0:T(8,128)(2,1)}, u32[]{:S(2)}) %copy-start.1) | copy-done | bytes 2986008
  47.0 2.2 %half_norms.1.bias_ref = f32[144,128]{1,0:T(8,128)S(1)} custom-call(bf16[144,10368]{1,0:T(8,128)(2,1)S(1)} %copy-done, bf16[144,10368]{1,0:T(8,128)(2,1)S(1)} %copy-done.1, f32[1,144]{1,0:T(1,128)S(1)} %copy-done.7, f32[160,128]{1,0:T(8,128)S(1)} %copy-done.6), custom_call_target="tpu_custom_call" | custom-call | flops 8847360 | bytes 5898240 | tf_op jit(solution)/shard_map/half_norms/pallas_call | solution.py:220
  49.1 1.7 %group_scores.4 = (f32[288,128]{1,0:T(8,128)S(1)}, bf16[128,1280]{1,0:T(8,128)(2,1)S(1)}) custom-call(bf16[144,10368]{1,0:T(8,128)(2,1)S(1)} %copy-done, bf16[144,10368]{1,0:T(8,128)(2,1)S(1)} %collective-permute-done.5.mate_ref, f32[144,128]{1,0:T(8,128)S(1)} %half_norms.1.bias_ref, bf16[64,7296]{1,0:T(8,128)(2,1)S(1)} %get-tuple-element.64.refs_0_, ...), custom_call_target="tpu_custom_call" | custom-call | flops 764411904 | bytes 8626176 | tf_op jit(solution)/shard_map/group_scores/pallas_call | solution.py:347
  50.9 11.1 %collective-permute-done.8.refs_4_ = bf16[128,3072]{1,0:T(8,128)(2,1)S(1)} collective-permute-done((bf16[128,3072]{1,0:T(8,128)(2,1)S(1)}, bf16[128,3072]{1,0:T(8,128)(2,1)S(1)}, u32[]{:S(2)}, u32[]{:S(2)}) %collective-permute-start.8) | collective-permute-done | bytes 786464 | tf_op jit(solution)/shard_map/ppermute | solution.py:509
  62.0 1.6 %collective-permute-done.6.refs_0_.refs_2_ = bf16[64,7296]{1,0:T(8,128)(2,1)S(1)} collective-permute-done((bf16[64,7296]{1,0:T(8,128)(2,1)S(1)}, bf16[64,7296]{1,0:T(8,128)(2,1)S(1)}, u32[]{:S(2)}, u32[]{:S(2)}) %collective-permute-start.6) | collective-permute-done | bytes 933920 | tf_op jit(solution)/shard_map/ppermute | solution.py:503
  63.6 1.2 collective-permute-done.7.refs_1_.refs_3_
  64.8 0.1 pack.6
  64.9 1.6 %collective-permute-start.11 = (bf16[128,3072]{1,0:T(8,128)(2,1)S(1)}, bf16[128,3072]{1,0:T(8,128)(2,1)S(1)}, u32[]{:S(2)}, u32[]{:S(2)}) collective-permute-start(bf16[128,3072]{1,0:T(8,128)(2,1)S(1)} %get-tuple-element.78), channel_id=1, source_target_pairs={{0,16},{8,24},{16,0},{24,8},{1,17},{9,25},{17,1},{25,9},{2,18},{10... | collective-permute-start | bytes 2359304 | tf_op jit(solution)/shard_map/ppermute | solution.py:509
  66.5 0.5 collective-permute-start.10
  67.0 1.5 %collective-permute-start.9 = (bf16[64,5632]{1,0:T(8,128)(2,1)S(1)}, bf16[64,5632]{1,0:T(8,128)(2,1)S(1)}, u32[]{:S(2)}, u32[]{:S(2)}) collective-permute-start(bf16[64,5632]{1,0:T(8,128)(2,1)S(1)} %get-tuple-element.76), channel_id=1, source_target_pairs={{0,2},{2,4},{4,6},{6,7},{7,5},{5,3},{3,1},{1,0},{8,10},{10,12},{12... | collective-permute-start | bytes 2162696 | tf_op jit(solution)/shard_map/ppermute | solution.py:503
  68.5 1.7 %group_scores.5 = (f32[288,128]{1,0:T(8,128)S(1)}, bf16[128,1280]{1,0:T(8,128)(2,1)S(1)}) custom-call(bf16[144,10368]{1,0:T(8,128)(2,1)S(1)} %copy-done, bf16[144,10368]{1,0:T(8,128)(2,1)S(1)} %collective-permute-done.5.mate_ref, f32[144,128]{1,0:T(8,128)S(1)} %half_norms.1.bias_ref, bf16[64,7296]{1,0:T(8,128)(2,1)S(1)} %collective-permute-done.2.refs_0_.refs_2_, ...), custom_call_target="tpu_custom_call" | custom-call | flops 764411904 | bytes 8626176 | tf_op jit(solution)/shard_map/group_scores/pallas_call | solution.py:347
  70.2 12.7 %collective-permute-done.9.refs_0_.refs_2_ = bf16[64,5632]{1,0:T(8,128)(2,1)S(1)} collective-permute-done((bf16[64,5632]{1,0:T(8,128)(2,1)S(1)}, bf16[64,5632]{1,0:T(8,128)(2,1)S(1)}, u32[]{:S(2)}, u32[]{:S(2)}) %collective-permute-start.9) | collective-permute-done | bytes 720928 | tf_op jit(solution)/shard_map/ppermute | solution.py:503
  83.0 0.0 collective-permute-done.10.refs_1_.refs_3_
  83.0 0.0 collective-permute-done.11.refs_4_
  83.0 0.1 pack.7
  83.1 1.2 collective-permute-start.14
  84.3 1.6 %collective-permute-start.12 = (bf16[64,2048]{1,0:T(8,128)(2,1)S(1)}, bf16[64,2048]{1,0:T(8,128)(2,1)S(1)}, u32[]{:S(2)}, u32[]{:S(2)}) collective-permute-start(bf16[64,2048]{1,0:T(8,128)(2,1)S(1)} %get-tuple-element.84), channel_id=1, source_target_pairs={{0,2},{2,4},{4,6},{6,7},{7,5},{5,3},{3,1},{1,0},{8,10},{10,12},{12... | collective-permute-start | bytes 786440 | tf_op jit(solution)/shard_map/ppermute | solution.py:503
  85.9 0.4 collective-permute-start.13
  86.3 1.7 %group_scores.7 = (f32[288,128]{1,0:T(8,128)S(1)}, bf16[128,1280]{1,0:T(8,128)(2,1)S(1)}) custom-call(bf16[144,10368]{1,0:T(8,128)(2,1)S(1)} %copy-done, bf16[144,10368]{1,0:T(8,128)(2,1)S(1)} %collective-permute-done.5.mate_ref, f32[144,128]{1,0:T(8,128)S(1)} %half_norms.1.bias_ref, bf16[64,7296]{1,0:T(8,128)(2,1)S(1)} %collective-permute-done.6.refs_0_.refs_2_, ...), custom_call_target="tpu_custom_call" | custom-call | flops 764411904 | bytes 8626176 | tf_op jit(solution)/shard_map/group_scores/pallas_call | solution.py:347
  88.1 0.6 collective-permute-start.18
  88.7 0.6 plane_scores.1.bias_ref
  89.3 1.4 %collective-permute-done.12.refs_3_ = bf16[64,2048]{1,0:T(8,128)(2,1)S(1)} collective-permute-done((bf16[64,2048]{1,0:T(8,128)(2,1)S(1)}, bf16[64,2048]{1,0:T(8,128)(2,1)S(1)}, u32[]{:S(2)}, u32[]{:S(2)}) %collective-permute-start.12) | collective-permute-done | bytes 262176 | tf_op jit(solution)/shard_map/ppermute | solution.py:503
  90.7 1.6 %collective-permute-done.13.refs_4_ = bf16[64,2048]{1,0:T(8,128)(2,1)S(1)} collective-permute-done((bf16[64,2048]{1,0:T(8,128)(2,1)S(1)}, bf16[64,2048]{1,0:T(8,128)(2,1)S(1)}, u32[]{:S(2)}, u32[]{:S(2)}) %collective-permute-start.13) | collective-permute-done | bytes 262176 | tf_op jit(solution)/shard_map/ppermute | solution.py:503
  92.3 1.2 group_scores.6
  93.5 0.1 collective-permute-start.15
  93.6 0.5 collective-permute-start.28
  94.1 0.8 collective-permute-done.15.refs_4_
  94.9 0.3 local_stats.1
  95.2 0.7 collective-permute-start.19
  95.9 3.0 %collective-permute-done.19.refs_1_ = f32[8,512]{1,0:T(8,128)S(1)} collective-permute-done((f32[8,512]{1,0:T(8,128)S(1)}, f32[8,512]{1,0:T(8,128)S(1)}, u32[]{:S(2)}, u32[]{:S(2)}) %collective-permute-start.19) | collective-permute-done | bytes 16416 | tf_op jit(solution)/shard_map/ppermute | solution.py:605
  99.0 0.1 payload.1.refs_0_
  99.0 0.6 collective-permute-start.24
  99.6 1.5 %collective-permute-start.20 = (bf16[160,512]{1,0:T(8,128)(2,1)S(1)}, bf16[160,512]{1,0:T(8,128)(2,1)S(1)}, u32[]{:S(2)}, u32[]{:S(2)}) collective-permute-start(bf16[160,512]{1,0:T(8,128)(2,1)S(1)} %payload.1.refs_0_), channel_id=1, source_target_pairs={{0,2},{2,4},{4,6},{6,7},{7,5},{5,3},{3,1},{1,0},{8,10},{10,12},{12... | collective-permute-start | bytes 491528 | tf_op jit(solution)/shard_map/ppermute | solution.py:503
  101.1 0.5 collective-permute-start.27
  101.6 2.8 %collective-permute-done.24.refs_7_ = bf16[160,512]{1,0:T(8,128)(2,1)S(1)} collective-permute-done((bf16[160,512]{1,0:T(8,128)(2,1)S(1)}, bf16[160,512]{1,0:T(8,128)(2,1)S(1)}, u32[]{:S(2)}, u32[]{:S(2)}) %collective-permute-start.24) | collective-permute-done | bytes 163872 | tf_op jit(solution)/shard_map/ppermute | solution.py:503
  104.4 0.5 collective-permute-start.25
  104.9 1.5 %collective-permute-start.21 = (bf16[160,512]{1,0:T(8,128)(2,1)S(1)}, bf16[160,512]{1,0:T(8,128)(2,1)S(1)}, u32[]{:S(2)}, u32[]{:S(2)}) collective-permute-start(bf16[160,512]{1,0:T(8,128)(2,1)S(1)} %collective-permute-done.20.refs_1_), channel_id=1, source_target_pairs={{0,2},{2,4},{4,6},{6,7},{7,5},{5,3},{3,1},{1,0},{8,10},{10,12},{12... | collective-permute-start | bytes 491528 | tf_op jit(solution)/shard_map/ppermute | solution.py:503
  106.5 2.9 %collective-permute-start.23 = (bf16[160,512]{1,0:T(8,128)(2,1)S(1)}, bf16[160,512]{1,0:T(8,128)(2,1)S(1)}, u32[]{:S(2)}, u32[]{:S(2)}) collective-permute-start(bf16[160,512]{1,0:T(8,128)(2,1)S(1)} %payload.1.refs_0_), channel_id=1, source_target_pairs={{0,7},{2,5},{4,3},{6,1},{7,0},{5,2},{3,4},{1,6},{8,15},{10,13},{12... | collective-permute-start | bytes 491528 | tf_op jit(solution)/shard_map/ppermute | solution.py:503
  109.3 3.1 %collective-permute-done.25.refs_6_ = bf16[160,512]{1,0:T(8,128)(2,1)S(1)} collective-permute-done((bf16[160,512]{1,0:T(8,128)(2,1)S(1)}, bf16[160,512]{1,0:T(8,128)(2,1)S(1)}, u32[]{:S(2)}, u32[]{:S(2)}) %collective-permute-start.25) | collective-permute-done | bytes 163872 | tf_op jit(solution)/shard_map/ppermute | solution.py:503
  112.5 3.9 %collective-permute-start.22 = (bf16[160,512]{1,0:T(8,128)(2,1)S(1)}, bf16[160,512]{1,0:T(8,128)(2,1)S(1)}, u32[]{:S(2)}, u32[]{:S(2)}) collective-permute-start(bf16[160,512]{1,0:T(8,128)(2,1)S(1)} %collective-permute-done.21.refs_2_), channel_id=1, source_target_pairs={{0,2},{2,4},{4,6},{6,7},{7,5},{5,3},{3,1},{1,0},{8,10},{10,12},{12... | collective-permute-start | bytes 491528 | tf_op jit(solution)/shard_map/ppermute | solution.py:503
  116.3 0.3 collective-permute-done.23.refs_4_
  116.7 3.0 %collective-permute-done.26.refs_5_ = bf16[160,512]{1,0:T(8,128)(2,1)S(1)} collective-permute-done((bf16[160,512]{1,0:T(8,128)(2,1)S(1)}, bf16[160,512]{1,0:T(8,128)(2,1)S(1)}, u32[]{:S(2)}, u32[]{:S(2)}) %collective-permute-start.26) | collective-permute-done | bytes 163872 | tf_op jit(solution)/shard_map/ppermute | solution.py:503
  119.6 5.2 %class_sums.1 = (bf16[1152,2560]{1,0:T(8,128)(2,1)}, f32[1,64]{1,0:T(1,128)}) custom-call(bf16[160,512]{1,0:T(8,128)(2,1)S(1)} %payload.1.refs_0_, bf16[160,512]{1,0:T(8,128)(2,1)S(1)} %collective-permute-done.20.refs_1_, bf16[160,512]{1,0:T(8,128)(2,1)S(1)} %collective-permute-done.21.refs_2_, bf16[160,512]{1,0:T(8,128)(2,1)S(1)} %collective-permute-done.22.refs_3_, ...), custom_call_target="tpu_custom_call" | custom-call | tf_op jit(solution)/shard_map/class_sums/pallas_call | solution.py:626
  (29 shorter events, 0.1 us)
Async XLA Ops:
  2.7 12.8 %collective-permute-start.1 = (bf16[64,3200]{1,0:T(8,128)(2,1)}, bf16[64,3200]{1,0:T(8,128)(2,1)S(1)}, u32[]{:S(2)}, u32[]{:S(2)}) collective-permute-start(bf16[64,3200]{1,0:T(8,128)(2,1)} %get-tuple-element.58.refs_0_), channel_id=1, source_target_pairs={{0,1},{2,0},{4,2},{6,4},{7,6},{5,7},{3,5},{1,3},{8,9},{10,8},{12,1... | collective-permute-start | bytes 1228808 | tf_op jit(solution)/shard_map/ppermute | solution.py:503
  5.7 11.1 %collective-permute-start = (bf16[64,3200]{1,0:T(8,128)(2,1)}, bf16[64,3200]{1,0:T(8,128)(2,1)S(1)}, u32[]{:S(2)}, u32[]{:S(2)}) collective-permute-start(bf16[64,3200]{1,0:T(8,128)(2,1)} %get-tuple-element.58.refs_0_), channel_id=1, source_target_pairs={{0,2},{2,4},{4,6},{6,7},{7,5},{5,3},{3,1},{1,0},{8,10},{10,12},{12... | collective-permute-start | bytes 1228808 | tf_op jit(solution)/shard_map/ppermute | solution.py:503
  5.8 39.3 %copy-start.6 = (f32[160,128]{1,0:T(8,128)S(1)}, f32[160,128]{1,0:T(8,128)}, u32[]{:S(2)}) copy-start(f32[160,128]{1,0:T(8,128)} %get-tuple-element.56.w_ref) | copy-start | bytes 245764
  5.8 39.3 %copy-start.7 = (f32[1,144]{1,0:T(1,128)S(1)}, f32[1,144]{1,0:T(1,128)}, u32[]{:S(2)}) copy-start(f32[1,144]{1,0:T(1,128)} %prior_ref.1) | copy-start | bytes 1732
  13.4 31.7 %copy-start = (bf16[144,10368]{1,0:T(8,128)(2,1)S(1)}, bf16[144,10368]{1,0:T(8,128)(2,1)}, u32[]{:S(2)}) copy-start(bf16[144,10368]{1,0:T(8,128)(2,1)} %get-tuple-element.57.keep_ref.own_ref) | copy-start | bytes 8957956
  16.8 24.5 %collective-permute-start.5 = (bf16[144,10368]{1,0:T(8,128)(2,1)}, bf16[144,10368]{1,0:T(8,128)(2,1)S(1)}, u32[]{:S(2)}, u32[]{:S(2)}) collective-permute-start(bf16[144,10368]{1,0:T(8,128)(2,1)} %get-tuple-element.67.send_ref), channel_id=1, source_target_pairs={{0,8},{8,0},{16,24},{24,16},{1,9},{9,1},{17,25},{25,17},{2,10},{10... | collective-permute-start | bytes 8957960 | tf_op jit(solution)/shard_map/ppermute | solution.py:506
  16.8 1.0 copy-start.2
  18.1 23.2 %collective-permute-start.2 = (bf16[64,7296]{1,0:T(8,128)(2,1)S(1)}, bf16[64,7296]{1,0:T(8,128)(2,1)S(1)}, u32[]{:S(2)}, u32[]{:S(2)}) collective-permute-start(bf16[64,7296]{1,0:T(8,128)(2,1)S(1)} %get-tuple-element.64.refs_0_), channel_id=1, source_target_pairs={{0,2},{2,4},{4,6},{6,7},{7,5},{5,3},{3,1},{1,0},{8,10},{10,12},{12... | collective-permute-start | bytes 2801672 | tf_op jit(solution)/shard_map/ppermute | solution.py:503
  18.5 22.8 %collective-permute-start.3 = (bf16[64,7296]{1,0:T(8,128)(2,1)S(1)}, bf16[64,7296]{1,0:T(8,128)(2,1)S(1)}, u32[]{:S(2)}, u32[]{:S(2)}) collective-permute-start(bf16[64,7296]{1,0:T(8,128)(2,1)S(1)} %get-tuple-element.65.refs_1_), channel_id=1, source_target_pairs={{0,1},{2,0},{4,2},{6,4},{7,6},{5,7},{3,5},{1,3},{8,9},{10,8},{12,1... | collective-permute-start | bytes 2801672 | tf_op jit(solution)/shard_map/ppermute | solution.py:503
  20.1 19.4 %collective-permute-start.4 = (bf16[128,3072]{1,0:T(8,128)(2,1)S(1)}, bf16[128,3072]{1,0:T(8,128)(2,1)S(1)}, u32[]{:S(2)}, u32[]{:S(2)}) collective-permute-start(bf16[128,3072]{1,0:T(8,128)(2,1)S(1)} %get-tuple-element.66), channel_id=1, source_target_pairs={{0,16},{8,24},{16,0},{24,8},{1,17},{9,25},{17,1},{25,9},{2,18},{10... | collective-permute-start | bytes 2359304 | tf_op jit(solution)/shard_map/ppermute | solution.py:509
  41.4 22.2 %collective-permute-start.6 = (bf16[64,7296]{1,0:T(8,128)(2,1)S(1)}, bf16[64,7296]{1,0:T(8,128)(2,1)S(1)}, u32[]{:S(2)}, u32[]{:S(2)}) collective-permute-start(bf16[64,7296]{1,0:T(8,128)(2,1)S(1)} %collective-permute-done.2.refs_0_.refs_2_), channel_id=1, source_target_pairs={{0,2},{2,4},{4,6},{6,7},{7,5},{5,3},{3,1},{1,0},{8,10},{10,12},{12... | collective-permute-start | bytes 2801672 | tf_op jit(solution)/shard_map/ppermute | solution.py:503
  43.0 21.7 %collective-permute-start.7 = (bf16[64,7296]{1,0:T(8,128)(2,1)S(1)}, bf16[64,7296]{1,0:T(8,128)(2,1)S(1)}, u32[]{:S(2)}, u32[]{:S(2)}) collective-permute-start(bf16[64,7296]{1,0:T(8,128)(2,1)S(1)} %collective-permute-done.3.refs_1_.refs_3_), channel_id=1, source_target_pairs={{0,1},{2,0},{4,2},{6,4},{7,6},{5,7},{3,5},{1,3},{8,9},{10,8},{12,1... | collective-permute-start | bytes 2801672 | tf_op jit(solution)/shard_map/ppermute | solution.py:503
  43.4 18.6 %collective-permute-start.8 = (bf16[128,3072]{1,0:T(8,128)(2,1)S(1)}, bf16[128,3072]{1,0:T(8,128)(2,1)S(1)}, u32[]{:S(2)}, u32[]{:S(2)}) collective-permute-start(bf16[128,3072]{1,0:T(8,128)(2,1)S(1)} %pack.5), channel_id=1, source_target_pairs={{0,16},{8,24},{16,0},{24,8},{1,17},{9,25},{17,1},{25,9},{2,18},{10... | collective-permute-start | bytes 2359304 | tf_op jit(solution)/shard_map/ppermute | solution.py:509
  45.1 1.8 %copy-start.1 = (bf16[144,10368]{1,0:T(8,128)(2,1)S(1)}, bf16[144,10368]{1,0:T(8,128)(2,1)}, u32[]{:S(2)}) copy-start(bf16[144,10368]{1,0:T(8,128)(2,1)} %get-tuple-element.67.send_ref) | copy-start | bytes 8957956
  64.9 18.1 %collective-permute-start.11 = (bf16[128,3072]{1,0:T(8,128)(2,1)S(1)}, bf16[128,3072]{1,0:T(8,128)(2,1)S(1)}, u32[]{:S(2)}, u32[]{:S(2)}) collective-permute-start(bf16[128,3072]{1,0:T(8,128)(2,1)S(1)} %get-tuple-element.78), channel_id=1, source_target_pairs={{0,16},{8,24},{16,0},{24,8},{1,17},{9,25},{17,1},{25,9},{2,18},{10... | collective-permute-start | bytes 2359304 | tf_op jit(solution)/shard_map/ppermute | solution.py:509
  66.5 16.5 %collective-permute-start.10 = (bf16[64,5760]{1,0:T(8,128)(2,1)S(1)}, bf16[64,5760]{1,0:T(8,128)(2,1)S(1)}, u32[]{:S(2)}, u32[]{:S(2)}) collective-permute-start(bf16[64,5760]{1,0:T(8,128)(2,1)S(1)} %get-tuple-element.77), channel_id=1, source_target_pairs={{0,1},{2,0},{4,2},{6,4},{7,6},{5,7},{3,5},{1,3},{8,9},{10,8},{12,1... | collective-permute-start | bytes 2211848 | tf_op jit(solution)/shard_map/ppermute | solution.py:503
  67.0 16.0 %collective-permute-start.9 = (bf16[64,5632]{1,0:T(8,128)(2,1)S(1)}, bf16[64,5632]{1,0:T(8,128)(2,1)S(1)}, u32[]{:S(2)}, u32[]{:S(2)}) collective-permute-start(bf16[64,5632]{1,0:T(8,128)(2,1)S(1)} %get-tuple-element.76), channel_id=1, source_target_pairs={{0,2},{2,4},{4,6},{6,7},{7,5},{5,3},{3,1},{1,0},{8,10},{10,12},{12... | collective-permute-start | bytes 2162696 | tf_op jit(solution)/shard_map/ppermute | solution.py:503
  83.1 9.2 %collective-permute-start.14 = (bf16[64,3072]{1,0:T(8,128)(2,1)S(1)}, bf16[64,3072]{1,0:T(8,128)(2,1)S(1)}, u32[]{:S(2)}, u32[]{:S(2)}) collective-permute-start(bf16[64,3072]{1,0:T(8,128)(2,1)S(1)} %get-tuple-element.86), channel_id=1, source_target_pairs={{0,16},{8,24},{16,0},{24,8},{1,17},{9,25},{17,1},{25,9},{2,18},{10... | collective-permute-start | bytes 1179656 | tf_op jit(solution)/shard_map/ppermute | solution.py:509
  84.3 6.4 %collective-permute-start.12 = (bf16[64,2048]{1,0:T(8,128)(2,1)S(1)}, bf16[64,2048]{1,0:T(8,128)(2,1)S(1)}, u32[]{:S(2)}, u32[]{:S(2)}) collective-permute-start(bf16[64,2048]{1,0:T(8,128)(2,1)S(1)} %get-tuple-element.84), channel_id=1, source_target_pairs={{0,2},{2,4},{4,6},{6,7},{7,5},{5,3},{3,1},{1,0},{8,10},{10,12},{12... | collective-permute-start | bytes 786440 | tf_op jit(solution)/shard_map/ppermute | solution.py:503
  85.9 2.8 %copy-start.4 = (bf16[64,3200]{1,0:T(8,128)(2,1)S(1)}, bf16[64,3200]{1,0:T(8,128)(2,1)}, u32[]{:S(2)}) copy-start(bf16[64,3200]{1,0:T(8,128)(2,1)} %get-tuple-element.58.refs_0_) | copy-start | bytes 1228804
  85.9 6.4 %collective-permute-start.13 = (bf16[64,2048]{1,0:T(8,128)(2,1)S(1)}, bf16[64,2048]{1,0:T(8,128)(2,1)S(1)}, u32[]{:S(2)}, u32[]{:S(2)}) collective-permute-start(bf16[64,2048]{1,0:T(8,128)(2,1)S(1)} %get-tuple-element.85), channel_id=1, source_target_pairs={{0,1},{2,0},{4,2},{6,4},{7,6},{5,7},{3,5},{1,3},{8,9},{10,8},{12,1... | collective-permute-start | bytes 786440 | tf_op jit(solution)/shard_map/ppermute | solution.py:503
  86.3 7.8 %collective-permute-start.16 = (f32[288,128]{1,0:T(8,128)S(1)}, f32[288,128]{1,0:T(8,128)S(1)}, u32[]{:S(2)}, u32[]{:S(2)}) collective-permute-start(f32[288,128]{1,0:T(8,128)S(1)} %get-tuple-element.94.refs_1_), channel_id=1, source_target_pairs={{0,8},{8,0},{16,24},{24,16},{1,9},{9,1},{17,25},{25,17},{2,10},{10... | collective-permute-start | bytes 442376 | tf_op jit(solution)/shard_map/ppermute | solution.py:506
  88.1 6.0 %collective-permute-start.18 = (f32[288,128]{1,0:T(8,128)S(1)}, f32[288,128]{1,0:T(8,128)S(1)}, u32[]{:S(2)}, u32[]{:S(2)}) collective-permute-start(f32[288,128]{1,0:T(8,128)S(1)} %get-tuple-element.97.refs_3_), channel_id=1, source_target_pairs={{0,8},{8,0},{16,24},{24,16},{1,9},{9,1},{17,25},{25,17},{2,10},{10... | collective-permute-start | bytes 442376 | tf_op jit(solution)/shard_map/ppermute | solution.py:506
  88.6 3.6 %copy-start.3 = (bf16[64,4096]{1,0:T(8,128)(2,1)S(1)}, bf16[64,4096]{1,0:T(8,128)(2,1)}, u32[]{:S(2)}) copy-start(bf16[64,4096]{1,0:T(8,128)(2,1)} %get-tuple-element.63.refs_2_) | copy-start | bytes 1572868
  88.7 3.6 %copy-start.5 = (bf16[64,3072]{1,0:T(8,128)(2,1)S(1)}, bf16[64,3072]{1,0:T(8,128)(2,1)}, u32[]{:S(2)}) copy-start(bf16[64,3072]{1,0:T(8,128)(2,1)} %get-tuple-element.91.refs_5_) | copy-start | bytes 1179652
  90.7 3.4 %collective-permute-start.17 = (f32[288,128]{1,0:T(8,128)S(1)}, f32[288,128]{1,0:T(8,128)S(1)}, u32[]{:S(2)}, u32[]{:S(2)}) collective-permute-start(f32[288,128]{1,0:T(8,128)S(1)} %get-tuple-element.95.refs_2_), channel_id=1, source_target_pairs={{0,8},{8,0},{16,24},{24,16},{1,9},{9,1},{17,25},{25,17},{2,10},{10... | collective-permute-start | bytes 442376 | tf_op jit(solution)/shard_map/ppermute | solution.py:506
  93.5 1.4 %collective-permute-start.15 = (f32[288,128]{1,0:T(8,128)S(1)}, f32[288,128]{1,0:T(8,128)S(1)}, u32[]{:S(2)}, u32[]{:S(2)}) collective-permute-start(f32[288,128]{1,0:T(8,128)S(1)} %get-tuple-element.93.refs_0_), channel_id=1, source_target_pairs={{0,8},{8,0},{16,24},{24,16},{1,9},{9,1},{17,25},{25,17},{2,10},{10... | collective-permute-start | bytes 442376 | tf_op jit(solution)/shard_map/ppermute | solution.py:506
  93.6 7.6 %collective-permute-start.28 = (bf16[128,1280]{1,0:T(8,128)(2,1)S(1)}, bf16[128,1280]{1,0:T(8,128)(2,1)S(1)}, u32[]{:S(2)}, u32[]{:S(2)}) collective-permute-start(bf16[128,1280]{1,0:T(8,128)(2,1)S(1)} %get-tuple-element.101.refs_9_), channel_id=1, source_target_pairs={{0,8},{8,0},{16,24},{24,16},{1,9},{9,1},{17,25},{25,17},{2,10},{10... | collective-permute-start | bytes 983048 | tf_op jit(solution)/shard_map/ppermute | solution.py:506
  95.2 3.8 %collective-permute-start.19 = (f32[8,512]{1,0:T(8,128)S(1)}, f32[8,512]{1,0:T(8,128)S(1)}, u32[]{:S(2)}, u32[]{:S(2)}) collective-permute-start(f32[8,512]{1,0:T(8,128)S(1)} %get-tuple-element.99.refs_0_), channel_id=1, source_target_pairs={{0,16},{8,24},{16,0},{24,8},{1,17},{9,25},{17,1},{25,9},{2,18},{10... | collective-permute-start | bytes 49160 | tf_op jit(solution)/shard_map/ppermute | solution.py:605
  95.9 10.5 %collective-permute-start.30 = (bf16[128,1280]{1,0:T(8,128)(2,1)S(1)}, bf16[128,1280]{1,0:T(8,128)(2,1)S(1)}, u32[]{:S(2)}, u32[]{:S(2)}) collective-permute-start(bf16[128,1280]{1,0:T(8,128)(2,1)S(1)} %get-tuple-element.103.refs_11_), channel_id=1, source_target_pairs={{0,8},{8,0},{16,24},{24,16},{1,9},{9,1},{17,25},{25,17},{2,10},{10... | collective-permute-start | bytes 983048 | tf_op jit(solution)/shard_map/ppermute | solution.py:506
  99.0 5.4 %collective-permute-start.24 = (bf16[160,512]{1,0:T(8,128)(2,1)S(1)}, bf16[160,512]{1,0:T(8,128)(2,1)S(1)}, u32[]{:S(2)}, u32[]{:S(2)}) collective-permute-start(bf16[160,512]{1,0:T(8,128)(2,1)S(1)} %payload.1.refs_0_), channel_id=1, source_target_pairs={{0,1},{2,0},{4,2},{6,4},{7,6},{5,7},{3,5},{1,3},{8,9},{10,8},{12,1... | collective-permute-start | bytes 491528 | tf_op jit(solution)/shard_map/ppermute | solution.py:503
  99.6 5.3 %collective-permute-start.20 = (bf16[160,512]{1,0:T(8,128)(2,1)S(1)}, bf16[160,512]{1,0:T(8,128)(2,1)S(1)}, u32[]{:S(2)}, u32[]{:S(2)}) collective-permute-start(bf16[160,512]{1,0:T(8,128)(2,1)S(1)} %payload.1.refs_0_), channel_id=1, source_target_pairs={{0,2},{2,4},{4,6},{6,7},{7,5},{5,3},{3,1},{1,0},{8,10},{10,12},{12... | collective-permute-start | bytes 491528 | tf_op jit(solution)/shard_map/ppermute | solution.py:503
  101.1 15.2 %collective-permute-start.29 = (bf16[128,1280]{1,0:T(8,128)(2,1)S(1)}, bf16[128,1280]{1,0:T(8,128)(2,1)S(1)}, u32[]{:S(2)}, u32[]{:S(2)}) collective-permute-start(bf16[128,1280]{1,0:T(8,128)(2,1)S(1)} %get-tuple-element.102.refs_10_), channel_id=1, source_target_pairs={{0,8},{8,0},{16,24},{24,16},{1,9},{9,1},{17,25},{25,17},{2,10},{10... | collective-permute-start | bytes 983048 | tf_op jit(solution)/shard_map/ppermute | solution.py:506
  101.1 15.5 %collective-permute-start.27 = (bf16[128,1280]{1,0:T(8,128)(2,1)S(1)}, bf16[128,1280]{1,0:T(8,128)(2,1)S(1)}, u32[]{:S(2)}, u32[]{:S(2)}) collective-permute-start(bf16[128,1280]{1,0:T(8,128)(2,1)S(1)} %get-tuple-element.100.refs_8_), channel_id=1, source_target_pairs={{0,8},{8,0},{16,24},{24,16},{1,9},{9,1},{17,25},{25,17},{2,10},{10... | collective-permute-start | bytes 983048 | tf_op jit(solution)/shard_map/ppermute | solution.py:506
  104.4 8.0 %collective-permute-start.25 = (bf16[160,512]{1,0:T(8,128)(2,1)S(1)}, bf16[160,512]{1,0:T(8,128)(2,1)S(1)}, u32[]{:S(2)}, u32[]{:S(2)}) collective-permute-start(bf16[160,512]{1,0:T(8,128)(2,1)S(1)} %collective-permute-done.24.refs_7_), channel_id=1, source_target_pairs={{0,1},{2,0},{4,2},{6,4},{7,6},{5,7},{3,5},{1,3},{8,9},{10,8},{12,1... | collective-permute-start | bytes 491528 | tf_op jit(solution)/shard_map/ppermute | solution.py:503
  104.9 7.5 %collective-permute-start.21 = (bf16[160,512]{1,0:T(8,128)(2,1)S(1)}, bf16[160,512]{1,0:T(8,128)(2,1)S(1)}, u32[]{:S(2)}, u32[]{:S(2)}) collective-permute-start(bf16[160,512]{1,0:T(8,128)(2,1)S(1)} %collective-permute-done.20.refs_1_), channel_id=1, source_target_pairs={{0,2},{2,4},{4,6},{6,7},{7,5},{5,3},{3,1},{1,0},{8,10},{10,12},{12... | collective-permute-start | bytes 491528 | tf_op jit(solution)/shard_map/ppermute | solution.py:503
  106.5 10.2 %collective-permute-start.23 = (bf16[160,512]{1,0:T(8,128)(2,1)S(1)}, bf16[160,512]{1,0:T(8,128)(2,1)S(1)}, u32[]{:S(2)}, u32[]{:S(2)}) collective-permute-start(bf16[160,512]{1,0:T(8,128)(2,1)S(1)} %payload.1.refs_0_), channel_id=1, source_target_pairs={{0,7},{2,5},{4,3},{6,1},{7,0},{5,2},{3,4},{1,6},{8,15},{10,13},{12... | collective-permute-start | bytes 491528 | tf_op jit(solution)/shard_map/ppermute | solution.py:503
  112.5 7.2 %collective-permute-start.26 = (bf16[160,512]{1,0:T(8,128)(2,1)S(1)}, bf16[160,512]{1,0:T(8,128)(2,1)S(1)}, u32[]{:S(2)}, u32[]{:S(2)}) collective-permute-start(bf16[160,512]{1,0:T(8,128)(2,1)S(1)} %collective-permute-done.25.refs_6_), channel_id=1, source_target_pairs={{0,1},{2,0},{4,2},{6,4},{7,6},{5,7},{3,5},{1,3},{8,9},{10,8},{12,1... | collective-permute-start | bytes 491528 | tf_op jit(solution)/shard_map/ppermute | solution.py:503
  112.5 7.2 %collective-permute-start.22 = (bf16[160,512]{1,0:T(8,128)(2,1)S(1)}, bf16[160,512]{1,0:T(8,128)(2,1)S(1)}, u32[]{:S(2)}, u32[]{:S(2)}) collective-permute-start(bf16[160,512]{1,0:T(8,128)(2,1)S(1)} %collective-permute-done.21.refs_2_), channel_id=1, source_target_pairs={{0,2},{2,4},{4,6},{6,7},{7,5},{5,3},{3,1},{1,0},{8,10},{10,12},{12... | collective-permute-start | bytes 491528 | tf_op jit(solution)/shard_map/ppermute | solution.py:503
